TPU v7x, 32 devices: a whole 2x2x4 slice. The times are simulated.
32 devices in a mesh: fsdp: 4 (over z), ctx: 4 (over y, x), tp: 2 (over core).
Axes of the slice: x: 2, y: 2, z: 4, core: 2. Of those that a mesh axis runs over, the one named last changes fastest.
Arguments:
- hidden_in: bfloat16 [2, 4, 1024, 1024], P(None, 'fsdp', 'ctx', 'tp'), may hold values from -6 to 6
- lengths: int32 [2, 4], P(None, 'fsdp'), may hold values from 512 to 1024, as said below
- norm_gains: bfloat16 [2, 2, 1024], replicated, may hold values from 0.5 to 1.5
- mamba_zx: bfloat16 [2, 1024, 2, 1536], P(None, ('fsdp', 'ctx'), None, 'tp'), may hold values from -0.1875 to 0.1875
- mamba_shared: bfloat16 [2, 1024, 280], replicated, may hold values from -0.1875 to 0.1875
- conv_weight: bfloat16 [2, 4, 1792], replicated, may hold values from -3 to 3
- conv_bias: bfloat16 [2, 1792], replicated, may hold values from -2 to 2
- head_params: float32 [2, 3, 24], replicated, may hold values from -14 to 3
- mamba_gain: bfloat16 [2, 1536], replicated, may hold values from 0.5 to 1.5
- mamba_out: bfloat16 [2, 1536, 1024], P(None, 'tp', ('fsdp', 'ctx')), may hold values from -0.15625 to 0.15625
- attn_in: bfloat16 [2, 1024, 2, 384], P(None, ('fsdp', 'ctx'), 'tp'), may hold values from -0.1875 to 0.1875
- attn_out: bfloat16 [2, 512, 1024], P(None, 'tp', ('fsdp', 'ctx')), may hold values from -0.75 to 0.75
- mlp_in: bfloat16 [2, 1024, 2, 2048], P(None, ('fsdp', 'ctx'), None, 'tp'), may hold values from -0.1875 to 0.1875
- mlp_out: bfloat16 [2, 2048, 1024], P(None, 'tp', ('fsdp', 'ctx')), may hold values from -0.125 to 0.125
- out_grad: bfloat16 [2, 4, 1024, 1024], P(None, 'fsdp', 'ctx', 'tp'), may hold values from -6 to 6
Outputs:
- mixed_out: bfloat16 [2, 4, 1024, 1024], P(None, 'fsdp', 'ctx', 'tp')
- input_grad: float32 [2, 4, 1024, 1024], P(None, 'fsdp', 'ctx', 'tp')
- grad_norm_gains: float32 [2, 2, 1024], replicated
- grad_mamba_zx: float32 [2, 1024, 2, 1536], P(None, ('fsdp', 'ctx'), None, 'tp')
- grad_mamba_shared: float32 [2, 1024, 280], replicated
- grad_conv_weight: float32 [2, 4, 1792], replicated
- grad_conv_bias: float32 [2, 1792], replicated
- grad_head_params: float32 [2, 3, 24], replicated
- grad_mamba_gain: float32 [2, 1536], replicated
- grad_mamba_out: float32 [2, 1536, 1024], P(None, 'tp', ('fsdp', 'ctx'))
- grad_attn_in: float32 [2, 1024, 2, 384], P(None, ('fsdp', 'ctx'), 'tp')
- grad_attn_out: float32 [2, 512, 1024], P(None, 'tp', ('fsdp', 'ctx'))
- grad_mlp_in: float32 [2, 1024, 2, 2048], P(None, ('fsdp', 'ctx'), None, 'tp')
- grad_mlp_out: float32 [2, 2048, 1024], P(None, 'tp', ('fsdp', 'ctx'))
Inputs may be any that keep to these rules, and one draw needn't show every extreme that they name: `lengths`: for each index along the second dimension one micro-batch, drawn from the seed, holds a sequence of all 1024 positions. Positions at or past a sequence's length are padding.
All inputs are finite; a program needn't handle non-finite values.
Results may differ from a plain program's by a relative error of at most 0.02.
Values may be sent and summed in bfloat16 or wider, within the bound.
No kernel may reach another device: no remote copies, remote signals or barrier semaphores. Data moves between devices by JAX's collectives and lax.ppermute only.
A program may use at most 256 MiB of HBM per device.

v0:
```python
import math

import jax
import jax.numpy as jnp
from jax import lax
from jax.sharding import PartitionSpec as P

D = 1024
HDIM = 64
STATE = 128
CONV = 4
ADIM = 64
GROUP = 4


EPSILON = 1e-05
THETA = 100000000000.0
HIGHEST_PREC = lax.Precision.HIGHEST
LOW_TYPE = jnp.bfloat16
WIDE_TYPE = jnp.float32


def passed_along(x, axis, by):
    devices = lax.axis_size(axis)
    pairs = [(i, i + by) for i in range(devices) if 0 <= i + by < devices]
    return lax.ppermute(x, axis, pairs)


def entering(part, axis, combine, identity, reverse):
    count = lax.axis_size(axis)
    place = lax.axis_index(axis)
    ahead = count - 1 - place if reverse else place
    gathered = jax.tree.map(lambda a: lax.all_gather(a, axis), part)
    state = jax.tree.map(lambda a, e: jnp.zeros_like(a) + jnp.asarray(e, a.dtype), part, identity)

    def one(step, state):
        source = count - 1 - step if reverse else step
        return combine(
            state, jax.tree.map(lambda a: lax.dynamic_index_in_dim(a, source, 0, False), gathered)
        )

    return lax.fori_loop(0, ahead, one, state)


def product(left_side, right_side):
    return jnp.dot(left_side, right_side, preferred_element_type=WIDE_TYPE)


def against_rows(left_side, right_side):
    return lax.dot_general(
        left_side, right_side, (((1,), (1,)), ((), ())), preferred_element_type=WIDE_TYPE
    )


def over_rows(left_side, right_side):
    return lax.dot_general(
        left_side, right_side, (((0,), (0,)), ((), ())), preferred_element_type=WIDE_TYPE
    )


def exact_against(left_side, right_side):
    return lax.dot_general(left_side, right_side, (((1,), (1,)), ((), ())), precision=HIGHEST_PREC)


def exact_over(left_side, right_side):
    return lax.dot_general(left_side, right_side, (((0,), (0,)), ((), ())), precision=HIGHEST_PREC)


def unit_scale(values):
    return lax.rsqrt(jnp.mean(values * values, axis=-1, keepdims=True) + EPSILON)


def spread(local_part, full_size, position, axis_number):
    full_shape = list(local_part.shape)
    full_shape[axis_number] = full_size
    return lax.dynamic_update_slice_in_dim(
        jnp.zeros(full_shape, WIDE_TYPE), local_part, position, axis_number
    )


def narrow(values):
    return lax.psum_scatter(values, "tp", scatter_dimension=1, tiled=True)


def narrow_grad(values):
    return lax.psum_scatter(values, "tp", scatter_dimension=1, tiled=True)


def normalize(values, gain_full):
    wide_rows = lax.all_gather(values, "tp", axis=1, tiled=True)
    row_scale = unit_scale(wide_rows)
    return ((wide_rows * row_scale * gain_full).astype(LOW_TYPE), wide_rows, row_scale)


def norm_grad(kept_rows, row_scale, gain_full, upstream):
    unit_part = kept_rows * row_scale
    scaled_grad = upstream * gain_full
    inner_mean = jnp.mean(scaled_grad * unit_part, axis=-1, keepdims=True)
    return (
        narrow_grad(row_scale * (scaled_grad - unit_part * inner_mean)),
        jnp.sum(upstream * unit_part, axis=0),
    )


def widen_grad(values):
    return lax.all_gather(values, "tp", axis=1, tiled=True).astype(LOW_TYPE)


def rotate(values, start_row, turn_sign):
    half_width = values.shape[-1] // 2
    places = (start_row + jnp.arange(values.shape[0])).astype(WIDE_TYPE)
    rate_values = jnp.exp(-math.log(THETA) * jnp.arange(half_width).astype(WIDE_TYPE) / half_width)
    angles = places[:, None] * rate_values[None, :]
    cosine = jnp.cos(angles)[:, None, :]
    sine_part = turn_sign * jnp.sin(angles)[:, None, :]
    first_half = values[..., :half_width]
    second = values[..., half_width:]
    return jnp.concatenate(
        [first_half * cosine - second * sine_part, second * cosine + first_half * sine_part],
        axis=-1,
    )


def convolve(padded, kernel, offset_bias):
    length = padded.shape[0] - kernel.shape[0] + 1
    running_sum = offset_bias[None, :]
    for tap_index in range(kernel.shape[0]):
        running_sum = (
            running_sum + kernel[tap_index][None, :] * padded[tap_index : tap_index + length]
        )
    return jax.nn.silu(running_sum)


def ssd_block(inputs, entry_rows, readout, step_sizes, rate_values, carried):
    log_decay = -step_sizes * rate_values[None, :]
    cumulative = jnp.cumsum(log_decay, axis=0)
    positions = jnp.arange(inputs.shape[0])
    causal = (positions[:, None] >= positions[None, :])[None]
    gap_values = jnp.where(causal, cumulative.T[:, :, None] - cumulative.T[:, None, :], 0.0)
    decay_table = jnp.where(causal, jnp.exp(gap_values), 0.0)
    intersection = jnp.dot(readout, entry_rows.T, precision=HIGHEST_PREC)
    weighted = step_sizes[:, :, None] * inputs
    outputs = jnp.einsum(
        "hts,shp->thp", decay_table * intersection[None], weighted, precision=HIGHEST_PREC
    )
    outputs = outputs + jnp.exp(cumulative)[:, :, None] * jnp.einsum(
        "tn,hpn->thp", readout, carried, precision=HIGHEST_PREC
    )
    tail_decay = jnp.exp(cumulative[-1][None, :] - cumulative)
    final_state = jnp.exp(cumulative[-1])[:, None, None] * carried + jnp.einsum(
        "shp,sn->hpn", tail_decay[:, :, None] * weighted, entry_rows, precision=HIGHEST_PREC
    )
    return (outputs, final_state)


def gate_tail(scanned, inputs, gate_pre, skip_values, gain_row):
    mixed_rows = (scanned + skip_values[None, :, None] * inputs).reshape(
        gate_pre.shape
    ) * jax.nn.silu(gate_pre)
    return mixed_rows * unit_scale(mixed_rows) * gain_row


def chain(earlier, later_part):
    return (earlier[0] * later_part[0], later_part[0][:, None, None] * earlier[1] + later_part[1])


def visible_mask(query_count, key_count, start_row):
    query_places = start_row + jnp.arange(query_count)
    return jnp.arange(key_count)[None, :] <= query_places[:, None]


def attention_scores(queries, all_keys, start_row):
    query_count, head_count, head_width = queries.shape
    kv_local = all_keys.shape[1]
    grouped = queries.reshape(query_count, kv_local, head_count // kv_local, head_width)
    scores = jnp.einsum(
        "tjga,sja->jgts", grouped, all_keys, preferred_element_type=WIDE_TYPE
    ) * head_width ** (-0.5)
    return (
        jnp.where(visible_mask(query_count, all_keys.shape[0], start_row), scores, -1e30),
        grouped,
    )


def attention_forward(queries, all_keys, all_values, start_row):
    query_count, head_count, head_width = queries.shape
    scores, _ = attention_scores(queries, all_keys, start_row)
    row_top = jnp.max(scores, axis=-1, keepdims=True)
    row_total = jnp.sum(jnp.exp(scores - row_top), axis=-1, keepdims=True)
    log_total = row_top + jnp.log(row_total)
    weights = jnp.exp(scores - log_total).astype(LOW_TYPE)
    outputs = jnp.einsum("jgts,sja->tjga", weights, all_values, preferred_element_type=WIDE_TYPE)
    return (outputs.reshape(query_count, head_count * head_width), log_total)


def attention_backward(queries, all_keys, all_values, log_total, start_row, grad_out):
    query_count, head_count, head_width = queries.shape
    kv_local = all_keys.shape[1]
    scores, grouped = attention_scores(queries, all_keys, start_row)
    grad_grouped = grad_out.reshape(query_count, kv_local, head_count // kv_local, head_width)
    probs_wide = jnp.exp(scores - log_total)
    grad_probs = jnp.einsum(
        "tjga,sja->jgts", grad_grouped, all_values, preferred_element_type=WIDE_TYPE
    )
    grad_values = jnp.einsum(
        "jgts,tjga->sja",
        probs_wide.astype(LOW_TYPE),
        grad_grouped,
        preferred_element_type=WIDE_TYPE,
    )
    grad_scores = (
        probs_wide * (grad_probs - jnp.sum(probs_wide * grad_probs, axis=-1, keepdims=True))
    ).astype(LOW_TYPE)
    grad_queries = jnp.einsum(
        "jgts,sja->tjga", grad_scores, all_keys, preferred_element_type=WIDE_TYPE
    ) * head_width ** (-0.5)
    grad_keys = jnp.einsum(
        "jgts,tjga->sja", grad_scores, grouped, preferred_element_type=WIDE_TYPE
    ) * head_width ** (-0.5)
    return (grad_queries.reshape(query_count, head_count, head_width), grad_keys, grad_values)


def fetch(layer_index, pieces):
    zx_w, mix_w, attn_w, attn_out_w, mlp_w, mlp_out_w = pieces
    return (
        lax.all_gather(zx_w[layer_index], ("fsdp", "ctx"), axis=0, tiled=True),
        lax.all_gather(mix_w[layer_index], ("fsdp", "ctx"), axis=1, tiled=True),
        lax.all_gather(attn_w[layer_index], ("fsdp", "ctx"), axis=0, tiled=True),
        lax.all_gather(attn_out_w[layer_index], ("fsdp", "ctx"), axis=1, tiled=True),
        lax.all_gather(mlp_w[layer_index], ("fsdp", "ctx"), axis=0, tiled=True),
        lax.all_gather(mlp_out_w[layer_index], ("fsdp", "ctx"), axis=1, tiled=True),
    )


def local_small(
    layer_index, norm_gains, mamba_shared, conv_weight, conv_bias, head_params, mamba_gain
):
    tensor_rank = lax.axis_index("tp")
    heads_local = head_params.shape[2] // lax.axis_size("tp")
    full_ssm = mamba_gain.shape[1]
    local_ssm = full_ssm // lax.axis_size("tp")
    shared_all = mamba_shared[layer_index]
    shared_local = jnp.concatenate(
        [
            shared_all[:, : 2 * STATE],
            lax.dynamic_slice_in_dim(
                shared_all, 2 * STATE + tensor_rank * heads_local, heads_local, 1
            ),
        ],
        axis=1,
    )
    kernel_all = conv_weight[layer_index].astype(WIDE_TYPE)
    kernel = jnp.concatenate(
        [
            lax.dynamic_slice_in_dim(kernel_all, tensor_rank * local_ssm, local_ssm, 1),
            kernel_all[:, full_ssm:],
        ],
        axis=1,
    )
    bias_all = conv_bias[layer_index].astype(WIDE_TYPE)
    offset_bias = jnp.concatenate(
        [
            lax.dynamic_slice_in_dim(bias_all, tensor_rank * local_ssm, local_ssm, 0),
            bias_all[full_ssm:],
        ],
        axis=0,
    )
    head_local = lax.dynamic_slice_in_dim(
        head_params[layer_index], tensor_rank * heads_local, heads_local, 1
    )
    gain_local = lax.dynamic_slice_in_dim(
        mamba_gain[layer_index].astype(WIDE_TYPE), tensor_rank * local_ssm, local_ssm, 0
    )
    return (
        norm_gains[layer_index].astype(WIDE_TYPE),
        shared_local,
        kernel,
        offset_bias,
        head_local,
        gain_local,
    )


def widen_small(small_grads, full_ssm, heads_total):
    gains_grad, shared_grad, kernel_grad, offset_grad, head_grad, gain_grad = small_grads
    tensor_rank = lax.axis_index("tp")
    local_ssm = gain_grad.shape[0]
    heads_local = head_grad.shape[1]
    state_cols = 2 * STATE
    shared_full = spread(shared_grad[:, :state_cols], state_cols + heads_total, 0, 1) + spread(
        shared_grad[:, state_cols:],
        state_cols + heads_total,
        state_cols + tensor_rank * heads_local,
        1,
    )
    channels = full_ssm + state_cols
    kernel_full = spread(kernel_grad[:, :local_ssm], channels, tensor_rank * local_ssm, 1) + spread(
        kernel_grad[:, local_ssm:], channels, full_ssm, 1
    )
    offset_full = spread(offset_grad[:local_ssm], channels, tensor_rank * local_ssm, 0) + spread(
        offset_grad[local_ssm:], channels, full_ssm, 0
    )
    head_full = spread(head_grad, heads_total, tensor_rank * heads_local, 1)
    gain_full = spread(gain_grad, full_ssm, tensor_rank * local_ssm, 0)
    return (gains_grad, shared_full, kernel_full, offset_full, head_full, gain_full)


def layer_forward(hidden, weights, small_params, start_row):
    zx_w, mix_w, attn_w, attn_out_w, mlp_w, mlp_out_w = weights
    norm_gain, shared_local, kernel, offset_bias, head_local, gain_local = small_params
    row_count = hidden.shape[0]
    local_ssm = gain_local.shape[0]
    heads_local = head_local.shape[1]
    kv_local = attn_w.shape[1]
    normed, kept_one, scale_one = normalize(hidden, norm_gain[0])
    zx_rows = product(normed, zx_w.reshape(D, 2 * local_ssm))
    gate_pre = zx_rows[:, :local_ssm]
    side_rows = product(normed, shared_local)
    stacked = jnp.concatenate([zx_rows[:, local_ssm:], side_rows[:, : 2 * STATE]], axis=1).astype(
        LOW_TYPE
    )
    step_pre = side_rows[:, 2 * STATE :]
    rim_rows = passed_along(stacked[row_count - CONV + 1 :], "ctx", 1)
    padded = jnp.concatenate([rim_rows, stacked], axis=0)
    active = convolve(padded.astype(WIDE_TYPE), kernel, offset_bias)
    inputs_low = active[:, :local_ssm].astype(LOW_TYPE)
    entry_low = active[:, local_ssm : local_ssm + STATE].astype(LOW_TYPE)
    readout_low = active[:, local_ssm + STATE :].astype(LOW_TYPE)
    step_sizes = jax.nn.softplus(step_pre + head_local[1][None, :])
    rate_values = jnp.exp(head_local[0])
    inputs_wide = inputs_low.astype(WIDE_TYPE).reshape(row_count, heads_local, HDIM)
    readout_wide = readout_low.astype(WIDE_TYPE)
    zero_state = jnp.zeros((heads_local, HDIM, STATE), WIDE_TYPE)
    local_out, local_state = ssd_block(
        inputs_wide, entry_low.astype(WIDE_TYPE), readout_wide, step_sizes, rate_values, zero_state
    )
    cumulative = jnp.cumsum(-step_sizes * rate_values[None, :], axis=0)
    decay_total = jnp.exp(cumulative[-1])
    start_state = entering(
        (decay_total, local_state), "ctx", chain, (jnp.ones_like(decay_total), zero_state), False
    )[1]
    scanned = local_out + jnp.exp(cumulative)[:, :, None] * jnp.einsum(
        "tn,hpn->thp", readout_wide, start_state, precision=HIGHEST_PREC
    )
    mamba_norm = gate_tail(scanned, inputs_wide, gate_pre, head_local[2], gain_local).astype(
        LOW_TYPE
    )
    mamba_part = product(mamba_norm, mix_w)
    qkv_rows = product(normed, attn_w.reshape(D, -1)).reshape(row_count, kv_local, GROUP + 2, ADIM)
    queries = rotate(
        qkv_rows[:, :, :GROUP].reshape(row_count, kv_local * GROUP, ADIM), start_row, 1.0
    ).astype(LOW_TYPE)
    key_rows = rotate(qkv_rows[:, :, GROUP], start_row, 1.0).astype(LOW_TYPE)
    value_rows = qkv_rows[:, :, GROUP + 1].astype(LOW_TYPE)
    all_keys, all_values = (
        lax.all_gather(key_rows, "ctx", axis=0, tiled=True),
        lax.all_gather(value_rows, "ctx", axis=0, tiled=True),
    )
    attended, log_total = attention_forward(queries, all_keys, all_values, start_row)
    attended_low = attended.astype(LOW_TYPE)
    after_mix = hidden + narrow(mamba_part + product(attended_low, attn_out_w))
    normed_two, kept_two, scale_two = normalize(after_mix, norm_gain[1])
    gate_up = product(normed_two, mlp_w.reshape(D, -1))
    ff_local = gate_up.shape[1] // 2
    activated = (jax.nn.silu(gate_up[:, :ff_local]) * gate_up[:, ff_local:]).astype(LOW_TYPE)
    result = after_mix + narrow(product(activated, mlp_out_w))
    saved = (
        kept_one,
        scale_one,
        normed,
        gate_pre,
        padded,
        step_pre,
        inputs_low,
        entry_low,
        readout_low,
        start_state,
        scanned,
        mamba_norm,
        queries,
        all_keys,
        all_values,
        log_total,
        attended_low,
        kept_two,
        scale_two,
        normed_two,
        gate_up,
        activated,
    )
    return (result, saved)


def layer_backward(upstream, saved, weights, small_params, start_row):
    (
        kept_one,
        scale_one,
        normed,
        gate_pre,
        padded,
        step_pre,
        inputs_low,
        entry_low,
        readout_low,
        start_state,
        scanned,
        mamba_norm,
        queries,
        all_keys,
        all_values,
        log_total,
        attended_low,
        kept_two,
        scale_two,
        normed_two,
        gate_up,
        activated,
    ) = saved
    zx_w, mix_w, attn_w, attn_out_w, mlp_w, mlp_out_w = weights
    norm_gain, shared_local, kernel, offset_bias, head_local, gain_local = small_params
    row_count = upstream.shape[0]
    local_ssm = gain_local.shape[0]
    heads_local = head_local.shape[1]
    grad_mlp = widen_grad(upstream)
    grad_mlp_out = over_rows(activated, grad_mlp)
    grad_act = against_rows(grad_mlp, mlp_out_w)
    ff_local = grad_act.shape[1]
    gate_part = gate_up[:, :ff_local]
    up_part = gate_up[:, ff_local:]
    sigma_gate = jax.nn.sigmoid(gate_part)
    grad_gate = grad_act * up_part * sigma_gate * (1.0 + gate_part * (1.0 - sigma_gate))
    grad_up = grad_act * gate_part * sigma_gate
    grad_gu = jnp.concatenate([grad_gate, grad_up], axis=1).astype(LOW_TYPE)
    grad_mlp_in = over_rows(normed_two, grad_gu).reshape(mlp_w.shape)
    mid_part, grad_gain_two = norm_grad(
        kept_two, scale_two, norm_gain[1], against_rows(grad_gu, mlp_w.reshape(D, -1))
    )
    grad_mid = upstream + mid_part
    grad_mix = widen_grad(grad_mid)
    grad_mix_out = over_rows(mamba_norm, grad_mix)
    grad_attn_out = over_rows(attended_low, grad_mix)
    grad_mamba_norm = against_rows(grad_mix, mix_w)
    grad_attended = against_rows(grad_mix, attn_out_w).astype(LOW_TYPE)
    grad_queries, grad_keys_all, grad_values_all = attention_backward(
        queries, all_keys, all_values, log_total, start_row, grad_attended
    )
    grad_keys, grad_values = (
        lax.psum_scatter(grad_keys_all, "ctx", scatter_dimension=0, tiled=True),
        lax.psum_scatter(grad_values_all, "ctx", scatter_dimension=0, tiled=True),
    )
    kv_local = grad_keys.shape[1]
    grad_query_raw = rotate(grad_queries, start_row, -1.0).reshape(row_count, kv_local, GROUP, ADIM)
    grad_key_raw = rotate(grad_keys, start_row, -1.0)
    grad_qkv = (
        jnp.concatenate([grad_query_raw, grad_key_raw[:, :, None], grad_values[:, :, None]], axis=2)
        .reshape(row_count, -1)
        .astype(LOW_TYPE)
    )
    grad_attn_in = over_rows(normed, grad_qkv).reshape(attn_w.shape)
    grad_normed = against_rows(grad_qkv, attn_w.reshape(D, -1))
    inputs_wide = inputs_low.astype(WIDE_TYPE).reshape(row_count, heads_local, HDIM)
    entry_wide = entry_low.astype(WIDE_TYPE)
    readout_wide = readout_low.astype(WIDE_TYPE)
    _, tail_pull = jax.vjp(gate_tail, scanned, inputs_wide, gate_pre, head_local[2], gain_local)
    grad_scanned, grad_inputs_tail, grad_gate_pre, grad_skip, grad_gain_mamba = tail_pull(
        grad_mamba_norm
    )
    step_sizes = jax.nn.softplus(step_pre + head_local[1][None, :])
    rate_values = jnp.exp(head_local[0])
    cumulative = jnp.cumsum(-step_sizes * rate_values[None, :], axis=0)
    decay_total = jnp.exp(cumulative[-1])
    from_outputs = jnp.einsum(
        "thp,tn->hpn",
        jnp.exp(cumulative)[:, :, None] * grad_scanned,
        readout_wide,
        precision=HIGHEST_PREC,
    )
    later_grad = entering(
        (decay_total, from_outputs),
        "ctx",
        chain,
        (jnp.ones_like(decay_total), jnp.zeros_like(from_outputs)),
        True,
    )[1]
    _, ssd_pull = jax.vjp(
        ssd_block, inputs_wide, entry_wide, readout_wide, step_sizes, rate_values, start_state
    )
    grad_inputs, grad_entry, grad_readout, grad_steps, grad_rates, _ = ssd_pull(
        (grad_scanned, later_grad)
    )
    grad_step_pre = grad_steps * jax.nn.sigmoid(step_pre + head_local[1][None, :])
    grad_active = jnp.concatenate(
        [(grad_inputs + grad_inputs_tail).reshape(row_count, local_ssm), grad_entry, grad_readout],
        axis=1,
    )
    _, conv_pull = jax.vjp(convolve, padded.astype(WIDE_TYPE), kernel, offset_bias)
    grad_padded, grad_kernel, grad_offset = conv_pull(grad_active)
    rim_width = CONV - 1
    returned = passed_along(grad_padded[:rim_width], "ctx", -1)
    grad_stacked = grad_padded[rim_width:] + jnp.concatenate(
        [jnp.zeros((row_count - rim_width, grad_padded.shape[1]), WIDE_TYPE), returned], axis=0
    )
    grad_zx = jnp.concatenate([grad_gate_pre, grad_stacked[:, :local_ssm]], axis=1).astype(LOW_TYPE)
    grad_entry_read = grad_stacked[:, local_ssm:]
    grad_step_low = grad_step_pre.astype(LOW_TYPE)
    grad_zx_w = over_rows(normed, grad_zx).reshape(zx_w.shape)
    grad_normed = (
        grad_normed
        + against_rows(grad_zx, zx_w.reshape(D, -1))
        + against_rows(grad_step_low, shared_local[:, 2 * STATE :])
    )
    grad_normed = grad_normed + exact_against(
        grad_entry_read, shared_local[:, : 2 * STATE].astype(WIDE_TYPE)
    )
    below_part, grad_gain_one = norm_grad(kept_one, scale_one, norm_gain[0], grad_normed)
    grad_hidden = grad_mid + below_part
    grad_shared_local = jnp.concatenate(
        [exact_over(normed.astype(WIDE_TYPE), grad_entry_read), over_rows(normed, grad_step_low)],
        axis=1,
    )
    grad_heads = jnp.stack([grad_rates * rate_values, jnp.sum(grad_step_pre, axis=0), grad_skip])
    big_grads = (grad_zx_w, grad_mix_out, grad_attn_in, grad_attn_out, grad_mlp_in, grad_mlp_out)
    small_grads = (
        jnp.stack([grad_gain_one, grad_gain_two]),
        grad_shared_local,
        grad_kernel,
        grad_offset,
        grad_heads,
        grad_gain_mamba,
    )
    return (grad_hidden, big_grads, small_grads)


def add_into(running, fresh):
    if running is None:
        return fresh
    return tuple((old_value + new_value for old_value, new_value in zip(running, fresh)))


def stack_layers(per_layer):
    return tuple(
        (
            jnp.stack([layer_grads[member] for layer_grads in per_layer])
            for member in range(len(per_layer[0]))
        )
    )


def settle(big_grads, small_grads):
    owned_grads = (
        lax.psum_scatter(big_grads[0], ("fsdp", "ctx"), scatter_dimension=1, tiled=True),
        lax.psum_scatter(big_grads[1], ("fsdp", "ctx"), scatter_dimension=2, tiled=True),
        lax.psum_scatter(big_grads[2], ("fsdp", "ctx"), scatter_dimension=1, tiled=True),
        lax.psum_scatter(big_grads[3], ("fsdp", "ctx"), scatter_dimension=2, tiled=True),
        lax.psum_scatter(big_grads[4], ("fsdp", "ctx"), scatter_dimension=1, tiled=True),
        lax.psum_scatter(big_grads[5], ("fsdp", "ctx"), scatter_dimension=2, tiled=True),
    )
    summed = lax.psum(
        (
            small_grads[0],
            small_grads[1],
            small_grads[2],
            small_grads[3],
            small_grads[4],
            small_grads[5],
        ),
        ("fsdp", "ctx", "tp"),
    )
    return (owned_grads, summed)


def local(
    hidden_in,
    lengths,
    norm_gains,
    mamba_zx,
    mamba_shared,
    conv_weight,
    conv_bias,
    head_params,
    mamba_gain,
    mamba_out,
    attn_in,
    attn_out,
    mlp_in,
    mlp_out,
    out_grad,
):
    layer_count = norm_gains.shape[0]
    micro_count = hidden_in.shape[0]
    row_count = hidden_in.shape[2]
    full_ssm = mamba_gain.shape[1]
    heads_total = head_params.shape[2]
    start_row = lax.axis_index("ctx") * row_count
    pieces = (mamba_zx, mamba_out, attn_in, attn_out, mlp_in, mlp_out)
    smalls = [
        local_small(
            layer_index, norm_gains, mamba_shared, conv_weight, conv_bias, head_params, mamba_gain
        )
        for layer_index in range(layer_count)
    ]
    big_acc = [None] * layer_count
    small_acc = [None] * layer_count
    owned_total = None
    summed_total = None
    out_list = []
    grad_list = []
    for micro_index in range(micro_count):
        keep_mask = (start_row + jnp.arange(row_count) < lengths[micro_index, 0]).astype(WIDE_TYPE)[
            :, None
        ]
        hidden = hidden_in[micro_index, 0].astype(WIDE_TYPE)
        saved_all = []
        for layer_index in range(layer_count):
            weights = fetch(layer_index, pieces)
            hidden, saved = layer_forward(hidden, weights, smalls[layer_index], start_row)
            saved_all.append(saved)
        out_list.append((hidden * keep_mask).astype(LOW_TYPE))
        upstream = out_grad[micro_index, 0].astype(WIDE_TYPE) * keep_mask
        for layer_index in reversed(range(layer_count)):
            weights = fetch(layer_index, pieces)
            upstream, big_grads, small_grads = layer_backward(
                upstream, saved_all[layer_index], weights, smalls[layer_index], start_row
            )
            big_acc[layer_index] = add_into(big_acc[layer_index], big_grads)
            small_acc[layer_index] = add_into(
                small_acc[layer_index], widen_small(small_grads, full_ssm, heads_total)
            )
        grad_list.append(upstream)
    owned_total, summed_total = settle(stack_layers(big_acc), stack_layers(small_acc))
    mixed_out = jnp.stack(out_list).reshape(hidden_in.shape)
    input_grad = jnp.stack(grad_list).reshape(hidden_in.shape)
    return (
        mixed_out,
        input_grad,
        summed_total[0],
        owned_total[0],
        summed_total[1],
        summed_total[2],
        summed_total[3],
        summed_total[4],
        summed_total[5],
        owned_total[1],
        owned_total[2],
        owned_total[3],
        owned_total[4],
        owned_total[5],
    )


def solution(mesh):
    placed = (
        P(None, "fsdp", "ctx", "tp"),
        P(None, "fsdp"),
        P(),
        P(None, ("fsdp", "ctx"), None, "tp"),
        P(),
        P(),
        P(),
        P(),
        P(),
        P(None, "tp", ("fsdp", "ctx")),
        P(None, ("fsdp", "ctx"), "tp", None),
        P(None, "tp", ("fsdp", "ctx")),
        P(None, ("fsdp", "ctx"), None, "tp"),
        P(None, "tp", ("fsdp", "ctx")),
        P(None, "fsdp", "ctx", "tp"),
    )
    return jax.shard_map(
        local,
        mesh=mesh,
        in_specs=placed,
        out_specs=(
            P(None, "fsdp", "ctx", "tp"),
            P(None, "fsdp", "ctx", "tp"),
            P(),
            P(None, ("fsdp", "ctx"), None, "tp"),
            P(),
            P(),
            P(),
            P(),
            P(),
            P(None, "tp", ("fsdp", "ctx")),
            P(None, ("fsdp", "ctx"), "tp", None),
            P(None, "tp", ("fsdp", "ctx")),
            P(None, ("fsdp", "ctx"), None, "tp"),
            P(None, "tp", ("fsdp", "ctx")),
        ),
        check_vma=False,
    )
```

profile of v0, /device:TPU:1, one launch (start us, length us, event | category | flops | bytes accessed | tf_op | source)
XLA Modules:
  0.0 3206.7 jit_solution(399088974996350235)
XLA Ops:
  23.0 11.0 all-gather.89.cloned.1.call-done
  40.7 64.6 %all-gather.69.cloned.1.call-done = bf16[1,1024,2,768]{3,2,0,1:T(2,128)(2,1)} async-done(((bf16[1,64,2,768]{3,2,0,1:T(2,128)(2,1)}), bf16[1,1024,2,768]{3,2,0,1:T(2,128)(2,1)}) %all-gather.69.cloned.1.call-update) | async-done | bytes 3145744 | tf_op jit(solution)/shard_map/all_gather | solution.py:226
  123.4 36.9 %all-gather.4 = bf16[1,1024,1,384]{3,1,2,0:T(8,128)(2,1)S(1)} all-gather(bf16[1,64,1,384]{3,1,2,0:T(8,128)(2,1)S(1)} %get-tuple-element.912), channel_id=6, replica_groups=mesh['fsdp'=4,'ctx'=4,'tp'=2] {'fsdp','ctx'}, dimensions={1}, use_global_device_ids=true | all-gather | bytes 835584 | tf_op jit(solution)/shard_map/all_gather | solution.py:228
  163.3 37.4 %all-gather.6 = bf16[1,256,1024]{1,2,0:T(8,128)(2,1)S(1)} all-gather(bf16[1,256,64]{1,2,0:T(8,128)(2,1)S(1)} %get-tuple-element.932), channel_id=8, replica_groups=mesh['fsdp'=4,'ctx'=4,'tp'=2] {'fsdp','ctx'}, dimensions={2}, use_global_device_ids=true | all-gather | bytes 557056 | tf_op jit(solution)/shard_map/all_gather | solution.py:229
  204.4 6.4 all-gather.5
  211.1 9.5 all_gather.224
  247.6 26.2 reduce-scatter.34.cloned.1.call-done
  276.6 76.7 %all-gather.75.cloned.1.call-done = bf16[1,1024,2,1024]{3,2,0,1:T(2,128)(2,1)} async-done(((bf16[1,64,2,1024]{3,2,0,1:T(2,128)(2,1)}), bf16[1,1024,2,1024]{3,2,0,1:T(2,128)(2,1)}) %all-gather.75.cloned.1.call-update) | async-done | bytes 4194320 | tf_op jit(solution)/shard_map/all_gather | solution.py:230
  371.7 57.8 %all-gather.77.cloned.1.call-done = bf16[1,1024,1024]{1,2,0:T(8,128)(2,1)} async-done(((bf16[1,1024,64]{1,2,0:T(8,128)(2,1)}), bf16[1,1024,1024]{1,2,0:T(8,128)(2,1)}) %all-gather.77.cloned.1.call-update) | async-done | bytes 2097168 | tf_op jit(solution)/shard_map/all_gather | solution.py:231
  433.6 7.4 reduce-scatter.36.cloned.1.call-done
  446.0 66.2 %all-gather.79.cloned.1.call-done = bf16[1,1024,2,768]{3,2,0,1:T(2,128)(2,1)} async-done(((bf16[1,64,2,768]{3,2,0,1:T(2,128)(2,1)}), bf16[1,1024,2,768]{3,2,0,1:T(2,128)(2,1)}) %all-gather.79.cloned.1.call-update) | async-done | bytes 3145744 | tf_op jit(solution)/shard_map/all_gather | solution.py:226
  516.3 6.9 all-gather.57.cloned.1.call-done
  544.8 37.6 %all-gather.12 = bf16[1,1024,1,384]{3,1,2,0:T(8,128)(2,1)S(1)} all-gather(bf16[1,64,1,384]{3,1,2,0:T(8,128)(2,1)S(1)} %copy-done.320), channel_id=14, replica_groups=mesh['fsdp'=4,'ctx'=4,'tp'=2] {'fsdp','ctx'}, dimensions={1}, use_global_device_ids=true | all-gather | bytes 835584 | tf_op jit(solution)/shard_map/all_gather | solution.py:228
  583.6 36.6 %all-gather.14 = bf16[1,256,1024]{1,2,0:T(8,128)(2,1)S(1)} all-gather(bf16[1,256,64]{1,2,0:T(8,128)(2,1)S(1)} %copy-done.321), channel_id=16, replica_groups=mesh['fsdp'=4,'ctx'=4,'tp'=2] {'fsdp','ctx'}, dimensions={2}, use_global_device_ids=true | all-gather | bytes 557056 | tf_op jit(solution)/shard_map/all_gather | solution.py:229
  629.9 9.1 all_gather.237
  667.7 27.4 reduce-scatter.38.cloned.1.call-done
  704.1 69.7 %all-gather.85.cloned.1.call-done = bf16[1,1024,2,1024]{3,2,0,1:T(2,128)(2,1)} async-done(((bf16[1,64,2,1024]{3,2,0,1:T(2,128)(2,1)}), bf16[1,1024,2,1024]{3,2,0,1:T(2,128)(2,1)}) %all-gather.85.cloned.1.call-update) | async-done | bytes 4194320 | tf_op jit(solution)/shard_map/all_gather | solution.py:230
  791.6 57.5 %all-gather.87.cloned.1.call-done = bf16[1,1024,1024]{1,2,0:T(8,128)(2,1)} async-done(((bf16[1,1024,64]{1,2,0:T(8,128)(2,1)}), bf16[1,1024,1024]{1,2,0:T(8,128)(2,1)}) %all-gather.87.cloned.1.call-update) | async-done | bytes 2097168 | tf_op jit(solution)/shard_map/all_gather | solution.py:231
  866.3 12.4 reduce-scatter.40.cloned.1.call-done
  912.4 6.2 fusion.69
  921.1 20.9 reduce-scatter.54.cloned.1.call-done
  943.5 32.5 %all-gather.95.cloned.1.call-done = f32[48,64,128]{2,1,0:T(8,128)} async-done(((f32[12,64,128]{2,1,0:T(8,128)}), f32[48,64,128]{2,1,0:T(8,128)}) %all-gather.95.cloned.1.call-update) | async-done | bytes 1572880 | tf_op jit(solution)/shard_map/all_gather | solution.py:33
  1022.4 7.1 all-gather.28
  1030.3 7.2 all-gather.19
  1046.7 6.5 all_gather.260
  1061.9 13.1 all-gather.91.cloned.1.call-done
  1082.5 11.2 all_gather.247
  1103.8 7.8 fusion.6
  1115.8 9.3 reduce-scatter.42.cloned.1.call-done
  1127.1 10.4 all-gather.61.cloned.1.call-done
  1146.4 9.8 reduce-scatter.44.cloned.1.call-done
  1158.3 10.3 all-gather.63.cloned.1.call-done
  1176.6 7.3 all_gather.254
  1193.6 7.6 all-gather.21
  1214.5 7.6 fusion.49
  1231.4 19.1 all-gather.93.cloned.1.call-done
  1263.6 14.5 reduce-scatter.46.cloned.1.call-done
  1282.9 7.6 all-gather.65.cloned.1.call-done
  1306.9 6.2 reduce-scatter.66.cloned.1.call-done
  1313.1 12.1 reduce-scatter.48.cloned.1.call-done
  1369.6 19.7 reduce-scatter.70.cloned.1.call-done
  1390.8 32.3 %all-gather.99.cloned.1.call-done = f32[48,64,128]{2,1,0:T(8,128)} async-done(((f32[12,64,128]{2,1,0:T(8,128)}), f32[48,64,128]{2,1,0:T(8,128)}) %all-gather.99.cloned.1.call-update) | async-done | bytes 1572880 | tf_op jit(solution)/shard_map/all_gather | solution.py:33
  1460.5 10.2 reduce-scatter.72.cloned.1.call-done
  1551.5 7.0 fusion.71
  1576.1 25.5 reduce-scatter.78.cloned.1.call-done
  1603.1 31.6 all-gather.101.cloned.1.call-done
  1644.6 23.4 all-gather.97.cloned.1.call-done
  1689.5 6.7 multiply_reduce_fusion.59
  1761.9 13.5 copy.596
  1781.5 10.4 copy.594
  1805.0 8.4 add.1384
  1818.2 8.3 add.1382
  1826.5 11.4 copy_bitcast_fusion.1
  1837.9 16.5 reshape.2154
  1868.9 11.9 add.1416
  1880.8 8.3 convolution_add_fusion.3
  1889.1 11.7 add.1414
  1900.8 12.4 copy_bitcast_fusion
  1913.2 22.2 reshape.2156
  1963.7 58.9 %reduce-scatter.82.cloned.1.call-done = f32[2,64,1,384]{3,1,2,0:T(8,128)} async-done(((f32[2,1024,1,384]{3,1,2,0:T(8,128)}), f32[2,64,1,384]{3,1,2,0:T(8,128)}) %reduce-scatter.82.cloned.1.call-update) | async-done | bytes 196624 | tf_op jit(solution)/shard_map/reduce_scatter | solution.py:553
  2024.4 465.4 %all-reduce.69.cloned.1.call-done = (f32[2,768,1024]{1,0,2:T(2,128)}, f32[2,256,1024]{1,0,2:T(2,128)}, f32[2,1024,1024]{1,0,2:T(2,128)}) async-done(((f32[2,768,1024]{1,0,2:T(2,128)}, f32[2,256,1024]{1,0,2:T(2,128)}, f32[2,1024,1024]{1,0,2:T(2,128)}), (f32[2,768,1024]{1,0,2:T(2,128)}, f32[2,256,1024]{1,0,2:T(2,128)}, f32[2,1024,1024]{1,0,2:T(2,128)})) %all-reduce.69.cloned.1.call-update) | async-done | bytes 16777232
  2495.2 203.9 %reduce-scatter.84.cloned.1.call-done = f32[64,3072]{1,0:T(8,128)} async-done(((f32[1024,3072]{1,0:T(8,128)}), f32[64,3072]{1,0:T(8,128)}) %reduce-scatter.84.cloned.1.call-update) | async-done | bytes 786448
  2701.9 345.6 %reduce-scatter.86.cloned.1.call-done = f32[64,4096]{1,0:T(8,128)} async-done(((f32[1024,4096]{1,0:T(8,128)}), f32[64,4096]{1,0:T(8,128)}) %reduce-scatter.86.cloned.1.call-update) | async-done | bytes 1048592
  3050.7 142.9 %all-reduce.65.cloned.1.call-done = f32[2,1024,280]{1,2,0:T(8,128)} async-done(((f32[2,1024,280]{1,2,0:T(8,128)}), f32[2,1024,280]{1,2,0:T(8,128)}) %all-reduce.65.cloned.1.call-update) | async-done | bytes 2293776 | tf_op jit(solution)/shard_map/psum | solution.py:558
  (1840 shorter events, 805.3 us)
Async XLA Ops:
  7.2 14.5 all-gather.67.cloned.1.call-start
  9.5 24.5 all-gather.89.cloned.1.call-start
  10.3 95.0 %all-gather.69.cloned.1.call-start = ((), (), s32[]{:S(2)}) async-start(), calls=%async_computation.60 | async-start | bytes 3342336 | tf_op jit(solution)/shard_map/all_gather | solution.py:226
  12.4 222.8 %all-gather.71.cloned.1.call-start = ((), (), s32[]{:S(2)}) async-start(), calls=%async_computation.61 | async-start | bytes 1966080 | tf_op jit(solution)/shard_map/all_gather | solution.py:33
  17.9 506.7 %copy-start.311 = (f32[1,1,1024]{2,1,0:T(1,128)}, f32[1,1,1024]{2,1,0:T(1,128)S(1)}, u32[]{:S(2)}) copy-start(f32[1,1,1024]{2,1,0:T(1,128)S(1)} %get-tuple-element.966) | copy-start | bytes 12292
  37.2 584.3 %copy-start.26 = (bf16[256,1024]{1,0:T(8,128)(2,1)}, bf16[256,1024]{1,0:T(8,128)(2,1)S(1)}, u32[]{:S(2)}) copy-start(bf16[256,1024]{1,0:T(8,128)(2,1)S(1)} %get-tuple-element.979) | copy-start | bytes 1572868
  110.0 6.3 collective-permute-start.2
  113.1 3.9 collective-permute-start
  121.2 121.5 %all-gather.73.cloned.1.call-start = ((), (), s32[]{:S(2)}) async-start(), calls=%async_computation.62 | async-start | bytes 1671168 | tf_op jit(solution)/shard_map/all_gather | solution.py:227
  122.0 151.8 %reduce-scatter.34.cloned.1.call-start = ((), (), s32[]{:S(2)}) async-start(), calls=%async_computation.27 | async-start | bytes 1572864 | tf_op jit(solution)/shard_map/reduce_scatter | solution.py:82
  246.3 106.9 %all-gather.75.cloned.1.call-start = ((), (), s32[]{:S(2)}) async-start(), calls=%async_computation.63 | async-start | bytes 4456448 | tf_op jit(solution)/shard_map/all_gather | solution.py:230
  247.6 117.1 %all-gather.55.cloned.1.call-start = ((), (), s32[]{:S(2)}) async-start(), calls=%async_computation.28 | async-start | bytes 1572864 | tf_op jit(solution)/shard_map/all_gather | solution.py:90
  275.7 153.8 %all-gather.77.cloned.1.call-start = ((), (), s32[]{:S(2)}) async-start(), calls=%async_computation.64 | async-start | bytes 2228224 | tf_op jit(solution)/shard_map/all_gather | solution.py:231
  276.5 164.4 %reduce-scatter.36.cloned.1.call-start = ((), (), s32[]{:S(2)}) async-start(), calls=%async_computation.29 | async-start | bytes 1572864 | tf_op jit(solution)/shard_map/reduce_scatter | solution.py:82
  432.8 79.4 %all-gather.79.cloned.1.call-start = ((), (), s32[]{:S(2)}) async-start(), calls=%async_computation.65 | async-start | bytes 3342336 | tf_op jit(solution)/shard_map/all_gather | solution.py:226
  433.5 89.7 %all-gather.57.cloned.1.call-start = ((), (), s32[]{:S(2)}) async-start(), calls=%async_computation.30 | async-start | bytes 1572864 | tf_op jit(solution)/shard_map/all_gather | solution.py:90
  442.9 212.2 %all-gather.81.cloned.1.call-start = ((), (), s32[]{:S(2)}) async-start(), calls=%async_computation.66 | async-start | bytes 1966080 | tf_op jit(solution)/shard_map/all_gather | solution.py:33
  530.6 6.3 collective-permute-start.1
  544.2 119.3 %all-gather.83.cloned.1.call-start = ((), (), s32[]{:S(2)}) async-start(), calls=%async_computation.67 | async-start | bytes 1671168 | tf_op jit(solution)/shard_map/all_gather | solution.py:227
  544.8 150.3 %reduce-scatter.38.cloned.1.call-start = ((), (), s32[]{:S(2)}) async-start(), calls=%async_computation.31 | async-start | bytes 1572864 | tf_op jit(solution)/shard_map/reduce_scatter | solution.py:82
  667.0 106.7 %all-gather.85.cloned.1.call-start = ((), (), s32[]{:S(2)}) async-start(), calls=%async_computation.68 | async-start | bytes 4456448 | tf_op jit(solution)/shard_map/all_gather | solution.py:230
  667.6 117.4 %all-gather.59.cloned.1.call-start = ((), (), s32[]{:S(2)}) async-start(), calls=%async_computation.32 | async-start | bytes 1572864 | tf_op jit(solution)/shard_map/all_gather | solution.py:90
  697.2 152.0 %all-gather.87.cloned.1.call-start = ((), (), s32[]{:S(2)}) async-start(), calls=%async_computation.69 | async-start | bytes 2228224 | tf_op jit(solution)/shard_map/all_gather | solution.py:231
  697.7 168.6 %reduce-scatter.50.cloned.1.call-start = ((), (), s32[]{:S(2)}) async-start(), calls=%async_computation.41 | async-start | bytes 1572864 | tf_op jit(solution)/shard_map/reduce_scatter | solution.py:86
  858.2 20.6 reduce-scatter.40.cloned.1.call-start
  861.7 57.8 %reduce-scatter.52.cloned.1.call-start = ((), (), s32[]{:S(2)}) async-start(), calls=%async_computation.42 | async-start | bytes 327680 | tf_op jit(solution)/shard_map/reduce_scatter | solution.py:448
  890.5 51.4 %reduce-scatter.54.cloned.1.call-start = ((), (), s32[]{:S(2)}) async-start(), calls=%async_computation.43 | async-start | bytes 327680 | tf_op jit(solution)/shard_map/reduce_scatter | solution.py:449
  898.2 77.8 %all-gather.95.cloned.1.call-start = ((), (), s32[]{:S(2)}) async-start(), calls=%async_computation.73 | async-start | bytes 1966080 | tf_op jit(solution)/shard_map/all_gather | solution.py:33
  907.2 137.6 %reduce-scatter.56.cloned.1.call-start = ((), (), s32[]{:S(2)}) async-start(), calls=%async_computation.44 | async-start | bytes 1572864 | tf_op jit(solution)/shard_map/reduce_scatter | solution.py:86
  997.2 17.9 collective-permute-start.4
  1021.2 53.8 %all-gather.91.cloned.1.call-start = ((), (), s32[]{:S(2)}) async-start(), calls=%async_computation.71 | async-start | bytes 1966080 | tf_op jit(solution)/shard_map/all_gather | solution.py:33
  1039.9 56.6 %reduce-scatter.58.cloned.1.call-start = ((), (), s32[]{:S(2)}) async-start(), calls=%async_computation.45 | async-start | bytes 1572864 | tf_op jit(solution)/shard_map/reduce_scatter | solution.py:86
  1061.9 63.3 %reduce-scatter.42.cloned.1.call-start = ((), (), s32[]{:S(2)}) async-start(), calls=%async_computation.34 | async-start | bytes 1572864 | tf_op jit(solution)/shard_map/reduce_scatter | solution.py:82
  1115.8 21.7 all-gather.61.cloned.1.call-start
  1127.0 29.1 reduce-scatter.44.cloned.1.call-start
  1146.3 22.3 all-gather.63.cloned.1.call-start
  1158.3 92.2 %all-gather.93.cloned.1.call-start = ((), (), s32[]{:S(2)}) async-start(), calls=%async_computation.72 | async-start | bytes 1966080 | tf_op jit(solution)/shard_map/all_gather | solution.py:33
  1185.3 21.9 collective-permute-start.3
  1214.4 63.6 %reduce-scatter.46.cloned.1.call-start = ((), (), s32[]{:S(2)}) async-start(), calls=%async_computation.38 | async-start | bytes 1572864 | tf_op jit(solution)/shard_map/reduce_scatter | solution.py:82
  1263.5 27.0 all-gather.65.cloned.1.call-start
  1280.1 33.0 %reduce-scatter.66.cloned.1.call-start = ((), (), s32[]{:S(2)}) async-start(), calls=%async_computation.49 | async-start | bytes 1572864 | tf_op jit(solution)/shard_map/reduce_scatter | solution.py:86
  1303.3 21.9 reduce-scatter.48.cloned.1.call-start
  1306.9 61.1 %reduce-scatter.68.cloned.1.call-start = ((), (), s32[]{:S(2)}) async-start(), calls=%async_computation.50 | async-start | bytes 327680 | tf_op jit(solution)/shard_map/reduce_scatter | solution.py:448
  1337.7 51.5 %reduce-scatter.70.cloned.1.call-start = ((), (), s32[]{:S(2)}) async-start(), calls=%async_computation.51 | async-start | bytes 327680 | tf_op jit(solution)/shard_map/reduce_scatter | solution.py:449
  1345.7 77.5 %all-gather.99.cloned.1.call-start = ((), (), s32[]{:S(2)}) async-start(), calls=%async_computation.75 | async-start | bytes 1966080 | tf_op jit(solution)/shard_map/all_gather | solution.py:33
  1354.7 116.0 %reduce-scatter.72.cloned.1.call-start = ((), (), s32[]{:S(2)}) async-start(), calls=%async_computation.52 | async-start | bytes 1572864 | tf_op jit(solution)/shard_map/reduce_scatter | solution.py:86
  1446.0 8.8 collective-permute-start.6
  1460.5 33.0 %reduce-scatter.74.cloned.1.call-start = ((), (), s32[]{:S(2)}) async-start(), calls=%async_computation.53 | async-start | bytes 1572864 | tf_op jit(solution)/shard_map/reduce_scatter | solution.py:86
  1483.6 87.5 %reduce-scatter.60.cloned.1.call-start = ((), (), s32[]{:S(2)}) async-start(), calls=%async_computation.46 | async-start | bytes 327680 | tf_op jit(solution)/shard_map/reduce_scatter | solution.py:448
  1493.2 77.8 %reduce-scatter.76.cloned.1.call-start = ((), (), s32[]{:S(2)}) async-start(), calls=%async_computation.54 | async-start | bytes 327680 | tf_op jit(solution)/shard_map/reduce_scatter | solution.py:448
  1506.7 67.9 %reduce-scatter.62.cloned.1.call-start = ((), (), s32[]{:S(2)}) async-start(), calls=%async_computation.47 | async-start | bytes 327680 | tf_op jit(solution)/shard_map/reduce_scatter | solution.py:449
  1511.5 90.1 %reduce-scatter.78.cloned.1.call-start = ((), (), s32[]{:S(2)}) async-start(), calls=%async_computation.55 | async-start | bytes 327680 | tf_op jit(solution)/shard_map/reduce_scatter | solution.py:449
  1534.3 100.5 %all-gather.101.cloned.1.call-start = ((), (), s32[]{:S(2)}) async-start(), calls=%async_computation.76 | async-start | bytes 1966080 | tf_op jit(solution)/shard_map/all_gather | solution.py:33
  1539.2 128.8 %all-gather.97.cloned.1.call-start = ((), (), s32[]{:S(2)}) async-start(), calls=%async_computation.74 | async-start | bytes 1966080 | tf_op jit(solution)/shard_map/all_gather | solution.py:33
  1564.8 394.3 %all-reduce.67.cloned.1.call-start = ((), (), s32[]{:S(2)}) async-start(), calls=%async_computation.79 | async-start | bytes 208896 | tf_op jit(solution)/shard_map/psum | solution.py:558
  1707.2 17.4 collective-permute-start.5
  1717.2 14.0 collective-permute-start.7
  1736.7 223.7 %reduce-scatter.80.cloned.1.call-start = ((), (), s32[]{:S(2)}) async-start(), calls=%async_computation.56 | async-start | bytes 1572864 | tf_op jit(solution)/shard_map/reduce_scatter | solution.py:86
  1739.3 222.2 %reduce-scatter.64.cloned.1.call-start = ((), (), s32[]{:S(2)}) async-start(), calls=%async_computation.48 | async-start | bytes 1572864 | tf_op jit(solution)/shard_map/reduce_scatter | solution.py:86
  1739.8 282.7 %reduce-scatter.82.cloned.1.call-start = ((), (), s32[]{:S(2)}) async-start(), calls=%async_computation.58 | async-start | bytes 3342336 | tf_op jit(solution)/shard_map/reduce_scatter | solution.py:553
  1744.0 745.8 %all-reduce.69.cloned.1.call-start = ((), (), s32[]{:S(2)}) async-start(), calls=%async_computation.80 | async-start | bytes 33554432
  1799.2 899.9 %reduce-scatter.84.cloned.1.call-start = ((), (), s32[]{:S(2)}) async-start(), calls=%async_computation.77 | async-start | bytes 13369344
  1854.4 1193.1 %reduce-scatter.86.cloned.1.call-start = ((), (), s32[]{:S(2)}) async-start(), calls=%async_computation.78 | async-start | bytes 17825792
  1935.4 1258.1 %all-reduce.65.cloned.1.call-start = ((), (), s32[]{:S(2)}) async-start(), calls=%async_computation.57 | async-start | bytes 4587520 | tf_op jit(solution)/shard_map/psum | solution.py:558
  (509 other events, 8064.5 us)
Sparse Core Ops, SparseCore 0:
  10.1 11.4 all-gather.66
  23.8 10.1 all-gather.88
  37.4 67.8 all-gather.68
  121.3 39.8 all-gather.70
  164.5 59.5 all-gather.72
  246.5 27.2 reduce-scatter.33
  277.5 75.6 all-gather.74
  355.4 9.1 all-gather.54
  368.4 61.0 all-gather.76
  432.9 7.9 reduce-scatter.35
  444.3 67.8 all-gather.78
  514.2 8.9 all-gather.56
  544.3 38.1 all-gather.80
  585.1 58.3 all-gather.82
  667.2 27.8 reduce-scatter.37
  698.1 75.6 all-gather.84
  775.8 9.1 all-gather.58
  788.1 61.0 all-gather.86
  858.3 7.9 reduce-scatter.49
  869.0 9.6 reduce-scatter.39
  890.6 24.4 reduce-scatter.51
  917.8 24.0 reduce-scatter.53
  944.5 31.4 all-gather.94
  1021.3 10.0 reduce-scatter.55
  1040.0 35.0 all-gather.90
  1077.7 8.8 reduce-scatter.57
  1115.9 9.1 reduce-scatter.41
  1127.2 10.2 all-gather.60
  1146.4 9.6 reduce-scatter.43
  1158.4 10.2 all-gather.62
  1214.6 35.8 all-gather.92
  1263.7 14.3 reduce-scatter.45
  1280.3 10.2 all-gather.64
  1303.4 9.6 reduce-scatter.65
  1315.4 9.6 reduce-scatter.47
  1337.8 24.4 reduce-scatter.67
  1365.2 24.0 reduce-scatter.69
  1391.7 31.4 all-gather.98
  1460.6 10.0 reduce-scatter.71
  1483.7 9.6 reduce-scatter.73
  1496.2 24.3 reduce-scatter.59
  1523.6 24.1 reduce-scatter.75
  1550.4 24.0 reduce-scatter.61
  1577.5 24.0 reduce-scatter.77
  1603.3 31.4 all-gather.100
  1637.0 30.9 all-gather.96
  1736.8 125.7 all-reduce.66
  1865.2 10.0 reduce-scatter.79
  1878.1 9.6 reduce-scatter.63
  1892.8 129.7 reduce-scatter.81
  2028.8 460.9 all-reduce.68
  2496.4 202.7 reduce-scatter.83
  2701.3 346.1 reduce-scatter.85
  3053.7 139.8 all-reduce.64
where the time goes:
time: 3230 us; the launch traced here: 3210 us
  waiting for transfers between devices  2040 us (63%)
  matrix products  363 us (11%)
  blocking collectives  261 us (8%)
  local copies, waits for them, and re-layouts  252 us (8%)
  other arithmetic  247 us (8%)
    unnamed x57, waiting for transfers between devices  1020 us
    all_gather x8, waiting for transfers between devices, entering(): gathered = jax.tree.map(lambda a: lax.all_gather(a, axis), part)  152 us
    all_gather x2, waiting for transfers between devices, fetch(): lax.all_gather(mlp_w[layer_index], ('fsdp', 'ctx'), axis=0, tiled=True)  146 us
    psum x2, waiting for transfers between devices, settle(): lax.psum((small_grads[0], small_grads[1], small_grads[2], small_grads[3],...  143 us
    all_gather x2, waiting for transfers between devices, fetch(): lax.all_gather(zx_w[layer_index], ('fsdp', 'ctx'), axis=0, tiled=True)  131 us
    reduce_scatter x8, waiting for transfers between devices, narrow(): return lax.psum_scatter(values, 'tp', scatter_dimension=1, tiled=True)  119 us
    all_gather x2, waiting for transfers between devices, fetch(): lax.all_gather(mlp_out_w[layer_index], ('fsdp', 'ctx'), axis=1, tiled=True)  115 us
    unnamed x1064, local copies, waits for them, and re-layouts  107 us
  transfers between devices with their start and end apart: 62, of which 42 were waited for; matrix products, arithmetic and copies ran while one was open for 19% of the time, Pallas kernels for 0%

commit v1 on v0

v1 whole, which is shorter than its diff:
```python
import functools
import math

import jax
import jax.numpy as jnp
from jax import lax
from jax.experimental import pallas as pl
from jax.experimental.pallas import tpu as pltpu
from jax.sharding import PartitionSpec as P

HDIM = 64
STATE = 128
CONV = 4
ADIM = 64
GROUP = 4
LANES = 128
EPSILON = 1e-05
THETA = 100000000000.0
HIGHEST = lax.Precision.HIGHEST
LOW = jnp.bfloat16
WIDE = jnp.float32
MASKED = -1e30
VMEM_LIMIT = 56 * 1024 * 1024


def dot(a, b, ca=1, cb=0, precision=None):
    return lax.dot_general(
        a, b, (((ca,), (cb,)), ((), ())), preferred_element_type=WIDE, precision=precision
    )


def lane_iota(shape):
    return lax.broadcasted_iota(jnp.int32, shape, len(shape) - 1)


def row_iota(shape):
    return lax.broadcasted_iota(jnp.int32, shape, 0)


def kernel_call(body, grid, in_specs, out_specs, out_shape, scratch=(), flops=0, moved=0):
    return pl.pallas_call(
        body,
        grid=grid,
        in_specs=in_specs,
        out_specs=out_specs,
        out_shape=out_shape,
        scratch_shapes=list(scratch),
        compiler_params=pltpu.CompilerParams(vmem_limit_bytes=VMEM_LIMIT),
        cost_estimate=pl.CostEstimate(flops=flops, bytes_accessed=moved, transcendentals=0),
    )


def whole(shape):
    return pl.BlockSpec(shape, lambda s: (0,) * len(shape))


def rows_block(rows, cols, col=0):
    return pl.BlockSpec((rows, cols), lambda s: (s, col))


def sequence_block(*shape):
    return pl.BlockSpec((None,) + shape, lambda s: (s,) + (0,) * len(shape))


def xor_pairs(count, bit):
    return [(i, i ^ bit) for i in range(count)]


def shifted(x, axis, by):
    count = lax.axis_size(axis)
    pairs = [(i, i + by) for i in range(count) if 0 <= i + by < count]
    return lax.ppermute(x, axis, pairs)


def tp_peer(x):
    return lax.ppermute(x, "tp", xor_pairs(lax.axis_size("tp"), 1))


def tp_join(x):
    peer = tp_peer(x)
    first = lax.axis_index("tp") == 0
    return jnp.where(
        first, jnp.concatenate([x, peer], axis=-1), jnp.concatenate([peer, x], axis=-1)
    )


def tp_sum(partial_sum):
    low = partial_sum.astype(LOW)
    peer = tp_peer(low)
    return low.astype(WIDE) + peer.astype(WIDE)


def halve(values, dim, bit, axis, step):
    mine = lax.dynamic_index_in_dim(values, bit, dim, False)
    other = lax.dynamic_index_in_dim(values, 1 - bit, dim, False)
    came = lax.ppermute(other, axis, xor_pairs(lax.axis_size(axis), step))
    return mine.astype(WIDE) + came.astype(WIDE)


def bits_of(axis):
    return [1 << i for i in range(lax.axis_size(axis).bit_length() - 1)]


def scatter_rows(table):
    fsdp, ctx = lax.axis_size("fsdp"), lax.axis_size("ctx")
    width = table.shape[1]
    rows = table.shape[0] // (fsdp * ctx)
    steps = bits_of("ctx")
    place = lax.axis_index("ctx")
    cut = width // 256 * 128
    done = []
    for order, part in ((steps, table[:, :cut]), (steps[::-1], table[:, cut:])):
        left = steps[::-1]
        v = part.reshape((fsdp,) + (2,) * len(steps) + (rows, part.shape[1]))
        for step in order:
            dim = 1 + left.index(step)
            left = [b for b in left if b != step]
            v = halve(v, dim, jnp.where((place & step) != 0, 1, 0), "ctx", step).astype(LOW)
        done.append(v)
    v = jnp.concatenate(done, axis=-1)
    place = lax.axis_index("fsdp")
    for step in bits_of("fsdp")[::-1]:
        v = v.reshape((2, step, rows, width))
        v = halve(v, 0, jnp.where((place & step) != 0, 1, 0), "fsdp", step)
        if step > 1:
            v = v.astype(LOW)
    return v.reshape(rows, width)


def join_rows(piece):
    v = piece[None]
    for axis in ("ctx", "fsdp"):
        place = lax.axis_index(axis)
        for step in bits_of(axis):
            came = lax.ppermute(v, axis, xor_pairs(lax.axis_size(axis), step))
            v = jnp.where(
                (place & step) == 0,
                jnp.concatenate([v, came], axis=0),
                jnp.concatenate([came, v], axis=0),
            )
    return v.reshape((-1,) + piece.shape[1:])


def sum_everywhere(v):
    for axis in ("ctx", "fsdp"):
        for step in bits_of(axis):
            v = v + lax.ppermute(v, axis, xor_pairs(lax.axis_size(axis), step))
    return v


def turn_tables(start_row, rows):
    half = ADIM // 2
    places = (start_row + jnp.arange(rows)).astype(WIDE)
    rates = jnp.exp(-math.log(THETA) * jnp.arange(half).astype(WIDE) / half)
    angles = places[:, None] * rates[None, :]
    cosine, sine = jnp.cos(angles), jnp.sin(angles)
    one_cos = jnp.concatenate([cosine, cosine], axis=1)
    one_sin = jnp.concatenate([-sine, sine], axis=1)
    still = jnp.ones_like(one_cos)
    return (
        jnp.concatenate([one_cos, one_cos, one_cos, still], axis=1),
        jnp.concatenate([one_sin, one_sin, one_sin, jnp.zeros_like(one_sin)], axis=1),
    )


def turned(values, cosine, sine):
    lanes = lane_iota(values.shape) % ADIM
    swapped = jnp.where(
        lanes < ADIM // 2,
        pltpu.roll(values, LANES - ADIM // 2, 1),
        pltpu.roll(values, ADIM // 2, 1),
    )
    return values * cosine + swapped * sine


def qkv_body(rows_ref, cos_ref, sin_ref, q_ref, kv_ref):
    for pair in range(GROUP // 2):
        lanes = slice(pair * LANES, (pair + 1) * LANES)
        q_ref[:, lanes] = turned(
            rows_ref[:, lanes], cos_ref[:, :LANES], sin_ref[:, :LANES]
        ).astype(LOW)
    width = GROUP * ADIM
    kv_ref[...] = turned(
        rows_ref[:, width : width + LANES], cos_ref[:, LANES:], sin_ref[:, LANES:]
    ).astype(LOW)


def split_qkv(projected, tables, rows, column):
    total = projected.shape[0]
    width = GROUP * ADIM
    return kernel_call(
        qkv_body,
        (total // rows,),
        [rows_block(rows, width + LANES, column), whole((rows, 2 * LANES)), whole((rows, 2 * LANES))],
        [rows_block(rows, width), rows_block(rows, LANES)],
        [
            jax.ShapeDtypeStruct((total, width), LOW),
            jax.ShapeDtypeStruct((total, LANES), LOW),
        ],
        flops=total * 400 * 4,
        moved=total * 384 * 6,
    )(projected, *tables)


def head_lanes(values, head):
    pair = values[:, head // 2 * LANES : (head // 2 + 1) * LANES]
    if head % 2:
        pair = pltpu.roll(pair, ADIM, 1)
    return jnp.where(lane_iota(pair.shape) < ADIM, pair, jnp.zeros_like(pair))


def load_keys(kv_refs, keys):
    rows = kv_refs[0].shape[0]
    for i, ref in enumerate(kv_refs):
        keys[i * rows : (i + 1) * rows, :] = ref[...]


def attention_bias(place, rows, count):
    shape = (rows, rows * count)
    column = lane_iota(shape)
    earlier = (column >= rows) & (column < rows * (place + 1))
    return (column <= row_iota(shape)) | earlier


def attend_body(count, place_ref, q_ref, *refs):
    kv_refs, (out_ref, total_ref, keys) = refs[:count], refs[count:]
    rows = q_ref.shape[0]
    load_keys(kv_refs, keys)
    seen = attention_bias(place_ref[0], rows, count)
    q_all = q_ref[...].astype(WIDE)
    all_keys = keys[...]
    totals = jnp.zeros((rows, LANES), WIDE)
    lanes = lane_iota((rows, LANES))
    outs = []
    for head in range(GROUP):
        query = head_lanes(q_all, head).astype(LOW)
        scores = jnp.where(seen, dot(query, all_keys, 1, 1) * ADIM**-0.5, MASKED)
        top = jnp.max(scores, axis=1, keepdims=True)
        raised = jnp.exp(scores - top)
        total = jnp.sum(raised, axis=1, keepdims=True)
        weights = (raised * (1.0 / total)).astype(LOW)
        outs.append(dot(weights, all_keys))
        totals = jnp.where(lanes == head, top + jnp.log(total), totals)
    total_ref[...] = totals
    for pair in range(GROUP // 2):
        first = pltpu.roll(outs[2 * pair], ADIM, 1)
        out_ref[:, pair * LANES : (pair + 1) * LANES] = jnp.where(
            lanes < ADIM, first, outs[2 * pair + 1]
        ).astype(LOW)


def attend(place, queries, kv_list, rows):
    total = queries.shape[0]
    width = queries.shape[1]
    count = len(kv_list)
    return kernel_call(
        functools.partial(attend_body, count),
        (total // rows,),
        [pl.BlockSpec(memory_space=pltpu.SMEM), rows_block(rows, width)]
        + [rows_block(rows, LANES)] * count,
        [rows_block(rows, width), rows_block(rows, LANES)],
        [
            jax.ShapeDtypeStruct((total, width), LOW),
            jax.ShapeDtypeStruct((total, LANES), WIDE),
        ],
        [pltpu.VMEM((rows * count, LANES), LOW)],
        flops=total * rows * count * GROUP * LANES * 4,
        moved=total * (width * 4 + LANES * 12),
    )(place, queries, *kv_list)


def attend_back_body(count, place_ref, q_ref, grad_ref, total_ref, cos_ref, sin_ref, *refs):
    kv_refs = refs[:count]
    dq_ref = refs[count]
    dkv_refs = refs[count + 1 : 2 * count + 1]
    keys = refs[2 * count + 1]
    rows = q_ref.shape[0]
    load_keys(kv_refs, keys)
    seen = attention_bias(place_ref[0], rows, count)
    q_all = q_ref[...].astype(WIDE)
    grad_all = grad_ref[...].astype(WIDE)
    all_keys = keys[...]
    lanes = lane_iota((rows, LANES))
    grad_kv = None
    dqs = []
    for head in range(GROUP):
        query = head_lanes(q_all, head).astype(LOW)
        upper = pltpu.roll(head_lanes(grad_all, head), ADIM, 1).astype(LOW)
        scores = jnp.where(seen, dot(query, all_keys, 1, 1) * ADIM**-0.5, MASKED)
        probs = jnp.exp(scores - total_ref[:, head : head + 1])
        grad_probs = dot(upper, all_keys, 1, 1)
        inner = jnp.sum(probs * grad_probs, axis=1, keepdims=True)
        grad_scores = (probs * (grad_probs - inner)).astype(LOW)
        dqs.append(dot(grad_scores, all_keys) * ADIM**-0.5)
        fresh = dot(grad_scores, query, 0, 0) * ADIM**-0.5 + dot(
            probs.astype(LOW), upper, 0, 0
        )
        grad_kv = fresh if grad_kv is None else grad_kv + fresh
    for pair in range(GROUP // 2):
        both = jnp.where(lanes < ADIM, dqs[2 * pair], pltpu.roll(dqs[2 * pair + 1], ADIM, 1))
        dq_ref[:, pair * LANES : (pair + 1) * LANES] = turned(
            both, cos_ref[:, :LANES], -sin_ref[:, :LANES]
        ).astype(LOW)
    for i, ref in enumerate(dkv_refs):
        ref[...] = grad_kv[i * rows : (i + 1) * rows].astype(ref.dtype)


def attend_back(place, queries, grad_out, log_total, tables, kv_list, rows):
    total, width = queries.shape
    count = len(kv_list)
    return kernel_call(
        functools.partial(attend_back_body, count),
        (total // rows,),
        [
            pl.BlockSpec(memory_space=pltpu.SMEM),
            rows_block(rows, width),
            rows_block(rows, width),
            rows_block(rows, LANES),
            whole((rows, 2 * LANES)),
            whole((rows, 2 * LANES)),
        ]
        + [rows_block(rows, LANES)] * count,
        [rows_block(rows, width)] + [rows_block(rows, LANES)] * count,
        [jax.ShapeDtypeStruct((total, width), LOW), jax.ShapeDtypeStruct((total, LANES), WIDE)]
        + [jax.ShapeDtypeStruct((total, LANES), LOW)] * (count - 1),
        [pltpu.VMEM((rows * count, LANES), LOW)],
        flops=total * rows * count * GROUP * LANES * 10,
        moved=total * (width * 6 + LANES * 20),
    )(place, queries, grad_out, log_total, *tables, *kv_list)


def key_body(own_ref, *refs):
    came, (cos_ref, sin_ref, out_ref) = refs[:-3], refs[-3:]
    values = own_ref[...]
    for ref in came:
        values = values + ref[...].astype(WIDE)
    out_ref[...] = turned(values, cos_ref[:, LANES:], -sin_ref[:, LANES:]).astype(LOW)


def finish_keys(own, came, tables, rows):
    total = own.shape[0]
    return kernel_call(
        key_body,
        (total // rows,),
        [rows_block(rows, LANES)] * (1 + len(came)) + [whole((rows, 2 * LANES))] * 2,
        rows_block(rows, LANES),
        jax.ShapeDtypeStruct((total, LANES), LOW),
        flops=total * LANES * 10,
        moved=total * LANES * 12,
    )(own, *came, *tables)


def sigmoid(v):
    return 1.0 / (1.0 + jnp.exp(-v))


def softplus(v):
    return jnp.maximum(v, 0.0) + jnp.log1p(jnp.exp(-jnp.abs(v)))


def over_pair(values, pair, shape):
    first = values[:, 2 * pair : 2 * pair + 1]
    second = values[:, 2 * pair + 1 : 2 * pair + 2]
    return jnp.where(lane_iota(shape) < HDIM, first, second)


def lower_ones(rows, flip):
    shape = (rows, rows)
    t, s = row_iota(shape), lane_iota(shape)
    return jnp.where((t <= s) if flip else (t >= s), 1.0, 0.0).astype(WIDE)


def convolved(padded, taps_ref, rows):
    total = taps_ref[CONV : CONV + 1, :]
    for j in range(CONV):
        first = 8 - CONV + 1 + j
        total = total + taps_ref[j : j + 1, :] * padded[first : first + rows, :]
    return total


def scan_body(
    zx_ref, side_ref, rim_ref, taps_ref, heads_ref,
    stk_ref, x_ref, bc_ref, y_ref, state_ref, cum_ref, step_ref, padded,
):
    rows, channels = zx_ref.shape
    heads = channels // HDIM
    stk_ref[:, :channels] = zx_ref[...].astype(LOW)
    stk_ref[:, channels:] = side_ref[:, : 2 * STATE].astype(LOW)
    padded[0:8, :] = rim_ref[...]
    padded[8 : 8 + rows, :] = stk_ref[...].astype(WIDE)
    before = convolved(padded, taps_ref, rows)
    active = (before * sigmoid(before)).astype(LOW)
    x_ref[...] = active[:, :channels]
    bc_ref[...] = active[:, channels:]
    step = softplus(side_ref[:, 2 * STATE :] + heads_ref[1:2, :])
    cum = dot(lower_ones(rows, False), -step * jnp.exp(heads_ref[0:1, :]), precision=HIGHEST)
    step_ref[...] = step
    cum_ref[...] = cum
    cum_rows, step_rows = cum.T, step.T
    tail = jnp.exp(cum[rows - 1 : rows, :] - cum) * step
    entry, readout = bc_ref[:, :STATE], bc_ref[:, STATE:]
    cross = dot(readout, entry, 1, 1)
    shape = (rows, rows)
    causal = row_iota(shape) >= lane_iota(shape)
    lanes = lane_iota((rows, LANES))
    for pair in range(heads // 2):
        block = slice(pair * LANES, (pair + 1) * LANES)
        inputs = x_ref[:, block]
        outs = []
        for head in (2 * pair, 2 * pair + 1):
            gap = cum[:, head : head + 1] - cum_rows[head : head + 1, :]
            decay = jnp.exp(jnp.where(causal, gap, MASKED))
            mixed = (decay * cross * step_rows[head : head + 1, :]).astype(LOW)
            outs.append(dot(mixed, inputs))
        y_ref[:, block] = jnp.where(lanes < HDIM, outs[0], outs[1])
        scaled = (over_pair(tail, pair, (rows, LANES)) * inputs.astype(WIDE)).astype(LOW)
        state_ref[block, :] = dot(scaled, entry, 0, 0)


def scan_local(projected, side, rim, taps, heads, rows, channels):
    total = projected.shape[0]
    count = total // rows
    width = channels + 2 * STATE
    return kernel_call(
        scan_body,
        (count,),
        [
            rows_block(rows, channels, 1),
            rows_block(rows, side.shape[1]),
            sequence_block(8, width),
            whole((8, width)),
            whole((8, LANES)),
        ],
        [
            rows_block(rows, width),
            rows_block(rows, channels),
            rows_block(rows, 2 * STATE),
            rows_block(rows, channels),
            rows_block(channels, STATE),
            rows_block(rows, LANES),
            rows_block(rows, LANES),
        ],
        [
            jax.ShapeDtypeStruct((total, width), LOW),
            jax.ShapeDtypeStruct((total, channels), LOW),
            jax.ShapeDtypeStruct((total, 2 * STATE), LOW),
            jax.ShapeDtypeStruct((total, channels), WIDE),
            jax.ShapeDtypeStruct((count * channels, STATE), WIDE),
            jax.ShapeDtypeStruct((total, LANES), WIDE),
            jax.ShapeDtypeStruct((total, LANES), WIDE),
        ],
        [pltpu.VMEM((rows + 8, width), WIDE)],
        flops=total * rows * channels * 8,
        moved=total * width * 16,
    )(projected, side, rim, taps, heads)


def tail_body(
    y_ref, cum_ref, bc_ref, x_ref, gate_ref, start_ref, heads_ref, gain_ref, out_ref, norm_ref
):
    rows, channels = y_ref.shape
    readout = bc_ref[:, STATE:]
    grown = jnp.exp(cum_ref[...])
    square = jnp.zeros((rows, 1), WIDE)
    for pair in range(channels // LANES):
        block = slice(pair * LANES, (pair + 1) * LANES)
        carried = dot(readout, start_ref[block, :].astype(LOW), 1, 1)
        y = y_ref[:, block] + over_pair(grown, pair, carried.shape) * carried
        out_ref[:, block] = y
        skip = over_pair(heads_ref[2:3, :], pair, (1, LANES))
        gate = gate_ref[:, block]
        mixed = (y + skip * x_ref[:, block].astype(WIDE)) * (gate * sigmoid(gate))
        square = square + jnp.sum(mixed * mixed, axis=1, keepdims=True)
    scale = lax.rsqrt(square * (1.0 / channels) + EPSILON)
    for pair in range(channels // LANES):
        block = slice(pair * LANES, (pair + 1) * LANES)
        skip = over_pair(heads_ref[2:3, :], pair, (1, LANES))
        gate = gate_ref[:, block]
        mixed = (out_ref[:, block] + skip * x_ref[:, block].astype(WIDE)) * (gate * sigmoid(gate))
        norm_ref[:, block] = (mixed * scale * gain_ref[:, block]).astype(LOW)


def gate_tail(y, cum, bc, x, projected, start, heads, gain, rows):
    total, channels = y.shape
    return kernel_call(
        tail_body,
        (total // rows,),
        [
            rows_block(rows, channels),
            rows_block(rows, LANES),
            rows_block(rows, 2 * STATE),
            rows_block(rows, channels),
            rows_block(rows, channels, 0),
            rows_block(channels, STATE),
            whole((8, LANES)),
            whole((1, channels)),
        ],
        [rows_block(rows, channels), rows_block(rows, channels)],
        [
            jax.ShapeDtypeStruct((total, channels), WIDE),
            jax.ShapeDtypeStruct((total, channels), LOW),
        ],
        flops=total * channels * (2 * STATE + 40),
        moved=total * channels * 18,
    )(y, cum, bc, x, projected, start, heads, gain)


def tail_back_body(
    dn_ref, y_ref, cum_ref, bc_ref, x_ref, gate_ref, heads_ref, gain_ref,
    du_ref, dgate_ref, state_ref, sums_ref,
):
    rows, channels = y_ref.shape
    readout = bc_ref[:, STATE:]
    grown = jnp.exp(cum_ref[...])
    square = jnp.zeros((rows, 1), WIDE)
    inner = jnp.zeros((rows, 1), WIDE)
    for pair in range(channels // LANES):
        block = slice(pair * LANES, (pair + 1) * LANES)
        skip = over_pair(heads_ref[2:3, :], pair, (1, LANES))
        gate = gate_ref[:, block]
        mixed = (y_ref[:, block] + skip * x_ref[:, block].astype(WIDE)) * (gate * sigmoid(gate))
        square = square + jnp.sum(mixed * mixed, axis=1, keepdims=True)
        inner = inner + jnp.sum(
            dn_ref[:, block] * gain_ref[:, block] * mixed, axis=1, keepdims=True
        )
    scale = lax.rsqrt(square * (1.0 / channels) + EPSILON)
    inner = inner * scale * (1.0 / channels)
    sums_ref[...] = jnp.zeros(sums_ref.shape, WIDE)
    for pair in range(channels // LANES):
        block = slice(pair * LANES, (pair + 1) * LANES)
        skip = over_pair(heads_ref[2:3, :], pair, (1, LANES))
        gate = gate_ref[:, block]
        inputs = x_ref[:, block].astype(WIDE)
        sigma = sigmoid(gate)
        value = y_ref[:, block] + skip * inputs
        unit = value * (gate * sigma) * scale
        upstream = dn_ref[:, block]
        dmixed = scale * (upstream * gain_ref[:, block] - unit * inner)
        du = dmixed * gate * sigma
        du_ref[:, block] = du
        dgate_ref[:, block] = (
            dmixed * value * (sigma * (1.0 + gate * (1.0 - sigma)))
        ).astype(LOW)
        sums_ref[0:1, block] = jnp.sum(upstream * unit, axis=0, keepdims=True)
        sums_ref[1:2, block] = jnp.sum(du * inputs, axis=0, keepdims=True)
        state_ref[block, :] = dot(
            (over_pair(grown, pair, du.shape) * du).astype(LOW), readout, 0, 0
        )


def gate_tail_back(dn, y, cum, bc, x, projected, heads, gain, rows):
    total, channels = y.shape
    count = total // rows
    return kernel_call(
        tail_back_body,
        (count,),
        [
            rows_block(rows, channels),
            rows_block(rows, channels),
            rows_block(rows, LANES),
            rows_block(rows, 2 * STATE),
            rows_block(rows, channels),
            rows_block(rows, channels, 0),
            whole((8, LANES)),
            whole((1, channels)),
        ],
        [
            rows_block(rows, channels),
            rows_block(rows, channels),
            rows_block(channels, STATE),
            sequence_block(8, channels),
        ],
        [
            jax.ShapeDtypeStruct((total, channels), WIDE),
            jax.ShapeDtypeStruct((total, channels), LOW),
            jax.ShapeDtypeStruct((count * channels, STATE), WIDE),
            jax.ShapeDtypeStruct((count, 8, channels), WIDE),
        ],
        flops=total * channels * (2 * STATE + 60),
        moved=total * channels * 22,
    )(dn, y, cum, bc, x, projected, heads, gain)


def lane_sums(values):
    first = lane_iota(values.shape) < HDIM
    return (
        jnp.sum(jnp.where(first, values, 0.0), axis=1, keepdims=True),
        jnp.sum(jnp.where(first, 0.0, values), axis=1, keepdims=True),
    )


def scan_back_body(
    du_ref, x_ref, bc_ref, stk_ref, rim_ref, cum_ref, step_ref, side_ref, start_ref, later_ref,
    taps_ref, heads_ref,
    dstk_ref, drim_ref, dstep_ref, dtaps_ref, dheads_ref, padded, dact, after,
):
    rows, channels = du_ref.shape
    heads = channels // HDIM
    width = channels + 2 * STATE
    entry, readout = bc_ref[:, :STATE], bc_ref[:, STATE:]
    cum, step = cum_ref[...], step_ref[...]
    cum_rows = cum.T
    last = cum[rows - 1 : rows, :]
    grown = jnp.exp(cum)
    decayed = jnp.exp(last - cum)
    tail = decayed * step
    cross = dot(entry, readout, 1, 1)
    shape = (rows, rows)
    causal = row_iota(shape) <= lane_iota(shape)
    lanes = lane_iota((rows, LANES))
    small = lane_iota((1, LANES))
    dcross = jnp.zeros(shape, WIDE)
    entry_grad = jnp.zeros((rows, STATE), WIDE)
    readout_grad = jnp.zeros((rows, STATE), WIDE)
    pulled = jnp.zeros((rows, LANES), WIDE)
    arrived = []
    carried_sum = jnp.zeros((rows, LANES), WIDE)
    final_sum = jnp.zeros((rows, LANES), WIDE)
    state_sum = jnp.zeros((1, LANES), WIDE)
    for pair in range(heads // 2):
        block = slice(pair * LANES, (pair + 1) * LANES)
        inputs = x_ref[:, block]
        inputs_wide = inputs.astype(WIDE)
        du = du_ref[:, block]
        du_low = du.astype(LOW)
        start = start_ref[block, :]
        later = later_ref[block, :]
        start_low, later_low = start.astype(LOW), later.astype(LOW)
        pulls = []
        for k in range(2):
            head = 2 * pair + k
            own = (lanes < HDIM) if k == 0 else (lanes >= HDIM)
            gap = cum_rows[head : head + 1, :] - cum[:, head : head + 1]
            decay = jnp.exp(jnp.where(causal, gap, MASKED))
            pulls.append(dot((decay * cross).astype(LOW), du_low))
            dmix = dot(jnp.where(own, inputs, jnp.zeros_like(inputs)), du_low, 1, 1) * decay
            stepped = step[:, head : head + 1]
            dcross = dcross + dmix * stepped
            dgap = dmix * cross
            pulled = jnp.where(lanes == head, jnp.sum(dgap, axis=1, keepdims=True), pulled)
            arrived.append(jnp.sum(dgap * stepped, axis=0, keepdims=True))
        pull = jnp.where(lanes < HDIM, pulls[0], pulls[1])
        grown_pair = over_pair(grown, pair, du.shape)
        grown_du = grown_pair * du
        readout_grad = readout_grad + dot(grown_du.astype(LOW), start_low)
        sums = lane_sums(grown_du * dot(readout, start_low, 1, 1))
        carried_sum = jnp.where(lanes == 2 * pair, sums[0], carried_sum)
        carried_sum = jnp.where(lanes == 2 * pair + 1, sums[1], carried_sum)
        tail_pair = over_pair(tail, pair, du.shape)
        from_later = dot(entry, later_low, 1, 1)
        entry_grad = entry_grad + dot((tail_pair * inputs_wide).astype(LOW), later_low)
        sums = lane_sums(inputs_wide * from_later)
        final_sum = jnp.where(lanes == 2 * pair, sums[0], final_sum)
        final_sum = jnp.where(lanes == 2 * pair + 1, sums[1], final_sum)
        product = start * later
        for k in range(2):
            total = jnp.sum(
                jnp.sum(product[k * HDIM : (k + 1) * HDIM], axis=0, keepdims=True),
                axis=1,
                keepdims=True,
            )
            state_sum = jnp.where(small == 2 * pair + k, total, state_sum)
        skip = over_pair(heads_ref[2:3, :], pair, (1, LANES))
        dact[:, block] = (
            skip * du + over_pair(step, pair, du.shape) * pull + tail_pair * from_later
        )
    dcross_low = dcross.astype(LOW)
    dact[:, channels : channels + STATE] = entry_grad + dot(dcross_low, readout)
    dact[:, channels + STATE :] = readout_grad + dot(dcross_low, entry, 0, 0)
    arrived.append(jnp.zeros((LANES - heads, rows), WIDE))
    arrived_columns = jnp.concatenate(arrived, axis=0).T
    weighted = tail * final_sum
    dcum = arrived_columns - step * pulled + carried_sum - weighted
    at_last = jnp.sum(weighted, axis=0, keepdims=True) + jnp.exp(last) * state_sum
    dcum = dcum + jnp.where(row_iota(dcum.shape) == rows - 1, at_last, 0.0)
    dlog = dot(lower_ones(rows, True), dcum, precision=HIGHEST)
    rate = jnp.exp(heads_ref[0:1, :])
    dstep = pulled + decayed * final_sum - rate * dlog
    dstep_pre = dstep * sigmoid(side_ref[...] + heads_ref[1:2, :])
    dstep_pre = jnp.where(lanes < heads, dstep_pre, 0.0)
    dstep_ref[...] = dstep_pre.astype(LOW)
    dheads_ref[...] = jnp.zeros(dheads_ref.shape, WIDE)
    dheads_ref[0:1, :] = -rate * jnp.sum(step * dlog, axis=0, keepdims=True)
    dheads_ref[1:2, :] = jnp.sum(dstep_pre, axis=0, keepdims=True)

    padded[0:8, :] = rim_ref[...]
    padded[8 : 8 + rows, :] = stk_ref[...].astype(WIDE)
    before = convolved(padded, taps_ref, rows)
    sigma = sigmoid(before)
    dbefore = dact[...] * sigma * (1.0 + before * (1.0 - sigma))
    after[0:8, :] = jnp.zeros((8, width), WIDE)
    after[8 : 8 + rows, :] = dbefore
    after[8 + rows : 16 + rows, :] = jnp.zeros((8, width), WIDE)
    dtaps_ref[...] = jnp.zeros(dtaps_ref.shape, WIDE)
    back = None
    for j in range(CONV):
        first = 8 - CONV + 1 + j
        dtaps_ref[j : j + 1, :] = jnp.sum(
            after[8 : 8 + rows, :] * padded[first : first + rows, :], axis=0, keepdims=True
        )
        first = CONV - 1 - j
        term = taps_ref[j : j + 1, :] * after[first : first + rows + 8, :]
        back = term if back is None else back + term
    dtaps_ref[CONV : CONV + 1, :] = jnp.sum(after[8 : 8 + rows, :], axis=0, keepdims=True)
    drim_ref[...] = back[0:8]
    dstk_ref[...] = back[8:]


def scan_back(du, x, bc, stk, rim, cum, step, side, start, later, taps, heads, rows):
    total, channels = du.shape
    count = total // rows
    width = channels + 2 * STATE
    return kernel_call(
        scan_back_body,
        (count,),
        [
            rows_block(rows, channels),
            rows_block(rows, channels),
            rows_block(rows, 2 * STATE),
            rows_block(rows, width),
            sequence_block(8, width),
            rows_block(rows, LANES),
            rows_block(rows, LANES),
            rows_block(rows, LANES, 2 * STATE // LANES),
            rows_block(channels, STATE),
            rows_block(channels, STATE),
            whole((8, width)),
            whole((8, LANES)),
        ],
        [
            rows_block(rows, width),
            sequence_block(8, width),
            rows_block(rows, LANES),
            sequence_block(8, width),
            sequence_block(8, LANES),
        ],
        [
            jax.ShapeDtypeStruct((total, width), WIDE),
            jax.ShapeDtypeStruct((count, 8, width), WIDE),
            jax.ShapeDtypeStruct((total, LANES), LOW),
            jax.ShapeDtypeStruct((count, 8, width), WIDE),
            jax.ShapeDtypeStruct((count, 8, LANES), WIDE),
        ],
        [
            pltpu.VMEM((rows + 8, width), WIDE),
            pltpu.VMEM((rows, width), WIDE),
            pltpu.VMEM((rows + 16, width), WIDE),
        ],
        flops=total * rows * channels * 20,
        moved=total * width * 24,
    )(du, x, bc, stk, rim, cum, step, side, start, later, taps, heads)


def pass_states(states, decays, heads, forward):
    count = lax.axis_size("ctx")
    place = lax.axis_index("ctx")
    sequences = decays.shape[0]
    channels = states.shape[0] // sequences
    high = decays.astype(LOW)
    low = (decays - high.astype(WIDE)).astype(LOW)
    extra = jnp.concatenate(
        [high[..., None], low[..., None], jnp.zeros((sequences, LANES, 14), LOW)], axis=2
    ).transpose(0, 2, 1)
    parcel = jnp.concatenate([states.reshape(sequences, channels, STATE).astype(LOW), extra], axis=1)
    total = None
    for by in range(count - 1, 0, -1):
        came = shifted(parcel, "ctx", by if forward else -by).astype(WIDE)
        fresh = came[:, :channels]
        if total is not None:
            factor = (came[:, channels] + came[:, channels + 1])[:, :heads]
            fresh = fresh + jnp.repeat(factor, HDIM, axis=1)[:, :, None] * total
        total = fresh
    return total.reshape(states.shape)


def unit_scale(values):
    return lax.rsqrt(jnp.mean(values * values, axis=-1, keepdims=True) + EPSILON)


def normalize(values, gain):
    return (values * unit_scale(values) * gain).astype(LOW)


def norm_grad(kept, gain, upstream):
    scale = unit_scale(kept)
    unit = kept * scale
    scaled = upstream * gain
    inner = jnp.mean(scaled * unit, axis=-1, keepdims=True)
    return scale * (scaled - unit * inner), jnp.sum(upstream * unit, axis=0)


def product(a, b):
    return jnp.dot(a, b, preferred_element_type=WIDE)


def against_rows(a, b):
    return dot(a, b, 1, 1)


def over_rows(a, b):
    return dot(a, b, 0, 0).astype(LOW)


def gathered(piece):
    return lax.all_gather(piece, ("fsdp", "ctx"), axis=0, tiled=True)


def fetch(layer, pieces):
    zx, mix, attn, attn_out, mlp, mlp_out = (p[layer] for p in pieces)
    rows = zx.shape[0]
    return (
        gathered(jnp.concatenate([zx.reshape(rows, -1), attn.reshape(rows, -1)], axis=1)),
        gathered(jnp.concatenate([mix.T, attn_out.T], axis=1)),
        gathered(mlp.reshape(rows, -1)),
        gathered(mlp_out.T),
    )


def own_part(values, size, axis):
    return lax.dynamic_slice_in_dim(values, lax.axis_index("tp") * size, size, axis)


def padded_to(values, rows, lanes):
    return jnp.pad(values, ((0, rows - values.shape[0]), (0, lanes - values.shape[1])))


def local_small(layer, norm_gains, mamba_shared, conv_weight, conv_bias, head_params, mamba_gain):
    tp = lax.axis_size("tp")
    heads = head_params.shape[2] // tp
    full_ssm = mamba_gain.shape[1]
    channels = full_ssm // tp
    shared_all = mamba_shared[layer]
    shared = jnp.concatenate(
        [
            shared_all[:, : 2 * STATE],
            own_part(shared_all[:, 2 * STATE :], heads, 1),
            jnp.zeros((shared_all.shape[0], LANES - heads), LOW),
        ],
        axis=1,
    )
    taps_all = jnp.concatenate([conv_weight[layer], conv_bias[layer][None]], axis=0).astype(WIDE)
    taps = jnp.concatenate(
        [own_part(taps_all[:, :full_ssm], channels, 1), taps_all[:, full_ssm:]], axis=1
    )
    return (
        norm_gains[layer].astype(WIDE),
        shared,
        padded_to(taps, 8, taps.shape[1]),
        padded_to(own_part(head_params[layer], heads, 1), 8, LANES),
        own_part(mamba_gain[layer].astype(WIDE), channels, 0)[None],
    )


def layer_forward(hidden, weights, small, tables, place, sequences):
    zx_w, mix_w, mlp_w, mlp_out_w = weights
    gains, shared, taps, heads, gain = small
    rows = hidden.shape[0] // sequences
    channels = gain.shape[1]
    head_count = channels // HDIM
    normed = normalize(hidden, gains[0])
    projected = product(normed, zx_w)
    side = product(normed, shared)
    edge = jnp.concatenate(
        [projected[:, channels : 2 * channels], side[:, : 2 * STATE]], axis=1
    ).reshape(sequences, rows, -1)[:, rows - CONV + 1 :]
    came = shifted(edge.astype(LOW), "ctx", 1).astype(WIDE)
    rim = jnp.pad(came, ((0, 0), (8 - CONV + 1, 0), (0, 0)))
    queries, kv = split_qkv(projected, tables, rows, 2 * channels // (zx_w.shape[1] - 2 * channels))
    kv_list = [kv] + [shifted(kv, "ctx", by) for by in range(1, lax.axis_size("ctx"))]
    stk, x, bc, y_local, states, cum, step = scan_local(
        projected, side, rim, taps, heads, rows, channels
    )
    decays = jnp.exp(cum.reshape(sequences, rows, LANES)[:, -1])
    start = pass_states(states, decays, head_count, True)
    attended, log_total = attend(place, queries, kv_list, rows)
    y, mamba_norm = gate_tail(y_local, cum, bc, x, projected, start, heads, gain, rows)
    both = jnp.concatenate([mamba_norm, attended], axis=1)
    after_mix = hidden + tp_sum(against_rows(both, mix_w))
    normed_two = normalize(after_mix, gains[1])
    gate_up = product(normed_two, mlp_w)
    ff = gate_up.shape[1] // 2
    activated = (jax.nn.silu(gate_up[:, :ff]) * gate_up[:, ff:]).astype(LOW)
    result = after_mix + tp_sum(against_rows(activated, mlp_out_w))
    saved = (
        hidden, normed, projected, side, rim, queries, kv_list, stk, x, bc, cum, step, decays,
        start, log_total, y, both, after_mix, normed_two, gate_up, activated,
    )
    return result, saved


def layer_backward(upstream, saved, weights, small, tables, place, sequences):
    (
        hidden, normed, projected, side, rim, queries, kv_list, stk, x, bc, cum, step, decays,
        start, log_total, y, both, after_mix, normed_two, gate_up, activated,
    ) = saved
    zx_w, mix_w, mlp_w, mlp_out_w = weights
    gains, shared, taps, heads, gain = small
    rows = hidden.shape[0] // sequences
    channels = gain.shape[1]
    head_count = channels // HDIM
    grad_mlp = upstream.astype(LOW)
    grad_mlp_out = scatter_rows(over_rows(grad_mlp, activated))
    grad_act = product(grad_mlp, mlp_out_w)
    ff = grad_act.shape[1]
    gate_part, up_part = gate_up[:, :ff], gate_up[:, ff:]
    sigma = jax.nn.sigmoid(gate_part)
    grad_gu = jnp.concatenate(
        [
            grad_act * up_part * sigma * (1.0 + gate_part * (1.0 - sigma)),
            grad_act * gate_part * sigma,
        ],
        axis=1,
    ).astype(LOW)
    grad_mlp_in = scatter_rows(over_rows(normed_two, grad_gu))
    mid_part, grad_gain_two = norm_grad(
        after_mix, gains[1], tp_sum(against_rows(grad_gu, mlp_w))
    )
    grad_mid = upstream + mid_part
    grad_mix = grad_mid.astype(LOW)
    grad_mix_out = scatter_rows(over_rows(grad_mix, both))
    grad_norm = product(grad_mix, mix_w[:, :channels])
    grad_attended = product(grad_mix, mix_w[:, channels:]).astype(LOW)
    du, grad_gate, state_grads, tail_sums = gate_tail_back(
        grad_norm, y, cum, bc, x, projected, heads, gain, rows
    )
    later = pass_states(state_grads, decays, head_count, False)
    grad_q, own_kv, *sent_kv = attend_back(
        place, queries, grad_attended, log_total, tables, kv_list, rows
    )
    came_kv = [shifted(v, "ctx", -by) for by, v in enumerate(sent_kv, 1)]
    dstk, drim, grad_step, dtaps, dheads = scan_back(
        du, x, bc, stk, rim, cum, step, side, start, later, taps, heads, rows
    )
    returned = shifted(drim[:, 8 - CONV + 1 :], "ctx", -1)
    dstk = (
        dstk.reshape(sequences, rows, -1)
        + jnp.pad(returned, ((0, 0), (rows - CONV + 1, 0), (0, 0)))
    ).reshape(dstk.shape)
    grad_kv = finish_keys(own_kv, came_kv, tables, rows)
    grad_first = jnp.concatenate(
        [grad_gate, dstk[:, :channels].astype(LOW), grad_q, grad_kv], axis=1
    )
    grad_side = jnp.concatenate([dstk[:, channels:].astype(LOW), grad_step], axis=1)
    grad_in = scatter_rows(over_rows(normed, jnp.concatenate([grad_first, grad_side], axis=1)))
    below, grad_gain_one = norm_grad(
        hidden,
        gains[0],
        tp_sum(against_rows(grad_first, zx_w) + against_rows(grad_side, shared)),
    )
    tail_sums = jnp.sum(tail_sums, axis=0)
    dheads = jnp.sum(dheads, axis=0)
    skip_grad = jnp.sum(tail_sums[1].reshape(head_count, HDIM), axis=1)
    small_grads = (
        jnp.stack([grad_gain_one, grad_gain_two]),
        jnp.sum(dtaps, axis=0)[: CONV + 1],
        jnp.concatenate([dheads[:2, :head_count], skip_grad[None]], axis=0),
        tail_sums[0],
    )
    return grad_mid + below, (grad_in, grad_mix_out, grad_mlp_in, grad_mlp_out), small_grads


def settle_small(small_grads, side_grad, full_ssm, heads_total):
    gains, taps, heads, gain = small_grads
    channels = gain.shape[0]
    shapes = [v.shape for v in small_grads]
    flat = [jnp.pad(v.reshape(-1), (0, -v.size % LANES)) for v in small_grads]
    sizes = [v.shape[0] for v in flat]
    packed = sum_everywhere(jnp.concatenate(flat).reshape(-1, LANES)).reshape(-1)
    own = []
    first = 0
    for size, shape in zip(sizes, shapes):
        own.append(packed[first : first + math.prod(shape)].reshape(shape))
        first += size
    shifted_in = tp_peer(packed)
    peer = []
    first = 0
    for size, shape in zip(sizes, shapes):
        peer.append(shifted_in[first : first + math.prod(shape)].reshape(shape))
        first += size
    low_half = lax.axis_index("tp") == 0

    def ordered(a, b):
        return jnp.where(
            low_half, jnp.concatenate([a, b], axis=-1), jnp.concatenate([b, a], axis=-1)
        )

    gains_full = jnp.where(low_half, own[0], peer[0])
    taps_full = jnp.concatenate(
        [
            ordered(own[1][:, :channels], peer[1][:, :channels]),
            own[1][:, channels:] + peer[1][:, channels:],
        ],
        axis=1,
    )
    half_heads = heads_total // lax.axis_size("tp")
    side_peer = tp_peer(side_grad)
    side = jnp.concatenate(
        [
            side_grad[:, : 2 * STATE] + side_peer[:, : 2 * STATE],
            ordered(
                side_grad[:, 2 * STATE : 2 * STATE + half_heads],
                side_peer[:, 2 * STATE : 2 * STATE + half_heads],
            ),
        ],
        axis=1,
    )
    return (
        gains_full,
        join_rows(side),
        taps_full[:CONV],
        taps_full[CONV],
        ordered(own[2], peer[2]),
        ordered(own[3], peer[3]),
    )


def local(
    hidden_in, lengths, norm_gains, mamba_zx, mamba_shared, conv_weight, conv_bias, head_params,
    mamba_gain, mamba_out, attn_in, attn_out, mlp_in, mlp_out, out_grad,
):
    layers = norm_gains.shape[0]
    micro, own_seqs, rows, features = hidden_in.shape
    sequences = micro * own_seqs
    full_ssm = mamba_gain.shape[1]
    heads_total = head_params.shape[2]
    ctx_place = lax.axis_index("ctx")
    start_row = ctx_place * rows
    place = ctx_place.astype(jnp.int32).reshape(1)
    tables = turn_tables(start_row, rows)
    pieces = (mamba_zx, mamba_out, attn_in, attn_out, mlp_in, mlp_out)
    smalls = [
        local_small(l, norm_gains, mamba_shared, conv_weight, conv_bias, head_params, mamba_gain)
        for l in range(layers)
    ]
    weights = [fetch(l, pieces) for l in range(layers)]
    keep = (
        (start_row + jnp.arange(rows))[None, :] < lengths.reshape(sequences)[:, None]
    ).astype(WIDE).reshape(sequences * rows, 1)
    hidden = tp_join(hidden_in.reshape(sequences * rows, features)).astype(WIDE)
    upstream = tp_join(out_grad.reshape(sequences * rows, features)).astype(WIDE) * keep
    saved = []
    for l in range(layers):
        hidden, kept = layer_forward(hidden, weights[l], smalls[l], tables, place, sequences)
        saved.append(kept)
    mixed_out = own_part(hidden * keep, features, 1).astype(LOW).reshape(hidden_in.shape)
    big, rest = [None] * layers, [None] * layers
    for l in reversed(range(layers)):
        upstream, big[l], small_grads = layer_backward(
            upstream, saved[l], weights[l], smalls[l], tables, place, sequences
        )
        side_grad = big[l][0][:, -3 * LANES :]
        rest[l] = settle_small(small_grads, side_grad, full_ssm, heads_total)
    input_grad = own_part(upstream, features, 1).reshape(hidden_in.shape)

    def stacked(pick):
        return jnp.stack([pick(l) for l in range(layers)])

    zx_width = mamba_zx.shape[2] * mamba_zx.shape[3]
    attn_width = attn_in.shape[2] * attn_in.shape[3]
    channels = mamba_out.shape[1]
    return (
        mixed_out,
        input_grad,
        stacked(lambda l: rest[l][0]),
        stacked(lambda l: big[l][0][:, :zx_width]).reshape(mamba_zx.shape),
        stacked(lambda l: rest[l][1]),
        stacked(lambda l: rest[l][2]),
        stacked(lambda l: rest[l][3]),
        stacked(lambda l: rest[l][4]),
        stacked(lambda l: rest[l][5]),
        stacked(lambda l: big[l][1][:, :channels].T),
        stacked(lambda l: big[l][0][:, zx_width : zx_width + attn_width]).reshape(attn_in.shape),
        stacked(lambda l: big[l][1][:, channels:].T),
        stacked(lambda l: big[l][2]).reshape(mlp_in.shape),
        stacked(lambda l: big[l][3].T),
    )


def solution(mesh):
    placed = (
        P(None, "fsdp", "ctx", "tp"),
        P(None, "fsdp"),
        P(),
        P(None, ("fsdp", "ctx"), None, "tp"),
        P(),
        P(),
        P(),
        P(),
        P(),
        P(None, "tp", ("fsdp", "ctx")),
        P(None, ("fsdp", "ctx"), "tp", None),
        P(None, "tp", ("fsdp", "ctx")),
        P(None, ("fsdp", "ctx"), None, "tp"),
        P(None, "tp", ("fsdp", "ctx")),
        P(None, "fsdp", "ctx", "tp"),
    )
    return jax.shard_map(
        local,
        mesh=mesh,
        in_specs=placed,
        out_specs=(
            P(None, "fsdp", "ctx", "tp"),
            P(None, "fsdp", "ctx", "tp"),
            P(),
            P(None, ("fsdp", "ctx"), None, "tp"),
            P(),
            P(),
            P(),
            P(),
            P(),
            P(None, "tp", ("fsdp", "ctx")),
            P(None, ("fsdp", "ctx"), "tp", None),
            P(None, "tp", ("fsdp", "ctx")),
            P(None, ("fsdp", "ctx"), None, "tp"),
            P(None, "tp", ("fsdp", "ctx")),
        ),
        check_vma=False,
    )
```

time: 3230 us -> 1330 us (0.41)
  waiting for transfers between devices: 2040 us -> 698 us
  matrix products: 363 us -> 86.4 us
  blocking collectives: 261 us -> 0 us
  local copies, waits for them, and re-layouts: 252 us -> 123 us
  Pallas kernels: 0 us -> 128 us
  other arithmetic: 247 us -> 120 us
  starting transfers between devices: 23.5 us -> 140 us
    unnamed x57 -> x8, waiting for transfers between devices: 1020 us -> 0.13 us
    ppermute x8 -> x106, waiting for transfers between devices: 0.61 us -> 316 us  [the longest x48 187 us: halve(): came = lax.ppermute(other, axis, xor_pairs(lax.axis_size(axis), step))]
    dot_general x168 -> x30, matrix products: 363 us -> 86.4 us  [the longest x18 46.9 us: dot(): lax.dot_general(a, b, (((ca,), (cb,)), ((), ())), preferred_element_type=...]
    reduce_scatter x25 -> x0, waiting for transfers between devices: 267 us -> none  [the longest x8 119 us: narrow(): return lax.psum_scatter(values, 'tp', scatter_dimension=1, tiled=True)]
    all_gather x24 -> x0, blocking collectives: 261 us -> none  [the longest x2 74.6 us: fetch(): lax.all_gather(attn_w[layer_index], ('fsdp', 'ctx'), axis=0, tiled=True)]
    all_gather x24 -> x8, waiting for transfers between devices: 606 us -> 382 us  [gathered(): return lax.all_gather(piece, ('fsdp', 'ctx'), axis=0, tiled=True)]
    psum x2 -> x0, waiting for transfers between devices: 143 us -> none  [settle(): lax.psum((small_grads[0], small_grads[1], small_grads[2], small_grads[3],...]
    pallas_call x0 -> x16, Pallas kernels: none -> 128 us  [the longest x2 39.4 us: scan_back(): kernel_call(scan_back_body, (count,), [rows_block(rows, channels), rows_b...]
  transfers between devices with their start and end apart: 62 -> 114, of which waited for: 42 -> 51; matrix products, arithmetic and copies ran while one was open for 19% -> 23% of each run, Pallas kernels for 0% -> 10%
where the time goes in v1:
time: 1330 us; the launch traced here: 1310 us
  waiting for transfers between devices  698 us (52%)
  starting transfers between devices  140 us (11%)
  Pallas kernels  128 us (10%)
  local copies, waits for them, and re-layouts  123 us (9%)
  other arithmetic  120 us (9%)
  matrix products  86.4 us (6%)
  between operations  18.2 us (1%)
    all_gather x8, waiting for transfers between devices, gathered(): return lax.all_gather(piece, ('fsdp', 'ctx'), axis=0, tiled=True)  382 us
    ppermute x48, waiting for transfers between devices, halve(): came = lax.ppermute(other, axis, xor_pairs(lax.axis_size(axis), step))  187 us
    ppermute x8, waiting for transfers between devices, join_rows(): came = lax.ppermute(v, axis, xor_pairs(lax.axis_size(axis), step))  62.1 us
    ppermute x28, starting transfers between devices, shifted(): return lax.ppermute(x, axis, pairs)  52.7 us
    ppermute x48, starting transfers between devices, halve(): came = lax.ppermute(other, axis, xor_pairs(lax.axis_size(axis), step))  48.1 us
    dot_general x18, matrix products, dot(): lax.dot_general(a, b, (((ca,), (cb,)), ((), ())), preferred_element_type=...  46.9 us
    dot_general x12, matrix products, product(): return jnp.dot(a, b, preferred_element_type=WIDE)  39.5 us
    pallas_call x2, Pallas kernels, scan_back(): kernel_call(scan_back_body, (count,), [rows_block(rows, channels), rows_b...  39.4 us
  transfers between devices with their start and end apart: 114, of which 51 were waited for; matrix products, arithmetic and copies ran while one was open for 23% of the time, Pallas kernels for 10%

profile of v1, /device:TPU:1, one launch (start us, length us, event | category | flops | bytes accessed | tf_op | source)
XLA Modules:
  0.0 1313.5 jit_solution(4036848554041566693)
XLA Ops:
  21.4 64.8 %all-gather.9.cloned.1.call-done = bf16[1024,1920]{1,0:T(8,128)(2,1)} async-done(((bf16[64,1920]{1,0:T(8,128)(2,1)}), bf16[1024,1920]{1,0:T(8,128)(2,1)}) %all-gather.9.cloned.1.call-update) | async-done | bytes 3932176 | tf_op jit(solution)/shard_map/all_gather | solution.py:805
  86.2 4.6 fusion.136.zx_ref.gate_ref.rows_ref
  108.0 8.5 shard_map.254
  125.6 7.1 shard_map.257
  132.9 9.1 collective-permute-done.3
  144.6 5.6 shard_map.255
  154.7 3.6 collective-permute-start.8
  161.3 71.1 %all-gather.13.cloned.1.call-done = bf16[1024,2048]{1,0:T(8,128)(2,1)} async-done(((bf16[64,2048]{1,0:T(8,128)(2,1)}), bf16[1024,2048]{1,0:T(8,128)(2,1)}) %all-gather.13.cloned.1.call-update) | async-done | bytes 4194320 | tf_op jit(solution)/shard_map/all_gather | solution.py:805
  232.4 4.6 fusion.134
  239.7 55.4 %all-gather.15.cloned.1.call-done = bf16[1024,1024]{1,0:T(8,128)(2,1)} async-done(((bf16[64,1024]{1,0:T(8,128)(2,1)}), bf16[1024,1024]{1,0:T(8,128)(2,1)}) %all-gather.15.cloned.1.call-update) | async-done | bytes 2097168 | tf_op jit(solution)/shard_map/all_gather | solution.py:805
  302.4 67.2 %all-gather.17.cloned.1.call-done = bf16[1024,1920]{1,0:T(8,128)(2,1)} async-done(((bf16[64,1920]{1,0:T(8,128)(2,1)}), bf16[1024,1920]{1,0:T(8,128)(2,1)}) %all-gather.17.cloned.1.call-update) | async-done | bytes 3932176 | tf_op jit(solution)/shard_map/all_gather | solution.py:805
  369.5 4.5 fusion.153.zx_ref.gate_ref.rows_ref
  381.1 8.5 shard_map.258
  391.5 4.0 collective-permute-start.11
  407.8 5.4 collective-permute-start.13
  413.9 7.1 shard_map.261
  429.8 5.6 shard_map.259
  441.5 3.6 collective-permute-start.17
  451.1 67.6 %all-gather.21.cloned.1.call-done = bf16[1024,2048]{1,0:T(8,128)(2,1)} async-done(((bf16[64,2048]{1,0:T(8,128)(2,1)}), bf16[1024,2048]{1,0:T(8,128)(2,1)}) %all-gather.21.cloned.1.call-update) | async-done | bytes 4194320 | tf_op jit(solution)/shard_map/all_gather | solution.py:805
  518.8 7.3 fusion.135
  526.1 55.5 %all-gather.23.cloned.1.call-done = bf16[1024,1024]{1,0:T(8,128)(2,1)} async-done(((bf16[64,1024]{1,0:T(8,128)(2,1)}), bf16[1024,1024]{1,0:T(8,128)(2,1)}) %all-gather.23.cloned.1.call-update) | async-done | bytes 2097168 | tf_op jit(solution)/shard_map/all_gather | solution.py:805
  581.6 5.6 multiply_convert_fusion.3
  603.1 7.2 collective-permute-done.100
  614.5 24.6 %collective-permute-done.101 = bf16[4,64,512]{2,1,0:T(8,128)(2,1)S(1)} collective-permute-done((bf16[4,64,512]{2,1,0:T(8,128)(2,1)S(1)}, bf16[4,64,512]{2,1,0:T(8,128)(2,1)S(1)}, u32[]{:S(2)}, u32[]{:S(2)}) %collective-permute-start.101) | collective-permute-done | bytes 262176 | tf_op jit(solution)/shard_map/ppermute | solution.py:96
  648.7 10.2 shard_map.264
  660.2 3.6 fusion.32.dn_ref
  663.8 8.0 shard_map.262
  703.2 4.1 collective-permute-start.89
  711.5 11.0 collective-permute-done.22
  727.1 19.7 %shard_map.263 = (f32[512,1024]{1,0:T(8,128)}, f32[2,8,1024]{2,1,0:T(8,128)}, bf16[512,128]{1,0:T(8,128)(2,1)}, f32[2,8,1024]{2,1,0:T(8,128)}, f32[2,8,128]{2,1,0:T(8,128)}) custom-call(f32[512,768]{1,0:T(8,128)} %get-tuple-element.88.du_ref, bf16[512,768]{1,0:T(8,128)(2,1)} %get-tuple-element.80.x_ref, bf16[512,256]{1,0:T(8,128)(2,1)} %get-tuple-element.79.bc_ref, ...), custom_call_target="tpu_custom_call" | custom-call | flops 2013265920 | bytes 12582912 | tf_op jit(solution)/shard_map/pallas_call | solution.py:713
  759.4 4.2 collective-permute-start.28
  779.0 22.9 %collective-permute-done.79 = bf16[4,64,512]{2,1,0:T(8,128)(2,1)S(1)} collective-permute-done((bf16[4,64,512]{2,1,0:T(8,128)(2,1)S(1)}, bf16[4,64,512]{2,1,0:T(8,128)(2,1)S(1)}, u32[]{:S(2)}, u32[]{:S(2)}) %collective-permute-start.79) | collective-permute-done | bytes 262176 | tf_op jit(solution)/shard_map/ppermute | solution.py:96
  806.7 9.6 collective-permute-done.80
  822.0 4.0 collective-permute-done.93
  839.0 3.3 convolution_convert_fusion.12
  866.9 6.8 collective-permute-start.47
  897.4 11.2 collective-permute-done.55
  911.3 4.2 collective-permute-done.95
  919.8 23.7 %collective-permute-done.98 = bf16[2,64,1024]{2,1,0:T(8,128)(2,1)S(1)} collective-permute-done((bf16[2,64,1024]{2,1,0:T(8,128)(2,1)S(1)}, bf16[2,64,1024]{2,1,0:T(8,128)(2,1)S(1)}, u32[]{:S(2)}, u32[]{:S(2)}) %collective-permute-start.98) | collective-permute-done | bytes 262176 | tf_op jit(solution)/shard_map/ppermute | solution.py:96
  960.3 10.2 shard_map.268
  976.6 8.1 shard_map.266
  994.3 5.0 collective-permute-start.83
  1007.6 4.9 collective-permute-done.32
  1014.9 19.7 %shard_map.267 = (f32[512,1024]{1,0:T(8,128)}, f32[2,8,1024]{2,1,0:T(8,128)}, bf16[512,128]{1,0:T(8,128)(2,1)}, f32[2,8,1024]{2,1,0:T(8,128)}, f32[2,8,128]{2,1,0:T(8,128)}) custom-call(f32[512,768]{1,0:T(8,128)} %get-tuple-element.103.du_ref, bf16[512,768]{1,0:T(8,128)(2,1)} %get-tuple-element.71.x_ref, bf16[512,256]{1,0:T(8,128)(2,1)} %get-tuple-element.70.bc_ref, ...), custom_call_target="tpu_custom_call" | custom-call | flops 2013265920 | bytes 12582912 | tf_op jit(solution)/shard_map/pallas_call | solution.py:713
  1038.4 3.4 collective-permute-done.33
  1049.2 5.3 convolution_convert_fusion.1
  1057.8 3.3 add_convert_fusion
  1068.8 4.5 collective-permute-start.37
  1084.2 6.3 collective-permute-done.66
  1092.2 4.5 collective-permute-done.71
  1099.6 3.3 collective-permute-done.67
  1104.9 23.7 %collective-permute-done.86 = bf16[2,64,2048]{2,1,0:T(8,128)(2,1)S(1)} collective-permute-done((bf16[2,64,2048]{2,1,0:T(8,128)(2,1)}, bf16[2,64,2048]{2,1,0:T(8,128)(2,1)S(1)}, u32[]{:S(2)}, u32[]{:S(2)}) %collective-permute-start.86) | collective-permute-done | bytes 524320 | tf_op jit(solution)/shard_map/ppermute | solution.py:96
  1128.8 5.5 collective-permute-done.74
  1134.3 8.3 collective-permute-done.68
  1143.6 7.5 collective-permute-done.75
  1152.6 4.5 multiply_reduce_fusion.3
  1165.0 3.8 collective-permute-done.40
  1173.7 15.2 %collective-permute-done.41 = f32[63,128]{1,0:T(8,128)S(1)} collective-permute-done((f32[63,128]{1,0:T(8,128)S(1)}, f32[63,128]{1,0:T(8,128)S(1)}, u32[]{:S(2)}, u32[]{:S(2)}) %collective-permute-start.41) | collective-permute-done | bytes 32288 | tf_op jit(solution)/shard_map/ppermute | solution.py:147
  1210.9 26.9 %collective-permute-done.52 = bf16[2,64,2304]{2,1,0:T(8,128)(2,1)S(1)} collective-permute-done((bf16[2,64,2304]{2,1,0:T(8,128)(2,1)S(1)}, bf16[2,64,2304]{2,1,0:T(8,128)(2,1)S(1)}, u32[]{:S(2)}, u32[]{:S(2)}) %collective-permute-start.52) | collective-permute-done | bytes 589856 | tf_op jit(solution)/shard_map/ppermute | solution.py:96
  1240.2 5.9 collective-permute-done.53
  1254.5 3.6 collective-permute-done.62
  1258.9 7.8 collective-permute-done.63
  1268.5 3.4 maximum_select_fusion.1
  1274.4 29.5 %collective-permute-done.64 = f32[8,64,280]{2,1,0:T(8,128)S(1)} collective-permute-done((f32[8,64,280]{2,1,0:T(8,128)S(1)}, f32[8,64,280]{2,1,0:T(8,128)S(1)}, u32[]{:S(2)}, u32[]{:S(2)}) %collective-permute-start.64) | collective-permute-done | bytes 573472 | tf_op jit(solution)/shard_map/ppermute | solution.py:135
  (955 shorter events, 416.3 us)
Async XLA Ops:
  7.2 79.0 %all-gather.9.cloned.1.call-start = ((), (), s32[]{:S(2)}) async-start(), calls=%async_computation | async-start | bytes 4177920 | tf_op jit(solution)/shard_map/all_gather | solution.py:805
  10.3 141.2 %all-gather.11.cloned.1.call-start = ((), (), s32[]{:S(2)}) async-start(), calls=%async_computation.1 | async-start | bytes 2228224 | tf_op jit(solution)/shard_map/all_gather | solution.py:805
  11.1 221.3 %all-gather.13.cloned.1.call-start = ((), (), s32[]{:S(2)}) async-start(), calls=%async_computation.2 | async-start | bytes 4456448 | tf_op jit(solution)/shard_map/all_gather | solution.py:805
  12.3 282.8 %all-gather.15.cloned.1.call-start = ((), (), s32[]{:S(2)}) async-start(), calls=%async_computation.3 | async-start | bytes 2228224 | tf_op jit(solution)/shard_map/all_gather | solution.py:805
  13.2 356.4 %all-gather.17.cloned.1.call-start = ((), (), s32[]{:S(2)}) async-start(), calls=%async_computation.4 | async-start | bytes 4177920 | tf_op jit(solution)/shard_map/all_gather | solution.py:805
  14.0 424.3 %all-gather.19.cloned.1.call-start = ((), (), s32[]{:S(2)}) async-start(), calls=%async_computation.5 | async-start | bytes 2228224 | tf_op jit(solution)/shard_map/all_gather | solution.py:805
  14.7 504.1 %all-gather.21.cloned.1.call-start = ((), (), s32[]{:S(2)}) async-start(), calls=%async_computation.6 | async-start | bytes 4456448 | tf_op jit(solution)/shard_map/all_gather | solution.py:805
  15.7 565.9 %all-gather.23.cloned.1.call-start = ((), (), s32[]{:S(2)}) async-start(), calls=%async_computation.7 | async-start | bytes 2228224 | tf_op jit(solution)/shard_map/all_gather | solution.py:805
  101.7 21.0 %collective-permute-start.5 = (bf16[512,128]{1,0:T(8,128)(2,1)}, bf16[512,128]{1,0:T(8,128)(2,1)S(1)}, u32[]{:S(2)}, u32[]{:S(2)}) collective-permute-start(bf16[512,128]{1,0:T(8,128)(2,1)} %get-tuple-element.75.refs_0_), channel_id=1, source_target_pairs={{0,2},{2,4},{4,6},{1,3},{3,5},{5,7},{8,10},{10,12},{12,14},{9,11},... | collective-permute-start | bytes 393224 | tf_op jit(solution)/shard_map/ppermute | solution.py:72
  104.8 20.1 %collective-permute-start.6 = (bf16[512,128]{1,0:T(8,128)(2,1)}, bf16[512,128]{1,0:T(8,128)(2,1)S(1)}, u32[]{:S(2)}, u32[]{:S(2)}) collective-permute-start(bf16[512,128]{1,0:T(8,128)(2,1)} %get-tuple-element.75.refs_0_), channel_id=1, source_target_pairs={{0,4},{2,6},{1,5},{3,7},{8,12},{10,14},{9,13},{11,15},{16,20},{18,... | collective-permute-start | bytes 393224 | tf_op jit(solution)/shard_map/ppermute | solution.py:72
  106.1 18.8 %collective-permute-start.7 = (bf16[512,128]{1,0:T(8,128)(2,1)}, bf16[512,128]{1,0:T(8,128)(2,1)S(1)}, u32[]{:S(2)}, u32[]{:S(2)}) collective-permute-start(bf16[512,128]{1,0:T(8,128)(2,1)} %get-tuple-element.75.refs_0_), channel_id=1, source_target_pairs={{0,6},{1,7},{8,14},{9,15},{16,22},{17,23},{24,30},{25,31}} | collective-permute-start | bytes 393224 | tf_op jit(solution)/shard_map/ppermute | solution.py:72
  120.8 21.2 %collective-permute-start.3 = (bf16[2,784,128]{2,1,0:T(8,128)(2,1)S(1)}, bf16[2,784,128]{2,1,0:T(8,128)(2,1)S(1)}, u32[]{:S(2)}, u32[]{:S(2)}) collective-permute-start(bf16[2,784,128]{2,1,0:T(8,128)(2,1)S(1)} %pad_maximum_fusion.16), channel_id=1, source_target_pairs={{0,4},{2,6},{1,5},{3,7},{8,12},{10,14},{9,13},{11,15},{16,20},{18,... | collective-permute-start | bytes 1204232 | tf_op jit(solution)/shard_map/ppermute | solution.py:72
  122.7 19.5 %collective-permute-start.4 = (bf16[2,784,128]{2,1,0:T(8,128)(2,1)S(1)}, bf16[2,784,128]{2,1,0:T(8,128)(2,1)}, u32[]{:S(2)}, u32[]{:S(2)}) collective-permute-start(bf16[2,784,128]{2,1,0:T(8,128)(2,1)S(1)} %pad_maximum_fusion.16), channel_id=1, source_target_pairs={{0,6},{1,7},{8,14},{9,15},{16,22},{17,23},{24,30},{25,31}} | collective-permute-start | bytes 1204232 | tf_op jit(solution)/shard_map/ppermute | solution.py:72
  391.5 29.4 %collective-permute-start.11 = (bf16[2,784,128]{2,1,0:T(8,128)(2,1)S(1)}, bf16[2,784,128]{2,1,0:T(8,128)(2,1)}, u32[]{:S(2)}, u32[]{:S(2)}) collective-permute-start(bf16[2,784,128]{2,1,0:T(8,128)(2,1)S(1)} %pad_maximum_fusion.18), channel_id=1, source_target_pairs={{0,2},{2,4},{4,6},{1,3},{3,5},{5,7},{8,10},{10,12},{12,14},{9,11},... | collective-permute-start | bytes 1204232 | tf_op jit(solution)/shard_map/ppermute | solution.py:72
  404.2 20.9 %collective-permute-start.12 = (bf16[2,784,128]{2,1,0:T(8,128)(2,1)S(1)}, bf16[2,784,128]{2,1,0:T(8,128)(2,1)}, u32[]{:S(2)}, u32[]{:S(2)}) collective-permute-start(bf16[2,784,128]{2,1,0:T(8,128)(2,1)S(1)} %pad_maximum_fusion.18), channel_id=1, source_target_pairs={{0,4},{2,6},{1,5},{3,7},{8,12},{10,14},{9,13},{11,15},{16,20},{18,... | collective-permute-start | bytes 1204232 | tf_op jit(solution)/shard_map/ppermute | solution.py:72
  407.8 19.5 %collective-permute-start.13 = (bf16[2,784,128]{2,1,0:T(8,128)(2,1)S(1)}, bf16[2,784,128]{2,1,0:T(8,128)(2,1)}, u32[]{:S(2)}, u32[]{:S(2)}) collective-permute-start(bf16[2,784,128]{2,1,0:T(8,128)(2,1)S(1)} %pad_maximum_fusion.18), channel_id=1, source_target_pairs={{0,6},{1,7},{8,14},{9,15},{16,22},{17,23},{24,30},{25,31}} | collective-permute-start | bytes 1204232 | tf_op jit(solution)/shard_map/ppermute | solution.py:72
  445.0 81.0 %collective-permute-start.19 = (bf16[512,512]{1,0:T(8,128)(2,1)}, bf16[512,512]{1,0:T(8,128)(2,1)}, u32[]{:S(2)}, u32[]{:S(2)}) collective-permute-start(bf16[512,512]{1,0:T(8,128)(2,1)} %bitcast.43), channel_id=1, source_target_pairs={{0,1},{1,0},{2,3},{3,2},{4,5},{5,4},{6,7},{7,6},{8,9},{9,8},{10,11... | collective-permute-start | bytes 1572872 | tf_op jit(solution)/shard_map/ppermute | solution.py:76
  592.2 49.9 %collective-permute-start.20 = (bf16[512,1024]{1,0:T(8,128)(2,1)S(1)}, bf16[512,1024]{1,0:T(8,128)(2,1)S(1)}, u32[]{:S(2)}, u32[]{:S(2)}) collective-permute-start(bf16[512,1024]{1,0:T(8,128)(2,1)S(1)} %convolution_convert_fusion.13), channel_id=1, source_target_pairs={{0,1},{1,0},{2,3},{3,2},{4,5},{5,4},{6,7},{7,6},{8,9},{9,8},{10,11... | collective-permute-start | bytes 3145736 | tf_op jit(solution)/shard_map/ppermute | solution.py:76
  600.5 72.4 %collective-permute-start.88 = (bf16[4,2,64,1024]{3,2,0,1:T(8,128)(2,1)}, bf16[4,2,64,1024]{3,2,0,1:T(8,128)(2,1)}, u32[]{:S(2)}, u32[]{:S(2)}) collective-permute-start(bf16[4,2,64,1024]{3,2,0,1:T(8,128)(2,1)} %bitcast.458), channel_id=1, source_target_pairs={{0,2},{2,0},{4,6},{6,4},{1,3},{3,1},{5,7},{7,5},{8,10},{10,8},{12,... | collective-permute-start | bytes 3145736 | tf_op jit(solution)/shard_map/ppermute | solution.py:96
  602.8 74.2 %collective-permute-start.90 = (bf16[4,2,64,1024]{3,2,1,0:T(8,128)(2,1)}, bf16[4,2,64,1024]{3,2,1,0:T(8,128)(2,1)}, u32[]{:S(2)}, u32[]{:S(2)}) collective-permute-start(bf16[4,2,64,1024]{3,2,1,0:T(8,128)(2,1)} %dynamic-slice_bitcast_fusion.2), channel_id=1, source_target_pairs={{0,4},{2,6},{4,0},{6,2},{1,5},{3,7},{5,1},{7,3},{8,12},{10,14},{12... | collective-permute-start | bytes 3145736 | tf_op jit(solution)/shard_map/ppermute | solution.py:96
  610.5 28.7 %collective-permute-start.101 = (bf16[4,64,512]{2,1,0:T(8,128)(2,1)S(1)}, bf16[4,64,512]{2,1,0:T(8,128)(2,1)S(1)}, u32[]{:S(2)}, u32[]{:S(2)}) collective-permute-start(bf16[4,64,512]{2,1,0:T(8,128)(2,1)S(1)} %dynamic-slice_bitcast_fusion.22), channel_id=1, source_target_pairs={{0,4},{2,6},{4,0},{6,2},{1,5},{3,7},{5,1},{7,3},{8,12},{10,14},{12... | collective-permute-start | bytes 786440 | tf_op jit(solution)/shard_map/ppermute | solution.py:96
  611.9 28.4 %collective-permute-start.103 = (bf16[4,64,512]{2,1,0:T(8,128)(2,1)S(1)}, bf16[4,64,512]{2,1,0:T(8,128)(2,1)S(1)}, u32[]{:S(2)}, u32[]{:S(2)}) collective-permute-start(bf16[4,64,512]{2,1,0:T(8,128)(2,1)S(1)} %dynamic-slice_bitcast_fusion.21), channel_id=1, source_target_pairs={{0,2},{2,0},{4,6},{6,4},{1,3},{3,1},{5,7},{7,5},{8,10},{10,8},{12,... | collective-permute-start | bytes 786440 | tf_op jit(solution)/shard_map/ppermute | solution.py:96
  639.2 54.7 %collective-permute-start.18 = (bf16[512,1024]{1,0:T(8,128)(2,1)}, bf16[512,1024]{1,0:T(8,128)(2,1)}, u32[]{:S(2)}, u32[]{:S(2)}) collective-permute-start(bf16[512,1024]{1,0:T(8,128)(2,1)} %convolution_convert_fusion.8), channel_id=1, source_target_pairs={{0,1},{1,0},{2,3},{3,2},{4,5},{5,4},{6,7},{7,6},{8,9},{9,8},{10,11... | collective-permute-start | bytes 3145736 | tf_op jit(solution)/shard_map/ppermute | solution.py:76
  640.5 57.1 %collective-permute-start.104 = (bf16[2,64,1024]{2,1,0:T(8,128)(2,1)S(1)}, bf16[2,64,1024]{2,1,0:T(8,128)(2,1)S(1)}, u32[]{:S(2)}, u32[]{:S(2)}) collective-permute-start(bf16[2,64,1024]{2,1,0:T(8,128)(2,1)S(1)} %dynamic-slice_bitcast_fusion.20), channel_id=1, source_target_pairs={{0,16},{8,24},{16,0},{24,8},{1,17},{9,25},{17,1},{25,9},{2,18},{10... | collective-permute-start | bytes 786440 | tf_op jit(solution)/shard_map/ppermute | solution.py:96
  658.9 41.6 %collective-permute-start.25 = (bf16[512,128]{1,0:T(8,128)(2,1)}, bf16[512,128]{1,0:T(8,128)(2,1)S(1)}, u32[]{:S(2)}, u32[]{:S(2)}) collective-permute-start(bf16[512,128]{1,0:T(8,128)(2,1)} %get-tuple-element.97), channel_id=1, source_target_pairs={{2,0},{4,2},{6,4},{3,1},{5,3},{7,5},{10,8},{12,10},{14,12},{11,9},... | collective-permute-start | bytes 393224 | tf_op jit(solution)/shard_map/ppermute | solution.py:72
  673.0 28.8 %collective-permute-start.26 = (bf16[512,128]{1,0:T(8,128)(2,1)}, bf16[512,128]{1,0:T(8,128)(2,1)S(1)}, u32[]{:S(2)}, u32[]{:S(2)}) collective-permute-start(bf16[512,128]{1,0:T(8,128)(2,1)} %get-tuple-element.98), channel_id=1, source_target_pairs={{4,0},{6,2},{5,1},{7,3},{12,8},{14,10},{13,9},{15,11},{20,16},{22,... | collective-permute-start | bytes 393224 | tf_op jit(solution)/shard_map/ppermute | solution.py:72
  677.0 26.1 %collective-permute-start.27 = (bf16[512,128]{1,0:T(8,128)(2,1)}, bf16[512,128]{1,0:T(8,128)(2,1)S(1)}, u32[]{:S(2)}, u32[]{:S(2)}) collective-permute-start(bf16[512,128]{1,0:T(8,128)(2,1)} %get-tuple-element.99), channel_id=1, source_target_pairs={{6,0},{7,1},{14,8},{15,9},{22,16},{23,17},{30,24},{31,25}} | collective-permute-start | bytes 393224 | tf_op jit(solution)/shard_map/ppermute | solution.py:72
  700.5 21.9 %collective-permute-start.22 = (bf16[2,784,128]{2,1,0:T(8,128)(2,1)}, bf16[2,784,128]{2,1,0:T(8,128)(2,1)}, u32[]{:S(2)}, u32[]{:S(2)}) collective-permute-start(bf16[2,784,128]{2,1,0:T(8,128)(2,1)} %pad_maximum_fusion.17), channel_id=1, source_target_pairs={{4,0},{6,2},{5,1},{7,3},{12,8},{14,10},{13,9},{15,11},{20,16},{22,... | collective-permute-start | bytes 1204232 | tf_op jit(solution)/shard_map/ppermute | solution.py:72
  701.8 22.7 %collective-permute-start.23 = (bf16[2,784,128]{2,1,0:T(8,128)(2,1)}, bf16[2,784,128]{2,1,0:T(8,128)(2,1)}, u32[]{:S(2)}, u32[]{:S(2)}) collective-permute-start(bf16[2,784,128]{2,1,0:T(8,128)(2,1)} %pad_maximum_fusion.17), channel_id=1, source_target_pairs={{6,0},{7,1},{14,8},{15,9},{22,16},{23,17},{30,24},{31,25}} | collective-permute-start | bytes 1204232 | tf_op jit(solution)/shard_map/ppermute | solution.py:72
  703.2 70.7 %collective-permute-start.89 = (bf16[4,64,1024]{2,1,0:T(8,128)(2,1)}, bf16[4,64,1024]{2,1,0:T(8,128)(2,1)}, u32[]{:S(2)}, u32[]{:S(2)}) collective-permute-start(bf16[4,64,1024]{2,1,0:T(8,128)(2,1)} %dynamic-slice_bitcast_fusion.14), channel_id=1, source_target_pairs={{0,4},{2,6},{4,0},{6,2},{1,5},{3,7},{5,1},{7,3},{8,12},{10,14},{12... | collective-permute-start | bytes 1572872 | tf_op jit(solution)/shard_map/ppermute | solution.py:96
  709.5 66.2 %collective-permute-start.91 = (bf16[4,64,1024]{2,1,0:T(8,128)(2,1)}, bf16[4,64,1024]{2,1,0:T(8,128)(2,1)}, u32[]{:S(2)}, u32[]{:S(2)}) collective-permute-start(bf16[4,64,1024]{2,1,0:T(8,128)(2,1)} %dynamic-slice_bitcast_fusion.13), channel_id=1, source_target_pairs={{0,2},{2,0},{4,6},{6,4},{1,3},{3,1},{5,7},{7,5},{8,10},{10,8},{12,... | collective-permute-start | bytes 1572872 | tf_op jit(solution)/shard_map/ppermute | solution.py:96
  711.2 57.4 %collective-permute-start.76 = (bf16[4,2,64,512]{3,2,0,1:T(8,128)(2,1)}, bf16[4,2,64,512]{3,2,0,1:T(8,128)(2,1)}, u32[]{:S(2)}, u32[]{:S(2)}) collective-permute-start(bf16[4,2,64,512]{3,2,0,1:T(8,128)(2,1)} %bitcast.462), channel_id=1, source_target_pairs={{0,2},{2,0},{4,6},{6,4},{1,3},{3,1},{5,7},{7,5},{8,10},{10,8},{12,... | collective-permute-start | bytes 1572872 | tf_op jit(solution)/shard_map/ppermute | solution.py:96
  722.4 48.7 %collective-permute-start.78 = (bf16[4,2,64,512]{3,2,1,0:T(8,128)(2,1)}, bf16[4,2,64,512]{3,2,1,0:T(8,128)(2,1)}, u32[]{:S(2)}, u32[]{:S(2)}) collective-permute-start(bf16[4,2,64,512]{3,2,1,0:T(8,128)(2,1)} %dynamic-slice_bitcast_fusion.18), channel_id=1, source_target_pairs={{0,4},{2,6},{4,0},{6,2},{1,5},{3,7},{5,1},{7,3},{8,12},{10,14},{12... | collective-permute-start | bytes 1572872 | tf_op jit(solution)/shard_map/ppermute | solution.py:96
  759.4 67.4 %collective-permute-start.28 = (bf16[512,1024]{1,0:T(8,128)(2,1)S(1)}, bf16[512,1024]{1,0:T(8,128)(2,1)S(1)}, u32[]{:S(2)}, u32[]{:S(2)}) collective-permute-start(bf16[512,1024]{1,0:T(8,128)(2,1)S(1)} %add_convert_fusion.2), channel_id=1, source_target_pairs={{0,1},{1,0},{2,3},{3,2},{4,5},{5,4},{6,7},{7,6},{8,9},{9,8},{10,11... | collective-permute-start | bytes 3145736 | tf_op jit(solution)/shard_map/ppermute | solution.py:76
  768.5 94.2 %collective-permute-start.54 = (bf16[4,2,64,1152]{3,2,0,1:T(8,128)(2,1)}, bf16[4,2,64,1152]{3,2,0,1:T(8,128)(2,1)}, u32[]{:S(2)}, u32[]{:S(2)}) collective-permute-start(bf16[4,2,64,1152]{3,2,0,1:T(8,128)(2,1)} %bitcast.456), channel_id=1, source_target_pairs={{0,2},{2,0},{4,6},{6,4},{1,3},{3,1},{5,7},{7,5},{8,10},{10,8},{12,... | collective-permute-start | bytes 3538952 | tf_op jit(solution)/shard_map/ppermute | solution.py:96
  773.8 28.1 %collective-permute-start.79 = (bf16[4,64,512]{2,1,0:T(8,128)(2,1)S(1)}, bf16[4,64,512]{2,1,0:T(8,128)(2,1)S(1)}, u32[]{:S(2)}, u32[]{:S(2)}) collective-permute-start(bf16[4,64,512]{2,1,0:T(8,128)(2,1)S(1)} %dynamic-slice_bitcast_fusion.27), channel_id=1, source_target_pairs={{0,2},{2,0},{4,6},{6,4},{1,3},{3,1},{5,7},{7,5},{8,10},{10,8},{12,... | collective-permute-start | bytes 786440 | tf_op jit(solution)/shard_map/ppermute | solution.py:96
  777.1 39.4 %collective-permute-start.92 = (bf16[2,64,2048]{2,1,0:T(8,128)(2,1)S(1)}, bf16[2,64,2048]{2,1,0:T(8,128)(2,1)S(1)}, u32[]{:S(2)}, u32[]{:S(2)}) collective-permute-start(bf16[2,64,2048]{2,1,0:T(8,128)(2,1)S(1)} %dynamic-slice_bitcast_fusion.12), channel_id=1, source_target_pairs={{0,16},{8,24},{16,0},{24,8},{1,17},{9,25},{17,1},{25,9},{2,18},{10... | collective-permute-start | bytes 1572872 | tf_op jit(solution)/shard_map/ppermute | solution.py:96
  804.9 61.9 %collective-permute-start.56 = (bf16[4,2,64,1152]{3,2,1,0:T(8,128)(2,1)}, bf16[4,2,64,1152]{3,2,1,0:T(8,128)(2,1)}, u32[]{:S(2)}, u32[]{:S(2)}) collective-permute-start(bf16[4,2,64,1152]{3,2,1,0:T(8,128)(2,1)} %dynamic-slice_bitcast_fusion), channel_id=1, source_target_pairs={{0,4},{2,6},{4,0},{6,2},{1,5},{3,7},{5,1},{7,3},{8,12},{10,14},{12... | collective-permute-start | bytes 3538952 | tf_op jit(solution)/shard_map/ppermute | solution.py:96
  832.9 60.5 %collective-permute-start.94 = (bf16[4,2,64,512]{3,2,0,1:T(8,128)(2,1)}, bf16[4,2,64,512]{3,2,0,1:T(8,128)(2,1)}, u32[]{:S(2)}, u32[]{:S(2)}) collective-permute-start(bf16[4,2,64,512]{3,2,0,1:T(8,128)(2,1)} %bitcast.461), channel_id=1, source_target_pairs={{0,2},{2,0},{4,6},{6,4},{1,3},{3,1},{5,7},{7,5},{8,10},{10,8},{12,... | collective-permute-start | bytes 1572872 | tf_op jit(solution)/shard_map/ppermute | solution.py:96
  835.1 59.9 %collective-permute-start.96 = (bf16[4,2,64,512]{3,2,1,0:T(8,128)(2,1)}, bf16[4,2,64,512]{3,2,1,0:T(8,128)(2,1)}, u32[]{:S(2)}, u32[]{:S(2)}) collective-permute-start(bf16[4,2,64,512]{3,2,1,0:T(8,128)(2,1)} %dynamic-slice_bitcast_fusion.11), channel_id=1, source_target_pairs={{0,4},{2,6},{4,0},{6,2},{1,5},{3,7},{5,1},{7,3},{8,12},{10,14},{12... | collective-permute-start | bytes 1572872 | tf_op jit(solution)/shard_map/ppermute | solution.py:96
  856.3 88.0 %collective-permute-start.82 = (bf16[4,2,64,1024]{3,2,0,1:T(8,128)(2,1)}, bf16[4,2,64,1024]{3,2,0,1:T(8,128)(2,1)}, u32[]{:S(2)}, u32[]{:S(2)}) collective-permute-start(bf16[4,2,64,1024]{3,2,0,1:T(8,128)(2,1)} %bitcast.459), channel_id=1, source_target_pairs={{0,2},{2,0},{4,6},{6,4},{1,3},{3,1},{5,7},{7,5},{8,10},{10,8},{12,... | collective-permute-start | bytes 3145736 | tf_op jit(solution)/shard_map/ppermute | solution.py:96
  862.8 84.4 %collective-permute-start.84 = (bf16[4,2,64,1024]{3,2,1,0:T(8,128)(2,1)}, bf16[4,2,64,1024]{3,2,1,0:T(8,128)(2,1)}, u32[]{:S(2)}, u32[]{:S(2)}) collective-permute-start(bf16[4,2,64,1024]{3,2,1,0:T(8,128)(2,1)} %dynamic-slice_bitcast_fusion.3), channel_id=1, source_target_pairs={{0,4},{2,6},{4,0},{6,2},{1,5},{3,7},{5,1},{7,3},{8,12},{10,14},{12... | collective-permute-start | bytes 3145736 | tf_op jit(solution)/shard_map/ppermute | solution.py:96
  876.2 73.6 %collective-permute-start.29 = (bf16[512,1024]{1,0:T(8,128)(2,1)}, bf16[512,1024]{1,0:T(8,128)(2,1)}, u32[]{:S(2)}, u32[]{:S(2)}) collective-permute-start(bf16[512,1024]{1,0:T(8,128)(2,1)} %convolution_convert_fusion.12), channel_id=1, source_target_pairs={{0,1},{1,0},{2,3},{3,2},{4,5},{5,4},{6,7},{7,6},{8,9},{9,8},{10,11... | collective-permute-start | bytes 3145736 | tf_op jit(solution)/shard_map/ppermute | solution.py:76
  916.5 27.0 %collective-permute-start.98 = (bf16[2,64,1024]{2,1,0:T(8,128)(2,1)S(1)}, bf16[2,64,1024]{2,1,0:T(8,128)(2,1)S(1)}, u32[]{:S(2)}, u32[]{:S(2)}) collective-permute-start(bf16[2,64,1024]{2,1,0:T(8,128)(2,1)S(1)} %dynamic-slice_bitcast_fusion.23), channel_id=1, source_target_pairs={{0,16},{8,24},{16,0},{24,8},{1,17},{9,25},{17,1},{25,9},{2,18},{10... | collective-permute-start | bytes 786440 | tf_op jit(solution)/shard_map/ppermute | solution.py:96
  918.4 82.7 %collective-permute-start.58 = (bf16[2,64,2304]{2,1,0:T(8,128)(2,1)}, bf16[2,64,2304]{2,1,0:T(8,128)(2,1)}, u32[]{:S(2)}, u32[]{:S(2)}) collective-permute-start(bf16[2,64,2304]{2,1,0:T(8,128)(2,1)} %dynamic-slice_bitcast_fusion.4), channel_id=1, source_target_pairs={{0,16},{8,24},{16,0},{24,8},{1,17},{9,25},{17,1},{25,9},{2,18},{10... | collective-permute-start | bytes 1769480 | tf_op jit(solution)/shard_map/ppermute | solution.py:96
  944.4 49.9 %collective-permute-start.99 = (bf16[1,64,1024]{2,1,0:T(8,128)(2,1)}, bf16[1,64,1024]{2,1,0:T(8,128)(2,1)}, u32[]{:S(2)}, u32[]{:S(2)}) collective-permute-start(bf16[1,64,1024]{2,1,0:T(8,128)(2,1)} %constant_dynamic-slice_fusion.3), channel_id=1, source_target_pairs={{0,8},{8,0},{16,24},{24,16},{1,9},{9,1},{17,25},{25,17},{2,10},{10... | collective-permute-start | bytes 393224 | tf_op jit(solution)/shard_map/ppermute | solution.py:96
  973.1 17.5 %collective-permute-start.36 = (bf16[512,128]{1,0:T(8,128)(2,1)}, bf16[512,128]{1,0:T(8,128)(2,1)}, u32[]{:S(2)}, u32[]{:S(2)}) collective-permute-start(bf16[512,128]{1,0:T(8,128)(2,1)} %get-tuple-element.114), channel_id=1, source_target_pairs={{6,0},{7,1},{14,8},{15,9},{22,16},{23,17},{30,24},{31,25}} | collective-permute-start | bytes 393224 | tf_op jit(solution)/shard_map/ppermute | solution.py:72
  990.6 21.9 %collective-permute-start.32 = (bf16[2,784,128]{2,1,0:T(8,128)(2,1)S(1)}, bf16[2,784,128]{2,1,0:T(8,128)(2,1)}, u32[]{:S(2)}, u32[]{:S(2)}) collective-permute-start(bf16[2,784,128]{2,1,0:T(8,128)(2,1)S(1)} %pad_maximum_fusion.15), channel_id=1, source_target_pairs={{6,0},{7,1},{14,8},{15,9},{22,16},{23,17},{30,24},{31,25}} | collective-permute-start | bytes 1204232 | tf_op jit(solution)/shard_map/ppermute | solution.py:72
  994.3 69.4 %collective-permute-start.83 = (bf16[4,64,1024]{2,1,0:T(8,128)(2,1)}, bf16[4,64,1024]{2,1,0:T(8,128)(2,1)}, u32[]{:S(2)}, u32[]{:S(2)}) collective-permute-start(bf16[4,64,1024]{2,1,0:T(8,128)(2,1)} %dynamic-slice_bitcast_fusion.17), channel_id=1, source_target_pairs={{0,4},{2,6},{4,0},{6,2},{1,5},{3,7},{5,1},{7,3},{8,12},{10,14},{12... | collective-permute-start | bytes 1572872 | tf_op jit(solution)/shard_map/ppermute | solution.py:96
  1001.1 66.2 %collective-permute-start.85 = (bf16[4,64,1024]{2,1,0:T(8,128)(2,1)}, bf16[4,64,1024]{2,1,0:T(8,128)(2,1)}, u32[]{:S(2)}, u32[]{:S(2)}) collective-permute-start(bf16[4,64,1024]{2,1,0:T(8,128)(2,1)} %dynamic-slice_bitcast_fusion.16), channel_id=1, source_target_pairs={{0,2},{2,0},{4,6},{6,4},{1,3},{3,1},{5,7},{7,5},{8,10},{10,8},{12,... | collective-permute-start | bytes 1572872 | tf_op jit(solution)/shard_map/ppermute | solution.py:96
  1005.4 70.1 %collective-permute-start.70 = (bf16[4,2,64,512]{3,2,0,1:T(8,128)(2,1)}, bf16[4,2,64,512]{3,2,0,1:T(8,128)(2,1)}, u32[]{:S(2)}, u32[]{:S(2)}) collective-permute-start(bf16[4,2,64,512]{3,2,0,1:T(8,128)(2,1)} %bitcast.463), channel_id=1, source_target_pairs={{0,2},{2,0},{4,6},{6,4},{1,3},{3,1},{5,7},{7,5},{8,10},{10,8},{12,... | collective-permute-start | bytes 1572872 | tf_op jit(solution)/shard_map/ppermute | solution.py:96
  1006.3 62.5 %collective-permute-start.72 = (bf16[4,2,64,512]{3,2,1,0:T(8,128)(2,1)}, bf16[4,2,64,512]{3,2,1,0:T(8,128)(2,1)}, u32[]{:S(2)}, u32[]{:S(2)}) collective-permute-start(bf16[4,2,64,512]{3,2,1,0:T(8,128)(2,1)} %dynamic-slice_bitcast_fusion.19), channel_id=1, source_target_pairs={{0,4},{2,6},{4,0},{6,2},{1,5},{3,7},{5,1},{7,3},{8,12},{10,14},{12... | collective-permute-start | bytes 1572872 | tf_op jit(solution)/shard_map/ppermute | solution.py:96
  1041.8 34.9 %collective-permute-start.59 = (bf16[1,64,2304]{2,1,0:T(8,128)(2,1)}, bf16[1,64,2304]{2,1,0:T(8,128)(2,1)S(1)}, u32[]{:S(2)}, u32[]{:S(2)}) collective-permute-start(bf16[1,64,2304]{2,1,0:T(8,128)(2,1)} %constant_dynamic-slice_fusion.18), channel_id=1, source_target_pairs={{0,8},{8,0},{16,24},{24,16},{1,9},{9,1},{17,25},{25,17},{2,10},{10... | collective-permute-start | bytes 884744 | tf_op jit(solution)/shard_map/ppermute | solution.py:96
  1063.7 126.3 %collective-permute-start.48 = (bf16[4,2,64,1152]{3,2,0,1:T(8,128)(2,1)}, bf16[4,2,64,1152]{3,2,0,1:T(8,128)(2,1)}, u32[]{:S(2)}, u32[]{:S(2)}) collective-permute-start(bf16[4,2,64,1152]{3,2,0,1:T(8,128)(2,1)} %bitcast.457), channel_id=1, source_target_pairs={{0,2},{2,0},{4,6},{6,4},{1,3},{3,1},{5,7},{7,5},{8,10},{10,8},{12,... | collective-permute-start | bytes 3538952 | tf_op jit(solution)/shard_map/ppermute | solution.py:96
  1067.3 124.5 %collective-permute-start.50 = (bf16[4,2,64,1152]{3,2,1,0:T(8,128)(2,1)}, bf16[4,2,64,1152]{3,2,1,0:T(8,128)(2,1)}, u32[]{:S(2)}, u32[]{:S(2)}) collective-permute-start(bf16[4,2,64,1152]{3,2,1,0:T(8,128)(2,1)} %dynamic-slice_bitcast_fusion.1), channel_id=1, source_target_pairs={{0,4},{2,6},{4,0},{6,2},{1,5},{3,7},{5,1},{7,3},{8,12},{10,14},{12... | collective-permute-start | bytes 3538952 | tf_op jit(solution)/shard_map/ppermute | solution.py:96
  1068.8 83.8 %collective-permute-start.37 = (bf16[512,1024]{1,0:T(8,128)(2,1)}, bf16[512,1024]{1,0:T(8,128)(2,1)}, u32[]{:S(2)}, u32[]{:S(2)}) collective-permute-start(bf16[512,1024]{1,0:T(8,128)(2,1)} %add_convert_fusion), channel_id=1, source_target_pairs={{0,1},{1,0},{2,3},{3,2},{4,5},{5,4},{6,7},{7,6},{8,9},{9,8},{10,11... | collective-permute-start | bytes 3145736 | tf_op jit(solution)/shard_map/ppermute | solution.py:76
  1078.3 18.4 %collective-permute-start.71 = (bf16[4,64,512]{2,1,0:T(8,128)(2,1)}, bf16[4,64,512]{2,1,0:T(8,128)(2,1)}, u32[]{:S(2)}, u32[]{:S(2)}) collective-permute-start(bf16[4,64,512]{2,1,0:T(8,128)(2,1)} %dynamic-slice_bitcast_fusion.31), channel_id=1, source_target_pairs={{0,4},{2,6},{4,0},{6,2},{1,5},{3,7},{5,1},{7,3},{8,12},{10,14},{12... | collective-permute-start | bytes 786440 | tf_op jit(solution)/shard_map/ppermute | solution.py:96
  1096.8 31.8 %collective-permute-start.86 = (bf16[2,64,2048]{2,1,0:T(8,128)(2,1)}, bf16[2,64,2048]{2,1,0:T(8,128)(2,1)S(1)}, u32[]{:S(2)}, u32[]{:S(2)}) collective-permute-start(bf16[2,64,2048]{2,1,0:T(8,128)(2,1)} %dynamic-slice_bitcast_fusion.15), channel_id=1, source_target_pairs={{0,16},{8,24},{16,0},{24,8},{1,17},{9,25},{17,1},{25,9},{2,18},{10... | collective-permute-start | bytes 1572872 | tf_op jit(solution)/shard_map/ppermute | solution.py:96
  1103.0 31.2 %collective-permute-start.74 = (bf16[2,64,1024]{2,1,0:T(8,128)(2,1)S(1)}, bf16[2,64,1024]{2,1,0:T(8,128)(2,1)S(1)}, u32[]{:S(2)}, u32[]{:S(2)}) collective-permute-start(bf16[2,64,1024]{2,1,0:T(8,128)(2,1)S(1)} %dynamic-slice_bitcast_fusion.29), channel_id=1, source_target_pairs={{0,16},{8,24},{16,0},{24,8},{1,17},{9,25},{17,1},{25,9},{2,18},{10... | collective-permute-start | bytes 786440 | tf_op jit(solution)/shard_map/ppermute | solution.py:96
  1134.2 23.0 %collective-permute-start.87 = (bf16[1,64,2048]{2,1,0:T(8,128)(2,1)S(1)}, bf16[1,64,2048]{2,1,0:T(8,128)(2,1)S(1)}, u32[]{:S(2)}, u32[]{:S(2)}) collective-permute-start(bf16[1,64,2048]{2,1,0:T(8,128)(2,1)S(1)} %constant_dynamic-slice_fusion.9), channel_id=1, source_target_pairs={{0,8},{8,0},{16,24},{24,16},{1,9},{9,1},{17,25},{25,17},{2,10},{10... | collective-permute-start | bytes 786440 | tf_op jit(solution)/shard_map/ppermute | solution.py:96
  1151.1 117.4 %collective-permute-start.69 = (f32[8,64,280]{2,1,0:T(8,128)}, f32[8,64,280]{2,1,0:T(8,128)}, u32[]{:S(2)}, u32[]{:S(2)}) collective-permute-start(f32[8,64,280]{2,1,0:T(8,128)} %maximum_select_fusion.5), channel_id=1, source_target_pairs={{0,16},{8,24},{16,0},{24,8},{1,17},{9,25},{17,1},{25,9},{2,18},{10... | collective-permute-start | bytes 1720328 | tf_op jit(solution)/shard_map/ppermute | solution.py:135
  1168.8 20.1 %collective-permute-start.41 = (f32[63,128]{1,0:T(8,128)S(1)}, f32[63,128]{1,0:T(8,128)S(1)}, u32[]{:S(2)}, u32[]{:S(2)}) collective-permute-start(f32[63,128]{1,0:T(8,128)S(1)} %add.597), channel_id=1, source_target_pairs={{0,16},{8,24},{16,0},{24,8},{1,17},{9,25},{17,1},{25,9},{2,18},{10... | collective-permute-start | bytes 96776 | tf_op jit(solution)/shard_map/ppermute | solution.py:147
  1210.2 27.5 %collective-permute-start.52 = (bf16[2,64,2304]{2,1,0:T(8,128)(2,1)S(1)}, bf16[2,64,2304]{2,1,0:T(8,128)(2,1)S(1)}, u32[]{:S(2)}, u32[]{:S(2)}) collective-permute-start(bf16[2,64,2304]{2,1,0:T(8,128)(2,1)S(1)} %dynamic-slice_bitcast_fusion.7), channel_id=1, source_target_pairs={{0,16},{8,24},{16,0},{24,8},{1,17},{9,25},{17,1},{25,9},{2,18},{10... | collective-permute-start | bytes 1769480 | tf_op jit(solution)/shard_map/ppermute | solution.py:96
  1266.8 37.1 %collective-permute-start.64 = (f32[8,64,280]{2,1,0:T(8,128)S(1)}, f32[8,64,280]{2,1,0:T(8,128)S(1)}, u32[]{:S(2)}, u32[]{:S(2)}) collective-permute-start(f32[8,64,280]{2,1,0:T(8,128)S(1)} %maximum_select_fusion.4), channel_id=1, source_target_pairs={{0,16},{8,24},{16,0},{24,8},{1,17},{9,25},{17,1},{25,9},{2,18},{10... | collective-permute-start | bytes 1720328 | tf_op jit(solution)/shard_map/ppermute | solution.py:135
  (215 other events, 2766.7 us)
Sparse Core Ops, SparseCore 0:
  11.4 74.7 all-gather.8
  89.6 60.1 all-gather.10
  153.1 79.2 all-gather.12
  235.0 60.0 all-gather.14
  297.7 71.7 all-gather.16
  372.2 62.5 all-gather.18
  437.6 81.1 all-gather.20
  521.5 60.0 all-gather.22

commit v2 on v1

v2 whole, which is shorter than its diff:
```python
import functools
import math

import jax
import jax.numpy as jnp
from jax import lax
from jax.experimental import pallas as pl
from jax.experimental.pallas import tpu as pltpu
from jax.sharding import PartitionSpec as P

HDIM = 64
STATE = 128
CONV = 4
ADIM = 64
GROUP = 4
LANES = 128
EPSILON = 1e-05
THETA = 100000000000.0
HIGHEST = lax.Precision.HIGHEST
LOW = jnp.bfloat16
WIDE = jnp.float32
MASKED = -1e30
VMEM_LIMIT = 56 * 1024 * 1024
PARCEL_ROWS = 16


def dot(a, b, ca=1, cb=0, precision=None):
    return lax.dot_general(
        a, b, (((ca,), (cb,)), ((), ())), preferred_element_type=WIDE, precision=precision
    )


def lane_iota(shape):
    return lax.broadcasted_iota(jnp.int32, shape, len(shape) - 1)


def row_iota(shape):
    return lax.broadcasted_iota(jnp.int32, shape, 0)


def kernel_call(body, grid, in_specs, out_specs, out_shape, scratch=(), flops=0, moved=0):
    return pl.pallas_call(
        body,
        grid=grid,
        in_specs=in_specs,
        out_specs=out_specs,
        out_shape=out_shape,
        scratch_shapes=list(scratch),
        compiler_params=pltpu.CompilerParams(vmem_limit_bytes=VMEM_LIMIT),
        cost_estimate=pl.CostEstimate(flops=flops, bytes_accessed=moved, transcendentals=0),
    )


def whole(shape):
    return pl.BlockSpec(shape, lambda s: (0,) * len(shape))


def rows_block(rows, cols, col=0):
    return pl.BlockSpec((rows, cols), lambda s: (s, col))


def sequence_block(*shape):
    return pl.BlockSpec((None,) + shape, lambda s: (s,) + (0,) * len(shape))


def xor_pairs(count, bit):
    return [(i, i ^ bit) for i in range(count)]


def next_half(x, forward):
    firsts = range(0, lax.axis_size("ctx"), 2)
    return lax.ppermute(x, "ctx", [(i, i + 1) if forward else (i + 1, i) for i in firsts])


STRAIGHT = ((0, 0), (2, 1), (1, 2), (3, 3))
CROSSED = ((1, 0), (3, 1), (0, 2), (2, 3))


def to_halves_moves(quarters):
    place = lax.axis_index("ctx")
    a = lax.ppermute(pick(quarters, place % 2, 0), "ctx", STRAIGHT)
    b = lax.ppermute(pick(quarters, 1 - place % 2, 0), "ctx", CROSSED)
    return a, b


def to_halves(a, b):
    place = lax.axis_index("ctx")
    return jnp.where(place < 2, jnp.concatenate([a, b]), jnp.concatenate([b, a]))


def to_quarters(half):
    place = lax.axis_index("ctx")
    parts = half.reshape((2, -1) + half.shape[1:])
    late = place // 2
    a = lax.ppermute(pick(parts, late, 0), "ctx", [(j, i) for i, j in STRAIGHT])
    b = lax.ppermute(pick(parts, 1 - late, 0), "ctx", [(j, i) for i, j in CROSSED])
    return jnp.where(place % 2 == 0, jnp.stack([a, b]), jnp.stack([b, a]))


def tp_peer(x):
    return lax.ppermute(x, "tp", xor_pairs(lax.axis_size("tp"), 1))


def tp_join(x):
    peer = tp_peer(x)
    first = lax.axis_index("tp") == 0
    return jnp.where(
        first, jnp.concatenate([x, peer], axis=-1), jnp.concatenate([peer, x], axis=-1)
    )


def tp_sum(partial_sum):
    low = partial_sum.astype(LOW)
    peer = tp_peer(low)
    return low.astype(WIDE) + peer.astype(WIDE)


def bits_of(axis):
    return [1 << i for i in range(lax.axis_size(axis).bit_length() - 1)]


def together(values, anchor):
    return lax.optimization_barrier((tuple(values), anchor))


def added(*parts):
    total = parts[0].astype(WIDE)
    for part in parts[1:]:
        total = total + part.astype(WIDE)
    return total


def ctx_swap(values, step):
    return lax.ppermute(values, "ctx", xor_pairs(lax.axis_size("ctx"), step))


def pick(values, place, dim):
    return lax.dynamic_index_in_dim(values, place, dim, False)


def half_lanes(width):
    return width // 256 * 128


FLIPS = (0, 1, 3, 2)


def own_order(features, dtype):
    fsdp, ctx = lax.axis_size("fsdp"), lax.axis_size("ctx")
    rows = features // (fsdp * ctx)
    own = jnp.arange(features)
    flip, rest = jnp.array(FLIPS)[own // (fsdp * rows)], own % (fsdp * rows)
    common = (rest // rows) * ctx * rows + (flip ^ lax.axis_index("ctx")) * rows + rest % rows
    return (jnp.arange(features)[:, None] == common[None, :]).astype(dtype)


def spread_first(block):
    return ctx_swap(block, 1), ctx_swap(block, 2)


def spread_parts(came):
    cut = half_lanes(came[0].shape[-1])
    return came[0][..., :cut], came[1][..., cut:]


def spread_second(parts):
    return ctx_swap(parts[0], 2), ctx_swap(parts[1], 1)


def spread_whole(block, came, far):
    width = block.shape[-1]
    return jnp.concatenate(
        [v.reshape(-1, width) for v in (block, came[0], jnp.concatenate(far, axis=-1), came[1])], axis=0
    )


def fsdp_moves(piece):
    count = lax.axis_size("fsdp")
    if count > 4:
        return ()
    return tuple(lax.ppermute(piece, "fsdp", xor_pairs(count, step)) for step in range(1, count))


def fsdp_join(piece, came):
    if not came:
        return lax.all_gather(piece, "fsdp", axis=0)
    place = lax.axis_index("fsdp")
    shape = (len(came) + 1,) + piece.shape
    out = lax.dynamic_update_index_in_dim(jnp.zeros(shape, piece.dtype), piece, place, 0)
    for step, values in enumerate(came, 1):
        out = lax.dynamic_update_index_in_dim(out, values, place ^ step, 0)
    return out


def gathered_blocks(pieces, anchor):
    following, anchor = together((pieces[1], jnp.concatenate(pieces[2:], axis=1)), anchor)
    blocks = [lax.all_gather(following[0], "fsdp", axis=0)]
    rest = lax.all_gather(following[1], "fsdp", axis=0)
    first = 0
    for piece in pieces[2:]:
        blocks.append(rest[..., first : first + piece.shape[1]])
        first += piece.shape[1]
    return blocks, anchor


class Gathers:
    def __init__(self, blocks):
        self.blocks = blocks
        self.near = [None] * len(blocks)
        self.far = [None] * len(blocks)
        self.first = 0
        self.near[0] = spread_first(self.blocks[0])

    def step(self, anchor):
        i = self.first
        if i >= len(self.blocks):
            return anchor
        self.near[i], anchor = together(self.near[i], anchor)
        parts = spread_parts(self.near[i])
        self.far[i] = spread_second(parts)
        _, anchor = together(parts, anchor)
        self.first = i + 1
        return anchor

    def begin(self, anchor):
        i = self.first
        if i < len(self.blocks) and self.near[i] is None:
            (self.blocks[i],), anchor = together((self.blocks[i],), anchor)
            self.near[i] = spread_first(self.blocks[i])
        return anchor

    def take(self, i):
        if self.first <= i:
            self.step(self.near[i][0])
        return spread_whole(self.blocks[i], self.near[i], self.far[i])


def gathered_ctx(block, near, count):
    far = spread_second(spread_parts(near))
    rows = spread_whole(block, near, far).reshape((4,) + block.shape[1:])
    width = rows.shape[-1] // count
    return [rows[..., i * width : (i + 1) * width] for i in range(count)]


def table_body(spans, *refs):
    count = len(spans)
    left_refs, a_refs, b_refs = (refs[i * count : (i + 1) * count] for i in range(3))
    up_ref, across_ref, x_ref, y_ref, own_a_ref, own_b_ref, turned_ref = refs[3 * count :]
    size = own_a_ref.shape[0]
    place = pl.program_id(0)
    for left_ref, a_ref, b_ref, (first, last) in zip(left_refs, a_refs, b_refs, spans):

        @pl.when(place == first)
        def _(left_ref=left_ref):
            turned_ref[...] = left_ref[...].astype(WIDE).T.astype(LOW)

        @pl.when((place >= first) & (place < last))
        def _(a_ref=a_ref, b_ref=b_ref):
            table = dot(turned_ref[...], a_ref[...]).astype(LOW)
            own_a_ref[...] = table[:size]
            x_ref[...] = table[size : 2 * size]
            up_ref[...] = table[2 * size :]
            table = dot(turned_ref[...], b_ref[...]).astype(LOW)
            own_b_ref[...] = table[:size]
            across_ref[...] = table[size : 3 * size]
            y_ref[...] = table[3 * size :]


def tables(pairs, tile):
    rows, features = pairs[0][0].shape
    size = features // len(FLIPS)
    spans, first = [], 0
    for _, right in pairs:
        spans.append((first, first + right.shape[1] // (2 * tile)))
        first = spans[-1][1]
    width = first * tile

    def columns(first, last, skip):
        return pl.BlockSpec(
            (rows, tile), lambda j: (0, skip + jnp.clip(j, first, last - 1) - first)
        )

    def tall(height):
        return pl.BlockSpec((height, tile), lambda j: (0, j))

    heights = (2 * size, 2 * size, size, size, size, size)
    return kernel_call(
        functools.partial(table_body, tuple(spans)),
        (first,),
        [whole((rows, features))] * len(pairs)
        + [columns(*span, 0) for span in spans]
        + [columns(*span, span[1] - span[0]) for span in spans],
        [tall(h) for h in heights],
        [jax.ShapeDtypeStruct((h, width), LOW) for h in heights],
        [pltpu.VMEM((features, rows), LOW)],
        flops=4 * rows * features * width,
        moved=width * (4 * rows + 4 * features),
    )(*[p[0] for p in pairs], *[p[1] for p in pairs], *[p[1] for p in pairs])


def fsdp_table_body(left_ref, right_ref, out_ref, turned_ref):
    @pl.when(pl.program_id(0) == 0)
    def _():
        turned_ref[...] = left_ref[...].astype(WIDE).T.astype(LOW)

    table = dot(turned_ref[...], right_ref[...])
    fsdp, flips, rows, _ = out_ref.shape
    for flip in range(flips):
        for place in range(fsdp):
            first = (flip * fsdp + place) * rows
            out_ref[place, flip] = table[first : first + rows].astype(LOW)


def fsdp_table(left, right, tile):
    rows, features = left.shape
    width = right.shape[1]
    fsdp, flips = lax.axis_size("fsdp"), len(FLIPS)
    shape = (fsdp, flips, features // (fsdp * flips))
    return kernel_call(
        fsdp_table_body,
        (width // tile,),
        [whole((rows, features)), pl.BlockSpec((rows, tile), lambda j: (0, j))],
        pl.BlockSpec(shape + (tile,), lambda j: (0, 0, 0, j)),
        jax.ShapeDtypeStruct(shape + (width,), LOW),
        [pltpu.VMEM((features, rows), LOW)],
        flops=2 * rows * features * width,
        moved=width * (2 * rows + 2 * features),
    )(left, right)


def pass_body(x_ref, y_ref, from_y_ref, from_x_ref, to_x_ref, to_y_ref):
    size = x_ref.shape[0]
    to_x_ref[...] = (x_ref[...].astype(WIDE) + from_y_ref[:size].astype(WIDE)).astype(LOW)
    to_y_ref[...] = (y_ref[...].astype(WIDE) + from_x_ref[size:].astype(WIDE)).astype(LOW)


def keep_body(own_a_ref, own_b_ref, from_y_ref, from_x_ref, last_x_ref, last_y_ref, out_ref):
    size, width = own_a_ref.shape
    out_ref[:, :width] = (
        own_a_ref[...].astype(WIDE) + from_y_ref[size:].astype(WIDE) + last_x_ref[...].astype(WIDE)
    ).astype(LOW)
    out_ref[:, width:] = (
        own_b_ref[...].astype(WIDE) + from_x_ref[:size].astype(WIDE) + last_y_ref[...].astype(WIDE)
    ).astype(LOW)


def once(body, out_shapes, *operands):
    outs = [jax.ShapeDtypeStruct(shape, LOW) for shape in out_shapes]
    return kernel_call(
        body,
        (1,),
        [whole(v.shape) for v in operands],
        [whole(shape) for shape in out_shapes],
        outs,
        moved=sum(v.size * 2 for v in operands) + sum(2 * math.prod(x) for x in out_shapes),
    )(*operands)


def ctx_scatter(cuts, waits):
    up, across, x, y, own_a, own_b = cuts
    from_y, from_x = yield (ctx_swap(up, 2), ctx_swap(across, 1)), waits[0], (up, across)
    to_x, to_y = once(pass_body, (x.shape, y.shape), x, y, from_y, from_x)
    last_x, last_y = yield (ctx_swap(to_x, 1), ctx_swap(to_y, 2)), waits[1], (to_x, to_y)
    size, width = own_a.shape
    (out,) = once(keep_body, ((size, 2 * width),), own_a, own_b, from_y, from_x, last_x, last_y)
    return out


def fsdp_scatter(table, direct):
    count = lax.axis_size("fsdp")
    if count > 4 or not direct:
        total = lax.psum_scatter(table, "fsdp", scatter_dimension=0, tiled=False)
        if direct is None:
            (total,) = yield (total,), 0, (table,)
        else:
            yield (), 0, (table,)
        return total.astype(WIDE)
    place = lax.axis_index("fsdp")
    came = tuple(
        lax.ppermute(pick(table, place ^ step, 0), "fsdp", xor_pairs(count, step))
        for step in range(1, count)
    )
    came = yield came, 0, (table,)
    return added(pick(table, place, 0), *came)


class Scatters:
    def __init__(self):
        self.active = []

    def add(self, pairs, tile, direct, waits, done):
        cuts = tables(pairs, tile)

        def run():
            part = yield from ctx_scatter(cuts, waits)
            fsdp = lax.axis_size("fsdp")
            part = part.reshape(fsdp, -1, part.shape[1])
            done((yield from fsdp_scatter(part, direct)))

        self.begin(run())
        return cuts[0]

    def add_fsdp_first(self, left, right, waits, done):
        table = fsdp_table(left, right, 256)
        fsdp, flips, rows, width = table.shape

        def run():
            moved = table.reshape(fsdp, flips * rows, width)
            total = lax.psum_scatter(moved, "fsdp", scatter_dimension=0, tiled=False)
            (total,) = yield (total,), waits, (moved,)
            cut = half_lanes(width)
            own, x, far, y = (total[i * rows : (i + 1) * rows] for i in range(flips))
            cuts = (
                total[2 * rows :, :cut],
                total[rows : 3 * rows, cut:],
                x[:, :cut],
                y[:, cut:],
                own[:, :cut],
                own[:, cut:],
            )
            done((yield from ctx_scatter(cuts, (0, 0))).astype(WIDE))

        self.begin(run())
        return table

    def begin(self, work):
        self.active.append([work, *next(work)])

    def step(self, anchor):
        ready = [item for item in self.active if anchor is None or item[2] == 0]
        for item in self.active:
            item[2] = max(item[2] - 1, 0)
        values = [v for item in ready for v in item[1]]
        if anchor is not None:
            values, anchor = together(values, anchor)
        elif values:
            values = lax.optimization_barrier(tuple(values))
        first, sent = 0, ()
        for item in ready:
            came = tuple(values[first : first + len(item[1])])
            first += len(item[1])
            try:
                item[1:] = item[0].send(came)
                sent += item[3]
            except StopIteration:
                self.active.remove(item)
        if sent and anchor is not None:
            _, anchor = together(sent, anchor)
        return anchor

    def finish(self):
        while self.active:
            self.step(None)


def join_rows(piece):
    v = piece[None, None]
    for dim, axis in enumerate(("fsdp", "ctx")):
        place = lax.axis_index(axis)
        for step in bits_of(axis):
            (came,) = yield (lax.ppermute(v, axis, xor_pairs(lax.axis_size(axis), step)),), 0, ()
            v = jnp.where(
                (place & step) == 0,
                jnp.concatenate([v, came], axis=dim),
                jnp.concatenate([came, v], axis=dim),
            )
    return v


def sum_everywhere(v):
    for axis in ("fsdp", "ctx"):
        for step in bits_of(axis):
            (came,) = yield (lax.ppermute(v, axis, xor_pairs(lax.axis_size(axis), step)),), 0, ()
            v = v + came
    return v


def turn_tables(start_row, rows):
    half = ADIM // 2
    places = (start_row + jnp.arange(rows)).astype(WIDE)
    rates = jnp.exp(-math.log(THETA) * jnp.arange(half).astype(WIDE) / half)
    angles = places[:, None] * rates[None, :]
    cosine, sine = jnp.cos(angles), jnp.sin(angles)
    one_cos = jnp.concatenate([cosine, cosine], axis=1)
    one_sin = jnp.concatenate([-sine, sine], axis=1)
    still = jnp.ones_like(one_cos)
    return (
        jnp.concatenate([one_cos, one_cos, one_cos, still], axis=1),
        jnp.concatenate([one_sin, one_sin, one_sin, jnp.zeros_like(one_sin)], axis=1),
    )


def turned(values, cosine, sine):
    lanes = lane_iota(values.shape) % ADIM
    swapped = jnp.where(
        lanes < ADIM // 2,
        pltpu.roll(values, LANES - ADIM // 2, 1),
        pltpu.roll(values, ADIM // 2, 1),
    )
    return values * cosine + swapped * sine


def qkv_body(rows_ref, cos_ref, sin_ref, q_ref, kv_ref):
    for pair in range(GROUP // 2):
        lanes = slice(pair * LANES, (pair + 1) * LANES)
        q_ref[:, lanes] = turned(
            rows_ref[:, lanes], cos_ref[:, :LANES], sin_ref[:, :LANES]
        ).astype(LOW)
    width = GROUP * ADIM
    kv_ref[...] = turned(
        rows_ref[:, width : width + LANES], cos_ref[:, LANES:], sin_ref[:, LANES:]
    ).astype(LOW)


def split_qkv(projected, tables, rows, column):
    total = projected.shape[0]
    width = GROUP * ADIM
    return kernel_call(
        qkv_body,
        (total // rows,),
        [rows_block(rows, width + LANES, column)] + [rows_block(rows, 2 * LANES)] * 2,
        [rows_block(rows, width), rows_block(rows, LANES)],
        [
            jax.ShapeDtypeStruct((total, width), LOW),
            jax.ShapeDtypeStruct((total, LANES), LOW),
        ],
        flops=total * 400 * 4,
        moved=total * 384 * 6,
    )(projected, *tables)


def head_lanes(values, head):
    pair = values[:, head // 2 * LANES : (head // 2 + 1) * LANES]
    if head % 2:
        pair = pltpu.roll(pair, ADIM, 1)
    return jnp.where(lane_iota(pair.shape) < ADIM, pair, jnp.zeros_like(pair))


def seen_keys(place, rows, total):
    shape = (rows, 2 * total)
    column = lane_iota(shape)
    own = (column < total) & (column <= row_iota(shape) + pl.program_id(0) * rows)
    return own | ((column >= total) & (column < total * (1 + place)))


def attend_body(place_ref, q_ref, own_ref, came_ref, out_ref, total_ref, keys):
    rows, total = q_ref.shape[0], own_ref.shape[0]
    keys[:total, :] = own_ref[...]
    keys[total:, :] = came_ref[...]
    seen = seen_keys(place_ref[0], rows, total)
    q_all = q_ref[...].astype(WIDE)
    all_keys = keys[...]
    totals = jnp.zeros((rows, LANES), WIDE)
    lanes = lane_iota((rows, LANES))
    outs = []
    for head in range(GROUP):
        query = head_lanes(q_all, head).astype(LOW)
        scores = jnp.where(seen, dot(query, all_keys, 1, 1) * ADIM**-0.5, MASKED)
        top = jnp.max(scores, axis=1, keepdims=True)
        raised = jnp.exp(scores - top)
        row_total = jnp.sum(raised, axis=1, keepdims=True)
        weights = (raised * (1.0 / row_total)).astype(LOW)
        outs.append(dot(weights, all_keys))
        totals = jnp.where(lanes == head, top + jnp.log(row_total), totals)
    total_ref[...] = totals
    for pair in range(GROUP // 2):
        first = pltpu.roll(outs[2 * pair], ADIM, 1)
        out_ref[:, pair * LANES : (pair + 1) * LANES] = jnp.where(
            lanes < ADIM, first, outs[2 * pair + 1]
        ).astype(LOW)


def attend(place, queries, own, came, rows):
    total, width = queries.shape
    return kernel_call(
        attend_body,
        (total // rows,),
        [
            pl.BlockSpec(memory_space=pltpu.SMEM),
            rows_block(rows, width),
            whole((total, LANES)),
            whole((total, LANES)),
        ],
        [rows_block(rows, width), rows_block(rows, LANES)],
        [
            jax.ShapeDtypeStruct((total, width), LOW),
            jax.ShapeDtypeStruct((total, LANES), WIDE),
        ],
        [pltpu.VMEM((2 * total, LANES), LOW)],
        flops=total * total * 2 * GROUP * LANES * 4,
        moved=total * (width * 4 + LANES * 12),
    )(place, queries, own, came)


def attend_back_body(
    place_ref, q_ref, grad_ref, total_ref, cos_ref, sin_ref, own_ref, came_ref,
    dq_ref, own_grad_ref, came_grad_ref, keys, grads,
):
    rows, total = q_ref.shape[0], own_ref.shape[0]
    keys[:total, :] = own_ref[...]
    keys[total:, :] = came_ref[...]
    seen = seen_keys(place_ref[0], rows, total)
    q_all = q_ref[...].astype(WIDE)
    grad_all = grad_ref[...].astype(WIDE)
    all_keys = keys[...]
    lanes = lane_iota((rows, LANES))
    grad_kv = None
    dqs = []
    for head in range(GROUP):
        query = head_lanes(q_all, head).astype(LOW)
        upper = pltpu.roll(head_lanes(grad_all, head), ADIM, 1).astype(LOW)
        scores = jnp.where(seen, dot(query, all_keys, 1, 1) * ADIM**-0.5, MASKED)
        probs = jnp.exp(scores - total_ref[:, head : head + 1])
        grad_probs = dot(upper, all_keys, 1, 1)
        inner = jnp.sum(probs * grad_probs, axis=1, keepdims=True)
        grad_scores = (probs * (grad_probs - inner)).astype(LOW)
        dqs.append(dot(grad_scores, all_keys) * ADIM**-0.5)
        fresh = dot(grad_scores, query, 0, 0) * ADIM**-0.5 + dot(
            probs.astype(LOW), upper, 0, 0
        )
        grad_kv = fresh if grad_kv is None else grad_kv + fresh
    for pair in range(GROUP // 2):
        both = jnp.where(lanes < ADIM, dqs[2 * pair], pltpu.roll(dqs[2 * pair + 1], ADIM, 1))
        dq_ref[:, pair * LANES : (pair + 1) * LANES] = turned(
            both, cos_ref[:, :LANES], -sin_ref[:, :LANES]
        ).astype(LOW)
    place = pl.program_id(0)

    @pl.when(place == 0)
    def _():
        grads[...] = grad_kv

    @pl.when(place > 0)
    def _():
        grads[...] += grad_kv

    own_grad_ref[...] = grads[:total, :]
    came_grad_ref[...] = grads[total:, :].astype(LOW)


def attend_back(place, queries, grad_out, log_total, tables, own, came, rows):
    total, width = queries.shape
    return kernel_call(
        attend_back_body,
        (total // rows,),
        [
            pl.BlockSpec(memory_space=pltpu.SMEM),
            rows_block(rows, width),
            rows_block(rows, width),
            rows_block(rows, LANES),
            rows_block(rows, 2 * LANES),
            rows_block(rows, 2 * LANES),
            whole((total, LANES)),
            whole((total, LANES)),
        ],
        [rows_block(rows, width), whole((total, LANES)), whole((total, LANES))],
        [
            jax.ShapeDtypeStruct((total, width), LOW),
            jax.ShapeDtypeStruct((total, LANES), WIDE),
            jax.ShapeDtypeStruct((total, LANES), LOW),
        ],
        [pltpu.VMEM((2 * total, LANES), LOW), pltpu.VMEM((2 * total, LANES), WIDE)],
        flops=total * total * 2 * GROUP * LANES * 10,
        moved=total * (width * 6 + LANES * 20),
    )(place, queries, grad_out, log_total, *tables, own, came)


def key_body(own_ref, *refs):
    came, (cos_ref, sin_ref, out_ref) = refs[:-3], refs[-3:]
    values = own_ref[...]
    for ref in came:
        values = values + ref[...].astype(WIDE)
    out_ref[...] = turned(values, cos_ref[:, LANES:], -sin_ref[:, LANES:]).astype(LOW)


def finish_keys(own, came, tables, rows):
    total = own.shape[0]
    return kernel_call(
        key_body,
        (total // rows,),
        [rows_block(rows, LANES)] * (1 + len(came)) + [rows_block(rows, 2 * LANES)] * 2,
        rows_block(rows, LANES),
        jax.ShapeDtypeStruct((total, LANES), LOW),
        flops=total * LANES * 10,
        moved=total * LANES * 12,
    )(own, *came, *tables)


def sigmoid(v):
    return 1.0 / (1.0 + jnp.exp(-v))


def softplus(v):
    return jnp.maximum(v, 0.0) + jnp.log1p(jnp.exp(-jnp.abs(v)))


def over_pair(values, pair, shape):
    first = values[:, 2 * pair : 2 * pair + 1]
    second = values[:, 2 * pair + 1 : 2 * pair + 2]
    return jnp.where(lane_iota(shape) < HDIM, first, second)


def down_pair(values, pair):
    shape = (LANES, LANES)
    first = jnp.broadcast_to(values[:, 2 * pair : 2 * pair + 1], shape)
    second = jnp.broadcast_to(values[:, 2 * pair + 1 : 2 * pair + 2], shape)
    return jnp.where(row_iota(shape) < HDIM, first, second)


def lower_ones(rows, flip):
    shape = (rows, rows)
    t, s = row_iota(shape), lane_iota(shape)
    return jnp.where((t <= s) if flip else (t >= s), 1.0, 0.0).astype(WIDE)


def convolved(padded, taps_ref, rows):
    total = taps_ref[CONV : CONV + 1, :]
    for j in range(CONV):
        first = 8 - CONV + 1 + j
        total = total + taps_ref[j : j + 1, :] * padded[first : first + rows, :]
    return total


def scan_body(
    zx_ref, side_ref, rim_ref, taps_ref, heads_ref,
    stk_ref, x_ref, bc_ref, y_ref, first_ref, parcel_ref, cum_ref, all_ref, step_ref,
    padded, state, before_it,
):
    rows, channels = zx_ref.shape
    heads = channels // HDIM
    place = pl.program_id(0)

    @pl.when(place == 0)
    def _():
        padded[0:8, :] = rim_ref[...]
        state[...] = jnp.zeros(state.shape, WIDE)
        before_it[...] = jnp.zeros(before_it.shape, WIDE)

    @pl.when(place > 0)
    def _():
        padded[0:8, :] = padded[rows : rows + 8, :]

    stk_ref[:, :channels] = zx_ref[...].astype(LOW)
    stk_ref[:, channels:] = side_ref[:, : 2 * STATE].astype(LOW)
    padded[8 : 8 + rows, :] = stk_ref[...].astype(WIDE)
    before = convolved(padded, taps_ref, rows)
    active = (before * sigmoid(before)).astype(LOW)
    x_ref[...] = active[:, :channels]
    bc_ref[...] = active[:, channels:]
    step = softplus(side_ref[:, 2 * STATE :] + heads_ref[1:2, :])
    cum = dot(lower_ones(rows, False), -step * jnp.exp(heads_ref[0:1, :]), precision=HIGHEST)
    step_ref[...] = step
    cum_ref[...] = cum
    all_ref[...] = cum + before_it[0:1, :]
    cum_rows, step_rows = cum.T, step.T
    last = cum[rows - 1 : rows, :]
    before_it[...] = jnp.broadcast_to(before_it[0:1, :] + last, before_it.shape)
    tail = jnp.exp(last - cum) * step
    grown, faded = jnp.exp(cum), jnp.exp(last)
    entry, readout = bc_ref[:, :STATE], bc_ref[:, STATE:]
    cross = dot(readout, entry, 1, 1)
    shape = (rows, rows)
    causal = row_iota(shape) >= lane_iota(shape)
    lanes = lane_iota((rows, LANES))
    for pair in range(heads // 2):
        block = slice(pair * LANES, (pair + 1) * LANES)
        inputs = x_ref[:, block]
        outs = []
        for head in (2 * pair, 2 * pair + 1):
            gap = cum[:, head : head + 1] - cum_rows[head : head + 1, :]
            decay = jnp.exp(jnp.where(causal, gap, MASKED))
            mixed = (decay * cross * step_rows[head : head + 1, :]).astype(LOW)
            outs.append(dot(mixed, inputs))
        carried = dot(readout, state[block, :].astype(LOW), 1, 1)
        y_ref[:, block] = jnp.where(lanes < HDIM, outs[0], outs[1]) + carried * over_pair(
            grown, pair, (rows, LANES)
        )
        scaled = (over_pair(tail, pair, (rows, LANES)) * inputs.astype(WIDE)).astype(LOW)
        fresh = down_pair(faded, pair) * state[block, :] + dot(scaled, entry, 0, 0)
        state[block, :] = fresh
        parcel_ref[block, :] = fresh.astype(LOW)
    write_decays(parcel_ref, channels, before_it[0:1, :])

    @pl.when(place == 0)
    def _():
        first_ref[...] = state[...]


def scan_local(projected, side, rim, taps, heads, rows, channels):
    total = projected.shape[0]
    count = total // rows
    width = channels + 2 * STATE
    return kernel_call(
        scan_body,
        (count,),
        [
            rows_block(rows, channels, 1),
            rows_block(rows, side.shape[1]),
            whole((8, width)),
            whole((8, width)),
            whole((8, LANES)),
        ],
        [
            rows_block(rows, width),
            rows_block(rows, channels),
            rows_block(rows, 2 * STATE),
            rows_block(rows, channels),
            whole((channels, STATE)),
            whole((channels + PARCEL_ROWS, STATE)),
            rows_block(rows, LANES),
            rows_block(rows, LANES),
            rows_block(rows, LANES),
        ],
        [
            jax.ShapeDtypeStruct((total, width), LOW),
            jax.ShapeDtypeStruct((total, channels), LOW),
            jax.ShapeDtypeStruct((total, 2 * STATE), LOW),
            jax.ShapeDtypeStruct((total, channels), WIDE),
            jax.ShapeDtypeStruct((channels, STATE), WIDE),
            jax.ShapeDtypeStruct((channels + PARCEL_ROWS, STATE), LOW),
            jax.ShapeDtypeStruct((total, LANES), WIDE),
            jax.ShapeDtypeStruct((total, LANES), WIDE),
            jax.ShapeDtypeStruct((total, LANES), WIDE),
        ],
        [
            pltpu.VMEM((rows + 8, width), WIDE),
            pltpu.VMEM((channels, STATE), WIDE),
            pltpu.VMEM((8, LANES), WIDE),
        ],
        flops=total * rows * channels * 8,
        moved=total * width * 16,
    )(projected, side, rim, taps, heads)


def tail_body(
    y_ref, cum_ref, bc_ref, x_ref, gate_ref, heads_ref, gain_ref, parcel_ref, out_ref, norm_ref
):
    rows, channels = y_ref.shape
    readout = bc_ref[:, STATE:]
    grown = jnp.exp(cum_ref[...])
    square = jnp.zeros((rows, 1), WIDE)
    for pair in range(channels // LANES):
        block = slice(pair * LANES, (pair + 1) * LANES)
        carried = dot(readout, parcel_ref[block, :], 1, 1)
        y = y_ref[:, block] + over_pair(grown, pair, carried.shape) * carried
        out_ref[:, block] = y
        skip = over_pair(heads_ref[2:3, :], pair, (1, LANES))
        gate = gate_ref[:, block]
        mixed = (y + skip * x_ref[:, block].astype(WIDE)) * (gate * sigmoid(gate))
        square = square + jnp.sum(mixed * mixed, axis=1, keepdims=True)
    scale = lax.rsqrt(square * (1.0 / channels) + EPSILON)
    for pair in range(channels // LANES):
        block = slice(pair * LANES, (pair + 1) * LANES)
        skip = over_pair(heads_ref[2:3, :], pair, (1, LANES))
        gate = gate_ref[:, block]
        mixed = (out_ref[:, block] + skip * x_ref[:, block].astype(WIDE)) * (gate * sigmoid(gate))
        norm_ref[:, block] = (mixed * scale * gain_ref[:, block]).astype(LOW)


def gate_tail(y, cum, bc, x, projected, heads, gain, parcel, rows):
    total, channels = y.shape
    return kernel_call(
        tail_body,
        (total // rows,),
        [
            rows_block(rows, channels),
            rows_block(rows, LANES),
            rows_block(rows, 2 * STATE),
            rows_block(rows, channels),
            rows_block(rows, channels, 0),
            whole((8, LANES)),
            whole((1, channels)),
            whole((channels + PARCEL_ROWS, STATE)),
        ],
        [rows_block(rows, channels), rows_block(rows, channels)],
        [
            jax.ShapeDtypeStruct((total, channels), WIDE),
            jax.ShapeDtypeStruct((total, channels), LOW),
        ],
        flops=total * channels * (2 * STATE + 40),
        moved=total * channels * 18,
    )(y, cum, bc, x, projected, heads, gain, parcel)


def tail_back_body(
    dn_ref, y_ref, cum_ref, bc_ref, x_ref, gate_ref, heads_ref, gain_ref,
    du_ref, dgate_ref, parcel_ref, sums_ref, state,
):
    @pl.when(pl.program_id(0) == 0)
    def _():
        state[...] = jnp.zeros(state.shape, WIDE)

    rows, channels = y_ref.shape
    readout = bc_ref[:, STATE:]
    grown = jnp.exp(cum_ref[...])
    square = jnp.zeros((rows, 1), WIDE)
    inner = jnp.zeros((rows, 1), WIDE)
    for pair in range(channels // LANES):
        block = slice(pair * LANES, (pair + 1) * LANES)
        skip = over_pair(heads_ref[2:3, :], pair, (1, LANES))
        gate = gate_ref[:, block]
        mixed = (y_ref[:, block] + skip * x_ref[:, block].astype(WIDE)) * (gate * sigmoid(gate))
        square = square + jnp.sum(mixed * mixed, axis=1, keepdims=True)
        inner = inner + jnp.sum(
            dn_ref[:, block] * gain_ref[:, block] * mixed, axis=1, keepdims=True
        )
    scale = lax.rsqrt(square * (1.0 / channels) + EPSILON)
    inner = inner * scale * (1.0 / channels)
    sums_ref[...] = jnp.zeros(sums_ref.shape, WIDE)
    for pair in range(channels // LANES):
        block = slice(pair * LANES, (pair + 1) * LANES)
        skip = over_pair(heads_ref[2:3, :], pair, (1, LANES))
        gate = gate_ref[:, block]
        inputs = x_ref[:, block].astype(WIDE)
        sigma = sigmoid(gate)
        value = y_ref[:, block] + skip * inputs
        unit = value * (gate * sigma) * scale
        upstream = dn_ref[:, block]
        dmixed = scale * (upstream * gain_ref[:, block] - unit * inner)
        du = dmixed * gate * sigma
        du_ref[:, block] = du
        dgate_ref[:, block] = (
            dmixed * value * (sigma * (1.0 + gate * (1.0 - sigma)))
        ).astype(LOW)
        sums_ref[0:1, block] = jnp.sum(upstream * unit, axis=0, keepdims=True)
        sums_ref[1:2, block] = jnp.sum(du * inputs, axis=0, keepdims=True)
        fresh = state[block, :] + dot(
            (over_pair(grown, pair, du.shape) * du).astype(LOW), readout, 0, 0
        )
        state[block, :] = fresh
        parcel_ref[block, :] = fresh.astype(LOW)
    write_decays(parcel_ref, channels, cum_ref[rows - 1 : rows, :])


def gate_tail_back(dn, y, cum, bc, x, projected, heads, gain, rows):
    total, channels = y.shape
    count = total // rows
    return kernel_call(
        tail_back_body,
        (count,),
        [
            rows_block(rows, channels),
            rows_block(rows, channels),
            rows_block(rows, LANES),
            rows_block(rows, 2 * STATE),
            rows_block(rows, channels),
            rows_block(rows, channels, 0),
            whole((8, LANES)),
            whole((1, channels)),
        ],
        [
            rows_block(rows, channels),
            rows_block(rows, channels),
            whole((channels + PARCEL_ROWS, STATE)),
            sequence_block(8, channels),
        ],
        [
            jax.ShapeDtypeStruct((total, channels), WIDE),
            jax.ShapeDtypeStruct((total, channels), LOW),
            jax.ShapeDtypeStruct((channels + PARCEL_ROWS, STATE), LOW),
            jax.ShapeDtypeStruct((count, 8, channels), WIDE),
        ],
        [pltpu.VMEM((channels, STATE), WIDE)],
        flops=total * channels * (2 * STATE + 60),
        moved=total * channels * 22,
    )(dn, y, cum, bc, x, projected, heads, gain)


def write_decays(parcel_ref, channels, last):
    high = jnp.broadcast_to(jnp.exp(last), (PARCEL_ROWS, LANES))
    top = high.astype(LOW).astype(WIDE)
    row = row_iota(high.shape)
    parcel_ref[channels:, :] = jnp.where(
        row == 0, top, jnp.where(row == 1, high - top, 0.0)
    ).astype(LOW)


def lane_sums(values):
    first = lane_iota(values.shape) < HDIM
    return (
        jnp.sum(jnp.where(first, values, 0.0), axis=1, keepdims=True),
        jnp.sum(jnp.where(first, 0.0, values), axis=1, keepdims=True),
    )


def scan_back_body(
    du_ref, x_ref, bc_ref, stk_ref, prior_ref, rim_ref, cum_ref, all_ref, step_ref, side_ref,
    first_ref, parcel_ref, later_ref, taps_ref, heads_ref,
    dstk_ref, drim_ref, dstep_ref, dtaps_ref, dheads_ref, padded, dact, after, behind,
):
    place = pl.program_id(0)
    second = jnp.where(place == 0, 1.0, 0.0).astype(WIDE)
    rows, channels = du_ref.shape
    heads = channels // HDIM
    width = channels + 2 * STATE
    entry, readout = bc_ref[:, :STATE], bc_ref[:, STATE:]
    cum, step = cum_ref[...], step_ref[...]
    cum_rows = cum.T
    last = cum[rows - 1 : rows, :]
    faded, arriving = jnp.exp(last), jnp.exp(all_ref[0:1, :] - cum[0:1, :])

    @pl.when(place == 0)
    def _():
        behind[...] = later_ref[:channels, :].astype(WIDE)
        after[8 + rows : 16 + rows, :] = jnp.zeros((8, width), WIDE)
        padded[0:8, :] = prior_ref[8:16, :].astype(WIDE)

    @pl.when(place > 0)
    def _():
        after[8 + rows : 16 + rows, :] = after[8:16, :]
        padded[0:8, :] = rim_ref[...]

    grown = jnp.exp(cum)
    decayed = jnp.exp(last - cum)
    tail = decayed * step
    cross = dot(entry, readout, 1, 1)
    shape = (rows, rows)
    causal = row_iota(shape) <= lane_iota(shape)
    lanes = lane_iota((rows, LANES))
    small = lane_iota((1, LANES))
    dcross = jnp.zeros(shape, WIDE)
    entry_grad = jnp.zeros((rows, STATE), WIDE)
    readout_grad = jnp.zeros((rows, STATE), WIDE)
    pulled = jnp.zeros((rows, LANES), WIDE)
    arrived = []
    carried_sum = jnp.zeros((rows, LANES), WIDE)
    final_sum = jnp.zeros((rows, LANES), WIDE)
    state_sum = jnp.zeros((1, LANES), WIDE)
    for pair in range(heads // 2):
        block = slice(pair * LANES, (pair + 1) * LANES)
        inputs = x_ref[:, block]
        inputs_wide = inputs.astype(WIDE)
        du = du_ref[:, block]
        du_low = du.astype(LOW)
        start = down_pair(arriving, pair) * parcel_ref[block, :].astype(WIDE)
        start = start + second * first_ref[block, :]
        later = behind[block, :]
        start_low, later_low = start.astype(LOW), later.astype(LOW)
        pulls = []
        for k in range(2):
            head = 2 * pair + k
            own = (lanes < HDIM) if k == 0 else (lanes >= HDIM)
            gap = cum_rows[head : head + 1, :] - cum[:, head : head + 1]
            decay = jnp.exp(jnp.where(causal, gap, MASKED))
            pulls.append(dot((decay * cross).astype(LOW), du_low))
            dmix = dot(jnp.where(own, inputs, jnp.zeros_like(inputs)), du_low, 1, 1) * decay
            stepped = step[:, head : head + 1]
            dcross = dcross + dmix * stepped
            dgap = dmix * cross
            pulled = jnp.where(lanes == head, jnp.sum(dgap, axis=1, keepdims=True), pulled)
            arrived.append(jnp.sum(dgap * stepped, axis=0, keepdims=True))
        pull = jnp.where(lanes < HDIM, pulls[0], pulls[1])
        grown_pair = over_pair(grown, pair, du.shape)
        grown_du = grown_pair * du
        grown_low = grown_du.astype(LOW)
        behind[block, :] = down_pair(faded, pair) * later + dot(grown_low, readout, 0, 0)
        readout_grad = readout_grad + dot(grown_low, start_low)
        sums = lane_sums(grown_du * dot(readout, start_low, 1, 1))
        carried_sum = jnp.where(lanes == 2 * pair, sums[0], carried_sum)
        carried_sum = jnp.where(lanes == 2 * pair + 1, sums[1], carried_sum)
        tail_pair = over_pair(tail, pair, du.shape)
        from_later = dot(entry, later_low, 1, 1)
        entry_grad = entry_grad + dot((tail_pair * inputs_wide).astype(LOW), later_low)
        sums = lane_sums(inputs_wide * from_later)
        final_sum = jnp.where(lanes == 2 * pair, sums[0], final_sum)
        final_sum = jnp.where(lanes == 2 * pair + 1, sums[1], final_sum)
        product = start * later
        for k in range(2):
            total = jnp.sum(
                jnp.sum(product[k * HDIM : (k + 1) * HDIM], axis=0, keepdims=True),
                axis=1,
                keepdims=True,
            )
            state_sum = jnp.where(small == 2 * pair + k, total, state_sum)
        skip = over_pair(heads_ref[2:3, :], pair, (1, LANES))
        dact[:, block] = (
            skip * du + over_pair(step, pair, du.shape) * pull + tail_pair * from_later
        )
    dcross_low = dcross.astype(LOW)
    dact[:, channels : channels + STATE] = entry_grad + dot(dcross_low, readout)
    dact[:, channels + STATE :] = readout_grad + dot(dcross_low, entry, 0, 0)
    arrived.append(jnp.zeros((LANES - heads, rows), WIDE))
    arrived_columns = jnp.concatenate(arrived, axis=0).T
    weighted = tail * final_sum
    dcum = arrived_columns - step * pulled + carried_sum - weighted
    at_last = jnp.sum(weighted, axis=0, keepdims=True) + faded * state_sum
    dcum = dcum + jnp.where(row_iota(dcum.shape) == rows - 1, at_last, 0.0)
    dlog = dot(lower_ones(rows, True), dcum, precision=HIGHEST)
    rate = jnp.exp(heads_ref[0:1, :])
    dstep = pulled + decayed * final_sum - rate * dlog
    dstep_pre = dstep * sigmoid(side_ref[...] + heads_ref[1:2, :])
    dstep_pre = jnp.where(lanes < heads, dstep_pre, 0.0)
    dstep_ref[...] = dstep_pre.astype(LOW)
    dheads_ref[...] = jnp.zeros(dheads_ref.shape, WIDE)
    dheads_ref[0:1, :] = -rate * jnp.sum(step * dlog, axis=0, keepdims=True)
    dheads_ref[1:2, :] = jnp.sum(dstep_pre, axis=0, keepdims=True)

    padded[8 : 8 + rows, :] = stk_ref[...].astype(WIDE)
    before = convolved(padded, taps_ref, rows)
    sigma = sigmoid(before)
    dbefore = dact[...] * sigma * (1.0 + before * (1.0 - sigma))
    after[0:8, :] = jnp.zeros((8, width), WIDE)
    after[8 : 8 + rows, :] = dbefore
    dtaps_ref[...] = jnp.zeros(dtaps_ref.shape, WIDE)
    back = None
    for j in range(CONV):
        first = 8 - CONV + 1 + j
        dtaps_ref[j : j + 1, :] = jnp.sum(
            after[8 : 8 + rows, :] * padded[first : first + rows, :], axis=0, keepdims=True
        )
        first = CONV - 1 - j
        term = taps_ref[j : j + 1, :] * after[first : first + rows + 8, :]
        back = term if back is None else back + term
    dtaps_ref[CONV : CONV + 1, :] = jnp.sum(after[8 : 8 + rows, :], axis=0, keepdims=True)
    drim_ref[...] = back[0:8]
    dstk_ref[...] = back[8:]


def scan_back(
    du, x, bc, stk, rim, cum, all_cum, step, side, first, parcel, later, taps, heads, rows
):
    total, channels = du.shape
    count = total // rows
    width = channels + 2 * STATE

    def back_block(cols, col=0):
        return pl.BlockSpec((rows, cols), lambda s: (count - 1 - s, col))

    return kernel_call(
        scan_back_body,
        (count,),
        [
            back_block(channels),
            back_block(channels),
            back_block(2 * STATE),
            back_block(width),
            pl.BlockSpec((16, width), lambda s: (rows // 16 - 1, 0)),
            whole((8, width)),
            back_block(LANES),
            back_block(LANES),
            back_block(LANES),
            back_block(LANES, 2 * STATE // LANES),
            whole((channels, STATE)),
            whole((channels + PARCEL_ROWS, STATE)),
            whole((channels + PARCEL_ROWS, STATE)),
            whole((8, width)),
            whole((8, LANES)),
        ],
        [
            back_block(width),
            whole((8, width)),
            back_block(LANES),
            sequence_block(8, width),
            sequence_block(8, LANES),
        ],
        [
            jax.ShapeDtypeStruct((total, width), WIDE),
            jax.ShapeDtypeStruct((8, width), WIDE),
            jax.ShapeDtypeStruct((total, LANES), LOW),
            jax.ShapeDtypeStruct((count, 8, width), WIDE),
            jax.ShapeDtypeStruct((count, 8, LANES), WIDE),
        ],
        [
            pltpu.VMEM((rows + 8, width), WIDE),
            pltpu.VMEM((rows, width), WIDE),
            pltpu.VMEM((rows + 16, width), WIDE),
            pltpu.VMEM((channels, STATE), WIDE),
        ],
        flops=total * rows * channels * 20,
        moved=total * width * 24,
    )(du, x, bc, stk, stk, rim, cum, all_cum, step, side, first, parcel, later, taps, heads)


def unit_scale(values):
    return lax.rsqrt(jnp.mean(values * values, axis=-1, keepdims=True) + EPSILON)


def normalize(values, gain):
    return (values * unit_scale(values) * gain).astype(LOW)


def norm_grad_body(
    kept_ref, gain_ref, own_ref, peer_ref, base_ref, out_ref, low_ref, sums_ref
):
    kept = kept_ref[...]
    scale = unit_scale(kept)
    unit = kept * scale
    upstream = own_ref[...].astype(WIDE) + peer_ref[...].astype(WIDE)
    scaled = upstream * gain_ref[...]
    inner = jnp.mean(scaled * unit, axis=-1, keepdims=True)
    out = base_ref[...] + scale * (scaled - unit * inner)
    out_ref[...] = out
    low_ref[...] = out.astype(LOW)
    sums = jnp.sum(upstream * unit, axis=0, keepdims=True)

    @pl.when(pl.program_id(0) == 0)
    def _():
        sums_ref[...] = jnp.broadcast_to(sums, sums_ref.shape)

    @pl.when(pl.program_id(0) > 0)
    def _():
        sums_ref[...] += jnp.broadcast_to(sums, sums_ref.shape)


def norm_grad(kept, gain, partial_grad, base):
    own = partial_grad.astype(LOW)
    rows, features = kept.shape
    tile = min(rows, 512)
    out, low, sums = kernel_call(
        norm_grad_body,
        (rows // tile,),
        [rows_block(tile, features), whole((1, features))] + [rows_block(tile, features)] * 3,
        [rows_block(tile, features), rows_block(tile, features), whole((8, features))],
        [
            jax.ShapeDtypeStruct((rows, features), WIDE),
            jax.ShapeDtypeStruct((rows, features), LOW),
            jax.ShapeDtypeStruct((8, features), WIDE),
        ],
        flops=rows * features * 12,
        moved=rows * features * 18,
    )(kept, gain[None], own, tp_peer(own), base)
    return out, low, sums[0]


def product(a, b):
    return jnp.dot(a, b, preferred_element_type=WIDE)


def against_rows(a, b):
    return dot(a, b, 1, 1)


def halves(values):
    cut = half_lanes(values.shape[1])
    return values[:, :cut], values[:, cut:]


def over_rows(a, b):
    return dot(a, b, 0, 0).astype(LOW)


def weight_rows(layer, pieces):
    zx, mix, attn, attn_out, mlp, mlp_out = (p[layer] for p in pieces)
    rows = zx.shape[0]
    return (
        jnp.concatenate([zx.reshape(rows, -1), attn.reshape(rows, -1)], axis=1),
        jnp.concatenate([mix.T, attn_out.T, mlp.reshape(rows, -1)], axis=1),
        mlp_out.T,
    )


def own_part(values, size, axis):
    return lax.dynamic_slice_in_dim(values, lax.axis_index("tp") * size, size, axis)


def padded_to(values, rows, lanes):
    return jnp.pad(values, ((0, rows - values.shape[0]), (0, lanes - values.shape[1])))


def local_small(order, layer, norm_gains, mamba_shared, conv_weight, conv_bias, head_params, mamba_gain):
    tp = lax.axis_size("tp")
    heads = head_params.shape[2] // tp
    full_ssm = mamba_gain.shape[1]
    channels = full_ssm // tp
    shared_all = mamba_shared[layer]
    shared = jnp.concatenate(
        [
            shared_all[:, : 2 * STATE],
            own_part(shared_all[:, 2 * STATE :], heads, 1),
            jnp.zeros((shared_all.shape[0], LANES - heads), LOW),
        ],
        axis=1,
    )
    taps_all = jnp.concatenate([conv_weight[layer], conv_bias[layer][None]], axis=0).astype(WIDE)
    taps = jnp.concatenate(
        [own_part(taps_all[:, :full_ssm], channels, 1), taps_all[:, full_ssm:]], axis=1
    )
    return (
        product(norm_gains[layer], order),
        dot(order, shared, 0, 0).astype(LOW),
        padded_to(taps, 8, taps.shape[1]),
        padded_to(own_part(head_params[layer], heads, 1), 8, LANES),
        own_part(mamba_gain[layer].astype(WIDE), channels, 0)[None],
    )


def layer_forward(hidden, layer, gathers, late, small, tables, place, sequences, moves):
    zx_w = gathers.take(2 * layer)
    gains, shared, taps, heads, gain = small
    rows = hidden.shape[0] // sequences
    channels = gain.shape[1]
    head_count = channels // HDIM
    normed = normalize(hidden, gains[0])
    projected = product(normed, zx_w)
    side = product(normed, shared)
    if layer == 0:
        late[:], projected = together(late, projected)
        late[:] = [lax.all_gather(v, "fsdp", axis=1).reshape(-1, v.shape[-1]) for v in late]
    mlp_out_w = late[layer]
    if layer > 0:
        (mlp_out_w,), projected = together((mlp_out_w,), projected)
    edge = jnp.concatenate(
        [projected[-CONV + 1 :, channels : 2 * channels], side[-CONV + 1 :, : 2 * STATE]], axis=1
    )
    came = next_half(edge.astype(LOW), True).astype(WIDE)
    rim = jnp.pad(came, ((8 - CONV + 1, 0), (0, 0)))
    queries, kv = split_qkv(projected, tables, rows, 2 * channels // (zx_w.shape[1] - 2 * channels))
    kv_came = next_half(kv, True)
    (kv_came,), rim = together((kv_came,), rim)
    rim = gathers.begin(rim)
    stk, x, bc, y_local, first, parcel_out, cum, all_cum, step = scan_local(
        projected, side, rim, taps, heads, rows, channels
    )
    parcel = next_half(parcel_out, True)
    attended, log_total = attend(place, queries, kv, kv_came, rows)
    if layer > 0:
        moves, parcel = together(moves, parcel)
    (attended, parcel), y_local = together((attended, parcel), y_local)
    parcel = gathers.step(parcel)
    parcel = gathers.begin(parcel)
    y, mamba_norm = gate_tail(y_local, all_cum, bc, x, projected, heads, gain, parcel, rows)
    both = jnp.concatenate([mamba_norm, attended], axis=1)
    rest = gathers.take(2 * layer + 1)
    mix_w, mlp_w = rest[:, : both.shape[1]], rest[:, both.shape[1] :]
    after_mix = hidden + tp_sum(against_rows(both, mix_w))
    normed_two = normalize(after_mix, gains[1])
    gate_up = product(normed_two, mlp_w)
    ff = gate_up.shape[1] // 2
    activated = (jax.nn.silu(gate_up[:, :ff]) * gate_up[:, ff:]).astype(LOW)
    if gathers.near[-1] is None:
        activated = gathers.step(activated)
    result = after_mix + tp_sum(against_rows(activated, mlp_out_w))
    saved = (
        hidden, normed, projected, side, rim, queries, kv, kv_came, stk, x, bc, cum, all_cum, step,
        first, parcel, log_total, y, both, after_mix, normed_two, gate_up, activated,
    )
    return result, saved, (zx_w, mix_w, mlp_w, mlp_out_w), moves


def layer_backward(
    upstream, grad_mlp, saved, weights, small, tables, place, sequences, scatters, split, done, extra
):
    (
        hidden, normed, projected, side, rim, queries, kv, kv_came, stk, x, bc, cum, all_cum, step,
        first, parcel, log_total, y, both, after_mix, normed_two, gate_up, activated,
    ) = saved
    zx_w, mix_w, mlp_w, mlp_out_w = weights
    gains, shared, taps, heads, gain = small
    rows = hidden.shape[0] // sequences
    channels = gain.shape[1]
    head_count = channels // HDIM
    grad_act = product(grad_mlp, mlp_out_w)
    ff = grad_act.shape[1]
    gate_part, up_part = gate_up[:, :ff], gate_up[:, ff:]
    sigma = jax.nn.sigmoid(gate_part)
    grad_gu = jnp.concatenate(
        [
            grad_act * up_part * sigma * (1.0 + gate_part * (1.0 - sigma)),
            grad_act * gate_part * sigma,
        ],
        axis=1,
    ).astype(LOW)
    table = scatters.add_fsdp_first(normed_two, grad_gu, 2, functools.partial(done, 3))
    _, grad_gu = together((table,), grad_gu)
    grad_mid, grad_mix, grad_gain_two = norm_grad(
        after_mix, gains[1], against_rows(grad_gu, mlp_w), upstream
    )
    grad_mid = scatters.step(grad_mid)
    if extra:
        extra[:], grad_mid = together(extra, grad_mid)
    table = scatters.add(
        [(grad_mlp, activated), (grad_mix, both)],
        256,
        None if split else False,
        (0, 0),
        functools.partial(done, 0),
    )
    _, grad_mix = together((table,), grad_mix)
    grad_norm = product(grad_mix, mix_w[:, :channels])
    grad_attended = product(grad_mix, mix_w[:, channels:]).astype(LOW)
    du, grad_gate, state_grads, tail_sums = gate_tail_back(
        grad_norm, y, all_cum, bc, x, projected, heads, gain, rows
    )
    later = next_half(state_grads, False)
    grad_q, own_kv, sent_kv = attend_back(
        place, queries, grad_attended, log_total, tables, kv, kv_came, rows
    )
    came_kv = [next_half(sent_kv, False)]
    (later, *came_kv), grad_gate = together((later, *came_kv), grad_gate)
    later = scatters.step(later)
    if split:
        mid = jnp.concatenate([grad_gate, grad_q], axis=1)
        table = scatters.add([(normed, mid)], 256, True, (0, 0), functools.partial(done, 2))
        _, later = together((table,), later)
    dstk, drim, grad_step, dtaps, dheads = scan_back(
        du, x, bc, stk, rim, cum, all_cum, step, side, first, parcel, later, taps, heads, rows
    )
    drim = scatters.step(drim)
    returned = next_half(drim[8 - CONV + 1 :], False)
    dstk = dstk + jnp.pad(returned, ((dstk.shape[0] - CONV + 1, 0), (0, 0)))
    grad_kv = finish_keys(own_kv, came_kv, tables, rows)
    grad_late = jnp.concatenate([dstk[:, :channels].astype(LOW), grad_kv], axis=1)
    grad_first = jnp.concatenate(
        [grad_gate, grad_late[:, :channels], grad_q, grad_late[:, channels:]], axis=1
    )
    grad_side = jnp.concatenate([dstk[:, channels:].astype(LOW), grad_step], axis=1)
    if split:
        late, tile = [grad_late, grad_side], 640
    else:
        late = [grad_gate, grad_q, grad_late[:, channels:], grad_late[:, :channels], grad_side]
        tile = 384
    late = jnp.concatenate(late, axis=1)
    table = scatters.add([(normed, late)], tile, split, (0, 0), functools.partial(done, 1))
    _, grad_first = together((table,), grad_first)
    below, grad_mlp, grad_gain_one = norm_grad(
        hidden,
        gains[0],
        against_rows(grad_first, zx_w) + against_rows(grad_side, shared),
        grad_mid,
    )
    tail_sums = jnp.sum(tail_sums, axis=0)
    dheads = jnp.sum(dheads, axis=0)
    skip_grad = jnp.sum(tail_sums[1].reshape(head_count, HDIM), axis=1)
    small_grads = (
        jnp.stack([grad_gain_one, grad_gain_two]),
        jnp.sum(dtaps, axis=0)[: CONV + 1],
        jnp.concatenate([dheads[:2, :head_count], skip_grad[None]], axis=0),
        tail_sums[0],
    )
    return scatters.step(below), grad_mlp, small_grads


def tp_ordered(a, b):
    low_half = lax.axis_index("tp") == 0
    return jnp.where(
        low_half, jnp.concatenate([a, b], axis=-1), jnp.concatenate([b, a], axis=-1)
    )


def settle_side(scatters, sums, half_heads, done):
    def run():
        fsdp = lax.axis_size("fsdp")
        layers = sums
        own = layers[0]
        rows = own.shape[0]
        wide = jnp.stack([v[:, : 2 * STATE].reshape(rows, 2, STATE) for v in layers])
        place = lax.axis_index("tp")
        (came,) = yield (tp_peer(pick(wide, 1 - place, 2)),), 0, ()
        mine = pick(wide, place, 2) + came
        steps = jnp.stack([v[:, 2 * STATE : 2 * STATE + half_heads] for v in layers]).reshape(-1)
        packed = jnp.concatenate([mine.reshape(-1), steps])
        packed = jnp.pad(packed, (0, -packed.size % (16 * LANES))).reshape(-1, LANES)
        joined = yield from join_rows(packed.astype(LOW))
        (theirs,) = yield (tp_peer(joined),), 0, ()
        count = len(layers)
        places = fsdp * lax.axis_size("ctx")

        def taken(values):
            flat = values.reshape(places, -1)
            wide_size = count * rows * STATE
            first = flat[:, :wide_size].reshape(places, count, rows, STATE)
            second = flat[:, wide_size : wide_size + count * rows * half_heads]
            return first, second.reshape(places, count, rows, half_heads)

        (wide_own, step_own), (wide_peer, step_peer) = taken(joined), taken(theirs)
        full = jnp.concatenate(
            [tp_ordered(wide_own, wide_peer), tp_ordered(step_own, step_peer)], axis=-1
        )
        done(full.transpose(1, 0, 2, 3).reshape(count, places * rows, -1).astype(WIDE))

    scatters.begin(run())


def settle_small(scatters, small_grads, done):
    def run():
        layers = len(small_grads)
        shapes = [v.shape for v in small_grads[0]]
        flat = [jnp.pad(v.reshape(-1), (0, -v.size % LANES)) for grads in small_grads for v in grads]
        packed = yield from sum_everywhere(jnp.concatenate(flat).reshape(-1, LANES))
        (packed_peer,) = yield (tp_peer(packed),), 0, ()
        own, peer = [], []
        first = 0
        for values, shape in zip(flat, shapes * layers):
            for source, parts in ((packed, own), (packed_peer, peer)):
                piece = source.reshape(-1)[first : first + math.prod(shape)]
                parts.append(piece.reshape(shape))
            first += values.shape[0]
        count = len(shapes)
        for l in range(layers):
            (gains, taps, heads, gain), (gains_p, taps_p, heads_p, gain_p) = (
                v[l * count : (l + 1) * count] for v in (own, peer)
            )
            channels = gain.shape[0]
            taps_full = jnp.concatenate(
                [
                    tp_ordered(taps[:, :channels], taps_p[:, :channels]),
                    taps[:, channels:] + taps_p[:, channels:],
                ],
                axis=1,
            )
            done(
                l,
                (
                    jnp.where(lax.axis_index("tp") == 0, gains, gains_p),
                    taps_full[:CONV],
                    taps_full[CONV],
                    tp_ordered(heads, heads_p),
                    tp_ordered(gain, gain_p),
                ),
            )

    scatters.begin(run())


def local(
    hidden_in, lengths, norm_gains, mamba_zx, mamba_shared, conv_weight, conv_bias, head_params,
    mamba_gain, mamba_out, attn_in, attn_out, mlp_in, mlp_out, out_grad,
):
    layers = norm_gains.shape[0]
    micro, own_seqs, rows, features = hidden_in.shape
    sequences = micro * own_seqs
    full_ssm = mamba_gain.shape[1]
    heads_total = head_params.shape[2]
    ctx_place = lax.axis_index("ctx")
    place = (ctx_place % 2).astype(jnp.int32).reshape(1)
    start_row = ctx_place % 2 * rows * 2
    tables = turn_tables(start_row, 2 * rows)
    pieces = (mamba_zx, mamba_out, attn_in, attn_out, mlp_in, mlp_out)
    shards = [weight_rows(l, pieces) for l in range(layers)]
    quarters = (sequences, rows, features)
    moves = to_halves_moves(hidden_in.reshape(quarters))
    first_shards = [shards[l][i] for l in range(layers) for i in range(2)]
    came = fsdp_moves(first_shards[0])
    late_block = jnp.concatenate([shards[l][2] for l in range(layers)], axis=1)[None]
    near = spread_first(late_block)
    moved = lax.optimization_barrier(moves + came + near)
    given = to_halves(*moved[:2])
    first_block = fsdp_join(first_shards[0], moved[2:-2])
    blocks, first_block = gathered_blocks(first_shards, first_block)
    gathers = Gathers([first_block] + blocks)
    late = gathered_ctx(late_block, moved[-2:], layers)
    order = own_order(features * lax.axis_size("tp"), LOW)
    smalls = [
        local_small(
            order, l, norm_gains, mamba_shared, conv_weight, conv_bias, head_params, mamba_gain
        )
        for l in range(layers)
    ]
    length = pick(lengths.reshape(sequences), ctx_place // 2, 0)
    keep = (start_row + jnp.arange(2 * rows) < length).astype(WIDE)[:, None]
    hidden = product(tp_join(given), order)
    saved, weights = [], []
    for l in range(layers):
        if l == layers - 1:
            (cotangent,), hidden = together((out_grad.reshape(quarters),), hidden)
            moves = to_halves_moves(cotangent)
        hidden, kept, used, moves = layer_forward(
            hidden, l, gathers, late, smalls[l], tables, place, sequences, moves
        )
        saved.append(kept)
        weights.append(used)
    upstream = product(tp_join(to_halves(*moves)), order) * keep
    own_rows = own_part(order, features, 0)
    mixed_out = against_rows((hidden * keep).astype(LOW), own_rows).astype(LOW)
    mixed_out = to_quarters(mixed_out)
    big, rest = [[None] * 4 for _ in range(layers)], [None] * layers
    scatters = Scatters()
    side_total = []

    def finished(layer, part, total):
        big[layer][part] = total
        if layer == 0 and part == 1:
            sides = [big[l][1][:, -3 * LANES :] for l in range(layers)]
            settle_side(scatters, sides, heads_total // lax.axis_size("tp"), side_total.append)

    small_grads = [None] * layers
    grad_low = upstream.astype(LOW)
    extra = [mixed_out]
    for l in reversed(range(layers)):
        upstream, grad_low, small_grads[l] = layer_backward(
            upstream, grad_low, saved[l], weights[l], smalls[l], tables, place, sequences,
            scatters, l == 0, functools.partial(finished, l), extra if l == layers - 1 else [],
        )
    input_grad = dot(upstream, own_rows.astype(WIDE), 1, 1, HIGHEST)
    input_grad = to_quarters(input_grad.astype(LOW)).astype(WIDE).reshape(hidden_in.shape)
    gains = jnp.concatenate([grads[0] for grads in small_grads], axis=0)
    gains = dot(gains, order.astype(WIDE), 1, 1, HIGHEST)
    small_grads = [
        (gains[2 * l : 2 * l + 2],) + small_grads[l][1:] for l in range(layers)
    ]
    settle_small(scatters, small_grads, rest.__setitem__)
    scatters.finish()
    channels = mamba_out.shape[1]
    ff = mlp_out.shape[1]
    zx_grads, attn_grads, mix_grads, up_grads, down_grads = [], [], [], [], []
    for l in range(layers):
        early, late, mid, up = big[l]
        half = early.shape[1] // 2
        firsts, seconds = early[:, :half], early[:, half:]

        def rejoined(first, last):
            return jnp.concatenate([firsts[:, first:last], seconds[:, first:last]], axis=1)

        down_grads.append(rejoined(0, ff // 2).T)
        up_grads.append(up)
        both = rejoined(ff // 2, half)
        mix_grads.append((both[:, :channels].T, both[:, channels:].T))
        if mid is None:
            half = late.shape[1] // 2
            gate, x_part = late[:, :channels], late[:, half : half + channels]
            attn_grads.append(late[:, channels:half])
        else:
            gate, x_part = mid[:, :channels], late[:, :channels]
            keys = late[:, channels : channels + LANES]
            attn_grads.append(jnp.concatenate([mid[:, channels:], keys], axis=1))
        zx_grads.append(jnp.concatenate([gate, x_part], axis=1))

    def stacked(pick):
        return jnp.stack([pick(l) for l in range(layers)])

    return (
        extra[0].reshape(hidden_in.shape),
        input_grad,
        stacked(lambda l: rest[l][0]),
        jnp.stack(zx_grads).reshape(mamba_zx.shape),
        side_total[0],
        stacked(lambda l: rest[l][1]),
        stacked(lambda l: rest[l][2]),
        stacked(lambda l: rest[l][3]),
        stacked(lambda l: rest[l][4]),
        stacked(lambda l: mix_grads[l][0]),
        jnp.stack(attn_grads).reshape(attn_in.shape),
        stacked(lambda l: mix_grads[l][1]),
        jnp.stack(up_grads).reshape(mlp_in.shape),
        jnp.stack(down_grads),
    )


def solution(mesh):
    placed = (
        P(None, "fsdp", "ctx", "tp"),
        P(None, "fsdp"),
        P(),
        P(None, ("fsdp", "ctx"), None, "tp"),
        P(),
        P(),
        P(),
        P(),
        P(),
        P(None, "tp", ("fsdp", "ctx")),
        P(None, ("fsdp", "ctx"), "tp", None),
        P(None, "tp", ("fsdp", "ctx")),
        P(None, ("fsdp", "ctx"), None, "tp"),
        P(None, "tp", ("fsdp", "ctx")),
        P(None, "fsdp", "ctx", "tp"),
    )
    return jax.shard_map(
        local,
        mesh=mesh,
        in_specs=placed,
        out_specs=(
            P(None, "fsdp", "ctx", "tp"),
            P(None, "fsdp", "ctx", "tp"),
            P(),
            P(None, ("fsdp", "ctx"), None, "tp"),
            P(),
            P(),
            P(),
            P(),
            P(),
            P(None, "tp", ("fsdp", "ctx")),
            P(None, ("fsdp", "ctx"), "tp", None),
            P(None, "tp", ("fsdp", "ctx")),
            P(None, ("fsdp", "ctx"), None, "tp"),
            P(None, "tp", ("fsdp", "ctx")),
        ),
        check_vma=False,
    )
```

time: 1330 us -> 837 us (0.63)
  waiting for transfers between devices: 698 us -> 187 us
  Pallas kernels: 128 us -> 246 us
  other arithmetic: 120 us -> 56.5 us
  local copies, waits for them, and re-layouts: 123 us -> 92.1 us
    all_gather x8 -> x4, waiting for transfers between devices: 382 us -> 0.03 us  [the longest x2 0.02 us: layer_forward(): lax.all_gather(v, 'fsdp', axis=1).reshape(-1, v.shape[-1])]
    ppermute x92 -> x85, waiting for transfers between devices: 309 us -> 181 us  [the longest x48 82.4 us: ctx_swap(): return lax.ppermute(values, 'ctx', xor_pairs(lax.axis_size('ctx'), step))]
    pallas_call x6 -> x31, Pallas kernels: 73.9 us -> 190 us  [the longest x2 44.2 us: scan_back(): kernel_call(scan_back_body, (count,), [back_block(channels), back_block(c...]
    convert_element_type x58 -> x8, other arithmetic: 45.1 us -> 5.31 us  [the longest x3 3.17 us: fsdp_scatter(): return total.astype(WIDE)]
    add x31 -> x10, other arithmetic: 21.3 us -> 4.49 us  [the longest x2 1.99 us: added(): total = total + part.astype(WIDE)]
    squeeze x40 -> x7, local copies, waits for them, and re-layouts: 18.1 us -> 3.12 us  [pick(): return lax.dynamic_index_in_dim(values, place, dim, False)]
    ppermute x92 -> x85, starting transfers between devices: 111 us -> 103 us  [the longest x48 52.3 us: ctx_swap(): return lax.ppermute(values, 'ctx', xor_pairs(lax.axis_size('ctx'), step))]
    ppermute x14 -> x13, starting transfers between devices: 28.5 us -> 33.3 us  [tp_peer(): return lax.ppermute(x, 'tp', xor_pairs(lax.axis_size('tp'), 1))]
  transfers between devices with their start and end apart: 114 -> 107, of which waited for: 51 -> 38; matrix products, arithmetic and copies ran while one was open for 23% -> 22% of each run, Pallas kernels for 10% -> 28%
where the time goes in v2:
time: 837 us; the launch traced here: 825 us
  Pallas kernels  246 us (29%)
  waiting for transfers between devices  187 us (22%)
  starting transfers between devices  137 us (16%)
  local copies, waits for them, and re-layouts  92.1 us (11%)
  matrix products  88.4 us (11%)
  other arithmetic  56.5 us (7%)
  between operations  17.4 us (2%)
    ppermute x48, waiting for transfers between devices, ctx_swap(): return lax.ppermute(values, 'ctx', xor_pairs(lax.axis_size('ctx'), step))  82.4 us
    ppermute x48, starting transfers between devices, ctx_swap(): return lax.ppermute(values, 'ctx', xor_pairs(lax.axis_size('ctx'), step))  52.3 us
    dot_general x15, matrix products, dot(): lax.dot_general(a, b, (((ca,), (cb,)), ((), ())), preferred_element_type=...  45.4 us
    pallas_call x2, Pallas kernels, scan_back(): kernel_call(scan_back_body, (count,), [back_block(channels), back_block(c...  44.2 us
    dot_general x16, matrix products, product(): return jnp.dot(a, b, preferred_element_type=WIDE)  43 us
    pallas_call x14, Pallas kernels, once(): kernel_call(body, (1,), [whole(v.shape) for v in operands], [whole(shape)...  38.5 us
    unnamed x360, local copies, waits for them, and re-layouts  36.7 us
    ppermute x13, starting transfers between devices, tp_peer(): return lax.ppermute(x, 'tp', xor_pairs(lax.axis_size('tp'), 1))  33.3 us
  transfers between devices with their start and end apart: 107, of which 38 were waited for; matrix products, arithmetic and copies ran while one was open for 22% of the time, Pallas kernels for 28%

profile of v2, /device:TPU:1, one launch (start us, length us, event | category | flops | bytes accessed | tf_op | source)
XLA Modules:
  0.0 825.0 jit_solution(1290755987174200748)
XLA Ops:
  24.0 15.3 %collective-permute-done.3 = bf16[64,1920]{1,0:T(8,128)(2,1)} collective-permute-done((bf16[64,1920]{1,0:T(8,128)(2,1)}, bf16[64,1920]{1,0:T(8,128)(2,1)}, u32[]{:S(2)}, u32[]{:S(2)}) %collective-permute-start.3) | collective-permute-done | bytes 245792 | tf_op jit(solution)/shard_map/ppermute | solution.py:181
  39.3 3.6 collective-permute-start
  54.7 3.9 collective-permute-start.9
  72.2 12.9 %collective-permute-done.11 = bf16[4,64,1920]{2,1,0:T(8,128)(2,1)} collective-permute-done((bf16[4,64,1920]{2,1,0:T(8,128)(2,1)}, bf16[4,64,1920]{2,1,0:T(8,128)(2,1)}, u32[]{:S(2)}, u32[]{:S(2)}) %collective-permute-start.11) | collective-permute-done | bytes 983072 | tf_op jit(solution)/shard_map/ppermute | solution.py:134
  90.0 6.2 collective-permute-done.12
  98.7 6.5 fusion.86.rows_ref.zx_ref.gate_ref
  118.3 9.9 %shard_map.265 = (bf16[512,1024]{1,0:T(8,128)(2,1)}, bf16[512,768]{1,0:T(8,128)(2,1)}, bf16[512,256]{1,0:T(8,128)(2,1)}, f32[512,768]{1,0:T(8,128)}, f32[768,128...) custom-call(f32[512,1920]{1,0:T(8,128)} %fusion.86.rows_ref.zx_ref.gate, ...), custom_call_target="tpu_custom_call" | custom-call | flops 805306368 | bytes 8388608 | tf_op jit(solution)/shard_map/pallas_call | solution.py:793
  130.2 7.3 shard_map.264
  137.5 15.0 %collective-permute-done.16.parcel_ref = bf16[784,128]{1,0:T(8,128)(2,1)S(1)} collective-permute-done((bf16[784,128]{1,0:T(8,128)(2,1)}, bf16[784,128]{1,0:T(8,128)(2,1)S(1)}, u32[]{:S(2)}, u32[]{:S(2)}) %collective-permute-start.16) | collective-permute-done | bytes 200736 | tf_op jit(solution)/shard_map/ppermute | solution.py:72
  161.7 5.7 shard_map.266
  168.6 3.7 collective-permute-done.20
  174.5 3.6 pad_maximum_fusion
  181.1 5.8 collective-permute-start.21
  197.9 13.3 %collective-permute-done.23 = bf16[4,64,1920]{2,1,0:T(8,128)(2,1)S(1)} collective-permute-done((bf16[4,64,1920]{2,1,0:T(8,128)(2,1)}, bf16[4,64,1920]{2,1,0:T(8,128)(2,1)S(1)}, u32[]{:S(2)}, u32[]{:S(2)}) %collective-permute-start.23) | collective-permute-done | bytes 983072 | tf_op jit(solution)/shard_map/ppermute | solution.py:134
  221.6 8.3 %collective-permute-done.25 = bf16[4,64,896]{2,1,0:T(8,128)(2,1)S(1)} collective-permute-done((bf16[4,64,896]{2,1,0:T(8,128)(2,1)S(1)}, bf16[4,64,896]{2,1,0:T(8,128)(2,1)S(1)}, u32[]{:S(2)}, u32[]{:S(2)}) %collective-permute-start.25) | collective-permute-done | bytes 458784 | tf_op jit(solution)/shard_map/ppermute | solution.py:134
  234.8 3.9 fusion.85.rows_ref.zx_ref.gate_ref
  254.6 9.9 %shard_map.269 = (bf16[512,1024]{1,0:T(8,128)(2,1)}, bf16[512,768]{1,0:T(8,128)(2,1)}, bf16[512,256]{1,0:T(8,128)(2,1)}, f32[512,768]{1,0:T(8,128)}, f32[768,128...) custom-call(f32[512,1920]{1,0:T(8,128)} %fusion.85.rows_ref.zx_ref.gate, ...), custom_call_target="tpu_custom_call" | custom-call | flops 805306368 | bytes 8388608 | tf_op jit(solution)/shard_map/pallas_call | solution.py:793
  264.6 4.5 collective-permute-start.31
  269.1 7.3 shard_map.268
  276.4 14.3 %collective-permute-done.30 = bf16[256,512]{1,0:T(8,128)(2,1)S(1)} collective-permute-done((bf16[256,512]{1,0:T(8,128)(2,1)S(1)}, bf16[256,512]{1,0:T(8,128)(2,1)S(1)}, u32[]{:S(2)}, u32[]{:S(2)}) %collective-permute-start.30) | collective-permute-done | bytes 262176 | tf_op jit(solution)/shard_map/ppermute | solution.py:82
  292.5 6.8 collective-permute-start.35
  299.3 3.6 collective-permute-start.34
  303.6 5.7 shard_map.270
  312.6 5.0 collective-permute-done.34
  322.9 4.0 collective-permute-start.36
  330.3 4.4 fusion.191
  344.2 8.8 %shard_map.271 = bf16[4,4,64,2048]{3,2,1,0:T(8,128)(2,1)} custom-call(bf16[512,1024]{1,0:T(8,128)(2,1)} %copy-done.63, bf16[512,2048]{1,0:T(8,128)(2,1)} %pad_maximum_fusion.4.right_ref), custom_call_target="tpu_custom_call" | custom-call | flops 2147483648 | bytes 6291456 | tf_op jit(solution)/shard_map/pallas_call | solution.py:319
  354.6 4.6 fusion.47.own_ref
  362.9 5.8 shard_map.272
  368.7 7.0 shard_map.273
  377.5 3.6 fusion.36.dn_ref
  381.1 8.1 shard_map.274
  392.9 10.6 %shard_map.275 = (bf16[512,256]{1,0:T(8,128)(2,1)}, f32[512,128]{1,0:T(8,128)}, bf16[512,128]{1,0:T(8,128)(2,1)}) custom-call(s32[1]{0:T(128)} %bitcast.10.place_ref, bf16[512,256]{1,0:T(8,128)(2,1)} %get-tuple-element.290.q_ref, bf16[512,256]{1,0:T(8,128)(2,1)} %convolution_convert_fusion.3.grad_ref, f32[512,128]{1,0:T(8,128)} %get-tuple-element.323.total_ref, ...), custom_call_target="tpu_custom_call" | custom-call | flops 2684354560 | bytes 2097152 | tf_op jit(solution)/shard_map/pallas_call | solution.py:643
  405.1 5.2 collective-permute-done.43.refs_0_
  422.7 22.2 %shard_map.278 = (f32[512,1024]{1,0:T(8,128)}, f32[8,1024]{1,0:T(8,128)}, bf16[512,128]{1,0:T(8,128)(2,1)}, f32[2,8,1024]{2,1,0:T(8,128)}, f32[2,8,128]{2,1,0:T(8,128)}) custom-call(f32[512,768]{1,0:T(8,128)} %get-tuple-element.330.du_ref, bf16[512,768]{1,0:T(8,128)(2,1)} %get-tuple-element.303.x_ref, bf16[512,256]{1,0:T(8,128)(2,1)} %get-tuple-element.302.bc_ref, ...), custom_call_target="tpu_custom_call" | custom-call | flops 2013265920 | bytes 12582912 | tf_op jit(solution)/shard_map/pallas_call | solution.py:1129
  447.2 3.6 shard_map.279
  459.0 7.7 shard_map.280
  466.7 5.3 add_convert_fusion.2.own_ref
  477.5 3.9 collective-permute-start.39
  481.4 5.5 collective-permute-done.39
  487.8 5.9 shard_map.281
  498.3 8.4 %shard_map.282 = bf16[4,4,64,2048]{3,2,1,0:T(8,128)(2,1)} custom-call(bf16[512,1024]{1,0:T(8,128)(2,1)} %copy-done.60, bf16[512,2048]{1,0:T(8,128)(2,1)} %pad_maximum_fusion.5.right_ref), custom_call_target="tpu_custom_call" | custom-call | flops 2147483648 | bytes 6291456 | tf_op jit(solution)/shard_map/pallas_call | solution.py:319
  512.6 6.9 fusion.44.own_ref
  525.2 15.3 %collective-permute-done.52.from_x_ref = bf16[128,1024]{1,0:T(8,128)(2,1)S(1)} collective-permute-done((bf16[128,1024]{1,0:T(8,128)(2,1)S(1)}, bf16[128,1024]{1,0:T(8,128)(2,1)S(1)}, u32[]{:S(2)}, u32[]{:S(2)}) %collective-permute-start.52) | collective-permute-done | bytes 262176 | tf_op jit(solution)/shard_map/ppermute | solution.py:134
  551.4 5.7 shard_map.285
  557.2 4.6 collective-permute-done.73.last_x_ref
  562.7 3.8 shard_map.296
  566.6 7.1 shard_map.286
  577.0 10.6 %shard_map.288 = (bf16[512,256]{1,0:T(8,128)(2,1)}, f32[512,128]{1,0:T(8,128)}, bf16[512,128]{1,0:T(8,128)(2,1)}) custom-call(s32[1]{0:T(128)} %bitcast.10.place_ref, bf16[512,256]{1,0:T(8,128)(2,1)} %get-tuple-element.258.q_ref, bf16[512,256]{1,0:T(8,128)(2,1)} %convolution_convert_fusion.2.grad_ref, f32[512,128]{1,0:T(8,128)} %get-tuple-element.382.total_ref, ...), custom_call_target="tpu_custom_call" | custom-call | flops 2684354560 | bytes 2097152 | tf_op jit(solution)/shard_map/pallas_call | solution.py:643
  589.1 3.5 fusion.34.dn_ref
  592.6 8.2 shard_map.287
  603.5 4.4 collective-permute-done.57.later_ref
  610.2 4.3 shard_map.290
  630.0 22.1 %shard_map.291 = (f32[512,1024]{1,0:T(8,128)}, f32[8,1024]{1,0:T(8,128)}, bf16[512,128]{1,0:T(8,128)(2,1)}, f32[2,8,1024]{2,1,0:T(8,128)}, f32[2,8,128]{2,1,0:T(8,128)}) custom-call(f32[512,768]{1,0:T(8,128)} %get-tuple-element.394.du_ref, bf16[512,768]{1,0:T(8,128)(2,1)} %get-tuple-element.270.x_ref, bf16[512,256]{1,0:T(8,128)(2,1)} %get-tuple-element.269.bc_ref, ...), custom_call_target="tpu_custom_call" | custom-call | flops 2013265920 | bytes 12582912 | tf_op jit(solution)/shard_map/pallas_call | solution.py:1129
  655.3 3.6 shard_map.292
  670.7 4.7 shard_map.295
  675.4 5.1 add_convert_fusion.own_ref
  680.5 7.0 collective-permute-start.70
  692.7 5.7 shard_map.297
  711.0 5.6 collective-permute-done.63.from_y_ref
  746.6 7.3 collective-permute-done.80
  768.4 8.5 %collective-permute-done.86 = bf16[64,1280]{1,0:T(8,128)(2,1)S(1)} collective-permute-done((bf16[64,1280]{1,0:T(8,128)(2,1)S(1)}, bf16[64,1280]{1,0:T(8,128)(2,1)S(1)}, u32[]{:S(2)}, u32[]{:S(2)}) %collective-permute-start.86) | collective-permute-done | bytes 163872 | tf_op jit(solution)/shard_map/ppermute | solution.py:380
  799.1 5.4 collective-permute-done.96
  804.5 4.7 collective-permute-start.97
  (841 shorter events, 346.8 us)
Async XLA Ops:
  7.2 108.0 %all-gather.9.cloned.1.call-start = ((), (), s32[]{:S(2)}) async-start(), calls=%async_computation.10 | async-start | bytes 1966080 | tf_op jit(solution)/shard_map/all_gather | solution.py:197
  9.1 35.8 %collective-permute-start.6 = (bf16[1,64,2048]{2,1,0:T(8,128)(2,1)}, bf16[1,64,2048]{2,1,0:T(8,128)(2,1)S(1)}, u32[]{:S(2)}, u32[]{:S(2)}) collective-permute-start(bf16[1,64,2048]{2,1,0:T(8,128)(2,1)} %maximum_bitcast_fusion), channel_id=1, source_target_pairs={{0,4},{2,6},{4,0},{6,2},{1,5},{3,7},{5,1},{7,3},{8,12},{10,14},{12... | collective-permute-start | bytes 786440 | tf_op jit(solution)/shard_map/ppermute | solution.py:134
  11.1 33.7 %collective-permute-start.5 = (bf16[1,64,2048]{2,1,0:T(8,128)(2,1)}, bf16[1,64,2048]{2,1,0:T(8,128)(2,1)S(1)}, u32[]{:S(2)}, u32[]{:S(2)}) collective-permute-start(bf16[1,64,2048]{2,1,0:T(8,128)(2,1)} %maximum_bitcast_fusion), channel_id=1, source_target_pairs={{0,2},{2,0},{4,6},{6,4},{1,3},{3,1},{5,7},{7,5},{8,10},{10,8},{12,... | collective-permute-start | bytes 786440 | tf_op jit(solution)/shard_map/ppermute | solution.py:134
  18.5 20.8 %collective-permute-start.3 = (bf16[64,1920]{1,0:T(8,128)(2,1)}, bf16[64,1920]{1,0:T(8,128)(2,1)}, u32[]{:S(2)}, u32[]{:S(2)}) collective-permute-start(bf16[64,1920]{1,0:T(8,128)(2,1)} %pad_maximum_fusion.25), channel_id=1, source_target_pairs={{0,16},{8,24},{16,0},{24,8},{1,17},{9,25},{17,1},{25,9},{2,18},{10... | collective-permute-start | bytes 737288 | tf_op jit(solution)/shard_map/ppermute | solution.py:181
  18.5 26.3 %collective-permute-start.2 = (bf16[64,1920]{1,0:T(8,128)(2,1)}, bf16[64,1920]{1,0:T(8,128)(2,1)}, u32[]{:S(2)}, u32[]{:S(2)}) collective-permute-start(bf16[64,1920]{1,0:T(8,128)(2,1)} %pad_maximum_fusion.25), channel_id=1, source_target_pairs={{0,8},{8,0},{16,24},{24,16},{1,9},{9,1},{17,25},{25,17},{2,10},{10... | collective-permute-start | bytes 737288 | tf_op jit(solution)/shard_map/ppermute | solution.py:181
  23.8 21.2 %collective-permute-start.1 = (bf16[256,512]{1,0:T(8,128)(2,1)}, bf16[256,512]{1,0:T(8,128)(2,1)S(1)}, u32[]{:S(2)}, u32[]{:S(2)}) collective-permute-start(bf16[256,512]{1,0:T(8,128)(2,1)} %get-tuple-element.615), channel_id=1, source_target_pairs={{2,0},{6,2},{0,4},{4,6},{3,1},{7,3},{1,5},{5,7},{10,8},{14,10},{8,... | collective-permute-start | bytes 786440 | tf_op jit(solution)/shard_map/ppermute | solution.py:82
  50.2 109.2 %all-gather.11.cloned.1.call-start = ((), (), s32[]{:S(2)}) async-start(), calls=%async_computation.11 | async-start | bytes 3194880 | tf_op jit(solution)/shard_map/all_gather | solution.py:198
  61.4 23.8 %collective-permute-start.11 = (bf16[4,64,1920]{2,1,0:T(8,128)(2,1)}, bf16[4,64,1920]{2,1,0:T(8,128)(2,1)}, u32[]{:S(2)}, u32[]{:S(2)}) collective-permute-start(bf16[4,64,1920]{2,1,0:T(8,128)(2,1)} %bitcast_dynamic-update-slice_fusion), channel_id=1, source_target_pairs={{0,4},{2,6},{4,0},{6,2},{1,5},{3,7},{5,1},{7,3},{8,12},{10,14},{12... | collective-permute-start | bytes 2949128 | tf_op jit(solution)/shard_map/ppermute | solution.py:134
  62.8 22.3 %collective-permute-start.10 = (bf16[4,64,1920]{2,1,0:T(8,128)(2,1)}, bf16[4,64,1920]{2,1,0:T(8,128)(2,1)}, u32[]{:S(2)}, u32[]{:S(2)}) collective-permute-start(bf16[4,64,1920]{2,1,0:T(8,128)(2,1)} %bitcast_dynamic-update-slice_fusion), channel_id=1, source_target_pairs={{0,2},{2,0},{4,6},{6,4},{1,3},{3,1},{5,7},{7,5},{8,10},{10,8},{12,... | collective-permute-start | bytes 2949128 | tf_op jit(solution)/shard_map/ppermute | solution.py:134
  67.4 145.7 %all-gather.13.cloned.1.call-start = ((), (), s32[]{:S(2)}) async-start(), calls=%async_computation.12 | async-start | bytes 2621440 | tf_op jit(solution)/shard_map/all_gather | solution.py:1298
  115.2 37.3 %collective-permute-start.18 = (bf16[4,64,3072]{2,1,0:T(8,128)(2,1)}, bf16[4,64,3072]{2,1,0:T(8,128)(2,1)}, u32[]{:S(2)}, u32[]{:S(2)}) collective-permute-start(bf16[4,64,3072]{2,1,0:T(8,128)(2,1)} %bitcast.317), channel_id=1, source_target_pairs={{0,4},{2,6},{4,0},{6,2},{1,5},{3,7},{5,1},{7,3},{8,12},{10,14},{12... | collective-permute-start | bytes 4718600 | tf_op jit(solution)/shard_map/ppermute | solution.py:134
  115.4 37.8 %collective-permute-start.17 = (bf16[4,64,3072]{2,1,0:T(8,128)(2,1)}, bf16[4,64,3072]{2,1,0:T(8,128)(2,1)}, u32[]{:S(2)}, u32[]{:S(2)}) collective-permute-start(bf16[4,64,3072]{2,1,0:T(8,128)(2,1)} %bitcast.318), channel_id=1, source_target_pairs={{0,2},{2,0},{4,6},{6,4},{1,3},{3,1},{5,7},{7,5},{8,10},{10,8},{12,... | collective-permute-start | bytes 4718600 | tf_op jit(solution)/shard_map/ppermute | solution.py:134
  128.2 24.3 %collective-permute-start.16 = (bf16[784,128]{1,0:T(8,128)(2,1)}, bf16[784,128]{1,0:T(8,128)(2,1)S(1)}, u32[]{:S(2)}, u32[]{:S(2)}) collective-permute-start(bf16[784,128]{1,0:T(8,128)(2,1)} %get-tuple-element.265), channel_id=1, source_target_pairs={{0,2},{4,6},{1,3},{5,7},{8,10},{12,14},{9,11},{13,15},{16,18},{20,... | collective-permute-start | bytes 602120 | tf_op jit(solution)/shard_map/ppermute | solution.py:72
  130.2 108.5 %all-gather.15.cloned.1.call-start = ((), (), s32[]{:S(2)}) async-start(), calls=%async_computation.13 | async-start | bytes 2621440 | tf_op jit(solution)/shard_map/all_gather | solution.py:1298
  156.5 15.8 %collective-permute-start.20 = (bf16[4,64,1536]{2,1,0:T(8,128)(2,1)}, bf16[4,64,1536]{2,1,0:T(8,128)(2,1)}, u32[]{:S(2)}, u32[]{:S(2)}) collective-permute-start(bf16[4,64,1536]{2,1,0:T(8,128)(2,1)} %slice.558), channel_id=1, source_target_pairs={{0,2},{2,0},{4,6},{6,4},{1,3},{3,1},{5,7},{7,5},{8,10},{10,8},{12,... | collective-permute-start | bytes 2359304 | tf_op jit(solution)/shard_map/ppermute | solution.py:134
  158.7 14.3 %collective-permute-start.19 = (bf16[4,64,1536]{2,1,0:T(8,128)(2,1)S(1)}, bf16[4,64,1536]{2,1,0:T(8,128)(2,1)}, u32[]{:S(2)}, u32[]{:S(2)}) collective-permute-start(bf16[4,64,1536]{2,1,0:T(8,128)(2,1)S(1)} %slice.557), channel_id=1, source_target_pairs={{0,4},{2,6},{4,0},{6,2},{1,5},{3,7},{5,1},{7,3},{8,12},{10,14},{12... | collective-permute-start | bytes 2359304 | tf_op jit(solution)/shard_map/ppermute | solution.py:134
  187.0 257.9 %reduce-scatter.6.cloned.1.call-start = ((), (), s32[]{:S(2)}) async-start(), calls=%async_computation.5 | async-start | bytes 5242880 | tf_op jit(solution)/shard_map/reduce_scatter | solution.py:409
  187.4 23.8 %collective-permute-start.23 = (bf16[4,64,1920]{2,1,0:T(8,128)(2,1)}, bf16[4,64,1920]{2,1,0:T(8,128)(2,1)S(1)}, u32[]{:S(2)}, u32[]{:S(2)}) collective-permute-start(bf16[4,64,1920]{2,1,0:T(8,128)(2,1)} %slice.692), channel_id=1, source_target_pairs={{0,4},{2,6},{4,0},{6,2},{1,5},{3,7},{5,1},{7,3},{8,12},{10,14},{12... | collective-permute-start | bytes 2949128 | tf_op jit(solution)/shard_map/ppermute | solution.py:134
  187.5 23.7 %collective-permute-start.22 = (bf16[4,64,1920]{2,1,0:T(8,128)(2,1)}, bf16[4,64,1920]{2,1,0:T(8,128)(2,1)S(1)}, u32[]{:S(2)}, u32[]{:S(2)}) collective-permute-start(bf16[4,64,1920]{2,1,0:T(8,128)(2,1)} %slice.692), channel_id=1, source_target_pairs={{0,2},{2,0},{4,6},{6,4},{1,3},{3,1},{5,7},{7,5},{8,10},{10,8},{12,... | collective-permute-start | bytes 2949128 | tf_op jit(solution)/shard_map/ppermute | solution.py:134
  216.0 15.4 %collective-permute-start.24 = (bf16[512,1024]{1,0:T(8,128)(2,1)S(1)}, bf16[512,1024]{1,0:T(8,128)(2,1)S(1)}, u32[]{:S(2)}, u32[]{:S(2)}) collective-permute-start(bf16[512,1024]{1,0:T(8,128)(2,1)S(1)} %convolution_convert_fusion.1), channel_id=1, source_target_pairs={{0,1},{1,0},{2,3},{3,2},{4,5},{5,4},{6,7},{7,6},{8,9},{9,8},{10,11... | collective-permute-start | bytes 3145736 | tf_op jit(solution)/shard_map/ppermute | solution.py:101
  217.6 13.6 %collective-permute-start.26 = (bf16[4,64,1024]{2,1,0:T(8,128)(2,1)S(1)}, bf16[4,64,1024]{2,1,0:T(8,128)(2,1)S(1)}, u32[]{:S(2)}, u32[]{:S(2)}) collective-permute-start(bf16[4,64,1024]{2,1,0:T(8,128)(2,1)S(1)} %slice.565), channel_id=1, source_target_pairs={{0,2},{2,0},{4,6},{6,4},{1,3},{3,1},{5,7},{7,5},{8,10},{10,8},{12,... | collective-permute-start | bytes 1572872 | tf_op jit(solution)/shard_map/ppermute | solution.py:134
  248.9 41.9 %collective-permute-start.33 = (bf16[4,64,3072]{2,1,0:T(8,128)(2,1)S(1)}, bf16[4,64,3072]{2,1,0:T(8,128)(2,1)S(1)}, u32[]{:S(2)}, u32[]{:S(2)}) collective-permute-start(bf16[4,64,3072]{2,1,0:T(8,128)(2,1)S(1)} %slice.703), channel_id=1, source_target_pairs={{0,4},{2,6},{4,0},{6,2},{1,5},{3,7},{5,1},{7,3},{8,12},{10,14},{12... | collective-permute-start | bytes 4718600 | tf_op jit(solution)/shard_map/ppermute | solution.py:134
  250.0 41.4 %collective-permute-start.32 = (bf16[4,64,3072]{2,1,0:T(8,128)(2,1)S(1)}, bf16[4,64,3072]{2,1,0:T(8,128)(2,1)S(1)}, u32[]{:S(2)}, u32[]{:S(2)}) collective-permute-start(bf16[4,64,3072]{2,1,0:T(8,128)(2,1)S(1)} %slice.703), channel_id=1, source_target_pairs={{0,2},{2,0},{4,6},{6,4},{1,3},{3,1},{5,7},{7,5},{8,10},{10,8},{12,... | collective-permute-start | bytes 4718600 | tf_op jit(solution)/shard_map/ppermute | solution.py:134
  253.6 37.1 %collective-permute-start.30 = (bf16[256,512]{1,0:T(8,128)(2,1)S(1)}, bf16[256,512]{1,0:T(8,128)(2,1)S(1)}, u32[]{:S(2)}, u32[]{:S(2)}) collective-permute-start(bf16[256,512]{1,0:T(8,128)(2,1)S(1)} %get-tuple-element.611), channel_id=1, source_target_pairs={{2,0},{6,2},{0,4},{4,6},{3,1},{7,3},{1,5},{5,7},{10,8},{14,10},{8,... | collective-permute-start | bytes 786440 | tf_op jit(solution)/shard_map/ppermute | solution.py:82
  254.0 36.7 %collective-permute-start.29 = (bf16[256,512]{1,0:T(8,128)(2,1)S(1)}, bf16[256,512]{1,0:T(8,128)(2,1)S(1)}, u32[]{:S(2)}, u32[]{:S(2)}) collective-permute-start(bf16[256,512]{1,0:T(8,128)(2,1)S(1)} %get-tuple-element.612), channel_id=1, source_target_pairs={{0,0},{4,2},{2,4},{6,6},{1,1},{5,3},{3,5},{7,7},{8,8},{12,10},{10,... | collective-permute-start | bytes 786440 | tf_op jit(solution)/shard_map/ppermute | solution.py:81
  264.6 26.1 %collective-permute-start.31 = (bf16[784,128]{1,0:T(8,128)(2,1)}, bf16[784,128]{1,0:T(8,128)(2,1)S(1)}, u32[]{:S(2)}, u32[]{:S(2)}) collective-permute-start(bf16[784,128]{1,0:T(8,128)(2,1)} %get-tuple-element.297), channel_id=1, source_target_pairs={{0,2},{4,6},{1,3},{5,7},{8,10},{12,14},{9,11},{13,15},{16,18},{20,... | collective-permute-start | bytes 602120 | tf_op jit(solution)/shard_map/ppermute | solution.py:72
  292.5 20.0 %collective-permute-start.35 = (bf16[4,64,1536]{2,1,0:T(8,128)(2,1)}, bf16[4,64,1536]{2,1,0:T(8,128)(2,1)}, u32[]{:S(2)}, u32[]{:S(2)}) collective-permute-start(bf16[4,64,1536]{2,1,0:T(8,128)(2,1)} %slice.581), channel_id=1, source_target_pairs={{0,2},{2,0},{4,6},{6,4},{1,3},{3,1},{5,7},{7,5},{8,10},{10,8},{12,... | collective-permute-start | bytes 2359304 | tf_op jit(solution)/shard_map/ppermute | solution.py:134
  299.3 18.2 %collective-permute-start.34 = (bf16[4,64,1536]{2,1,0:T(8,128)(2,1)S(1)}, bf16[4,64,1536]{2,1,0:T(8,128)(2,1)}, u32[]{:S(2)}, u32[]{:S(2)}) collective-permute-start(bf16[4,64,1536]{2,1,0:T(8,128)(2,1)S(1)} %slice.580), channel_id=1, source_target_pairs={{0,4},{2,6},{4,0},{6,2},{1,5},{3,7},{5,1},{7,3},{8,12},{10,14},{12... | collective-permute-start | bytes 2359304 | tf_op jit(solution)/shard_map/ppermute | solution.py:134
  353.1 197.3 %reduce-scatter.14.cloned.1.call-start = ((), (), s32[]{:S(2)}) async-start(), calls=%async_computation.9 | async-start | bytes 1310720 | tf_op jit(solution)/shard_map/reduce_scatter | solution.py:372
  375.7 34.5 %collective-permute-start.45 = (bf16[512,1024]{1,0:T(8,128)(2,1)}, bf16[512,1024]{1,0:T(8,128)(2,1)S(1)}, u32[]{:S(2)}, u32[]{:S(2)}) collective-permute-start(bf16[512,1024]{1,0:T(8,128)(2,1)} %get-tuple-element.337), channel_id=1, source_target_pairs={{0,2},{2,0},{4,6},{6,4},{1,3},{3,1},{5,7},{7,5},{8,10},{10,8},{12,... | collective-permute-start | bytes 3145736 | tf_op jit(solution)/shard_map/ppermute | solution.py:134
  375.8 34.5 %collective-permute-start.44 = (bf16[512,1024]{1,0:T(8,128)(2,1)}, bf16[512,1024]{1,0:T(8,128)(2,1)}, u32[]{:S(2)}, u32[]{:S(2)}) collective-permute-start(bf16[512,1024]{1,0:T(8,128)(2,1)} %get-tuple-element.319), channel_id=1, source_target_pairs={{0,4},{2,6},{4,0},{6,2},{1,5},{3,7},{5,1},{7,3},{8,12},{10,14},{12... | collective-permute-start | bytes 3145736 | tf_op jit(solution)/shard_map/ppermute | solution.py:134
  389.2 21.0 %collective-permute-start.42 = (bf16[784,128]{1,0:T(8,128)(2,1)}, bf16[784,128]{1,0:T(8,128)(2,1)S(1)}, u32[]{:S(2)}, u32[]{:S(2)}) collective-permute-start(bf16[784,128]{1,0:T(8,128)(2,1)} %get-tuple-element.322), channel_id=1, source_target_pairs={{2,0},{6,4},{3,1},{7,5},{10,8},{14,12},{11,9},{15,13},{18,16},{22,... | collective-permute-start | bytes 602120 | tf_op jit(solution)/shard_map/ppermute | solution.py:72
  414.3 30.6 %collective-permute-start.46 = (bf16[256,1024]{1,0:T(8,128)(2,1)}, bf16[256,1024]{1,0:T(8,128)(2,1)S(1)}, u32[]{:S(2)}, u32[]{:S(2)}) collective-permute-start(bf16[256,1024]{1,0:T(8,128)(2,1)} %get-tuple-element.341), channel_id=1, source_target_pairs={{0,2},{2,0},{4,6},{6,4},{1,3},{3,1},{5,7},{7,5},{8,10},{10,8},{12,... | collective-permute-start | bytes 1572872 | tf_op jit(solution)/shard_map/ppermute | solution.py:134
  414.3 30.6 %collective-permute-start.47 = (bf16[256,1024]{1,0:T(8,128)(2,1)}, bf16[256,1024]{1,0:T(8,128)(2,1)S(1)}, u32[]{:S(2)}, u32[]{:S(2)}) collective-permute-start(bf16[256,1024]{1,0:T(8,128)(2,1)} %get-tuple-element.342), channel_id=1, source_target_pairs={{0,4},{2,6},{4,0},{6,2},{1,5},{3,7},{5,1},{7,3},{8,12},{10,14},{12... | collective-permute-start | bytes 1572872 | tf_op jit(solution)/shard_map/ppermute | solution.py:134
  416.7 57.3 %collective-permute-start.37 = (bf16[512,1024]{1,0:T(8,128)(2,1)}, bf16[512,1024]{1,0:T(8,128)(2,1)}, u32[]{:S(2)}, u32[]{:S(2)}) collective-permute-start(bf16[512,1024]{1,0:T(8,128)(2,1)} %convolution_convert_fusion), channel_id=1, source_target_pairs={{0,1},{1,0},{2,3},{3,2},{4,5},{5,4},{6,7},{7,6},{8,9},{9,8},{10,11... | collective-permute-start | bytes 3145736 | tf_op jit(solution)/shard_map/ppermute | solution.py:101
  452.9 201.5 %reduce-scatter.8.cloned.1.call-start = ((), (), s32[]{:S(2)}) async-start(), calls=%async_computation.6 | async-start | bytes 5242880 | tf_op jit(solution)/shard_map/reduce_scatter | solution.py:409
  472.1 15.7 %collective-permute-start.49 = (bf16[512,1024]{1,0:T(8,128)(2,1)}, bf16[512,1024]{1,0:T(8,128)(2,1)}, u32[]{:S(2)}, u32[]{:S(2)}) collective-permute-start(bf16[512,1024]{1,0:T(8,128)(2,1)} %add_convert_fusion.2.own_ref), channel_id=1, source_target_pairs={{0,1},{1,0},{2,3},{3,2},{4,5},{5,4},{6,7},{7,6},{8,9},{9,8},{10,11... | collective-permute-start | bytes 3145736 | tf_op jit(solution)/shard_map/ppermute | solution.py:101
  506.8 157.0 %reduce-scatter.12.cloned.1.call-start = ((), (), s32[]{:S(2)}) async-start(), calls=%async_computation.8 | async-start | bytes 1474560 | tf_op jit(solution)/shard_map/reduce_scatter | solution.py:372
  507.2 34.2 %collective-permute-start.54 = (bf16[512,1152]{1,0:T(8,128)(2,1)}, bf16[512,1152]{1,0:T(8,128)(2,1)S(1)}, u32[]{:S(2)}, u32[]{:S(2)}) collective-permute-start(bf16[512,1152]{1,0:T(8,128)(2,1)} %get-tuple-element.360), channel_id=1, source_target_pairs={{0,2},{2,0},{4,6},{6,4},{1,3},{3,1},{5,7},{7,5},{8,10},{10,8},{12,... | collective-permute-start | bytes 3538952 | tf_op jit(solution)/shard_map/ppermute | solution.py:134
  509.4 32.0 %collective-permute-start.53 = (bf16[512,1152]{1,0:T(8,128)(2,1)}, bf16[512,1152]{1,0:T(8,128)(2,1)S(1)}, u32[]{:S(2)}, u32[]{:S(2)}) collective-permute-start(bf16[512,1152]{1,0:T(8,128)(2,1)} %get-tuple-element.355), channel_id=1, source_target_pairs={{0,4},{2,6},{4,0},{6,2},{1,5},{3,7},{5,1},{7,3},{8,12},{10,14},{12... | collective-permute-start | bytes 3538952 | tf_op jit(solution)/shard_map/ppermute | solution.py:134
  511.3 29.2 %collective-permute-start.52 = (bf16[128,1024]{1,0:T(8,128)(2,1)S(1)}, bf16[128,1024]{1,0:T(8,128)(2,1)S(1)}, u32[]{:S(2)}, u32[]{:S(2)}) collective-permute-start(bf16[128,1024]{1,0:T(8,128)(2,1)S(1)} %copy-done.107), channel_id=1, source_target_pairs={{0,2},{2,0},{4,6},{6,4},{1,3},{3,1},{5,7},{7,5},{8,10},{10,8},{12,... | collective-permute-start | bytes 786440 | tf_op jit(solution)/shard_map/ppermute | solution.py:134
  512.5 28.9 %collective-permute-start.51 = (bf16[128,1024]{1,0:T(8,128)(2,1)S(1)}, bf16[128,1024]{1,0:T(8,128)(2,1)S(1)}, u32[]{:S(2)}, u32[]{:S(2)}) collective-permute-start(bf16[128,1024]{1,0:T(8,128)(2,1)S(1)} %copy-done.106), channel_id=1, source_target_pairs={{0,4},{2,6},{4,0},{6,2},{1,5},{3,7},{5,1},{7,3},{8,12},{10,14},{12... | collective-permute-start | bytes 786440 | tf_op jit(solution)/shard_map/ppermute | solution.py:134
  519.6 31.8 %collective-permute-start.50 = (bf16[512,1024]{1,0:T(8,128)(2,1)}, bf16[512,1024]{1,0:T(8,128)(2,1)}, u32[]{:S(2)}, u32[]{:S(2)}) collective-permute-start(bf16[512,1024]{1,0:T(8,128)(2,1)} %fusion.44.own_ref), channel_id=1, source_target_pairs={{0,1},{1,0},{2,3},{3,2},{4,5},{5,4},{6,7},{7,6},{8,9},{9,8},{10,11... | collective-permute-start | bytes 3145736 | tf_op jit(solution)/shard_map/ppermute | solution.py:101
  566.5 150.1 %reduce-scatter.10.cloned.1.call-start = ((), (), s32[]{:S(2)}) async-start(), calls=%async_computation.7 | async-start | bytes 1310720 | tf_op jit(solution)/shard_map/reduce_scatter | solution.py:372
  573.8 42.3 %collective-permute-start.55 = (bf16[512,1024]{1,0:T(8,128)(2,1)}, bf16[512,1024]{1,0:T(8,128)(2,1)S(1)}, u32[]{:S(2)}, u32[]{:S(2)}) collective-permute-start(bf16[512,1024]{1,0:T(8,128)(2,1)} %get-tuple-element.377), channel_id=1, source_target_pairs={{0,4},{2,6},{4,0},{6,2},{1,5},{3,7},{5,1},{7,3},{8,12},{10,14},{12... | collective-permute-start | bytes 3145736 | tf_op jit(solution)/shard_map/ppermute | solution.py:134
  574.4 41.7 %collective-permute-start.56 = (bf16[512,1024]{1,0:T(8,128)(2,1)}, bf16[512,1024]{1,0:T(8,128)(2,1)S(1)}, u32[]{:S(2)}, u32[]{:S(2)}) collective-permute-start(bf16[512,1024]{1,0:T(8,128)(2,1)} %get-tuple-element.378), channel_id=1, source_target_pairs={{0,2},{2,0},{4,6},{6,4},{1,3},{3,1},{5,7},{7,5},{8,10},{10,8},{12,... | collective-permute-start | bytes 3145736 | tf_op jit(solution)/shard_map/ppermute | solution.py:134
  587.6 15.9 %collective-permute-start.58 = (bf16[512,128]{1,0:T(8,128)(2,1)}, bf16[512,128]{1,0:T(8,128)(2,1)S(1)}, u32[]{:S(2)}, u32[]{:S(2)}) collective-permute-start(bf16[512,128]{1,0:T(8,128)(2,1)} %get-tuple-element.383), channel_id=1, source_target_pairs={{2,0},{6,4},{3,1},{7,5},{10,8},{14,12},{11,9},{15,13},{18,16},{22,... | collective-permute-start | bytes 393224 | tf_op jit(solution)/shard_map/ppermute | solution.py:72
  614.5 39.7 %collective-permute-start.62 = (bf16[512,512]{1,0:T(8,128)(2,1)}, bf16[512,512]{1,0:T(8,128)(2,1)S(1)}, u32[]{:S(2)}, u32[]{:S(2)}) collective-permute-start(bf16[512,512]{1,0:T(8,128)(2,1)} %get-tuple-element.393), channel_id=1, source_target_pairs={{0,2},{2,0},{4,6},{6,4},{1,3},{3,1},{5,7},{7,5},{8,10},{10,8},{12,... | collective-permute-start | bytes 1572872 | tf_op jit(solution)/shard_map/ppermute | solution.py:134
  614.6 39.7 %collective-permute-start.61 = (bf16[512,512]{1,0:T(8,128)(2,1)}, bf16[512,512]{1,0:T(8,128)(2,1)S(1)}, u32[]{:S(2)}, u32[]{:S(2)}) collective-permute-start(bf16[512,512]{1,0:T(8,128)(2,1)} %get-tuple-element.392), channel_id=1, source_target_pairs={{0,4},{2,6},{4,0},{6,2},{1,5},{3,7},{5,1},{7,3},{8,12},{10,14},{12... | collective-permute-start | bytes 1572872 | tf_op jit(solution)/shard_map/ppermute | solution.py:134
  620.4 33.9 %collective-permute-start.59 = (bf16[256,1024]{1,0:T(8,128)(2,1)}, bf16[256,1024]{1,0:T(8,128)(2,1)S(1)}, u32[]{:S(2)}, u32[]{:S(2)}) collective-permute-start(bf16[256,1024]{1,0:T(8,128)(2,1)} %get-tuple-element.388), channel_id=1, source_target_pairs={{0,2},{2,0},{4,6},{6,4},{1,3},{3,1},{5,7},{7,5},{8,10},{10,8},{12,... | collective-permute-start | bytes 1572872 | tf_op jit(solution)/shard_map/ppermute | solution.py:134
  621.8 32.5 %collective-permute-start.60 = (bf16[256,1024]{1,0:T(8,128)(2,1)}, bf16[256,1024]{1,0:T(8,128)(2,1)S(1)}, u32[]{:S(2)}, u32[]{:S(2)}) collective-permute-start(bf16[256,1024]{1,0:T(8,128)(2,1)} %get-tuple-element.389), channel_id=1, source_target_pairs={{0,4},{2,6},{4,0},{6,2},{1,5},{3,7},{5,1},{7,3},{8,12},{10,14},{12... | collective-permute-start | bytes 1572872 | tf_op jit(solution)/shard_map/ppermute | solution.py:134
  688.6 17.6 %collective-permute-start.65 = (bf16[256,512]{1,0:T(8,128)(2,1)}, bf16[256,512]{1,0:T(8,128)(2,1)S(1)}, u32[]{:S(2)}, u32[]{:S(2)}) collective-permute-start(bf16[256,512]{1,0:T(8,128)(2,1)} %get-tuple-element.412), channel_id=1, source_target_pairs={{0,2},{2,0},{4,6},{6,4},{1,3},{3,1},{5,7},{7,5},{8,10},{10,8},{12,... | collective-permute-start | bytes 786440 | tf_op jit(solution)/shard_map/ppermute | solution.py:134
  688.7 22.3 %collective-permute-start.66 = (bf16[256,512]{1,0:T(8,128)(2,1)}, bf16[256,512]{1,0:T(8,128)(2,1)S(1)}, u32[]{:S(2)}, u32[]{:S(2)}) collective-permute-start(bf16[256,512]{1,0:T(8,128)(2,1)} %get-tuple-element.413), channel_id=1, source_target_pairs={{0,4},{2,6},{4,0},{6,2},{1,5},{3,7},{5,1},{7,3},{8,12},{10,14},{12... | collective-permute-start | bytes 786440 | tf_op jit(solution)/shard_map/ppermute | solution.py:134
  690.2 20.8 %collective-permute-start.64 = (bf16[128,1024]{1,0:T(8,128)(2,1)}, bf16[128,1024]{1,0:T(8,128)(2,1)S(1)}, u32[]{:S(2)}, u32[]{:S(2)}) collective-permute-start(bf16[128,1024]{1,0:T(8,128)(2,1)} %get-tuple-element.589), channel_id=1, source_target_pairs={{0,2},{2,0},{4,6},{6,4},{1,3},{3,1},{5,7},{7,5},{8,10},{10,8},{12,... | collective-permute-start | bytes 786440 | tf_op jit(solution)/shard_map/ppermute | solution.py:134
  692.4 24.2 %collective-permute-start.68 = (bf16[512,640]{1,0:T(8,128)(2,1)}, bf16[512,640]{1,0:T(8,128)(2,1)S(1)}, u32[]{:S(2)}, u32[]{:S(2)}) collective-permute-start(bf16[512,640]{1,0:T(8,128)(2,1)} %get-tuple-element.420), channel_id=1, source_target_pairs={{0,4},{2,6},{4,0},{6,2},{1,5},{3,7},{5,1},{7,3},{8,12},{10,14},{12... | collective-permute-start | bytes 1966088 | tf_op jit(solution)/shard_map/ppermute | solution.py:134
  692.5 24.1 %collective-permute-start.69 = (bf16[512,640]{1,0:T(8,128)(2,1)}, bf16[512,640]{1,0:T(8,128)(2,1)S(1)}, u32[]{:S(2)}, u32[]{:S(2)}) collective-permute-start(bf16[512,640]{1,0:T(8,128)(2,1)} %get-tuple-element.421), channel_id=1, source_target_pairs={{0,2},{2,0},{4,6},{6,4},{1,3},{3,1},{5,7},{7,5},{8,10},{10,8},{12,... | collective-permute-start | bytes 1966088 | tf_op jit(solution)/shard_map/ppermute | solution.py:134
  711.0 26.4 %collective-permute-start.84 = (f32[126,128]{1,0:T(8,128)}, f32[126,128]{1,0:T(8,128)}, u32[]{:S(2)}, u32[]{:S(2)}) collective-permute-start(f32[126,128]{1,0:T(8,128)} %bitcast.85), channel_id=1, source_target_pairs={{0,8},{8,0},{16,24},{24,16},{1,9},{9,1},{17,25},{25,17},{2,10},{10... | collective-permute-start | bytes 193544 | tf_op jit(solution)/shard_map/ppermute | solution.py:473
  720.8 16.8 %collective-permute-start.77 = (bf16[64,1024]{1,0:T(8,128)(2,1)}, bf16[64,1024]{1,0:T(8,128)(2,1)S(1)}, u32[]{:S(2)}, u32[]{:S(2)}) collective-permute-start(bf16[64,1024]{1,0:T(8,128)(2,1)} %get-tuple-element.433), channel_id=1, source_target_pairs={{0,2},{2,0},{4,6},{6,4},{1,3},{3,1},{5,7},{7,5},{8,10},{10,8},{12,... | collective-permute-start | bytes 393224 | tf_op jit(solution)/shard_map/ppermute | solution.py:134
  721.9 18.9 %collective-permute-start.78 = (bf16[64,1024]{1,0:T(8,128)(2,1)}, bf16[64,1024]{1,0:T(8,128)(2,1)S(1)}, u32[]{:S(2)}, u32[]{:S(2)}) collective-permute-start(bf16[64,1024]{1,0:T(8,128)(2,1)} %get-tuple-element.434), channel_id=1, source_target_pairs={{0,4},{2,6},{4,0},{6,2},{1,5},{3,7},{5,1},{7,3},{8,12},{10,14},{12... | collective-permute-start | bytes 393224 | tf_op jit(solution)/shard_map/ppermute | solution.py:134
  737.4 16.4 %collective-permute-start.82 = (bf16[256,640]{1,0:T(8,128)(2,1)S(1)}, bf16[256,640]{1,0:T(8,128)(2,1)S(1)}, u32[]{:S(2)}, u32[]{:S(2)}) collective-permute-start(bf16[256,640]{1,0:T(8,128)(2,1)S(1)} %copy-done.151), channel_id=1, source_target_pairs={{0,2},{2,0},{4,6},{6,4},{1,3},{3,1},{5,7},{7,5},{8,10},{10,8},{12,... | collective-permute-start | bytes 983048 | tf_op jit(solution)/shard_map/ppermute | solution.py:134
  737.5 16.3 %collective-permute-start.83 = (bf16[256,640]{1,0:T(8,128)(2,1)S(1)}, bf16[256,640]{1,0:T(8,128)(2,1)S(1)}, u32[]{:S(2)}, u32[]{:S(2)}) collective-permute-start(bf16[256,640]{1,0:T(8,128)(2,1)S(1)} %copy-done.150), channel_id=1, source_target_pairs={{0,4},{2,6},{4,0},{6,2},{1,5},{3,7},{5,1},{7,3},{8,12},{10,14},{12... | collective-permute-start | bytes 983048 | tf_op jit(solution)/shard_map/ppermute | solution.py:134
  754.9 13.5 %collective-permute-start.88 = (f32[126,128]{1,0:T(8,128)S(1)}, f32[126,128]{1,0:T(8,128)S(1)}, u32[]{:S(2)}, u32[]{:S(2)}) collective-permute-start(f32[126,128]{1,0:T(8,128)S(1)} %bitcast_add_fusion.1), channel_id=1, source_target_pairs={{0,16},{8,24},{16,0},{24,8},{1,17},{9,25},{17,1},{25,9},{2,18},{10... | collective-permute-start | bytes 193544 | tf_op jit(solution)/shard_map/ppermute | solution.py:473
  760.5 16.4 %collective-permute-start.86 = (bf16[64,1280]{1,0:T(8,128)(2,1)S(1)}, bf16[64,1280]{1,0:T(8,128)(2,1)S(1)}, u32[]{:S(2)}, u32[]{:S(2)}) collective-permute-start(bf16[64,1280]{1,0:T(8,128)(2,1)S(1)} %get-tuple-element.596), channel_id=1, source_target_pairs={{0,16},{8,24},{16,0},{24,8},{1,17},{9,25},{17,1},{25,9},{2,18},{10... | collective-permute-start | bytes 491528 | tf_op jit(solution)/shard_map/ppermute | solution.py:380
  762.0 15.0 %collective-permute-start.85 = (bf16[64,1280]{1,0:T(8,128)(2,1)S(1)}, bf16[64,1280]{1,0:T(8,128)(2,1)S(1)}, u32[]{:S(2)}, u32[]{:S(2)}) collective-permute-start(bf16[64,1280]{1,0:T(8,128)(2,1)S(1)} %get-tuple-element.597), channel_id=1, source_target_pairs={{0,8},{8,0},{16,24},{24,16},{1,9},{9,1},{17,25},{25,17},{2,10},{10... | collective-permute-start | bytes 491528 | tf_op jit(solution)/shard_map/ppermute | solution.py:380
  (205 other events, 2266.4 us)
Sparse Core Ops, SparseCore 0:
  50.3 39.7 all-gather.8
  92.2 52.6 all-gather.10
  146.5 44.7 all-gather.12
  193.3 44.6 all-gather.14
  353.2 75.6 reduce-scatter.5
  453.0 27.6 reduce-scatter.13
  506.9 77.1 reduce-scatter.7
  586.5 29.5 reduce-scatter.11
  687.8 25.6 reduce-scatter.9

commit v3 on v2

--- a/solution.py
+++ b/solution.py
@@ -235,11 +235,14 @@
         return spread_whole(self.blocks[i], self.near[i], self.far[i])
 
 
-def gathered_ctx(block, near, count):
+def gathered_ctx(block, near, widths):
     far = spread_second(spread_parts(near))
     rows = spread_whole(block, near, far).reshape((4,) + block.shape[1:])
-    width = rows.shape[-1] // count
-    return [rows[..., i * width : (i + 1) * width] for i in range(count)]
+    out, first = [], 0
+    for width in widths:
+        out.append(rows[..., first : first + width])
+        first += width
+    return out
 
 
 def table_body(spans, *refs):
@@ -401,7 +404,7 @@
         return cuts[0]
 
     def add_fsdp_first(self, left, right, waits, done):
-        table = fsdp_table(left, right, 256)
+        table = fsdp_table(left, right, 512)
         fsdp, flips, rows, width = table.shape
 
         def run():
@@ -1205,7 +1208,7 @@
 def norm_grad(kept, gain, partial_grad, base):
     own = partial_grad.astype(LOW)
     rows, features = kept.shape
-    tile = min(rows, 512)
+    tile = min(rows, 256)
     out, low, sums = kernel_call(
         norm_grad_body,
         (rows // tile,),
@@ -1244,7 +1247,8 @@
     rows = zx.shape[0]
     return (
         jnp.concatenate([zx.reshape(rows, -1), attn.reshape(rows, -1)], axis=1),
-        jnp.concatenate([mix.T, attn_out.T, mlp.reshape(rows, -1)], axis=1),
+        jnp.concatenate([mix.T, attn_out.T], axis=1),
+        mlp.reshape(rows, -1),
         mlp_out.T,
     )
 
@@ -1297,8 +1301,6 @@
         late[:], projected = together(late, projected)
         late[:] = [lax.all_gather(v, "fsdp", axis=1).reshape(-1, v.shape[-1]) for v in late]
     mlp_out_w = late[layer]
-    if layer > 0:
-        (mlp_out_w,), projected = together((mlp_out_w,), projected)
     edge = jnp.concatenate(
         [projected[-CONV + 1 :, channels : 2 * channels], side[-CONV + 1 :, : 2 * STATE]], axis=1
     )
@@ -1315,13 +1317,19 @@
     attended, log_total = attend(place, queries, kv, kv_came, rows)
     if layer > 0:
         moves, parcel = together(moves, parcel)
+        mlp_w = late[len(late) // 2 + layer]
+        (mlp_w,), parcel = together((mlp_w,), parcel)
     (attended, parcel), y_local = together((attended, parcel), y_local)
     parcel = gathers.step(parcel)
     parcel = gathers.begin(parcel)
     y, mamba_norm = gate_tail(y_local, all_cum, bc, x, projected, heads, gain, parcel, rows)
     both = jnp.concatenate([mamba_norm, attended], axis=1)
     rest = gathers.take(2 * layer + 1)
-    mix_w, mlp_w = rest[:, : both.shape[1]], rest[:, both.shape[1] :]
+    mix_w = rest[:, : both.shape[1]]
+    if layer == 0:
+        mlp_w = rest[:, both.shape[1] :]
+    else:
+        (mlp_out_w,), both = together((mlp_out_w,), both)
     after_mix = hidden + tp_sum(against_rows(both, mix_w))
     normed_two = normalize(after_mix, gains[1])
     gate_up = product(normed_two, mlp_w)
@@ -1367,10 +1375,10 @@
     )
     grad_mid = scatters.step(grad_mid)
     if extra:
-        extra[:], grad_mid = together(extra, grad_mid)
+        extra[:], grad_mix = together(extra, grad_mix)
     table = scatters.add(
         [(grad_mlp, activated), (grad_mix, both)],
-        256,
+        512,
         None if split else False,
         (0, 0),
         functools.partial(done, 0),
@@ -1390,7 +1398,7 @@
     later = scatters.step(later)
     if split:
         mid = jnp.concatenate([grad_gate, grad_q], axis=1)
-        table = scatters.add([(normed, mid)], 256, True, (0, 0), functools.partial(done, 2))
+        table = scatters.add([(normed, mid)], 512, True, (0, 0), functools.partial(done, 2))
         _, later = together((table,), later)
     dstk, drim, grad_step, dtaps, dheads = scan_back(
         du, x, bc, stk, rim, cum, all_cum, step, side, first, parcel, later, taps, heads, rows
@@ -1421,13 +1429,15 @@
     tail_sums = jnp.sum(tail_sums, axis=0)
     dheads = jnp.sum(dheads, axis=0)
     skip_grad = jnp.sum(tail_sums[1].reshape(head_count, HDIM), axis=1)
+    skip_grad = jnp.pad(skip_grad, (0, LANES - head_count))[None]
     small_grads = (
         jnp.stack([grad_gain_one, grad_gain_two]),
-        jnp.sum(dtaps, axis=0)[: CONV + 1],
-        jnp.concatenate([dheads[:2, :head_count], skip_grad[None]], axis=0),
+        jnp.sum(dtaps, axis=0),
+        jnp.where(row_iota(dheads.shape) == 2, skip_grad, dheads),
         tail_sums[0],
     )
-    return scatters.step(below), grad_mlp, small_grads
+    below, grad_mlp = scatters.step((below, grad_mlp))
+    return below, grad_mlp, small_grads
 
 
 def tp_ordered(a, b):
@@ -1471,18 +1481,19 @@
     scatters.begin(run())
 
 
-def settle_small(scatters, small_grads, done):
+def settle_small(scatters, small_grads, half_heads, done):
     def run():
         layers = len(small_grads)
         shapes = [v.shape for v in small_grads[0]]
-        flat = [jnp.pad(v.reshape(-1), (0, -v.size % LANES)) for grads in small_grads for v in grads]
-        packed = yield from sum_everywhere(jnp.concatenate(flat).reshape(-1, LANES))
+        flat = [v.reshape(-1, LANES) for grads in small_grads for v in grads]
+        flat = [jnp.pad(v, ((0, -v.shape[0] % 8), (0, 0))) for v in flat]
+        packed = yield from sum_everywhere(jnp.concatenate(flat, axis=0))
         (packed_peer,) = yield (tp_peer(packed),), 0, ()
         own, peer = [], []
         first = 0
         for values, shape in zip(flat, shapes * layers):
             for source, parts in ((packed, own), (packed_peer, peer)):
-                piece = source.reshape(-1)[first : first + math.prod(shape)]
+                piece = source[first : first + math.prod(shape) // LANES]
                 parts.append(piece.reshape(shape))
             first += values.shape[0]
         count = len(shapes)
@@ -1504,7 +1515,7 @@
                     jnp.where(lax.axis_index("tp") == 0, gains, gains_p),
                     taps_full[:CONV],
                     taps_full[CONV],
-                    tp_ordered(heads, heads_p),
+                    tp_ordered(heads[:3, :half_heads], heads_p[:3, :half_heads]),
                     tp_ordered(gain, gain_p),
                 ),
             )
@@ -1524,26 +1535,30 @@
     ctx_place = lax.axis_index("ctx")
     place = (ctx_place % 2).astype(jnp.int32).reshape(1)
     start_row = ctx_place % 2 * rows * 2
-    tables = turn_tables(start_row, 2 * rows)
     pieces = (mamba_zx, mamba_out, attn_in, attn_out, mlp_in, mlp_out)
     shards = [weight_rows(l, pieces) for l in range(layers)]
     quarters = (sequences, rows, features)
     moves = to_halves_moves(hidden_in.reshape(quarters))
-    first_shards = [shards[l][i] for l in range(layers) for i in range(2)]
+    first_shards = [shards[0][0], jnp.concatenate(shards[0][1:3], axis=1)]
+    first_shards += [shards[l][i] for l in range(1, layers) for i in range(2)]
+    late_pieces = [shards[l][3] for l in range(layers)] + [shards[l][2] for l in range(1, layers)]
     came = fsdp_moves(first_shards[0])
-    late_block = jnp.concatenate([shards[l][2] for l in range(layers)], axis=1)[None]
+    late_block = jnp.concatenate(late_pieces, axis=1)[None]
     near = spread_first(late_block)
     moved = lax.optimization_barrier(moves + came + near)
     given = to_halves(*moved[:2])
     first_block = fsdp_join(first_shards[0], moved[2:-2])
     blocks, first_block = gathered_blocks(first_shards, first_block)
     gathers = Gathers([first_block] + blocks)
-    late = gathered_ctx(late_block, moved[-2:], layers)
+    late = gathered_ctx(late_block, moved[-2:], [v.shape[1] for v in late_pieces])
+    small_args = (norm_gains, mamba_shared, conv_weight, conv_bias, head_params, mamba_gain)
+    gathers.near[0], (given, small_args, start_row) = together(
+        gathers.near[0], (given, small_args, start_row)
+    )
+    tables = turn_tables(start_row, 2 * rows)
     order = own_order(features * lax.axis_size("tp"), LOW)
     smalls = [
-        local_small(
-            order, l, norm_gains, mamba_shared, conv_weight, conv_bias, head_params, mamba_gain
-        )
+        local_small(order, l, *small_args)
         for l in range(layers)
     ]
     length = pick(lengths.reshape(sequences), ctx_place // 2, 0)
@@ -1588,7 +1603,9 @@
     small_grads = [
         (gains[2 * l : 2 * l + 2],) + small_grads[l][1:] for l in range(layers)
     ]
-    settle_small(scatters, small_grads, rest.__setitem__)
+    settle_small(
+        scatters, small_grads, heads_total // lax.axis_size("tp"), rest.__setitem__
+    )
     scatters.finish()
     channels = mamba_out.shape[1]
     ff = mlp_out.shape[1]

time: 837 us -> 797 us (0.952)
  waiting for transfers between devices: 187 us -> 160 us
  other arithmetic: 56.5 us -> 66.5 us
    ppermute x4, waiting for transfers between devices: 2.51 us -> 14.8 us  [sum_everywhere(): lax.ppermute(v, axis, xor_pairs(lax.axis_size(axis), step))]
    ppermute x48, starting transfers between devices: 52.3 us -> 41.3 us  [ctx_swap(): return lax.ppermute(values, 'ctx', xor_pairs(lax.axis_size('ctx'), step))]
    ppermute x2, waiting for transfers between devices: 14.3 us -> 3.93 us  [to_halves_moves(): b = lax.ppermute(pick(quarters, 1 - place % 2, 0), 'ctx', CROSSED)]
    ppermute x6, waiting for transfers between devices: 16.9 us -> 6.68 us  [fsdp_scatter(): lax.ppermute(pick(table, place ^ step, 0), 'fsdp', xor_pairs(count, step))]
    ppermute x3, waiting for transfers between devices: 17 us -> 6.97 us  [fsdp_moves(): lax.ppermute(piece, 'fsdp', xor_pairs(count, step))]
    unnamed x360 -> x340, local copies, waits for them, and re-layouts: 36.7 us -> 30.1 us
  transfers between devices with their start and end apart: 107 -> 108, of which waited for: 38 -> 39; matrix products, arithmetic and copies ran while one was open for 22% -> 22% of each run, Pallas kernels for 28% -> 27%
where the time goes in v3:
time: 797 us; the launch traced here: 787 us
  Pallas kernels  238 us (30%)
  waiting for transfers between devices  160 us (20%)
  starting transfers between devices  132 us (17%)
  local copies, waits for them, and re-layouts  88.7 us (11%)
  matrix products  85.1 us (11%)
  other arithmetic  66.5 us (8%)
  between operations  17.4 us (2%)
    ppermute x48, waiting for transfers between devices, ctx_swap(): return lax.ppermute(values, 'ctx', xor_pairs(lax.axis_size('ctx'), step))  78.1 us
    dot_general x15, matrix products, dot(): lax.dot_general(a, b, (((ca,), (cb,)), ((), ())), preferred_element_type=...  46 us
    pallas_call x2, Pallas kernels, scan_back(): kernel_call(scan_back_body, (count,), [back_block(channels), back_block(c...  44.3 us
    ppermute x48, starting transfers between devices, ctx_swap(): return lax.ppermute(values, 'ctx', xor_pairs(lax.axis_size('ctx'), step))  41.3 us
    dot_general x16, matrix products, product(): return jnp.dot(a, b, preferred_element_type=WIDE)  39.2 us
    pallas_call x14, Pallas kernels, once(): kernel_call(body, (1,), [whole(v.shape) for v in operands], [whole(shape)...  38.6 us
    ppermute x13, starting transfers between devices, tp_peer(): return lax.ppermute(x, 'tp', xor_pairs(lax.axis_size('tp'), 1))  33.7 us
    ppermute x12, waiting for transfers between devices, next_half(): lax.ppermute(x, 'ctx', [(i, i + 1) if forward else (i + 1, i) for i in fi...  31.7 us
  transfers between devices with their start and end apart: 108, of which 39 were waited for; matrix products, arithmetic and copies ran while one was open for 22% of the time, Pallas kernels for 27%

profile of v3, /device:TPU:1, one launch (start us, length us, event | category | flops | bytes accessed | tf_op | source)
XLA Modules:
  0.0 787.3 jit_solution(5647414377048641900)
XLA Ops:
  21.2 4.0 collective-permute-done.2
  34.1 3.9 collective-permute-done.1
  50.9 3.4 pad_maximum_fusion.3
  56.6 10.8 %collective-permute-done.7 = bf16[4,64,1920]{2,1,0:T(8,128)(2,1)} collective-permute-done((bf16[4,64,1920]{2,1,0:T(8,128)(2,1)}, bf16[4,64,1920]{2,1,0:T(8,128)(2,1)}, u32[]{:S(2)}, u32[]{:S(2)}) %collective-permute-start.7) | collective-permute-done | bytes 983072 | tf_op jit(solution)/shard_map/ppermute | solution.py:134
  67.4 7.1 collective-permute-start.9
  81.5 7.2 collective-permute-done.12
  89.6 6.6 fusion.72.rows_ref.zx_ref.gate_ref
  117.9 9.9 %shard_map.265 = (bf16[512,1024]{1,0:T(8,128)(2,1)}, bf16[512,768]{1,0:T(8,128)(2,1)}, bf16[512,256]{1,0:T(8,128)(2,1)}, f32[512,768]{1,0:T(8,128)}, f32[768,128...) custom-call(f32[512,1920]{1,0:T(8,128)} %fusion.72.rows_ref.zx_ref.gate, ...), custom_call_target="tpu_custom_call" | custom-call | flops 805306368 | bytes 8388608 | tf_op jit(solution)/shard_map/pallas_call | solution.py:796
  129.9 7.3 shard_map.264
  137.1 15.1 %collective-permute-done.16.parcel_ref = bf16[784,128]{1,0:T(8,128)(2,1)S(1)} collective-permute-done((bf16[784,128]{1,0:T(8,128)(2,1)}, bf16[784,128]{1,0:T(8,128)(2,1)S(1)}, u32[]{:S(2)}, u32[]{:S(2)}) %collective-permute-start.16) | collective-permute-done | bytes 200736 | tf_op jit(solution)/shard_map/ppermute | solution.py:72
  160.7 6.0 shard_map.266
  170.0 4.3 collective-permute-done.20
  175.9 4.2 pad_maximum_fusion
  192.4 16.0 %collective-permute-done.22 = bf16[4,64,1920]{2,1,0:T(8,128)(2,1)S(1)} collective-permute-done((bf16[4,64,1920]{2,1,0:T(8,128)(2,1)S(1)}, bf16[4,64,1920]{2,1,0:T(8,128)(2,1)S(1)}, u32[]{:S(2)}, u32[]{:S(2)}) %collective-permute-start.22) | collective-permute-done | bytes 983072 | tf_op jit(solution)/shard_map/ppermute | solution.py:134
  219.5 9.2 %collective-permute-done.25 = bf16[4,64,896]{2,1,0:T(8,128)(2,1)S(1)} collective-permute-done((bf16[4,64,896]{2,1,0:T(8,128)(2,1)}, bf16[4,64,896]{2,1,0:T(8,128)(2,1)S(1)}, u32[]{:S(2)}, u32[]{:S(2)}) %collective-permute-start.25) | collective-permute-done | bytes 458784 | tf_op jit(solution)/shard_map/ppermute | solution.py:134
  255.1 10.1 %shard_map.269 = (bf16[512,1024]{1,0:T(8,128)(2,1)}, bf16[512,768]{1,0:T(8,128)(2,1)}, bf16[512,256]{1,0:T(8,128)(2,1)}, f32[512,768]{1,0:T(8,128)}, f32[768,128...) custom-call(f32[512,1920]{1,0:T(8,128)} %copy-done.2, ...), custom_call_target="tpu_custom_call" | custom-call | flops 805306368 | bytes 8388608 | tf_op jit(solution)/shard_map/pallas_call | solution.py:796
  265.3 3.4 collective-permute-start.31
  268.7 7.2 shard_map.268
  281.3 5.7 shard_map.270
  289.2 5.9 all-gather.17.cloned.1.call-done
  296.3 4.0 convolution_convert_fusion.1
  304.4 4.4 fusion.176
  318.9 6.8 shard_map.271
  325.7 4.3 convolution_convert_fusion
  330.4 6.0 convolution_convert_fusion.3.own_ref
  340.9 3.9 collective-permute-start.39
  345.8 4.6 shard_map.272
  352.0 6.9 shard_map.273
  363.9 8.1 %shard_map.274 = (f32[512,768]{1,0:T(8,128)}, bf16[512,768]{1,0:T(8,128)(2,1)}, bf16[784,128]{1,0:T(8,128)(2,1)}, f32[2,8,768]{2,1,0:T(8,128)}) custom-call(f32[512,768]{1,0:T(8,128)} %fusion.30.dn_ref, f32[512,768]{1,0:T(8,128)} %get-tuple-element.352.y_ref, f32[512,128]{1,0:T(8,128)} %get-tuple-element.327.cum_ref.all_ref, ...), custom_call_target="tpu_custom_call" | custom-call | flops 124256256 | bytes 8650752 | tf_op jit(solution)/shard_map/pallas_call | solution.py:941
  375.3 10.6 %shard_map.275 = (bf16[512,256]{1,0:T(8,128)(2,1)}, f32[512,128]{1,0:T(8,128)}, bf16[512,128]{1,0:T(8,128)(2,1)}) custom-call(s32[1]{0:T(128)} %bitcast.23.place_ref, bf16[512,256]{1,0:T(8,128)(2,1)} %get-tuple-element.314.q_ref, bf16[512,256]{1,0:T(8,128)(2,1)} %convolution_convert_fusion.5.grad_ref, f32[512,128]{1,0:T(8,128)} %get-tuple-element.354.total_ref, ...), custom_call_target="tpu_custom_call" | custom-call | flops 2684354560 | bytes 2097152 | tf_op jit(solution)/shard_map/pallas_call | solution.py:646
  387.2 5.0 collective-permute-done.45.refs_0_
  401.9 22.1 %shard_map.277 = (f32[512,1024]{1,0:T(8,128)}, f32[8,1024]{1,0:T(8,128)}, bf16[512,128]{1,0:T(8,128)(2,1)}, f32[2,8,1024]{2,1,0:T(8,128)}, f32[2,8,128]{2,1,0:T(8,128)}) custom-call(f32[512,768]{1,0:T(8,128)} %get-tuple-element.362.du_ref, bf16[512,768]{1,0:T(8,128)(2,1)} %get-tuple-element.329.x_ref, bf16[512,256]{1,0:T(8,128)(2,1)} %get-tuple-element.328.bc_ref, ...), custom_call_target="tpu_custom_call" | custom-call | flops 2013265920 | bytes 12582912 | tf_op jit(solution)/shard_map/pallas_call | solution.py:1132
  426.2 3.6 shard_map.279
  438.6 7.6 shard_map.280
  448.0 6.0 add_convert_fusion.2.own_ref
  454.0 4.0 collective-permute-start.53
  462.7 4.6 shard_map.281
  467.3 8.4 %collective-permute-done.48.from_y_ref = bf16[128,1024]{1,0:T(8,128)(2,1)S(1)} collective-permute-done((bf16[128,1024]{1,0:T(8,128)(2,1)S(1)}, bf16[128,1024]{1,0:T(8,128)(2,1)S(1)}, u32[]{:S(2)}, u32[]{:S(2)}) %collective-permute-start.48) | collective-permute-done | bytes 262176 | tf_op jit(solution)/shard_map/ppermute | solution.py:134
  478.3 3.3 shard_map.283
  483.6 3.8 multiply_convert_fusion.1
  488.9 6.3 shard_map.284
  496.8 4.6 fusion.35.own_ref
  501.4 5.2 collective-permute-start.54
  516.2 5.1 shard_map.285
  524.7 3.9 shard_map.296
  528.7 7.0 shard_map.286
  539.8 10.5 %shard_map.288 = (bf16[512,256]{1,0:T(8,128)(2,1)}, f32[512,128]{1,0:T(8,128)}, bf16[512,128]{1,0:T(8,128)(2,1)}) custom-call(s32[1]{0:T(128)} %bitcast.23.place_ref, bf16[512,256]{1,0:T(8,128)(2,1)} %get-tuple-element.278.q_ref, bf16[512,256]{1,0:T(8,128)(2,1)} %convolution_convert_fusion.4.grad_ref, f32[512,128]{1,0:T(8,128)} %get-tuple-element.412.total_ref, ...), custom_call_target="tpu_custom_call" | custom-call | flops 2684354560 | bytes 2097152 | tf_op jit(solution)/shard_map/pallas_call | solution.py:646
  551.6 3.5 fusion.28.dn_ref
  555.2 8.1 %shard_map.287 = (f32[512,768]{1,0:T(8,128)}, bf16[512,768]{1,0:T(8,128)(2,1)}, bf16[784,128]{1,0:T(8,128)(2,1)}, f32[2,8,768]{2,1,0:T(8,128)}) custom-call(f32[512,768]{1,0:T(8,128)} %fusion.28.dn_ref, f32[512,768]{1,0:T(8,128)} %get-tuple-element.410.y_ref, f32[512,128]{1,0:T(8,128)} %get-tuple-element.292.cum_ref.all_ref, ...), custom_call_target="tpu_custom_call" | custom-call | flops 124256256 | bytes 8650752 | tf_op jit(solution)/shard_map/pallas_call | solution.py:941
  565.5 4.9 collective-permute-done.57.later_ref
  572.7 3.9 shard_map.290
  592.6 22.1 %shard_map.291 = (f32[512,1024]{1,0:T(8,128)}, f32[8,1024]{1,0:T(8,128)}, bf16[512,128]{1,0:T(8,128)(2,1)}, f32[2,8,1024]{2,1,0:T(8,128)}, f32[2,8,128]{2,1,0:T(8,128)}) custom-call(f32[512,768]{1,0:T(8,128)} %get-tuple-element.424.du_ref, bf16[512,768]{1,0:T(8,128)(2,1)} %get-tuple-element.294.x_ref, bf16[512,256]{1,0:T(8,128)(2,1)} %get-tuple-element.293.bc_ref, ...), custom_call_target="tpu_custom_call" | custom-call | flops 2013265920 | bytes 12582912 | tf_op jit(solution)/shard_map/pallas_call | solution.py:1132
  620.6 3.7 shard_map.292
  633.6 4.6 shard_map.295
  638.3 5.1 add_convert_fusion.own_ref
  643.4 4.6 collective-permute-start.70
  654.4 4.6 shard_map.297
  666.7 10.8 %collective-permute-done.64.from_x_ref = bf16[128,1024]{1,0:T(8,128)(2,1)S(1)} collective-permute-done((bf16[128,1024]{1,0:T(8,128)(2,1)S(1)}, bf16[128,1024]{1,0:T(8,128)(2,1)S(1)}, u32[]{:S(2)}, u32[]{:S(2)}) %collective-permute-start.64) | collective-permute-done | bytes 262176 | tf_op jit(solution)/shard_map/ppermute | solution.py:134
  691.9 3.5 collective-permute-start.76
  698.1 4.8 collective-permute-done.80
  726.2 12.0 %collective-permute-done.88 = f32[192,128]{1,0:T(8,128)S(1)} collective-permute-done((f32[192,128]{1,0:T(8,128)S(1)}, f32[192,128]{1,0:T(8,128)S(1)}, u32[]{:S(2)}, u32[]{:S(2)}) %collective-permute-start.88) | collective-permute-done | bytes 98336 | tf_op jit(solution)/shard_map/ppermute | solution.py:476
  752.5 3.4 collective-permute-done.94
  762.6 4.0 collective-permute-done.96
  766.7 4.6 collective-permute-start.97
  (824 shorter events, 343.5 us)
Async XLA Ops:
  7.2 106.5 %all-gather.11.cloned.1.call-start = ((), (), s32[]{:S(2)}) async-start(), calls=%async_computation.10 | async-start | bytes 1966080 | tf_op jit(solution)/shard_map/all_gather | solution.py:197
  10.6 27.4 %collective-permute-start.5 = (bf16[1,64,4096]{2,1,0:T(8,128)(2,1)}, bf16[1,64,4096]{2,1,0:T(8,128)(2,1)S(1)}, u32[]{:S(2)}, u32[]{:S(2)}) collective-permute-start(bf16[1,64,4096]{2,1,0:T(8,128)(2,1)} %maximum_bitcast_fusion), channel_id=1, source_target_pairs={{0,2},{2,0},{4,6},{6,4},{1,3},{3,1},{5,7},{7,5},{8,10},{10,8},{12,... | collective-permute-start | bytes 1572872 | tf_op jit(solution)/shard_map/ppermute | solution.py:134
  12.7 25.4 %collective-permute-start.6 = (bf16[1,64,4096]{2,1,0:T(8,128)(2,1)}, bf16[1,64,4096]{2,1,0:T(8,128)(2,1)S(1)}, u32[]{:S(2)}, u32[]{:S(2)}) collective-permute-start(bf16[1,64,4096]{2,1,0:T(8,128)(2,1)} %maximum_bitcast_fusion), channel_id=1, source_target_pairs={{0,4},{2,6},{4,0},{6,2},{1,5},{3,7},{5,1},{7,3},{8,12},{10,14},{12... | collective-permute-start | bytes 1572872 | tf_op jit(solution)/shard_map/ppermute | solution.py:134
  18.6 15.5 %collective-permute-start.4 = (bf16[64,1920]{1,0:T(8,128)(2,1)}, bf16[64,1920]{1,0:T(8,128)(2,1)}, u32[]{:S(2)}, u32[]{:S(2)}) collective-permute-start(bf16[64,1920]{1,0:T(8,128)(2,1)} %pad_maximum_fusion.27), channel_id=1, source_target_pairs={{0,24},{8,16},{16,8},{24,0},{1,25},{9,17},{17,9},{25,1},{2,26},{10... | collective-permute-start | bytes 737288 | tf_op jit(solution)/shard_map/ppermute | solution.py:181
  43.2 116.2 %all-gather.13.cloned.1.call-start = ((), (), s32[]{:S(2)}) async-start(), calls=%async_computation.11 | async-start | bytes 1884160 | tf_op jit(solution)/shard_map/all_gather | solution.py:198
  44.8 22.6 %collective-permute-start.7 = (bf16[4,64,1920]{2,1,0:T(8,128)(2,1)}, bf16[4,64,1920]{2,1,0:T(8,128)(2,1)}, u32[]{:S(2)}, u32[]{:S(2)}) collective-permute-start(bf16[4,64,1920]{2,1,0:T(8,128)(2,1)} %bitcast_dynamic-update-slice_fusion), channel_id=1, source_target_pairs={{0,2},{2,0},{4,6},{6,4},{1,3},{3,1},{5,7},{7,5},{8,10},{10,8},{12,... | collective-permute-start | bytes 2949128 | tf_op jit(solution)/shard_map/ppermute | solution.py:134
  46.2 21.2 %collective-permute-start.8 = (bf16[4,64,1920]{2,1,0:T(8,128)(2,1)}, bf16[4,64,1920]{2,1,0:T(8,128)(2,1)}, u32[]{:S(2)}, u32[]{:S(2)}) collective-permute-start(bf16[4,64,1920]{2,1,0:T(8,128)(2,1)} %bitcast_dynamic-update-slice_fusion), channel_id=1, source_target_pairs={{0,4},{2,6},{4,0},{6,2},{1,5},{3,7},{5,1},{7,3},{8,12},{10,14},{12... | collective-permute-start | bytes 2949128 | tf_op jit(solution)/shard_map/ppermute | solution.py:134
  46.6 164.6 %all-gather.15.cloned.1.call-start = ((), (), s32[]{:S(2)}) async-start(), calls=%async_computation.12 | async-start | bytes 2621440 | tf_op jit(solution)/shard_map/all_gather | solution.py:1302
  75.6 13.6 %collective-permute-start.13 = (bf16[4,64,1024]{2,1,0:T(8,128)(2,1)S(1)}, bf16[4,64,1024]{2,1,0:T(8,128)(2,1)S(1)}, u32[]{:S(2)}, u32[]{:S(2)}) collective-permute-start(bf16[4,64,1024]{2,1,0:T(8,128)(2,1)S(1)} %slice.524), channel_id=1, source_target_pairs={{0,2},{2,0},{4,6},{6,4},{1,3},{3,1},{5,7},{7,5},{8,10},{10,8},{12,... | collective-permute-start | bytes 1572872 | tf_op jit(solution)/shard_map/ppermute | solution.py:134
  96.2 181.2 %all-gather.19.cloned.1.call-start = ((), (), s32[]{:S(2)}) async-start(), calls=%async_computation.14 | async-start | bytes 5242880 | tf_op jit(solution)/shard_map/all_gather | solution.py:1302
  113.7 38.6 %collective-permute-start.17 = (bf16[4,64,3072]{2,1,0:T(8,128)(2,1)}, bf16[4,64,3072]{2,1,0:T(8,128)(2,1)}, u32[]{:S(2)}, u32[]{:S(2)}) collective-permute-start(bf16[4,64,3072]{2,1,0:T(8,128)(2,1)} %bitcast.300), channel_id=1, source_target_pairs={{0,2},{2,0},{4,6},{6,4},{1,3},{3,1},{5,7},{7,5},{8,10},{10,8},{12,... | collective-permute-start | bytes 4718600 | tf_op jit(solution)/shard_map/ppermute | solution.py:134
  115.8 36.5 %collective-permute-start.18 = (bf16[4,64,3072]{2,1,0:T(8,128)(2,1)}, bf16[4,64,3072]{2,1,0:T(8,128)(2,1)}, u32[]{:S(2)}, u32[]{:S(2)}) collective-permute-start(bf16[4,64,3072]{2,1,0:T(8,128)(2,1)} %bitcast.301), channel_id=1, source_target_pairs={{0,4},{2,6},{4,0},{6,2},{1,5},{3,7},{5,1},{7,3},{8,12},{10,14},{12... | collective-permute-start | bytes 4718600 | tf_op jit(solution)/shard_map/ppermute | solution.py:134
  127.8 24.5 %collective-permute-start.16 = (bf16[784,128]{1,0:T(8,128)(2,1)}, bf16[784,128]{1,0:T(8,128)(2,1)S(1)}, u32[]{:S(2)}, u32[]{:S(2)}) collective-permute-start(bf16[784,128]{1,0:T(8,128)(2,1)} %get-tuple-element.289), channel_id=1, source_target_pairs={{0,2},{4,6},{1,3},{5,7},{8,10},{12,14},{9,11},{13,15},{16,18},{20,... | collective-permute-start | bytes 602120 | tf_op jit(solution)/shard_map/ppermute | solution.py:72
  129.8 165.4 %all-gather.17.cloned.1.call-start = ((), (), s32[]{:S(2)}) async-start(), calls=%async_computation.13 | async-start | bytes 2621440 | tf_op jit(solution)/shard_map/all_gather | solution.py:1302
  153.6 16.4 %collective-permute-start.19 = (bf16[4,64,1536]{2,1,0:T(8,128)(2,1)S(1)}, bf16[4,64,1536]{2,1,0:T(8,128)(2,1)}, u32[]{:S(2)}, u32[]{:S(2)}) collective-permute-start(bf16[4,64,1536]{2,1,0:T(8,128)(2,1)S(1)} %slice.537), channel_id=1, source_target_pairs={{0,4},{2,6},{4,0},{6,2},{1,5},{3,7},{5,1},{7,3},{8,12},{10,14},{12... | collective-permute-start | bytes 2359304 | tf_op jit(solution)/shard_map/ppermute | solution.py:134
  156.6 17.6 %collective-permute-start.20 = (bf16[4,64,1536]{2,1,0:T(8,128)(2,1)}, bf16[4,64,1536]{2,1,0:T(8,128)(2,1)}, u32[]{:S(2)}, u32[]{:S(2)}) collective-permute-start(bf16[4,64,1536]{2,1,0:T(8,128)(2,1)} %slice.538), channel_id=1, source_target_pairs={{0,2},{2,0},{4,6},{6,4},{1,3},{3,1},{5,7},{7,5},{8,10},{10,8},{12,... | collective-permute-start | bytes 2359304 | tf_op jit(solution)/shard_map/ppermute | solution.py:134
  184.8 23.5 %collective-permute-start.22 = (bf16[4,64,1920]{2,1,0:T(8,128)(2,1)S(1)}, bf16[4,64,1920]{2,1,0:T(8,128)(2,1)S(1)}, u32[]{:S(2)}, u32[]{:S(2)}) collective-permute-start(bf16[4,64,1920]{2,1,0:T(8,128)(2,1)S(1)} %slice.667), channel_id=1, source_target_pairs={{0,2},{2,0},{4,6},{6,4},{1,3},{3,1},{5,7},{7,5},{8,10},{10,8},{12,... | collective-permute-start | bytes 2949128 | tf_op jit(solution)/shard_map/ppermute | solution.py:134
  186.4 23.0 %collective-permute-start.23 = (bf16[4,64,1920]{2,1,0:T(8,128)(2,1)S(1)}, bf16[4,64,1920]{2,1,0:T(8,128)(2,1)S(1)}, u32[]{:S(2)}, u32[]{:S(2)}) collective-permute-start(bf16[4,64,1920]{2,1,0:T(8,128)(2,1)S(1)} %slice.667), channel_id=1, source_target_pairs={{0,4},{2,6},{4,0},{6,2},{1,5},{3,7},{5,1},{7,3},{8,12},{10,14},{12... | collective-permute-start | bytes 2949128 | tf_op jit(solution)/shard_map/ppermute | solution.py:134
  214.2 15.8 %collective-permute-start.24 = (bf16[512,1024]{1,0:T(8,128)(2,1)S(1)}, bf16[512,1024]{1,0:T(8,128)(2,1)}, u32[]{:S(2)}, u32[]{:S(2)}) collective-permute-start(bf16[512,1024]{1,0:T(8,128)(2,1)S(1)} %convolution_convert_fusion.2), channel_id=1, source_target_pairs={{0,1},{1,0},{2,3},{3,2},{4,5},{5,4},{6,7},{7,6},{8,9},{9,8},{10,11... | collective-permute-start | bytes 3145736 | tf_op jit(solution)/shard_map/ppermute | solution.py:101
  216.2 13.6 %collective-permute-start.26 = (bf16[4,64,1024]{2,1,0:T(8,128)(2,1)S(1)}, bf16[4,64,1024]{2,1,0:T(8,128)(2,1)S(1)}, u32[]{:S(2)}, u32[]{:S(2)}) collective-permute-start(bf16[4,64,1024]{2,1,0:T(8,128)(2,1)S(1)} %slice.545), channel_id=1, source_target_pairs={{0,2},{2,0},{4,6},{6,4},{1,3},{3,1},{5,7},{7,5},{8,10},{10,8},{12,... | collective-permute-start | bytes 1572872 | tf_op jit(solution)/shard_map/ppermute | solution.py:134
  219.5 204.6 %reduce-scatter.6.cloned.1.call-start = ((), (), s32[]{:S(2)}) async-start(), calls=%async_computation.5 | async-start | bytes 5242880 | tf_op jit(solution)/shard_map/reduce_scatter | solution.py:412
  247.9 29.4 %collective-permute-start.32 = (bf16[4,64,1024]{2,1,0:T(8,128)(2,1)S(1)}, bf16[4,64,1024]{2,1,0:T(8,128)(2,1)S(1)}, u32[]{:S(2)}, u32[]{:S(2)}) collective-permute-start(bf16[4,64,1024]{2,1,0:T(8,128)(2,1)S(1)} %slice.678), channel_id=1, source_target_pairs={{0,2},{2,0},{4,6},{6,4},{1,3},{3,1},{5,7},{7,5},{8,10},{10,8},{12,... | collective-permute-start | bytes 1572872 | tf_op jit(solution)/shard_map/ppermute | solution.py:134
  250.0 27.3 %collective-permute-start.33 = (bf16[4,64,1024]{2,1,0:T(8,128)(2,1)S(1)}, bf16[4,64,1024]{2,1,0:T(8,128)(2,1)}, u32[]{:S(2)}, u32[]{:S(2)}) collective-permute-start(bf16[4,64,1024]{2,1,0:T(8,128)(2,1)S(1)} %slice.678), channel_id=1, source_target_pairs={{0,4},{2,6},{4,0},{6,2},{1,5},{3,7},{5,1},{7,3},{8,12},{10,14},{12... | collective-permute-start | bytes 1572872 | tf_op jit(solution)/shard_map/ppermute | solution.py:134
  252.0 24.0 %collective-permute-start.29 = (bf16[256,512]{1,0:T(8,128)(2,1)S(1)}, bf16[256,512]{1,0:T(8,128)(2,1)S(1)}, u32[]{:S(2)}, u32[]{:S(2)}) collective-permute-start(bf16[256,512]{1,0:T(8,128)(2,1)S(1)} %get-tuple-element.642), channel_id=1, source_target_pairs={{0,0},{4,2},{2,4},{6,6},{1,1},{5,3},{3,5},{7,7},{8,8},{12,10},{10,... | collective-permute-start | bytes 786440 | tf_op jit(solution)/shard_map/ppermute | solution.py:81
  252.7 23.3 %collective-permute-start.30 = (bf16[256,512]{1,0:T(8,128)(2,1)S(1)}, bf16[256,512]{1,0:T(8,128)(2,1)S(1)}, u32[]{:S(2)}, u32[]{:S(2)}) collective-permute-start(bf16[256,512]{1,0:T(8,128)(2,1)S(1)} %get-tuple-element.641), channel_id=1, source_target_pairs={{2,0},{6,2},{0,4},{4,6},{3,1},{7,3},{1,5},{5,7},{10,8},{14,10},{8,... | collective-permute-start | bytes 786440 | tf_op jit(solution)/shard_map/ppermute | solution.py:82
  277.4 17.8 %collective-permute-start.34 = (bf16[4,64,512]{2,1,0:T(8,128)(2,1)S(1)}, bf16[4,64,512]{2,1,0:T(8,128)(2,1)}, u32[]{:S(2)}, u32[]{:S(2)}) collective-permute-start(bf16[4,64,512]{2,1,0:T(8,128)(2,1)S(1)} %slice.560), channel_id=1, source_target_pairs={{0,4},{2,6},{4,0},{6,2},{1,5},{3,7},{5,1},{7,3},{8,12},{10,14},{12... | collective-permute-start | bytes 786440 | tf_op jit(solution)/shard_map/ppermute | solution.py:134
  280.7 14.5 %collective-permute-start.35 = (bf16[4,64,512]{2,1,0:T(8,128)(2,1)}, bf16[4,64,512]{2,1,0:T(8,128)(2,1)}, u32[]{:S(2)}, u32[]{:S(2)}) collective-permute-start(bf16[4,64,512]{2,1,0:T(8,128)(2,1)} %slice.561), channel_id=1, source_target_pairs={{0,2},{2,0},{4,6},{6,4},{1,3},{3,1},{5,7},{7,5},{8,10},{10,8},{12,... | collective-permute-start | bytes 786440 | tf_op jit(solution)/shard_map/ppermute | solution.py:134
  325.6 188.5 %reduce-scatter.14.cloned.1.call-start = ((), (), s32[]{:S(2)}) async-start(), calls=%async_computation.9 | async-start | bytes 1310720 | tf_op jit(solution)/shard_map/reduce_scatter | solution.py:375
  358.9 33.3 %collective-permute-start.42 = (bf16[512,1024]{1,0:T(8,128)(2,1)}, bf16[512,1024]{1,0:T(8,128)(2,1)S(1)}, u32[]{:S(2)}, u32[]{:S(2)}) collective-permute-start(bf16[512,1024]{1,0:T(8,128)(2,1)} %get-tuple-element.349), channel_id=1, source_target_pairs={{0,4},{2,6},{4,0},{6,2},{1,5},{3,7},{5,1},{7,3},{8,12},{10,14},{12... | collective-permute-start | bytes 3145736 | tf_op jit(solution)/shard_map/ppermute | solution.py:134
  360.1 32.2 %collective-permute-start.43 = (bf16[512,1024]{1,0:T(8,128)(2,1)}, bf16[512,1024]{1,0:T(8,128)(2,1)S(1)}, u32[]{:S(2)}, u32[]{:S(2)}) collective-permute-start(bf16[512,1024]{1,0:T(8,128)(2,1)} %get-tuple-element.350), channel_id=1, source_target_pairs={{0,2},{2,0},{4,6},{6,4},{1,3},{3,1},{5,7},{7,5},{8,10},{10,8},{12,... | collective-permute-start | bytes 3145736 | tf_op jit(solution)/shard_map/ppermute | solution.py:134
  371.9 20.3 %collective-permute-start.44 = (bf16[784,128]{1,0:T(8,128)(2,1)}, bf16[784,128]{1,0:T(8,128)(2,1)S(1)}, u32[]{:S(2)}, u32[]{:S(2)}) collective-permute-start(bf16[784,128]{1,0:T(8,128)(2,1)} %get-tuple-element.353), channel_id=1, source_target_pairs={{2,0},{6,4},{3,1},{7,5},{10,8},{14,12},{11,9},{15,13},{18,16},{22,... | collective-permute-start | bytes 602120 | tf_op jit(solution)/shard_map/ppermute | solution.py:72
  396.7 27.4 %collective-permute-start.46 = (bf16[256,1024]{1,0:T(8,128)(2,1)}, bf16[256,1024]{1,0:T(8,128)(2,1)S(1)}, u32[]{:S(2)}, u32[]{:S(2)}) collective-permute-start(bf16[256,1024]{1,0:T(8,128)(2,1)} %get-tuple-element.360), channel_id=1, source_target_pairs={{0,2},{2,0},{4,6},{6,4},{1,3},{3,1},{5,7},{7,5},{8,10},{10,8},{12,... | collective-permute-start | bytes 1572872 | tf_op jit(solution)/shard_map/ppermute | solution.py:134
  396.7 27.4 %collective-permute-start.47 = (bf16[256,1024]{1,0:T(8,128)(2,1)}, bf16[256,1024]{1,0:T(8,128)(2,1)S(1)}, u32[]{:S(2)}, u32[]{:S(2)}) collective-permute-start(bf16[256,1024]{1,0:T(8,128)(2,1)} %get-tuple-element.361), channel_id=1, source_target_pairs={{0,4},{2,6},{4,0},{6,2},{1,5},{3,7},{5,1},{7,3},{8,12},{10,14},{12... | collective-permute-start | bytes 1572872 | tf_op jit(solution)/shard_map/ppermute | solution.py:134
  446.2 30.6 %collective-permute-start.51 = (bf16[512,1152]{1,0:T(8,128)(2,1)}, bf16[512,1152]{1,0:T(8,128)(2,1)S(1)}, u32[]{:S(2)}, u32[]{:S(2)}) collective-permute-start(bf16[512,1152]{1,0:T(8,128)(2,1)} %get-tuple-element.383), channel_id=1, source_target_pairs={{0,4},{2,6},{4,0},{6,2},{1,5},{3,7},{5,1},{7,3},{8,12},{10,14},{12... | collective-permute-start | bytes 3538952 | tf_op jit(solution)/shard_map/ppermute | solution.py:134
  447.3 29.5 %collective-permute-start.52 = (bf16[512,1152]{1,0:T(8,128)(2,1)}, bf16[512,1152]{1,0:T(8,128)(2,1)S(1)}, u32[]{:S(2)}, u32[]{:S(2)}) collective-permute-start(bf16[512,1152]{1,0:T(8,128)(2,1)} %get-tuple-element.384), channel_id=1, source_target_pairs={{0,2},{2,0},{4,6},{6,4},{1,3},{3,1},{5,7},{7,5},{8,10},{10,8},{12,... | collective-permute-start | bytes 3538952 | tf_op jit(solution)/shard_map/ppermute | solution.py:134
  458.0 159.6 %reduce-scatter.8.cloned.1.call-start = ((), (), s32[]{:S(2)}) async-start(), calls=%async_computation.6 | async-start | bytes 5242880 | tf_op jit(solution)/shard_map/reduce_scatter | solution.py:412
  458.1 17.6 %collective-permute-start.48 = (bf16[128,1024]{1,0:T(8,128)(2,1)S(1)}, bf16[128,1024]{1,0:T(8,128)(2,1)S(1)}, u32[]{:S(2)}, u32[]{:S(2)}) collective-permute-start(bf16[128,1024]{1,0:T(8,128)(2,1)S(1)} %copy-done.97), channel_id=1, source_target_pairs={{0,4},{2,6},{4,0},{6,2},{1,5},{3,7},{5,1},{7,3},{8,12},{10,14},{12... | collective-permute-start | bytes 786440 | tf_op jit(solution)/shard_map/ppermute | solution.py:134
  459.1 17.7 %collective-permute-start.49 = (bf16[128,1024]{1,0:T(8,128)(2,1)S(1)}, bf16[128,1024]{1,0:T(8,128)(2,1)S(1)}, u32[]{:S(2)}, u32[]{:S(2)}) collective-permute-start(bf16[128,1024]{1,0:T(8,128)(2,1)S(1)} %get-tuple-element.623), channel_id=1, source_target_pairs={{0,2},{2,0},{4,6},{6,4},{1,3},{3,1},{5,7},{7,5},{8,10},{10,8},{12,... | collective-permute-start | bytes 786440 | tf_op jit(solution)/shard_map/ppermute | solution.py:134
  495.3 131.3 %reduce-scatter.12.cloned.1.call-start = ((), (), s32[]{:S(2)}) async-start(), calls=%async_computation.8 | async-start | bytes 1474560 | tf_op jit(solution)/shard_map/reduce_scatter | solution.py:375
  501.4 13.8 %collective-permute-start.54 = (bf16[512,1024]{1,0:T(8,128)(2,1)S(1)}, bf16[512,1024]{1,0:T(8,128)(2,1)S(1)}, u32[]{:S(2)}, u32[]{:S(2)}) collective-permute-start(bf16[512,1024]{1,0:T(8,128)(2,1)S(1)} %fusion.35.own_ref), channel_id=1, source_target_pairs={{0,1},{1,0},{2,3},{3,2},{4,5},{5,4},{6,7},{7,6},{8,9},{9,8},{10,11... | collective-permute-start | bytes 3145736 | tf_op jit(solution)/shard_map/ppermute | solution.py:101
  506.6 18.0 %collective-permute-start.73 = (bf16[256,1152]{1,0:T(8,128)(2,1)}, bf16[256,1152]{1,0:T(8,128)(2,1)}, u32[]{:S(2)}, u32[]{:S(2)}) collective-permute-start(bf16[256,1152]{1,0:T(8,128)(2,1)} %get-tuple-element.397), channel_id=1, source_target_pairs={{0,2},{2,0},{4,6},{6,4},{1,3},{3,1},{5,7},{7,5},{8,10},{10,8},{12,... | collective-permute-start | bytes 1769480 | tf_op jit(solution)/shard_map/ppermute | solution.py:134
  506.6 18.0 %collective-permute-start.74 = (bf16[256,1152]{1,0:T(8,128)(2,1)}, bf16[256,1152]{1,0:T(8,128)(2,1)}, u32[]{:S(2)}, u32[]{:S(2)}) collective-permute-start(bf16[256,1152]{1,0:T(8,128)(2,1)} %get-tuple-element.398), channel_id=1, source_target_pairs={{0,4},{2,6},{4,0},{6,2},{1,5},{3,7},{5,1},{7,3},{8,12},{10,14},{12... | collective-permute-start | bytes 1769480 | tf_op jit(solution)/shard_map/ppermute | solution.py:134
  512.0 12.6 %collective-permute-start.71 = (bf16[64,1024]{1,0:T(8,128)(2,1)S(1)}, bf16[64,1024]{1,0:T(8,128)(2,1)S(1)}, u32[]{:S(2)}, u32[]{:S(2)}) collective-permute-start(bf16[64,1024]{1,0:T(8,128)(2,1)S(1)} %copy-done.150), channel_id=1, source_target_pairs={{0,2},{2,0},{4,6},{6,4},{1,3},{3,1},{5,7},{7,5},{8,10},{10,8},{12,... | collective-permute-start | bytes 393224 | tf_op jit(solution)/shard_map/ppermute | solution.py:134
  528.6 148.9 %reduce-scatter.10.cloned.1.call-start = ((), (), s32[]{:S(2)}) async-start(), calls=%async_computation.7 | async-start | bytes 1310720 | tf_op jit(solution)/shard_map/reduce_scatter | solution.py:375
  535.7 41.6 %collective-permute-start.55 = (bf16[512,1024]{1,0:T(8,128)(2,1)}, bf16[512,1024]{1,0:T(8,128)(2,1)S(1)}, u32[]{:S(2)}, u32[]{:S(2)}) collective-permute-start(bf16[512,1024]{1,0:T(8,128)(2,1)} %get-tuple-element.407), channel_id=1, source_target_pairs={{0,4},{2,6},{4,0},{6,2},{1,5},{3,7},{5,1},{7,3},{8,12},{10,14},{12... | collective-permute-start | bytes 3145736 | tf_op jit(solution)/shard_map/ppermute | solution.py:134
  536.6 40.7 %collective-permute-start.56 = (bf16[512,1024]{1,0:T(8,128)(2,1)}, bf16[512,1024]{1,0:T(8,128)(2,1)S(1)}, u32[]{:S(2)}, u32[]{:S(2)}) collective-permute-start(bf16[512,1024]{1,0:T(8,128)(2,1)} %get-tuple-element.408), channel_id=1, source_target_pairs={{0,2},{2,0},{4,6},{6,4},{1,3},{3,1},{5,7},{7,5},{8,10},{10,8},{12,... | collective-permute-start | bytes 3145736 | tf_op jit(solution)/shard_map/ppermute | solution.py:134
  550.3 15.2 %collective-permute-start.58 = (bf16[512,128]{1,0:T(8,128)(2,1)}, bf16[512,128]{1,0:T(8,128)(2,1)S(1)}, u32[]{:S(2)}, u32[]{:S(2)}) collective-permute-start(bf16[512,128]{1,0:T(8,128)(2,1)} %get-tuple-element.413), channel_id=1, source_target_pairs={{2,0},{6,4},{3,1},{7,5},{10,8},{14,12},{11,9},{15,13},{18,16},{22,... | collective-permute-start | bytes 393224 | tf_op jit(solution)/shard_map/ppermute | solution.py:72
  576.6 40.9 %collective-permute-start.61 = (bf16[512,512]{1,0:T(8,128)(2,1)}, bf16[512,512]{1,0:T(8,128)(2,1)S(1)}, u32[]{:S(2)}, u32[]{:S(2)}) collective-permute-start(bf16[512,512]{1,0:T(8,128)(2,1)} %get-tuple-element.422), channel_id=1, source_target_pairs={{0,4},{2,6},{4,0},{6,2},{1,5},{3,7},{5,1},{7,3},{8,12},{10,14},{12... | collective-permute-start | bytes 1572872 | tf_op jit(solution)/shard_map/ppermute | solution.py:134
  577.3 40.2 %collective-permute-start.62 = (bf16[512,512]{1,0:T(8,128)(2,1)}, bf16[512,512]{1,0:T(8,128)(2,1)}, u32[]{:S(2)}, u32[]{:S(2)}) collective-permute-start(bf16[512,512]{1,0:T(8,128)(2,1)} %get-tuple-element.423), channel_id=1, source_target_pairs={{0,2},{2,0},{4,6},{6,4},{1,3},{3,1},{5,7},{7,5},{8,10},{10,8},{12,... | collective-permute-start | bytes 1572872 | tf_op jit(solution)/shard_map/ppermute | solution.py:134
  581.6 35.9 %collective-permute-start.59 = (bf16[256,1024]{1,0:T(8,128)(2,1)}, bf16[256,1024]{1,0:T(8,128)(2,1)S(1)}, u32[]{:S(2)}, u32[]{:S(2)}) collective-permute-start(bf16[256,1024]{1,0:T(8,128)(2,1)} %get-tuple-element.418), channel_id=1, source_target_pairs={{0,2},{2,0},{4,6},{6,4},{1,3},{3,1},{5,7},{7,5},{8,10},{10,8},{12,... | collective-permute-start | bytes 1572872 | tf_op jit(solution)/shard_map/ppermute | solution.py:134
  583.0 34.5 %collective-permute-start.60 = (bf16[256,1024]{1,0:T(8,128)(2,1)}, bf16[256,1024]{1,0:T(8,128)(2,1)S(1)}, u32[]{:S(2)}, u32[]{:S(2)}) collective-permute-start(bf16[256,1024]{1,0:T(8,128)(2,1)} %get-tuple-element.419), channel_id=1, source_target_pairs={{0,4},{2,6},{4,0},{6,2},{1,5},{3,7},{5,1},{7,3},{8,12},{10,14},{12... | collective-permute-start | bytes 1572872 | tf_op jit(solution)/shard_map/ppermute | solution.py:134
  649.7 15.7 %collective-permute-start.65 = (bf16[256,512]{1,0:T(8,128)(2,1)}, bf16[256,512]{1,0:T(8,128)(2,1)}, u32[]{:S(2)}, u32[]{:S(2)}) collective-permute-start(bf16[256,512]{1,0:T(8,128)(2,1)} %get-tuple-element.442), channel_id=1, source_target_pairs={{0,2},{2,0},{4,6},{6,4},{1,3},{3,1},{5,7},{7,5},{8,10},{10,8},{12,... | collective-permute-start | bytes 786440 | tf_op jit(solution)/shard_map/ppermute | solution.py:134
  649.7 17.0 %collective-permute-start.66 = (bf16[256,512]{1,0:T(8,128)(2,1)}, bf16[256,512]{1,0:T(8,128)(2,1)}, u32[]{:S(2)}, u32[]{:S(2)}) collective-permute-start(bf16[256,512]{1,0:T(8,128)(2,1)} %get-tuple-element.443), channel_id=1, source_target_pairs={{0,4},{2,6},{4,0},{6,2},{1,5},{3,7},{5,1},{7,3},{8,12},{10,14},{12... | collective-permute-start | bytes 786440 | tf_op jit(solution)/shard_map/ppermute | solution.py:134
  650.5 16.2 %collective-permute-start.63 = (bf16[128,1024]{1,0:T(8,128)(2,1)}, bf16[128,1024]{1,0:T(8,128)(2,1)S(1)}, u32[]{:S(2)}, u32[]{:S(2)}) collective-permute-start(bf16[128,1024]{1,0:T(8,128)(2,1)} %get-tuple-element.622), channel_id=1, source_target_pairs={{0,4},{2,6},{4,0},{6,2},{1,5},{3,7},{5,1},{7,3},{8,12},{10,14},{12... | collective-permute-start | bytes 786440 | tf_op jit(solution)/shard_map/ppermute | solution.py:134
  651.9 25.6 %collective-permute-start.68 = (bf16[512,640]{1,0:T(8,128)(2,1)}, bf16[512,640]{1,0:T(8,128)(2,1)S(1)}, u32[]{:S(2)}, u32[]{:S(2)}) collective-permute-start(bf16[512,640]{1,0:T(8,128)(2,1)} %get-tuple-element.450), channel_id=1, source_target_pairs={{0,4},{2,6},{4,0},{6,2},{1,5},{3,7},{5,1},{7,3},{8,12},{10,14},{12... | collective-permute-start | bytes 1966088 | tf_op jit(solution)/shard_map/ppermute | solution.py:134
  652.8 24.7 %collective-permute-start.69 = (bf16[512,640]{1,0:T(8,128)(2,1)}, bf16[512,640]{1,0:T(8,128)(2,1)S(1)}, u32[]{:S(2)}, u32[]{:S(2)}) collective-permute-start(bf16[512,640]{1,0:T(8,128)(2,1)} %get-tuple-element.451), channel_id=1, source_target_pairs={{0,2},{2,0},{4,6},{6,4},{1,3},{3,1},{5,7},{7,5},{8,10},{10,8},{12,... | collective-permute-start | bytes 1966088 | tf_op jit(solution)/shard_map/ppermute | solution.py:134
  666.7 29.6 %collective-permute-start.84 = (f32[192,128]{1,0:T(8,128)}, f32[192,128]{1,0:T(8,128)}, u32[]{:S(2)}, u32[]{:S(2)}) collective-permute-start(f32[192,128]{1,0:T(8,128)} %constant_dynamic-update-slice_fusion.7), channel_id=1, source_target_pairs={{0,8},{8,0},{16,24},{24,16},{1,9},{9,1},{17,25},{25,17},{2,10},{10... | collective-permute-start | bytes 294920 | tf_op jit(solution)/shard_map/ppermute | solution.py:476
  682.3 27.8 %collective-permute-start.82 = (bf16[256,640]{1,0:T(8,128)(2,1)}, bf16[256,640]{1,0:T(8,128)(2,1)S(1)}, u32[]{:S(2)}, u32[]{:S(2)}) collective-permute-start(bf16[256,640]{1,0:T(8,128)(2,1)} %get-tuple-element.473), channel_id=1, source_target_pairs={{0,2},{2,0},{4,6},{6,4},{1,3},{3,1},{5,7},{7,5},{8,10},{10,8},{12,... | collective-permute-start | bytes 983048 | tf_op jit(solution)/shard_map/ppermute | solution.py:134
  691.1 12.7 %collective-permute-start.75 = (bf16[256,512]{1,0:T(8,128)(2,1)S(1)}, bf16[256,512]{1,0:T(8,128)(2,1)S(1)}, u32[]{:S(2)}, u32[]{:S(2)}) collective-permute-start(bf16[256,512]{1,0:T(8,128)(2,1)S(1)} %get-tuple-element.637), channel_id=1, source_target_pairs={{0,0},{2,4},{4,2},{6,6},{1,1},{3,5},{5,3},{7,7},{8,8},{10,12},{12,... | collective-permute-start | bytes 786440 | tf_op jit(solution)/shard_map/ppermute | solution.py:95
  696.3 13.8 %collective-permute-start.83 = (bf16[256,640]{1,0:T(8,128)(2,1)S(1)}, bf16[256,640]{1,0:T(8,128)(2,1)S(1)}, u32[]{:S(2)}, u32[]{:S(2)}) collective-permute-start(bf16[256,640]{1,0:T(8,128)(2,1)S(1)} %copy-done.144), channel_id=1, source_target_pairs={{0,4},{2,6},{4,0},{6,2},{1,5},{3,7},{5,1},{7,3},{8,12},{10,14},{12... | collective-permute-start | bytes 983048 | tf_op jit(solution)/shard_map/ppermute | solution.py:134
  714.8 23.5 %collective-permute-start.85 = (bf16[64,1280]{1,0:T(8,128)(2,1)S(1)}, bf16[64,1280]{1,0:T(8,128)(2,1)S(1)}, u32[]{:S(2)}, u32[]{:S(2)}) collective-permute-start(bf16[64,1280]{1,0:T(8,128)(2,1)S(1)} %get-tuple-element.627), channel_id=1, source_target_pairs={{0,8},{8,0},{16,24},{24,16},{1,9},{9,1},{17,25},{25,17},{2,10},{10... | collective-permute-start | bytes 491528 | tf_op jit(solution)/shard_map/ppermute | solution.py:383
  716.9 21.4 %collective-permute-start.86 = (bf16[64,1280]{1,0:T(8,128)(2,1)S(1)}, bf16[64,1280]{1,0:T(8,128)(2,1)S(1)}, u32[]{:S(2)}, u32[]{:S(2)}) collective-permute-start(bf16[64,1280]{1,0:T(8,128)(2,1)S(1)} %get-tuple-element.626), channel_id=1, source_target_pairs={{0,16},{8,24},{16,0},{24,8},{1,17},{9,25},{17,1},{25,9},{2,18},{10... | collective-permute-start | bytes 491528 | tf_op jit(solution)/shard_map/ppermute | solution.py:383
  717.9 20.4 %collective-permute-start.87 = (bf16[64,1280]{1,0:T(8,128)(2,1)S(1)}, bf16[64,1280]{1,0:T(8,128)(2,1)S(1)}, u32[]{:S(2)}, u32[]{:S(2)}) collective-permute-start(bf16[64,1280]{1,0:T(8,128)(2,1)S(1)} %get-tuple-element.625), channel_id=1, source_target_pairs={{0,24},{8,16},{16,8},{24,0},{1,25},{9,17},{17,9},{25,1},{2,26},{10... | collective-permute-start | bytes 491528 | tf_op jit(solution)/shard_map/ppermute | solution.py:383
  724.3 14.0 %collective-permute-start.88 = (f32[192,128]{1,0:T(8,128)S(1)}, f32[192,128]{1,0:T(8,128)S(1)}, u32[]{:S(2)}, u32[]{:S(2)}) collective-permute-start(f32[192,128]{1,0:T(8,128)S(1)} %add.348), channel_id=1, source_target_pairs={{0,16},{8,24},{16,0},{24,8},{1,17},{9,25},{17,1},{25,9},{2,18},{10... | collective-permute-start | bytes 294920 | tf_op jit(solution)/shard_map/ppermute | solution.py:476
  (202 other events, 2072.1 us)
Sparse Core Ops, SparseCore 0:
  43.4 41.2 all-gather.10
  86.3 34.2 all-gather.12
  122.1 45.5 all-gather.14
  169.1 79.5 all-gather.18
  250.7 44.4 all-gather.16
  325.8 75.1 reduce-scatter.5
  458.1 25.1 reduce-scatter.13
  495.4 78.1 reduce-scatter.7
  576.0 29.4 reduce-scatter.11
  648.2 23.9 reduce-scatter.9

commit v4 on v3

--- a/solution.py
+++ b/solution.py
@@ -557,13 +557,12 @@
     lanes = lane_iota((rows, LANES))
     outs = []
     for head in range(GROUP):
-        query = head_lanes(q_all, head).astype(LOW)
-        scores = jnp.where(seen, dot(query, all_keys, 1, 1) * ADIM**-0.5, MASKED)
+        query = (head_lanes(q_all, head) * ADIM**-0.5).astype(LOW)
+        scores = jnp.where(seen, dot(query, all_keys, 1, 1), MASKED)
         top = jnp.max(scores, axis=1, keepdims=True)
         raised = jnp.exp(scores - top)
         row_total = jnp.sum(raised, axis=1, keepdims=True)
-        weights = (raised * (1.0 / row_total)).astype(LOW)
-        outs.append(dot(weights, all_keys))
+        outs.append(dot(raised.astype(LOW), all_keys) * (1.0 / row_total))
         totals = jnp.where(lanes == head, top + jnp.log(row_total), totals)
     total_ref[...] = totals
     for pair in range(GROUP // 2):
@@ -610,17 +609,15 @@
     grad_kv = None
     dqs = []
     for head in range(GROUP):
-        query = head_lanes(q_all, head).astype(LOW)
+        query = (head_lanes(q_all, head) * ADIM**-0.5).astype(LOW)
         upper = pltpu.roll(head_lanes(grad_all, head), ADIM, 1).astype(LOW)
-        scores = jnp.where(seen, dot(query, all_keys, 1, 1) * ADIM**-0.5, MASKED)
+        scores = jnp.where(seen, dot(query, all_keys, 1, 1), MASKED)
         probs = jnp.exp(scores - total_ref[:, head : head + 1])
         grad_probs = dot(upper, all_keys, 1, 1)
         inner = jnp.sum(probs * grad_probs, axis=1, keepdims=True)
         grad_scores = (probs * (grad_probs - inner)).astype(LOW)
         dqs.append(dot(grad_scores, all_keys) * ADIM**-0.5)
-        fresh = dot(grad_scores, query, 0, 0) * ADIM**-0.5 + dot(
-            probs.astype(LOW), upper, 0, 0
-        )
+        fresh = dot(grad_scores, query, 0, 0) + dot(probs.astype(LOW), upper, 0, 0)
         grad_kv = fresh if grad_kv is None else grad_kv + fresh
     for pair in range(GROUP // 2):
         both = jnp.where(lanes < ADIM, dqs[2 * pair], pltpu.roll(dqs[2 * pair + 1], ADIM, 1))
@@ -708,6 +705,26 @@
     first = jnp.broadcast_to(values[:, 2 * pair : 2 * pair + 1], shape)
     second = jnp.broadcast_to(values[:, 2 * pair + 1 : 2 * pair + 2], shape)
     return jnp.where(row_iota(shape) < HDIM, first, second)
+
+
+def head_matrix(channels):
+    shape = (LANES, channels)
+    return jnp.where(lane_iota(shape) // HDIM == row_iota(shape), 1.0, 0.0).astype(LOW)
+
+
+def two_parts(values):
+    high = values.astype(LOW)
+    return high, (values - high.astype(WIDE)).astype(LOW)
+
+
+def over_heads(values, matrix):
+    high, low = two_parts(values)
+    return dot(high, matrix) + dot(low, matrix)
+
+
+def by_heads(values, matrix):
+    high, low = two_parts(values)
+    return dot(high, matrix, 1, 1) + dot(low, matrix, 1, 1)
 
 
 def lower_ones(rows, flip):
@@ -758,8 +775,9 @@
     cum_rows, step_rows = cum.T, step.T
     last = cum[rows - 1 : rows, :]
     before_it[...] = jnp.broadcast_to(before_it[0:1, :] + last, before_it.shape)
-    tail = jnp.exp(last - cum) * step
-    grown, faded = jnp.exp(cum), jnp.exp(last)
+    matrix = head_matrix(channels)
+    tail = over_heads(jnp.exp(last - cum) * step, matrix)
+    grown, faded = over_heads(jnp.exp(cum), matrix), jnp.exp(last)
     entry, readout = bc_ref[:, :STATE], bc_ref[:, STATE:]
     cross = dot(readout, entry, 1, 1)
     shape = (rows, rows)
@@ -775,10 +793,8 @@
             mixed = (decay * cross * step_rows[head : head + 1, :]).astype(LOW)
             outs.append(dot(mixed, inputs))
         carried = dot(readout, state[block, :].astype(LOW), 1, 1)
-        y_ref[:, block] = jnp.where(lanes < HDIM, outs[0], outs[1]) + carried * over_pair(
-            grown, pair, (rows, LANES)
-        )
-        scaled = (over_pair(tail, pair, (rows, LANES)) * inputs.astype(WIDE)).astype(LOW)
+        y_ref[:, block] = jnp.where(lanes < HDIM, outs[0], outs[1]) + carried * grown[:, block]
+        scaled = (tail[:, block] * inputs.astype(WIDE)).astype(LOW)
         fresh = down_pair(faded, pair) * state[block, :] + dot(scaled, entry, 0, 0)
         state[block, :] = fresh
         parcel_ref[block, :] = fresh.astype(LOW)
@@ -840,12 +856,12 @@
 ):
     rows, channels = y_ref.shape
     readout = bc_ref[:, STATE:]
-    grown = jnp.exp(cum_ref[...])
+    grown = over_heads(jnp.exp(cum_ref[...]), head_matrix(channels))
     square = jnp.zeros((rows, 1), WIDE)
     for pair in range(channels // LANES):
         block = slice(pair * LANES, (pair + 1) * LANES)
         carried = dot(readout, parcel_ref[block, :], 1, 1)
-        y = y_ref[:, block] + over_pair(grown, pair, carried.shape) * carried
+        y = y_ref[:, block] + grown[:, block] * carried
         out_ref[:, block] = y
         skip = over_pair(heads_ref[2:3, :], pair, (1, LANES))
         gate = gate_ref[:, block]
@@ -895,7 +911,7 @@
 
     rows, channels = y_ref.shape
     readout = bc_ref[:, STATE:]
-    grown = jnp.exp(cum_ref[...])
+    grown = over_heads(jnp.exp(cum_ref[...]), head_matrix(channels))
     square = jnp.zeros((rows, 1), WIDE)
     inner = jnp.zeros((rows, 1), WIDE)
     for pair in range(channels // LANES):
@@ -928,7 +944,7 @@
         sums_ref[0:1, block] = jnp.sum(upstream * unit, axis=0, keepdims=True)
         sums_ref[1:2, block] = jnp.sum(du * inputs, axis=0, keepdims=True)
         fresh = state[block, :] + dot(
-            (over_pair(grown, pair, du.shape) * du).astype(LOW), readout, 0, 0
+            (grown[:, block] * du).astype(LOW), readout, 0, 0
         )
         state[block, :] = fresh
         parcel_ref[block, :] = fresh.astype(LOW)
@@ -978,18 +994,11 @@
     ).astype(LOW)
 
 
-def lane_sums(values):
-    first = lane_iota(values.shape) < HDIM
-    return (
-        jnp.sum(jnp.where(first, values, 0.0), axis=1, keepdims=True),
-        jnp.sum(jnp.where(first, 0.0, values), axis=1, keepdims=True),
-    )
-
-
 def scan_back_body(
     du_ref, x_ref, bc_ref, stk_ref, prior_ref, rim_ref, cum_ref, all_ref, step_ref, side_ref,
     first_ref, parcel_ref, later_ref, taps_ref, heads_ref,
     dstk_ref, drim_ref, dstep_ref, dtaps_ref, dheads_ref, padded, dact, after, behind,
+    carried_all, final_all,
 ):
     place = pl.program_id(0)
     second = jnp.where(place == 0, 1.0, 0.0).astype(WIDE)
@@ -1016,6 +1025,8 @@
     grown = jnp.exp(cum)
     decayed = jnp.exp(last - cum)
     tail = decayed * step
+    matrix = head_matrix(channels)
+    grown_all, tail_all, step_all = (over_heads(v, matrix) for v in (grown, tail, step))
     cross = dot(entry, readout, 1, 1)
     shape = (rows, rows)
     causal = row_iota(shape) <= lane_iota(shape)
@@ -1026,8 +1037,6 @@
     readout_grad = jnp.zeros((rows, STATE), WIDE)
     pulled = jnp.zeros((rows, LANES), WIDE)
     arrived = []
-    carried_sum = jnp.zeros((rows, LANES), WIDE)
-    final_sum = jnp.zeros((rows, LANES), WIDE)
     state_sum = jnp.zeros((1, LANES), WIDE)
     for pair in range(heads // 2):
         block = slice(pair * LANES, (pair + 1) * LANES)
@@ -1053,20 +1062,16 @@
             pulled = jnp.where(lanes == head, jnp.sum(dgap, axis=1, keepdims=True), pulled)
             arrived.append(jnp.sum(dgap * stepped, axis=0, keepdims=True))
         pull = jnp.where(lanes < HDIM, pulls[0], pulls[1])
-        grown_pair = over_pair(grown, pair, du.shape)
+        grown_pair = grown_all[:, block]
         grown_du = grown_pair * du
         grown_low = grown_du.astype(LOW)
         behind[block, :] = down_pair(faded, pair) * later + dot(grown_low, readout, 0, 0)
         readout_grad = readout_grad + dot(grown_low, start_low)
-        sums = lane_sums(grown_du * dot(readout, start_low, 1, 1))
-        carried_sum = jnp.where(lanes == 2 * pair, sums[0], carried_sum)
-        carried_sum = jnp.where(lanes == 2 * pair + 1, sums[1], carried_sum)
-        tail_pair = over_pair(tail, pair, du.shape)
+        carried_all[:, block] = grown_du * dot(readout, start_low, 1, 1)
+        tail_pair = tail_all[:, block]
         from_later = dot(entry, later_low, 1, 1)
         entry_grad = entry_grad + dot((tail_pair * inputs_wide).astype(LOW), later_low)
-        sums = lane_sums(inputs_wide * from_later)
-        final_sum = jnp.where(lanes == 2 * pair, sums[0], final_sum)
-        final_sum = jnp.where(lanes == 2 * pair + 1, sums[1], final_sum)
+        final_all[:, block] = inputs_wide * from_later
         product = start * later
         for k in range(2):
             total = jnp.sum(
@@ -1077,12 +1082,13 @@
             state_sum = jnp.where(small == 2 * pair + k, total, state_sum)
         skip = over_pair(heads_ref[2:3, :], pair, (1, LANES))
         dact[:, block] = (
-            skip * du + over_pair(step, pair, du.shape) * pull + tail_pair * from_later
+            skip * du + step_all[:, block] * pull + tail_pair * from_later
         )
     dcross_low = dcross.astype(LOW)
     dact[:, channels : channels + STATE] = entry_grad + dot(dcross_low, readout)
     dact[:, channels + STATE :] = readout_grad + dot(dcross_low, entry, 0, 0)
     arrived.append(jnp.zeros((LANES - heads, rows), WIDE))
+    carried_sum, final_sum = by_heads(carried_all[...], matrix), by_heads(final_all[...], matrix)
     arrived_columns = jnp.concatenate(arrived, axis=0).T
     weighted = tail * final_sum
     dcum = arrived_columns - step * pulled + carried_sum - weighted
@@ -1116,7 +1122,7 @@
         back = term if back is None else back + term
     dtaps_ref[CONV : CONV + 1, :] = jnp.sum(after[8 : 8 + rows, :], axis=0, keepdims=True)
     drim_ref[...] = back[0:8]
-    dstk_ref[...] = back[8:]
+    dstk_ref[...] = back[8:].astype(LOW)
 
 
 def scan_back(
@@ -1157,7 +1163,7 @@
             sequence_block(8, LANES),
         ],
         [
-            jax.ShapeDtypeStruct((total, width), WIDE),
+            jax.ShapeDtypeStruct((total, width), LOW),
             jax.ShapeDtypeStruct((8, width), WIDE),
             jax.ShapeDtypeStruct((total, LANES), LOW),
             jax.ShapeDtypeStruct((count, 8, width), WIDE),
@@ -1168,6 +1174,8 @@
             pltpu.VMEM((rows, width), WIDE),
             pltpu.VMEM((rows + 16, width), WIDE),
             pltpu.VMEM((channels, STATE), WIDE),
+            pltpu.VMEM((rows, channels), WIDE),
+            pltpu.VMEM((rows, channels), WIDE),
         ],
         flops=total * rows * channels * 20,
         moved=total * width * 24,
@@ -1391,7 +1399,7 @@
     )
     later = next_half(state_grads, False)
     grad_q, own_kv, sent_kv = attend_back(
-        place, queries, grad_attended, log_total, tables, kv, kv_came, rows
+        place, queries, grad_attended, log_total, tables, kv, kv_came, 2 * rows
     )
     came_kv = [next_half(sent_kv, False)]
     (later, *came_kv), grad_gate = together((later, *came_kv), grad_gate)
@@ -1405,18 +1413,19 @@
     )
     drim = scatters.step(drim)
     returned = next_half(drim[8 - CONV + 1 :], False)
-    dstk = dstk + jnp.pad(returned, ((dstk.shape[0] - CONV + 1, 0), (0, 0)))
+    last_rows = (dstk[-CONV + 1 :].astype(WIDE) + returned).astype(LOW)
+    dstk = lax.dynamic_update_slice(dstk, last_rows, (dstk.shape[0] - CONV + 1, 0))
     grad_kv = finish_keys(own_kv, came_kv, tables, rows)
-    grad_late = jnp.concatenate([dstk[:, :channels].astype(LOW), grad_kv], axis=1)
+    grad_late = jnp.concatenate([dstk[:, :channels], grad_kv], axis=1)
     grad_first = jnp.concatenate(
         [grad_gate, grad_late[:, :channels], grad_q, grad_late[:, channels:]], axis=1
     )
-    grad_side = jnp.concatenate([dstk[:, channels:].astype(LOW), grad_step], axis=1)
+    grad_side = jnp.concatenate([dstk[:, channels:], grad_step], axis=1)
     if split:
         late, tile = [grad_late, grad_side], 640
     else:
         late = [grad_gate, grad_q, grad_late[:, channels:], grad_late[:, :channels], grad_side]
-        tile = 384
+        tile = 1152
     late = jnp.concatenate(late, axis=1)
     table = scatters.add([(normed, late)], tile, split, (0, 0), functools.partial(done, 1))
     _, grad_first = together((table,), grad_first)

time: 797 us -> 783 us (0.982)
  Pallas kernels: 238 us -> 218 us
  waiting for transfers between devices: 160 us -> 168 us
    pallas_call x2, Pallas kernels: 44.3 us -> 36.1 us  [scan_back(): kernel_call(scan_back_body, (count,), [back_block(channels), back_block(c...]
    unnamed x340 -> x343, local copies, waits for them, and re-layouts: 30.1 us -> 28.9 us
  transfers between devices with their start and end apart: 108 -> 108, of which waited for: 39 -> 37; matrix products, arithmetic and copies ran while one was open for 22% -> 23% of each run, Pallas kernels for 27% -> 25%
where the time goes in v4:
time: 783 us; the launch traced here: 774 us
  Pallas kernels  218 us (28%)
  waiting for transfers between devices  168 us (21%)
  starting transfers between devices  133 us (17%)
  local copies, waits for them, and re-layouts  86.8 us (11%)
  matrix products  85.5 us (11%)
  other arithmetic  64.5 us (8%)
  between operations  17.6 us (2%)
    ppermute x48, waiting for transfers between devices, ctx_swap(): return lax.ppermute(values, 'ctx', xor_pairs(lax.axis_size('ctx'), step))  83.1 us
    dot_general x15, matrix products, dot(): lax.dot_general(a, b, (((ca,), (cb,)), ((), ())), preferred_element_type=...  45.5 us
    ppermute x48, starting transfers between devices, ctx_swap(): return lax.ppermute(values, 'ctx', xor_pairs(lax.axis_size('ctx'), step))  42.2 us
    dot_general x16, matrix products, product(): return jnp.dot(a, b, preferred_element_type=WIDE)  40 us
    pallas_call x14, Pallas kernels, once(): kernel_call(body, (1,), [whole(v.shape) for v in operands], [whole(shape)...  38.5 us
    pallas_call x2, Pallas kernels, scan_back(): kernel_call(scan_back_body, (count,), [back_block(channels), back_block(c...  36.1 us
    ppermute x12, waiting for transfers between devices, next_half(): lax.ppermute(x, 'ctx', [(i, i + 1) if forward else (i + 1, i) for i in fi...  34.2 us
    ppermute x13, starting transfers between devices, tp_peer(): return lax.ppermute(x, 'tp', xor_pairs(lax.axis_size('tp'), 1))  32.7 us
  transfers between devices with their start and end apart: 108, of which 37 were waited for; matrix products, arithmetic and copies ran while one was open for 23% of the time, Pallas kernels for 25%

profile of v4, /device:TPU:1, one launch (start us, length us, event | category | flops | bytes accessed | tf_op | source)
XLA Modules:
  0.0 773.5 jit_solution(8435013702716160697)
XLA Ops:
  21.2 4.0 collective-permute-done.2
  34.1 3.9 collective-permute-done.1
  50.9 3.4 pad_maximum_fusion.3
  56.6 10.8 %collective-permute-done.7 = bf16[4,64,1920]{2,1,0:T(8,128)(2,1)} collective-permute-done((bf16[4,64,1920]{2,1,0:T(8,128)(2,1)}, bf16[4,64,1920]{2,1,0:T(8,128)(2,1)}, u32[]{:S(2)}, u32[]{:S(2)}) %collective-permute-start.7) | collective-permute-done | bytes 983072 | tf_op jit(solution)/shard_map/ppermute | solution.py:134
  67.4 7.1 collective-permute-start.9
  81.9 6.8 collective-permute-done.12
  89.6 6.6 fusion.72.rows_ref.zx_ref.gate_ref
  119.9 9.2 %shard_map.265 = (bf16[512,1024]{1,0:T(8,128)(2,1)}, bf16[512,768]{1,0:T(8,128)(2,1)}, bf16[512,256]{1,0:T(8,128)(2,1)}, f32[512,768]{1,0:T(8,128)}, f32[768,128...) custom-call(f32[512,1920]{1,0:T(8,128)} %fusion.72.rows_ref.zx_ref.gate, ...), custom_call_target="tpu_custom_call" | custom-call | flops 805306368 | bytes 8388608 | tf_op jit(solution)/shard_map/pallas_call | solution.py:812
  131.2 6.2 shard_map.264
  137.4 16.9 %collective-permute-done.16.parcel_ref = bf16[784,128]{1,0:T(8,128)(2,1)S(1)} collective-permute-done((bf16[784,128]{1,0:T(8,128)(2,1)}, bf16[784,128]{1,0:T(8,128)(2,1)S(1)}, u32[]{:S(2)}, u32[]{:S(2)}) %collective-permute-start.16) | collective-permute-done | bytes 200736 | tf_op jit(solution)/shard_map/ppermute | solution.py:72
  163.3 4.9 shard_map.266
  172.6 4.2 collective-permute-done.20
  178.4 4.1 pad_maximum_fusion
  194.8 16.0 %collective-permute-done.22 = bf16[4,64,1920]{2,1,0:T(8,128)(2,1)S(1)} collective-permute-done((bf16[4,64,1920]{2,1,0:T(8,128)(2,1)S(1)}, bf16[4,64,1920]{2,1,0:T(8,128)(2,1)S(1)}, u32[]{:S(2)}, u32[]{:S(2)}) %collective-permute-start.22) | collective-permute-done | bytes 983072 | tf_op jit(solution)/shard_map/ppermute | solution.py:134
  213.0 3.9 convolution_convert_fusion.2
  221.2 9.8 %collective-permute-done.25 = bf16[4,64,896]{2,1,0:T(8,128)(2,1)S(1)} collective-permute-done((bf16[4,64,896]{2,1,0:T(8,128)(2,1)S(1)}, bf16[4,64,896]{2,1,0:T(8,128)(2,1)S(1)}, u32[]{:S(2)}, u32[]{:S(2)}) %collective-permute-start.25) | collective-permute-done | bytes 458784 | tf_op jit(solution)/shard_map/ppermute | solution.py:134
  257.2 9.6 %shard_map.269 = (bf16[512,1024]{1,0:T(8,128)(2,1)}, bf16[512,768]{1,0:T(8,128)(2,1)}, bf16[512,256]{1,0:T(8,128)(2,1)}, f32[512,768]{1,0:T(8,128)}, f32[768,128...) custom-call(f32[512,1920]{1,0:T(8,128)} %copy-done.2, ...), custom_call_target="tpu_custom_call" | custom-call | flops 805306368 | bytes 8388608 | tf_op jit(solution)/shard_map/pallas_call | solution.py:812
  266.8 3.4 collective-permute-start.31
  270.3 6.2 shard_map.268
  282.6 4.6 shard_map.270
  289.5 5.6 all-gather.17.cloned.1.call-done
  296.2 3.9 convolution_convert_fusion.1
  304.0 4.0 fusion.176
  318.2 6.3 shard_map.271
  324.8 4.3 convolution_convert_fusion
  329.5 5.9 convolution_convert_fusion.3.own_ref
  340.0 3.9 collective-permute-start.39
  344.8 4.6 shard_map.272
  351.0 6.9 shard_map.273
  362.9 7.5 shard_map.274
  374.2 9.1 %shard_map.275 = (bf16[512,256]{1,0:T(8,128)(2,1)}, f32[512,128]{1,0:T(8,128)}, bf16[512,128]{1,0:T(8,128)(2,1)}) custom-call(s32[1]{0:T(128)} %bitcast.23.place_ref, bf16[512,256]{1,0:T(8,128)(2,1)} %get-tuple-element.314.q_ref, bf16[512,256]{1,0:T(8,128)(2,1)} %convolution_convert_fusion.5.grad_ref, f32[512,128]{1,0:T(8,128)} %get-tuple-element.354.total_ref, ...), custom_call_target="tpu_custom_call" | custom-call | flops 2684354560 | bytes 2097152 | tf_op jit(solution)/shard_map/pallas_call | solution.py:643
  384.8 5.7 collective-permute-done.45.refs_0_
  399.2 18.1 %shard_map.277 = (bf16[512,1024]{1,0:T(8,128)(2,1)}, f32[8,1024]{1,0:T(8,128)}, bf16[512,128]{1,0:T(8,128)(2,1)}, f32[2,8,1024]{2,1,0:T(8,128)}, f32[2,8,128]{2,1,0:T(8,128)}) custom-call(f32[512,768]{1,0:T(8,128)} %get-tuple-element.362.du_ref, bf16[512,768]{1,0:T(8,128)(2,1)} %get-tuple-element.329.x_ref, bf16[512,256]{1,0:T(8,128)(2,1)} %get-tuple-element.328.bc_ref, ...), custom_call_target="tpu_custom_call" | custom-call | flops 2013265920 | bytes 12582912 | tf_op jit(solution)/shard_map/pallas_call | solution.py:1138
  418.7 3.6 shard_map.279
  430.5 6.7 shard_map.280
  439.3 4.6 add_convert_fusion.1.own_ref
  443.9 3.6 collective-permute-start.53
  452.1 4.6 shard_map.281
  456.7 10.1 %collective-permute-done.48.from_y_ref = bf16[128,1024]{1,0:T(8,128)(2,1)S(1)} collective-permute-done((bf16[128,1024]{1,0:T(8,128)(2,1)S(1)}, bf16[128,1024]{1,0:T(8,128)(2,1)S(1)}, u32[]{:S(2)}, u32[]{:S(2)}) %collective-permute-start.48) | collective-permute-done | bytes 262176 | tf_op jit(solution)/shard_map/ppermute | solution.py:134
  476.1 3.8 multiply_convert_fusion.1
  481.5 6.3 shard_map.284
  489.4 4.6 fusion.35.own_ref
  494.0 4.9 collective-permute-start.54
  508.4 4.7 shard_map.285
  513.1 3.8 collective-permute-done.71.last_x_ref
  516.9 3.9 shard_map.296
  521.3 7.0 shard_map.286
  531.9 9.0 %shard_map.288 = (bf16[512,256]{1,0:T(8,128)(2,1)}, f32[512,128]{1,0:T(8,128)}, bf16[512,128]{1,0:T(8,128)(2,1)}) custom-call(s32[1]{0:T(128)} %bitcast.23.place_ref, bf16[512,256]{1,0:T(8,128)(2,1)} %get-tuple-element.278.q_ref, bf16[512,256]{1,0:T(8,128)(2,1)} %convolution_convert_fusion.4.grad_ref, f32[512,128]{1,0:T(8,128)} %get-tuple-element.412.total_ref, ...), custom_call_target="tpu_custom_call" | custom-call | flops 2684354560 | bytes 2097152 | tf_op jit(solution)/shard_map/pallas_call | solution.py:643
  542.3 3.5 fusion.28.dn_ref
  545.8 7.5 shard_map.287
  555.5 5.2 collective-permute-done.57.later_ref
  563.1 3.8 shard_map.290
  582.8 18.0 %shard_map.291 = (bf16[512,1024]{1,0:T(8,128)(2,1)}, f32[8,1024]{1,0:T(8,128)}, bf16[512,128]{1,0:T(8,128)(2,1)}, f32[2,8,1024]{2,1,0:T(8,128)}, f32[2,8,128]{2,1,0:T(8,128)}) custom-call(f32[512,768]{1,0:T(8,128)} %get-tuple-element.424.du_ref, bf16[512,768]{1,0:T(8,128)(2,1)} %get-tuple-element.294.x_ref, bf16[512,256]{1,0:T(8,128)(2,1)} %get-tuple-element.293.bc_ref, ...), custom_call_target="tpu_custom_call" | custom-call | flops 2013265920 | bytes 12582912 | tf_op jit(solution)/shard_map/pallas_call | solution.py:1138
  606.9 3.7 shard_map.292
  619.1 4.6 shard_map.295
  623.7 5.1 add_convert_fusion.own_ref
  628.8 4.4 collective-permute-start.70
  640.6 4.6 shard_map.297
  653.0 10.4 %collective-permute-done.64.from_x_ref = bf16[128,1024]{1,0:T(8,128)(2,1)S(1)} collective-permute-done((bf16[128,1024]{1,0:T(8,128)(2,1)S(1)}, bf16[128,1024]{1,0:T(8,128)(2,1)S(1)}, u32[]{:S(2)}, u32[]{:S(2)}) %collective-permute-start.64) | collective-permute-done | bytes 262176 | tf_op jit(solution)/shard_map/ppermute | solution.py:134
  677.8 3.9 collective-permute-start.76
  684.2 5.0 collective-permute-done.80
  712.5 12.0 %collective-permute-done.88 = f32[192,128]{1,0:T(8,128)S(1)} collective-permute-done((f32[192,128]{1,0:T(8,128)S(1)}, f32[192,128]{1,0:T(8,128)S(1)}, u32[]{:S(2)}, u32[]{:S(2)}) %collective-permute-start.88) | collective-permute-done | bytes 98336 | tf_op jit(solution)/shard_map/ppermute | solution.py:476
  748.8 4.0 collective-permute-done.96
  752.9 4.6 collective-permute-start.97
  (829 shorter events, 346.8 us)
Async XLA Ops:
  7.2 108.4 %all-gather.11.cloned.1.call-start = ((), (), s32[]{:S(2)}) async-start(), calls=%async_computation.10 | async-start | bytes 1966080 | tf_op jit(solution)/shard_map/all_gather | solution.py:197
  10.6 27.4 %collective-permute-start.5 = (bf16[1,64,4096]{2,1,0:T(8,128)(2,1)}, bf16[1,64,4096]{2,1,0:T(8,128)(2,1)S(1)}, u32[]{:S(2)}, u32[]{:S(2)}) collective-permute-start(bf16[1,64,4096]{2,1,0:T(8,128)(2,1)} %maximum_bitcast_fusion), channel_id=1, source_target_pairs={{0,2},{2,0},{4,6},{6,4},{1,3},{3,1},{5,7},{7,5},{8,10},{10,8},{12,... | collective-permute-start | bytes 1572872 | tf_op jit(solution)/shard_map/ppermute | solution.py:134
  12.7 25.4 %collective-permute-start.6 = (bf16[1,64,4096]{2,1,0:T(8,128)(2,1)}, bf16[1,64,4096]{2,1,0:T(8,128)(2,1)S(1)}, u32[]{:S(2)}, u32[]{:S(2)}) collective-permute-start(bf16[1,64,4096]{2,1,0:T(8,128)(2,1)} %maximum_bitcast_fusion), channel_id=1, source_target_pairs={{0,4},{2,6},{4,0},{6,2},{1,5},{3,7},{5,1},{7,3},{8,12},{10,14},{12... | collective-permute-start | bytes 1572872 | tf_op jit(solution)/shard_map/ppermute | solution.py:134
  18.6 15.5 %collective-permute-start.4 = (bf16[64,1920]{1,0:T(8,128)(2,1)}, bf16[64,1920]{1,0:T(8,128)(2,1)}, u32[]{:S(2)}, u32[]{:S(2)}) collective-permute-start(bf16[64,1920]{1,0:T(8,128)(2,1)} %pad_maximum_fusion.27), channel_id=1, source_target_pairs={{0,24},{8,16},{16,8},{24,0},{1,25},{9,17},{17,9},{25,1},{2,26},{10... | collective-permute-start | bytes 737288 | tf_op jit(solution)/shard_map/ppermute | solution.py:181
  43.2 118.7 %all-gather.13.cloned.1.call-start = ((), (), s32[]{:S(2)}) async-start(), calls=%async_computation.11 | async-start | bytes 1884160 | tf_op jit(solution)/shard_map/all_gather | solution.py:198
  44.8 22.6 %collective-permute-start.7 = (bf16[4,64,1920]{2,1,0:T(8,128)(2,1)}, bf16[4,64,1920]{2,1,0:T(8,128)(2,1)}, u32[]{:S(2)}, u32[]{:S(2)}) collective-permute-start(bf16[4,64,1920]{2,1,0:T(8,128)(2,1)} %bitcast_dynamic-update-slice_fusion), channel_id=1, source_target_pairs={{0,2},{2,0},{4,6},{6,4},{1,3},{3,1},{5,7},{7,5},{8,10},{10,8},{12,... | collective-permute-start | bytes 2949128 | tf_op jit(solution)/shard_map/ppermute | solution.py:134
  46.2 21.2 %collective-permute-start.8 = (bf16[4,64,1920]{2,1,0:T(8,128)(2,1)}, bf16[4,64,1920]{2,1,0:T(8,128)(2,1)}, u32[]{:S(2)}, u32[]{:S(2)}) collective-permute-start(bf16[4,64,1920]{2,1,0:T(8,128)(2,1)} %bitcast_dynamic-update-slice_fusion), channel_id=1, source_target_pairs={{0,4},{2,6},{4,0},{6,2},{1,5},{3,7},{5,1},{7,3},{8,12},{10,14},{12... | collective-permute-start | bytes 2949128 | tf_op jit(solution)/shard_map/ppermute | solution.py:134
  46.6 166.4 %all-gather.15.cloned.1.call-start = ((), (), s32[]{:S(2)}) async-start(), calls=%async_computation.12 | async-start | bytes 2621440 | tf_op jit(solution)/shard_map/all_gather | solution.py:1310
  75.6 13.6 %collective-permute-start.13 = (bf16[4,64,1024]{2,1,0:T(8,128)(2,1)S(1)}, bf16[4,64,1024]{2,1,0:T(8,128)(2,1)S(1)}, u32[]{:S(2)}, u32[]{:S(2)}) collective-permute-start(bf16[4,64,1024]{2,1,0:T(8,128)(2,1)S(1)} %slice.527), channel_id=1, source_target_pairs={{0,2},{2,0},{4,6},{6,4},{1,3},{3,1},{5,7},{7,5},{8,10},{10,8},{12,... | collective-permute-start | bytes 1572872 | tf_op jit(solution)/shard_map/ppermute | solution.py:134
  96.2 181.7 %all-gather.19.cloned.1.call-start = ((), (), s32[]{:S(2)}) async-start(), calls=%async_computation.14 | async-start | bytes 5242880 | tf_op jit(solution)/shard_map/all_gather | solution.py:1310
  115.6 38.6 %collective-permute-start.17 = (bf16[4,64,3072]{2,1,0:T(8,128)(2,1)}, bf16[4,64,3072]{2,1,0:T(8,128)(2,1)}, u32[]{:S(2)}, u32[]{:S(2)}) collective-permute-start(bf16[4,64,3072]{2,1,0:T(8,128)(2,1)} %bitcast.300), channel_id=1, source_target_pairs={{0,2},{2,0},{4,6},{6,4},{1,3},{3,1},{5,7},{7,5},{8,10},{10,8},{12,... | collective-permute-start | bytes 4718600 | tf_op jit(solution)/shard_map/ppermute | solution.py:134
  117.8 37.2 %collective-permute-start.18 = (bf16[4,64,3072]{2,1,0:T(8,128)(2,1)}, bf16[4,64,3072]{2,1,0:T(8,128)(2,1)}, u32[]{:S(2)}, u32[]{:S(2)}) collective-permute-start(bf16[4,64,3072]{2,1,0:T(8,128)(2,1)} %bitcast.301), channel_id=1, source_target_pairs={{0,4},{2,6},{4,0},{6,2},{1,5},{3,7},{5,1},{7,3},{8,12},{10,14},{12... | collective-permute-start | bytes 4718600 | tf_op jit(solution)/shard_map/ppermute | solution.py:134
  129.1 25.1 %collective-permute-start.16 = (bf16[784,128]{1,0:T(8,128)(2,1)}, bf16[784,128]{1,0:T(8,128)(2,1)S(1)}, u32[]{:S(2)}, u32[]{:S(2)}) collective-permute-start(bf16[784,128]{1,0:T(8,128)(2,1)} %get-tuple-element.289), channel_id=1, source_target_pairs={{0,2},{4,6},{1,3},{5,7},{8,10},{12,14},{9,11},{13,15},{16,18},{20,... | collective-permute-start | bytes 602120 | tf_op jit(solution)/shard_map/ppermute | solution.py:72
  131.1 164.0 %all-gather.17.cloned.1.call-start = ((), (), s32[]{:S(2)}) async-start(), calls=%async_computation.13 | async-start | bytes 2621440 | tf_op jit(solution)/shard_map/all_gather | solution.py:1310
  156.1 16.4 %collective-permute-start.19 = (bf16[4,64,1536]{2,1,0:T(8,128)(2,1)S(1)}, bf16[4,64,1536]{2,1,0:T(8,128)(2,1)}, u32[]{:S(2)}, u32[]{:S(2)}) collective-permute-start(bf16[4,64,1536]{2,1,0:T(8,128)(2,1)S(1)} %slice.540), channel_id=1, source_target_pairs={{0,4},{2,6},{4,0},{6,2},{1,5},{3,7},{5,1},{7,3},{8,12},{10,14},{12... | collective-permute-start | bytes 2359304 | tf_op jit(solution)/shard_map/ppermute | solution.py:134
  159.2 17.6 %collective-permute-start.20 = (bf16[4,64,1536]{2,1,0:T(8,128)(2,1)}, bf16[4,64,1536]{2,1,0:T(8,128)(2,1)}, u32[]{:S(2)}, u32[]{:S(2)}) collective-permute-start(bf16[4,64,1536]{2,1,0:T(8,128)(2,1)} %slice.541), channel_id=1, source_target_pairs={{0,2},{2,0},{4,6},{6,4},{1,3},{3,1},{5,7},{7,5},{8,10},{10,8},{12,... | collective-permute-start | bytes 2359304 | tf_op jit(solution)/shard_map/ppermute | solution.py:134
  187.3 23.5 %collective-permute-start.22 = (bf16[4,64,1920]{2,1,0:T(8,128)(2,1)S(1)}, bf16[4,64,1920]{2,1,0:T(8,128)(2,1)S(1)}, u32[]{:S(2)}, u32[]{:S(2)}) collective-permute-start(bf16[4,64,1920]{2,1,0:T(8,128)(2,1)S(1)} %slice.671), channel_id=1, source_target_pairs={{0,2},{2,0},{4,6},{6,4},{1,3},{3,1},{5,7},{7,5},{8,10},{10,8},{12,... | collective-permute-start | bytes 2949128 | tf_op jit(solution)/shard_map/ppermute | solution.py:134
  188.8 23.1 %collective-permute-start.23 = (bf16[4,64,1920]{2,1,0:T(8,128)(2,1)S(1)}, bf16[4,64,1920]{2,1,0:T(8,128)(2,1)S(1)}, u32[]{:S(2)}, u32[]{:S(2)}) collective-permute-start(bf16[4,64,1920]{2,1,0:T(8,128)(2,1)S(1)} %slice.671), channel_id=1, source_target_pairs={{0,4},{2,6},{4,0},{6,2},{1,5},{3,7},{5,1},{7,3},{8,12},{10,14},{12... | collective-permute-start | bytes 2949128 | tf_op jit(solution)/shard_map/ppermute | solution.py:134
  216.9 15.6 %collective-permute-start.24 = (bf16[512,1024]{1,0:T(8,128)(2,1)}, bf16[512,1024]{1,0:T(8,128)(2,1)}, u32[]{:S(2)}, u32[]{:S(2)}) collective-permute-start(bf16[512,1024]{1,0:T(8,128)(2,1)} %convolution_convert_fusion.2), channel_id=1, source_target_pairs={{0,1},{1,0},{2,3},{3,2},{4,5},{5,4},{6,7},{7,6},{8,9},{9,8},{10,11... | collective-permute-start | bytes 3145736 | tf_op jit(solution)/shard_map/ppermute | solution.py:101
  218.7 13.6 %collective-permute-start.26 = (bf16[4,64,1024]{2,1,0:T(8,128)(2,1)S(1)}, bf16[4,64,1024]{2,1,0:T(8,128)(2,1)S(1)}, u32[]{:S(2)}, u32[]{:S(2)}) collective-permute-start(bf16[4,64,1024]{2,1,0:T(8,128)(2,1)S(1)} %slice.548), channel_id=1, source_target_pairs={{0,2},{2,0},{4,6},{6,4},{1,3},{3,1},{5,7},{7,5},{8,10},{10,8},{12,... | collective-permute-start | bytes 1572872 | tf_op jit(solution)/shard_map/ppermute | solution.py:134
  221.2 196.1 %reduce-scatter.6.cloned.1.call-start = ((), (), s32[]{:S(2)}) async-start(), calls=%async_computation.5 | async-start | bytes 5242880 | tf_op jit(solution)/shard_map/reduce_scatter | solution.py:412
  250.0 27.8 %collective-permute-start.32 = (bf16[4,64,1024]{2,1,0:T(8,128)(2,1)S(1)}, bf16[4,64,1024]{2,1,0:T(8,128)(2,1)S(1)}, u32[]{:S(2)}, u32[]{:S(2)}) collective-permute-start(bf16[4,64,1024]{2,1,0:T(8,128)(2,1)S(1)} %slice.682), channel_id=1, source_target_pairs={{0,2},{2,0},{4,6},{6,4},{1,3},{3,1},{5,7},{7,5},{8,10},{10,8},{12,... | collective-permute-start | bytes 1572872 | tf_op jit(solution)/shard_map/ppermute | solution.py:134
  252.1 25.7 %collective-permute-start.33 = (bf16[4,64,1024]{2,1,0:T(8,128)(2,1)S(1)}, bf16[4,64,1024]{2,1,0:T(8,128)(2,1)}, u32[]{:S(2)}, u32[]{:S(2)}) collective-permute-start(bf16[4,64,1024]{2,1,0:T(8,128)(2,1)S(1)} %slice.682), channel_id=1, source_target_pairs={{0,4},{2,6},{4,0},{6,2},{1,5},{3,7},{5,1},{7,3},{8,12},{10,14},{12... | collective-permute-start | bytes 1572872 | tf_op jit(solution)/shard_map/ppermute | solution.py:134
  254.1 22.4 %collective-permute-start.29 = (bf16[256,512]{1,0:T(8,128)(2,1)S(1)}, bf16[256,512]{1,0:T(8,128)(2,1)S(1)}, u32[]{:S(2)}, u32[]{:S(2)}) collective-permute-start(bf16[256,512]{1,0:T(8,128)(2,1)S(1)} %get-tuple-element.640), channel_id=1, source_target_pairs={{0,0},{4,2},{2,4},{6,6},{1,1},{5,3},{3,5},{7,7},{8,8},{12,10},{10,... | collective-permute-start | bytes 786440 | tf_op jit(solution)/shard_map/ppermute | solution.py:81
  254.8 21.7 %collective-permute-start.30 = (bf16[256,512]{1,0:T(8,128)(2,1)S(1)}, bf16[256,512]{1,0:T(8,128)(2,1)S(1)}, u32[]{:S(2)}, u32[]{:S(2)}) collective-permute-start(bf16[256,512]{1,0:T(8,128)(2,1)S(1)} %get-tuple-element.639), channel_id=1, source_target_pairs={{2,0},{6,2},{0,4},{4,6},{3,1},{7,3},{1,5},{5,7},{10,8},{14,10},{8,... | collective-permute-start | bytes 786440 | tf_op jit(solution)/shard_map/ppermute | solution.py:82
  277.9 17.2 %collective-permute-start.34 = (bf16[4,64,512]{2,1,0:T(8,128)(2,1)S(1)}, bf16[4,64,512]{2,1,0:T(8,128)(2,1)}, u32[]{:S(2)}, u32[]{:S(2)}) collective-permute-start(bf16[4,64,512]{2,1,0:T(8,128)(2,1)S(1)} %slice.563), channel_id=1, source_target_pairs={{0,4},{2,6},{4,0},{6,2},{1,5},{3,7},{5,1},{7,3},{8,12},{10,14},{12... | collective-permute-start | bytes 786440 | tf_op jit(solution)/shard_map/ppermute | solution.py:134
  281.0 14.1 %collective-permute-start.35 = (bf16[4,64,512]{2,1,0:T(8,128)(2,1)}, bf16[4,64,512]{2,1,0:T(8,128)(2,1)}, u32[]{:S(2)}, u32[]{:S(2)}) collective-permute-start(bf16[4,64,512]{2,1,0:T(8,128)(2,1)} %slice.564), channel_id=1, source_target_pairs={{0,2},{2,0},{4,6},{6,4},{1,3},{3,1},{5,7},{7,5},{8,10},{10,8},{12,... | collective-permute-start | bytes 786440 | tf_op jit(solution)/shard_map/ppermute | solution.py:134
  324.6 181.8 %reduce-scatter.14.cloned.1.call-start = ((), (), s32[]{:S(2)}) async-start(), calls=%async_computation.9 | async-start | bytes 1310720 | tf_op jit(solution)/shard_map/reduce_scatter | solution.py:375
  357.9 32.6 %collective-permute-start.42 = (bf16[512,1024]{1,0:T(8,128)(2,1)}, bf16[512,1024]{1,0:T(8,128)(2,1)S(1)}, u32[]{:S(2)}, u32[]{:S(2)}) collective-permute-start(bf16[512,1024]{1,0:T(8,128)(2,1)} %get-tuple-element.349), channel_id=1, source_target_pairs={{0,4},{2,6},{4,0},{6,2},{1,5},{3,7},{5,1},{7,3},{8,12},{10,14},{12... | collective-permute-start | bytes 3145736 | tf_op jit(solution)/shard_map/ppermute | solution.py:134
  359.1 31.4 %collective-permute-start.43 = (bf16[512,1024]{1,0:T(8,128)(2,1)}, bf16[512,1024]{1,0:T(8,128)(2,1)S(1)}, u32[]{:S(2)}, u32[]{:S(2)}) collective-permute-start(bf16[512,1024]{1,0:T(8,128)(2,1)} %get-tuple-element.350), channel_id=1, source_target_pairs={{0,2},{2,0},{4,6},{6,4},{1,3},{3,1},{5,7},{7,5},{8,10},{10,8},{12,... | collective-permute-start | bytes 3145736 | tf_op jit(solution)/shard_map/ppermute | solution.py:134
  370.5 20.0 %collective-permute-start.44 = (bf16[784,128]{1,0:T(8,128)(2,1)}, bf16[784,128]{1,0:T(8,128)(2,1)S(1)}, u32[]{:S(2)}, u32[]{:S(2)}) collective-permute-start(bf16[784,128]{1,0:T(8,128)(2,1)} %get-tuple-element.353), channel_id=1, source_target_pairs={{2,0},{6,4},{3,1},{7,5},{10,8},{14,12},{11,9},{15,13},{18,16},{22,... | collective-permute-start | bytes 602120 | tf_op jit(solution)/shard_map/ppermute | solution.py:72
  394.9 22.3 %collective-permute-start.46 = (bf16[256,1024]{1,0:T(8,128)(2,1)}, bf16[256,1024]{1,0:T(8,128)(2,1)S(1)}, u32[]{:S(2)}, u32[]{:S(2)}) collective-permute-start(bf16[256,1024]{1,0:T(8,128)(2,1)} %get-tuple-element.360), channel_id=1, source_target_pairs={{0,2},{2,0},{4,6},{6,4},{1,3},{3,1},{5,7},{7,5},{8,10},{10,8},{12,... | collective-permute-start | bytes 1572872 | tf_op jit(solution)/shard_map/ppermute | solution.py:134
  394.9 22.3 %collective-permute-start.47 = (bf16[256,1024]{1,0:T(8,128)(2,1)}, bf16[256,1024]{1,0:T(8,128)(2,1)S(1)}, u32[]{:S(2)}, u32[]{:S(2)}) collective-permute-start(bf16[256,1024]{1,0:T(8,128)(2,1)} %get-tuple-element.361), channel_id=1, source_target_pairs={{0,4},{2,6},{4,0},{6,2},{1,5},{3,7},{5,1},{7,3},{8,12},{10,14},{12... | collective-permute-start | bytes 1572872 | tf_op jit(solution)/shard_map/ppermute | solution.py:134
  437.2 32.2 %collective-permute-start.51 = (bf16[512,1152]{1,0:T(8,128)(2,1)}, bf16[512,1152]{1,0:T(8,128)(2,1)S(1)}, u32[]{:S(2)}, u32[]{:S(2)}) collective-permute-start(bf16[512,1152]{1,0:T(8,128)(2,1)} %get-tuple-element.383), channel_id=1, source_target_pairs={{0,4},{2,6},{4,0},{6,2},{1,5},{3,7},{5,1},{7,3},{8,12},{10,14},{12... | collective-permute-start | bytes 3538952 | tf_op jit(solution)/shard_map/ppermute | solution.py:134
  439.2 30.2 %collective-permute-start.52 = (bf16[512,1152]{1,0:T(8,128)(2,1)}, bf16[512,1152]{1,0:T(8,128)(2,1)S(1)}, u32[]{:S(2)}, u32[]{:S(2)}) collective-permute-start(bf16[512,1152]{1,0:T(8,128)(2,1)} %get-tuple-element.384), channel_id=1, source_target_pairs={{0,2},{2,0},{4,6},{6,4},{1,3},{3,1},{5,7},{7,5},{8,10},{10,8},{12,... | collective-permute-start | bytes 3538952 | tf_op jit(solution)/shard_map/ppermute | solution.py:134
  447.5 156.2 %reduce-scatter.8.cloned.1.call-start = ((), (), s32[]{:S(2)}) async-start(), calls=%async_computation.6 | async-start | bytes 5242880 | tf_op jit(solution)/shard_map/reduce_scatter | solution.py:412
  447.6 19.2 %collective-permute-start.48 = (bf16[128,1024]{1,0:T(8,128)(2,1)S(1)}, bf16[128,1024]{1,0:T(8,128)(2,1)S(1)}, u32[]{:S(2)}, u32[]{:S(2)}) collective-permute-start(bf16[128,1024]{1,0:T(8,128)(2,1)S(1)} %get-tuple-element.622), channel_id=1, source_target_pairs={{0,4},{2,6},{4,0},{6,2},{1,5},{3,7},{5,1},{7,3},{8,12},{10,14},{12... | collective-permute-start | bytes 786440 | tf_op jit(solution)/shard_map/ppermute | solution.py:134
  448.5 20.9 %collective-permute-start.49 = (bf16[128,1024]{1,0:T(8,128)(2,1)S(1)}, bf16[128,1024]{1,0:T(8,128)(2,1)S(1)}, u32[]{:S(2)}, u32[]{:S(2)}) collective-permute-start(bf16[128,1024]{1,0:T(8,128)(2,1)S(1)} %get-tuple-element.621), channel_id=1, source_target_pairs={{0,2},{2,0},{4,6},{6,4},{1,3},{3,1},{5,7},{7,5},{8,10},{10,8},{12,... | collective-permute-start | bytes 786440 | tf_op jit(solution)/shard_map/ppermute | solution.py:134
  487.9 125.1 %reduce-scatter.12.cloned.1.call-start = ((), (), s32[]{:S(2)}) async-start(), calls=%async_computation.8 | async-start | bytes 1474560 | tf_op jit(solution)/shard_map/reduce_scatter | solution.py:375
  494.0 13.4 %collective-permute-start.54 = (bf16[512,1024]{1,0:T(8,128)(2,1)S(1)}, bf16[512,1024]{1,0:T(8,128)(2,1)S(1)}, u32[]{:S(2)}, u32[]{:S(2)}) collective-permute-start(bf16[512,1024]{1,0:T(8,128)(2,1)S(1)} %fusion.35.own_ref), channel_id=1, source_target_pairs={{0,1},{1,0},{2,3},{3,2},{4,5},{5,4},{6,7},{7,6},{8,9},{9,8},{10,11... | collective-permute-start | bytes 3145736 | tf_op jit(solution)/shard_map/ppermute | solution.py:101
  498.8 18.0 %collective-permute-start.73 = (bf16[256,1152]{1,0:T(8,128)(2,1)}, bf16[256,1152]{1,0:T(8,128)(2,1)}, u32[]{:S(2)}, u32[]{:S(2)}) collective-permute-start(bf16[256,1152]{1,0:T(8,128)(2,1)} %get-tuple-element.397), channel_id=1, source_target_pairs={{0,2},{2,0},{4,6},{6,4},{1,3},{3,1},{5,7},{7,5},{8,10},{10,8},{12,... | collective-permute-start | bytes 1769480 | tf_op jit(solution)/shard_map/ppermute | solution.py:134
  498.8 18.0 %collective-permute-start.74 = (bf16[256,1152]{1,0:T(8,128)(2,1)}, bf16[256,1152]{1,0:T(8,128)(2,1)}, u32[]{:S(2)}, u32[]{:S(2)}) collective-permute-start(bf16[256,1152]{1,0:T(8,128)(2,1)} %get-tuple-element.398), channel_id=1, source_target_pairs={{0,4},{2,6},{4,0},{6,2},{1,5},{3,7},{5,1},{7,3},{8,12},{10,14},{12... | collective-permute-start | bytes 1769480 | tf_op jit(solution)/shard_map/ppermute | solution.py:134
  503.4 13.4 %collective-permute-start.71 = (bf16[64,1024]{1,0:T(8,128)(2,1)S(1)}, bf16[64,1024]{1,0:T(8,128)(2,1)S(1)}, u32[]{:S(2)}, u32[]{:S(2)}) collective-permute-start(bf16[64,1024]{1,0:T(8,128)(2,1)S(1)} %copy-done.150), channel_id=1, source_target_pairs={{0,2},{2,0},{4,6},{6,4},{1,3},{3,1},{5,7},{7,5},{8,10},{10,8},{12,... | collective-permute-start | bytes 393224 | tf_op jit(solution)/shard_map/ppermute | solution.py:134
  520.8 142.6 %reduce-scatter.10.cloned.1.call-start = ((), (), s32[]{:S(2)}) async-start(), calls=%async_computation.7 | async-start | bytes 1310720 | tf_op jit(solution)/shard_map/reduce_scatter | solution.py:375
  528.4 39.5 %collective-permute-start.55 = (bf16[512,1024]{1,0:T(8,128)(2,1)}, bf16[512,1024]{1,0:T(8,128)(2,1)S(1)}, u32[]{:S(2)}, u32[]{:S(2)}) collective-permute-start(bf16[512,1024]{1,0:T(8,128)(2,1)} %get-tuple-element.407), channel_id=1, source_target_pairs={{0,4},{2,6},{4,0},{6,2},{1,5},{3,7},{5,1},{7,3},{8,12},{10,14},{12... | collective-permute-start | bytes 3145736 | tf_op jit(solution)/shard_map/ppermute | solution.py:134
  528.5 39.4 %collective-permute-start.56 = (bf16[512,1024]{1,0:T(8,128)(2,1)}, bf16[512,1024]{1,0:T(8,128)(2,1)S(1)}, u32[]{:S(2)}, u32[]{:S(2)}) collective-permute-start(bf16[512,1024]{1,0:T(8,128)(2,1)} %get-tuple-element.408), channel_id=1, source_target_pairs={{0,2},{2,0},{4,6},{6,4},{1,3},{3,1},{5,7},{7,5},{8,10},{10,8},{12,... | collective-permute-start | bytes 3145736 | tf_op jit(solution)/shard_map/ppermute | solution.py:134
  541.0 14.6 %collective-permute-start.58 = (bf16[512,128]{1,0:T(8,128)(2,1)}, bf16[512,128]{1,0:T(8,128)(2,1)S(1)}, u32[]{:S(2)}, u32[]{:S(2)}) collective-permute-start(bf16[512,128]{1,0:T(8,128)(2,1)} %get-tuple-element.413), channel_id=1, source_target_pairs={{2,0},{6,4},{3,1},{7,5},{10,8},{14,12},{11,9},{15,13},{18,16},{22,... | collective-permute-start | bytes 393224 | tf_op jit(solution)/shard_map/ppermute | solution.py:72
  566.9 36.7 %collective-permute-start.61 = (bf16[512,512]{1,0:T(8,128)(2,1)}, bf16[512,512]{1,0:T(8,128)(2,1)S(1)}, u32[]{:S(2)}, u32[]{:S(2)}) collective-permute-start(bf16[512,512]{1,0:T(8,128)(2,1)} %get-tuple-element.422), channel_id=1, source_target_pairs={{0,4},{2,6},{4,0},{6,2},{1,5},{3,7},{5,1},{7,3},{8,12},{10,14},{12... | collective-permute-start | bytes 1572872 | tf_op jit(solution)/shard_map/ppermute | solution.py:134
  567.8 35.8 %collective-permute-start.62 = (bf16[512,512]{1,0:T(8,128)(2,1)}, bf16[512,512]{1,0:T(8,128)(2,1)}, u32[]{:S(2)}, u32[]{:S(2)}) collective-permute-start(bf16[512,512]{1,0:T(8,128)(2,1)} %get-tuple-element.423), channel_id=1, source_target_pairs={{0,2},{2,0},{4,6},{6,4},{1,3},{3,1},{5,7},{7,5},{8,10},{10,8},{12,... | collective-permute-start | bytes 1572872 | tf_op jit(solution)/shard_map/ppermute | solution.py:134
  572.1 31.5 %collective-permute-start.59 = (bf16[256,1024]{1,0:T(8,128)(2,1)}, bf16[256,1024]{1,0:T(8,128)(2,1)S(1)}, u32[]{:S(2)}, u32[]{:S(2)}) collective-permute-start(bf16[256,1024]{1,0:T(8,128)(2,1)} %get-tuple-element.418), channel_id=1, source_target_pairs={{0,2},{2,0},{4,6},{6,4},{1,3},{3,1},{5,7},{7,5},{8,10},{10,8},{12,... | collective-permute-start | bytes 1572872 | tf_op jit(solution)/shard_map/ppermute | solution.py:134
  573.6 30.0 %collective-permute-start.60 = (bf16[256,1024]{1,0:T(8,128)(2,1)}, bf16[256,1024]{1,0:T(8,128)(2,1)S(1)}, u32[]{:S(2)}, u32[]{:S(2)}) collective-permute-start(bf16[256,1024]{1,0:T(8,128)(2,1)} %get-tuple-element.419), channel_id=1, source_target_pairs={{0,4},{2,6},{4,0},{6,2},{1,5},{3,7},{5,1},{7,3},{8,12},{10,14},{12... | collective-permute-start | bytes 1572872 | tf_op jit(solution)/shard_map/ppermute | solution.py:134
  635.5 16.1 %collective-permute-start.65 = (bf16[256,512]{1,0:T(8,128)(2,1)}, bf16[256,512]{1,0:T(8,128)(2,1)}, u32[]{:S(2)}, u32[]{:S(2)}) collective-permute-start(bf16[256,512]{1,0:T(8,128)(2,1)} %get-tuple-element.442), channel_id=1, source_target_pairs={{0,2},{2,0},{4,6},{6,4},{1,3},{3,1},{5,7},{7,5},{8,10},{10,8},{12,... | collective-permute-start | bytes 786440 | tf_op jit(solution)/shard_map/ppermute | solution.py:134
  635.5 17.4 %collective-permute-start.66 = (bf16[256,512]{1,0:T(8,128)(2,1)}, bf16[256,512]{1,0:T(8,128)(2,1)}, u32[]{:S(2)}, u32[]{:S(2)}) collective-permute-start(bf16[256,512]{1,0:T(8,128)(2,1)} %get-tuple-element.443), channel_id=1, source_target_pairs={{0,4},{2,6},{4,0},{6,2},{1,5},{3,7},{5,1},{7,3},{8,12},{10,14},{12... | collective-permute-start | bytes 786440 | tf_op jit(solution)/shard_map/ppermute | solution.py:134
  636.7 16.3 %collective-permute-start.63 = (bf16[128,1024]{1,0:T(8,128)(2,1)}, bf16[128,1024]{1,0:T(8,128)(2,1)S(1)}, u32[]{:S(2)}, u32[]{:S(2)}) collective-permute-start(bf16[128,1024]{1,0:T(8,128)(2,1)} %get-tuple-element.620), channel_id=1, source_target_pairs={{0,4},{2,6},{4,0},{6,2},{1,5},{3,7},{5,1},{7,3},{8,12},{10,14},{12... | collective-permute-start | bytes 786440 | tf_op jit(solution)/shard_map/ppermute | solution.py:134
  637.8 25.5 %collective-permute-start.68 = (bf16[512,640]{1,0:T(8,128)(2,1)}, bf16[512,640]{1,0:T(8,128)(2,1)S(1)}, u32[]{:S(2)}, u32[]{:S(2)}) collective-permute-start(bf16[512,640]{1,0:T(8,128)(2,1)} %get-tuple-element.450), channel_id=1, source_target_pairs={{0,4},{2,6},{4,0},{6,2},{1,5},{3,7},{5,1},{7,3},{8,12},{10,14},{12... | collective-permute-start | bytes 1966088 | tf_op jit(solution)/shard_map/ppermute | solution.py:134
  639.0 24.3 %collective-permute-start.69 = (bf16[512,640]{1,0:T(8,128)(2,1)}, bf16[512,640]{1,0:T(8,128)(2,1)S(1)}, u32[]{:S(2)}, u32[]{:S(2)}) collective-permute-start(bf16[512,640]{1,0:T(8,128)(2,1)} %get-tuple-element.451), channel_id=1, source_target_pairs={{0,2},{2,0},{4,6},{6,4},{1,3},{3,1},{5,7},{7,5},{8,10},{10,8},{12,... | collective-permute-start | bytes 1966088 | tf_op jit(solution)/shard_map/ppermute | solution.py:134
  652.9 29.5 %collective-permute-start.84 = (f32[192,128]{1,0:T(8,128)}, f32[192,128]{1,0:T(8,128)}, u32[]{:S(2)}, u32[]{:S(2)}) collective-permute-start(f32[192,128]{1,0:T(8,128)} %constant_dynamic-update-slice_fusion.7), channel_id=1, source_target_pairs={{0,8},{8,0},{16,24},{24,16},{1,9},{9,1},{17,25},{25,17},{2,10},{10... | collective-permute-start | bytes 294920 | tf_op jit(solution)/shard_map/ppermute | solution.py:476
  668.1 28.1 %collective-permute-start.82 = (bf16[256,640]{1,0:T(8,128)(2,1)}, bf16[256,640]{1,0:T(8,128)(2,1)S(1)}, u32[]{:S(2)}, u32[]{:S(2)}) collective-permute-start(bf16[256,640]{1,0:T(8,128)(2,1)} %get-tuple-element.473), channel_id=1, source_target_pairs={{0,2},{2,0},{4,6},{6,4},{1,3},{3,1},{5,7},{7,5},{8,10},{10,8},{12,... | collective-permute-start | bytes 983048 | tf_op jit(solution)/shard_map/ppermute | solution.py:134
  677.8 12.8 %collective-permute-start.76 = (bf16[256,512]{1,0:T(8,128)(2,1)S(1)}, bf16[256,512]{1,0:T(8,128)(2,1)S(1)}, u32[]{:S(2)}, u32[]{:S(2)}) collective-permute-start(bf16[256,512]{1,0:T(8,128)(2,1)S(1)} %get-tuple-element.636), channel_id=1, source_target_pairs={{0,2},{2,6},{4,0},{6,4},{1,3},{3,7},{5,1},{7,5},{8,10},{10,14},{12... | collective-permute-start | bytes 786440 | tf_op jit(solution)/shard_map/ppermute | solution.py:96
  682.5 13.8 %collective-permute-start.83 = (bf16[256,640]{1,0:T(8,128)(2,1)S(1)}, bf16[256,640]{1,0:T(8,128)(2,1)S(1)}, u32[]{:S(2)}, u32[]{:S(2)}) collective-permute-start(bf16[256,640]{1,0:T(8,128)(2,1)S(1)} %copy-done.144), channel_id=1, source_target_pairs={{0,4},{2,6},{4,0},{6,2},{1,5},{3,7},{5,1},{7,3},{8,12},{10,14},{12... | collective-permute-start | bytes 983048 | tf_op jit(solution)/shard_map/ppermute | solution.py:134
  701.0 23.5 %collective-permute-start.85 = (bf16[64,1280]{1,0:T(8,128)(2,1)S(1)}, bf16[64,1280]{1,0:T(8,128)(2,1)S(1)}, u32[]{:S(2)}, u32[]{:S(2)}) collective-permute-start(bf16[64,1280]{1,0:T(8,128)(2,1)S(1)} %get-tuple-element.625), channel_id=1, source_target_pairs={{0,8},{8,0},{16,24},{24,16},{1,9},{9,1},{17,25},{25,17},{2,10},{10... | collective-permute-start | bytes 491528 | tf_op jit(solution)/shard_map/ppermute | solution.py:383
  703.1 21.4 %collective-permute-start.86 = (bf16[64,1280]{1,0:T(8,128)(2,1)S(1)}, bf16[64,1280]{1,0:T(8,128)(2,1)S(1)}, u32[]{:S(2)}, u32[]{:S(2)}) collective-permute-start(bf16[64,1280]{1,0:T(8,128)(2,1)S(1)} %get-tuple-element.624), channel_id=1, source_target_pairs={{0,16},{8,24},{16,0},{24,8},{1,17},{9,25},{17,1},{25,9},{2,18},{10... | collective-permute-start | bytes 491528 | tf_op jit(solution)/shard_map/ppermute | solution.py:383
  704.1 20.5 %collective-permute-start.87 = (bf16[64,1280]{1,0:T(8,128)(2,1)S(1)}, bf16[64,1280]{1,0:T(8,128)(2,1)S(1)}, u32[]{:S(2)}, u32[]{:S(2)}) collective-permute-start(bf16[64,1280]{1,0:T(8,128)(2,1)S(1)} %get-tuple-element.623), channel_id=1, source_target_pairs={{0,24},{8,16},{16,8},{24,0},{1,25},{9,17},{17,9},{25,1},{2,26},{10... | collective-permute-start | bytes 491528 | tf_op jit(solution)/shard_map/ppermute | solution.py:383
  710.6 13.9 %collective-permute-start.88 = (f32[192,128]{1,0:T(8,128)S(1)}, f32[192,128]{1,0:T(8,128)S(1)}, u32[]{:S(2)}, u32[]{:S(2)}) collective-permute-start(f32[192,128]{1,0:T(8,128)S(1)} %add.344), channel_id=1, source_target_pairs={{0,16},{8,24},{16,0},{24,8},{1,17},{9,25},{17,1},{25,9},{2,18},{10... | collective-permute-start | bytes 294920 | tf_op jit(solution)/shard_map/ppermute | solution.py:476
  (203 other events, 2175.3 us)
Sparse Core Ops, SparseCore 0:
  43.4 41.2 all-gather.10
  86.3 34.2 all-gather.12
  122.1 45.5 all-gather.14
  169.1 79.5 all-gather.18
  250.6 44.4 all-gather.16
  324.7 75.1 reduce-scatter.5
  447.6 25.3 reduce-scatter.13
  488.0 76.6 reduce-scatter.7
  567.1 29.4 reduce-scatter.11
  633.4 24.1 reduce-scatter.9

commit v5 on v4

--- a/solution.py
+++ b/solution.py
@@ -1322,7 +1322,7 @@
         projected, side, rim, taps, heads, rows, channels
     )
     parcel = next_half(parcel_out, True)
-    attended, log_total = attend(place, queries, kv, kv_came, rows)
+    attended, log_total = attend(place, queries, kv, kv_came, 2 * rows)
     if layer > 0:
         moves, parcel = together(moves, parcel)
         mlp_w = late[len(late) // 2 + layer]
@@ -1406,7 +1406,7 @@
     later = scatters.step(later)
     if split:
         mid = jnp.concatenate([grad_gate, grad_q], axis=1)
-        table = scatters.add([(normed, mid)], 512, True, (0, 0), functools.partial(done, 2))
+        table = scatters.add([(normed, mid)], 512, None, (0, 0), functools.partial(done, 2))
         _, later = together((table,), later)
     dstk, drim, grad_step, dtaps, dheads = scan_back(
         du, x, bc, stk, rim, cum, all_cum, step, side, first, parcel, later, taps, heads, rows

time: 783 us -> 774 us (0.989)
  waiting for transfers between devices: 168 us -> 160 us
    unnamed x343 -> x331, local copies, waits for them, and re-layouts: 28.9 us -> 28.7 us
  transfers between devices with their start and end apart: 108 -> 106, of which waited for: 37 -> 37; matrix products, arithmetic and copies ran while one was open for 23% -> 23% of each run, Pallas kernels for 25% -> 25%
where the time goes in v5:
time: 774 us; the launch traced here: 765 us
  Pallas kernels  216 us (28%)
  waiting for transfers between devices  160 us (21%)
  starting transfers between devices  134 us (17%)
  matrix products  87 us (11%)
  local copies, waits for them, and re-layouts  86.4 us (11%)
  other arithmetic  64 us (8%)
  between operations  17.2 us (2%)
    ppermute x48, waiting for transfers between devices, ctx_swap(): return lax.ppermute(values, 'ctx', xor_pairs(lax.axis_size('ctx'), step))  82.5 us
    dot_general x15, matrix products, dot(): lax.dot_general(a, b, (((ca,), (cb,)), ((), ())), preferred_element_type=...  47.1 us
    ppermute x48, starting transfers between devices, ctx_swap(): return lax.ppermute(values, 'ctx', xor_pairs(lax.axis_size('ctx'), step))  43.4 us
    dot_general x16, matrix products, product(): return jnp.dot(a, b, preferred_element_type=WIDE)  39.9 us
    pallas_call x14, Pallas kernels, once(): kernel_call(body, (1,), [whole(v.shape) for v in operands], [whole(shape)...  38.4 us
    pallas_call x2, Pallas kernels, scan_back(): kernel_call(scan_back_body, (count,), [back_block(channels), back_block(c...  36.1 us
    ppermute x12, waiting for transfers between devices, next_half(): lax.ppermute(x, 'ctx', [(i, i + 1) if forward else (i + 1, i) for i in fi...  35 us
    ppermute x13, starting transfers between devices, tp_peer(): return lax.ppermute(x, 'tp', xor_pairs(lax.axis_size('tp'), 1))  34.8 us
  transfers between devices with their start and end apart: 106, of which 37 were waited for; matrix products, arithmetic and copies ran while one was open for 23% of the time, Pallas kernels for 25%

profile of v5, /device:TPU:1, one launch (start us, length us, event | category | flops | bytes accessed | tf_op | source)
XLA Modules:
  0.0 764.7 jit_solution(15313106303599734690)
XLA Ops:
  21.2 4.0 collective-permute-done.2
  34.1 3.9 collective-permute-done.1
  50.9 3.4 pad_maximum_fusion.3
  56.5 10.9 %collective-permute-done.7 = bf16[4,64,1920]{2,1,0:T(8,128)(2,1)} collective-permute-done((bf16[4,64,1920]{2,1,0:T(8,128)(2,1)}, bf16[4,64,1920]{2,1,0:T(8,128)(2,1)}, u32[]{:S(2)}, u32[]{:S(2)}) %collective-permute-start.7) | collective-permute-done | bytes 983072 | tf_op jit(solution)/shard_map/ppermute | solution.py:134
  67.4 7.1 collective-permute-start.9
  81.9 6.8 collective-permute-done.12
  89.6 6.5 fusion.72.rows_ref.zx_ref.gate_ref
  119.8 9.2 %shard_map.265 = (bf16[512,1024]{1,0:T(8,128)(2,1)}, bf16[512,768]{1,0:T(8,128)(2,1)}, bf16[512,256]{1,0:T(8,128)(2,1)}, f32[512,768]{1,0:T(8,128)}, f32[768,128...) custom-call(f32[512,1920]{1,0:T(8,128)} %fusion.72.rows_ref.zx_ref.gate, ...), custom_call_target="tpu_custom_call" | custom-call | flops 805306368 | bytes 8388608 | tf_op jit(solution)/shard_map/pallas_call | solution.py:812
  131.1 5.3 shard_map.264
  136.4 17.8 %collective-permute-done.16.parcel_ref = bf16[784,128]{1,0:T(8,128)(2,1)S(1)} collective-permute-done((bf16[784,128]{1,0:T(8,128)(2,1)}, bf16[784,128]{1,0:T(8,128)(2,1)S(1)}, u32[]{:S(2)}, u32[]{:S(2)}) %collective-permute-start.16) | collective-permute-done | bytes 200736 | tf_op jit(solution)/shard_map/ppermute | solution.py:72
  163.2 4.9 shard_map.266
  172.4 4.3 collective-permute-done.20
  178.3 3.6 pad_maximum_fusion
  194.2 16.0 %collective-permute-done.22 = bf16[4,64,1920]{2,1,0:T(8,128)(2,1)S(1)} collective-permute-done((bf16[4,64,1920]{2,1,0:T(8,128)(2,1)S(1)}, bf16[4,64,1920]{2,1,0:T(8,128)(2,1)S(1)}, u32[]{:S(2)}, u32[]{:S(2)}) %collective-permute-start.22) | collective-permute-done | bytes 983072 | tf_op jit(solution)/shard_map/ppermute | solution.py:134
  212.5 3.9 convolution_convert_fusion.2
  221.0 9.5 %collective-permute-done.25 = bf16[4,64,896]{2,1,0:T(8,128)(2,1)S(1)} collective-permute-done((bf16[4,64,896]{2,1,0:T(8,128)(2,1)S(1)}, bf16[4,64,896]{2,1,0:T(8,128)(2,1)S(1)}, u32[]{:S(2)}, u32[]{:S(2)}) %collective-permute-start.25) | collective-permute-done | bytes 458784 | tf_op jit(solution)/shard_map/ppermute | solution.py:134
  256.6 9.4 %shard_map.269 = (bf16[512,1024]{1,0:T(8,128)(2,1)}, bf16[512,768]{1,0:T(8,128)(2,1)}, bf16[512,256]{1,0:T(8,128)(2,1)}, f32[512,768]{1,0:T(8,128)}, f32[768,128...) custom-call(f32[512,1920]{1,0:T(8,128)} %copy-done.2, ...), custom_call_target="tpu_custom_call" | custom-call | flops 805306368 | bytes 8388608 | tf_op jit(solution)/shard_map/pallas_call | solution.py:812
  266.0 3.5 collective-permute-start.31
  269.5 5.3 shard_map.268
  282.1 4.7 shard_map.270
  289.0 6.1 all-gather.17.cloned.1.call-done
  296.2 3.9 convolution_convert_fusion.1
  304.0 3.9 fusion.174
  318.1 6.3 shard_map.271
  324.7 4.4 convolution_convert_fusion
  329.5 5.9 convolution_convert_fusion.3.own_ref
  339.9 3.9 collective-permute-start.39
  344.7 4.6 shard_map.272
  350.9 6.9 shard_map.273
  362.9 7.5 shard_map.274
  374.2 9.1 %shard_map.275 = (bf16[512,256]{1,0:T(8,128)(2,1)}, f32[512,128]{1,0:T(8,128)}, bf16[512,128]{1,0:T(8,128)(2,1)}) custom-call(s32[1]{0:T(128)} %bitcast.23.place_ref, bf16[512,256]{1,0:T(8,128)(2,1)} %get-tuple-element.312.q_ref, bf16[512,256]{1,0:T(8,128)(2,1)} %convolution_convert_fusion.5.grad_ref, f32[512,128]{1,0:T(8,128)} %get-tuple-element.352.total_ref, ...), custom_call_target="tpu_custom_call" | custom-call | flops 2684354560 | bytes 2097152 | tf_op jit(solution)/shard_map/pallas_call | solution.py:643
  384.7 5.6 collective-permute-done.45.refs_0_
  399.0 18.1 %shard_map.277 = (bf16[512,1024]{1,0:T(8,128)(2,1)}, f32[8,1024]{1,0:T(8,128)}, bf16[512,128]{1,0:T(8,128)(2,1)}, f32[2,8,1024]{2,1,0:T(8,128)}, f32[2,8,128]{2,1,0:T(8,128)}) custom-call(f32[512,768]{1,0:T(8,128)} %get-tuple-element.360.du_ref, bf16[512,768]{1,0:T(8,128)(2,1)} %get-tuple-element.327.x_ref, bf16[512,256]{1,0:T(8,128)(2,1)} %get-tuple-element.326.bc_ref, ...), custom_call_target="tpu_custom_call" | custom-call | flops 2013265920 | bytes 12582912 | tf_op jit(solution)/shard_map/pallas_call | solution.py:1138
  418.6 3.6 shard_map.279
  430.4 6.6 shard_map.280
  439.1 4.6 add_convert_fusion.1.own_ref
  443.7 3.6 collective-permute-start.53
  451.9 4.7 shard_map.281
  456.6 10.0 %collective-permute-done.48.from_y_ref = bf16[128,1024]{1,0:T(8,128)(2,1)S(1)} collective-permute-done((bf16[128,1024]{1,0:T(8,128)(2,1)S(1)}, bf16[128,1024]{1,0:T(8,128)(2,1)S(1)}, u32[]{:S(2)}, u32[]{:S(2)}) %collective-permute-start.48) | collective-permute-done | bytes 262176 | tf_op jit(solution)/shard_map/ppermute | solution.py:134
  476.0 3.8 multiply_convert_fusion.1
  481.3 6.3 shard_map.284
  489.2 4.6 fusion.35.own_ref
  493.8 4.9 collective-permute-start.54
  508.3 4.6 shard_map.285
  512.9 3.8 collective-permute-done.71.last_x_ref
  516.7 3.9 shard_map.296
  521.1 7.1 shard_map.286
  531.7 9.0 %shard_map.288 = (bf16[512,256]{1,0:T(8,128)(2,1)}, f32[512,128]{1,0:T(8,128)}, bf16[512,128]{1,0:T(8,128)(2,1)}) custom-call(s32[1]{0:T(128)} %bitcast.23.place_ref, bf16[512,256]{1,0:T(8,128)(2,1)} %get-tuple-element.276.q_ref, bf16[512,256]{1,0:T(8,128)(2,1)} %convolution_convert_fusion.4.grad_ref, f32[512,128]{1,0:T(8,128)} %get-tuple-element.410.total_ref, ...), custom_call_target="tpu_custom_call" | custom-call | flops 2684354560 | bytes 2097152 | tf_op jit(solution)/shard_map/pallas_call | solution.py:643
  542.1 3.5 fusion.28.dn_ref
  545.6 7.5 shard_map.287
  555.3 5.2 collective-permute-done.57.later_ref
  562.9 3.8 shard_map.290
  582.8 18.0 %shard_map.291 = (bf16[512,1024]{1,0:T(8,128)(2,1)}, f32[8,1024]{1,0:T(8,128)}, bf16[512,128]{1,0:T(8,128)(2,1)}, f32[2,8,1024]{2,1,0:T(8,128)}, f32[2,8,128]{2,1,0:T(8,128)}) custom-call(f32[512,768]{1,0:T(8,128)} %get-tuple-element.422.du_ref, bf16[512,768]{1,0:T(8,128)(2,1)} %get-tuple-element.292.x_ref, bf16[512,256]{1,0:T(8,128)(2,1)} %get-tuple-element.291.bc_ref, ...), custom_call_target="tpu_custom_call" | custom-call | flops 2013265920 | bytes 12582912 | tf_op jit(solution)/shard_map/pallas_call | solution.py:1138
  606.8 3.7 shard_map.292
  619.0 4.6 shard_map.295
  623.6 5.1 add_convert_fusion.own_ref
  628.8 4.4 collective-permute-start.70
  640.6 4.6 shard_map.297
  653.0 10.3 %collective-permute-done.64.from_x_ref = bf16[128,1024]{1,0:T(8,128)(2,1)S(1)} collective-permute-done((bf16[128,1024]{1,0:T(8,128)(2,1)S(1)}, bf16[128,1024]{1,0:T(8,128)(2,1)S(1)}, u32[]{:S(2)}, u32[]{:S(2)}) %collective-permute-start.64) | collective-permute-done | bytes 262176 | tf_op jit(solution)/shard_map/ppermute | solution.py:134
  677.2 3.5 fusion.47
  683.1 4.0 collective-permute-start.76
  705.4 9.5 %collective-permute-done.85 = f32[192,128]{1,0:T(8,128)S(1)} collective-permute-done((f32[192,128]{1,0:T(8,128)S(1)}, f32[192,128]{1,0:T(8,128)S(1)}, u32[]{:S(2)}, u32[]{:S(2)}) %collective-permute-start.85) | collective-permute-done | bytes 98336 | tf_op jit(solution)/shard_map/ppermute | solution.py:476
  740.0 4.2 collective-permute-done.93
  744.2 4.8 collective-permute-start.94
  (810 shorter events, 343.6 us)
Async XLA Ops:
  7.2 108.3 %all-gather.11.cloned.1.call-start = ((), (), s32[]{:S(2)}) async-start(), calls=%async_computation.12 | async-start | bytes 1966080 | tf_op jit(solution)/shard_map/all_gather | solution.py:197
  10.6 27.4 %collective-permute-start.5 = (bf16[1,64,4096]{2,1,0:T(8,128)(2,1)}, bf16[1,64,4096]{2,1,0:T(8,128)(2,1)S(1)}, u32[]{:S(2)}, u32[]{:S(2)}) collective-permute-start(bf16[1,64,4096]{2,1,0:T(8,128)(2,1)} %maximum_bitcast_fusion), channel_id=1, source_target_pairs={{0,2},{2,0},{4,6},{6,4},{1,3},{3,1},{5,7},{7,5},{8,10},{10,8},{12,... | collective-permute-start | bytes 1572872 | tf_op jit(solution)/shard_map/ppermute | solution.py:134
  12.7 25.4 %collective-permute-start.6 = (bf16[1,64,4096]{2,1,0:T(8,128)(2,1)}, bf16[1,64,4096]{2,1,0:T(8,128)(2,1)S(1)}, u32[]{:S(2)}, u32[]{:S(2)}) collective-permute-start(bf16[1,64,4096]{2,1,0:T(8,128)(2,1)} %maximum_bitcast_fusion), channel_id=1, source_target_pairs={{0,4},{2,6},{4,0},{6,2},{1,5},{3,7},{5,1},{7,3},{8,12},{10,14},{12... | collective-permute-start | bytes 1572872 | tf_op jit(solution)/shard_map/ppermute | solution.py:134
  18.6 15.5 %collective-permute-start.4 = (bf16[64,1920]{1,0:T(8,128)(2,1)}, bf16[64,1920]{1,0:T(8,128)(2,1)}, u32[]{:S(2)}, u32[]{:S(2)}) collective-permute-start(bf16[64,1920]{1,0:T(8,128)(2,1)} %pad_maximum_fusion.27), channel_id=1, source_target_pairs={{0,24},{8,16},{16,8},{24,0},{1,25},{9,17},{17,9},{25,1},{2,26},{10... | collective-permute-start | bytes 737288 | tf_op jit(solution)/shard_map/ppermute | solution.py:181
  43.2 118.6 %all-gather.13.cloned.1.call-start = ((), (), s32[]{:S(2)}) async-start(), calls=%async_computation.13 | async-start | bytes 1884160 | tf_op jit(solution)/shard_map/all_gather | solution.py:198
  44.8 22.6 %collective-permute-start.7 = (bf16[4,64,1920]{2,1,0:T(8,128)(2,1)}, bf16[4,64,1920]{2,1,0:T(8,128)(2,1)}, u32[]{:S(2)}, u32[]{:S(2)}) collective-permute-start(bf16[4,64,1920]{2,1,0:T(8,128)(2,1)} %bitcast_dynamic-update-slice_fusion), channel_id=1, source_target_pairs={{0,2},{2,0},{4,6},{6,4},{1,3},{3,1},{5,7},{7,5},{8,10},{10,8},{12,... | collective-permute-start | bytes 2949128 | tf_op jit(solution)/shard_map/ppermute | solution.py:134
  46.2 21.2 %collective-permute-start.8 = (bf16[4,64,1920]{2,1,0:T(8,128)(2,1)}, bf16[4,64,1920]{2,1,0:T(8,128)(2,1)}, u32[]{:S(2)}, u32[]{:S(2)}) collective-permute-start(bf16[4,64,1920]{2,1,0:T(8,128)(2,1)} %bitcast_dynamic-update-slice_fusion), channel_id=1, source_target_pairs={{0,4},{2,6},{4,0},{6,2},{1,5},{3,7},{5,1},{7,3},{8,12},{10,14},{12... | collective-permute-start | bytes 2949128 | tf_op jit(solution)/shard_map/ppermute | solution.py:134
  46.6 165.9 %all-gather.15.cloned.1.call-start = ((), (), s32[]{:S(2)}) async-start(), calls=%async_computation.14 | async-start | bytes 2621440 | tf_op jit(solution)/shard_map/all_gather | solution.py:1310
  75.6 13.6 %collective-permute-start.13 = (bf16[4,64,1024]{2,1,0:T(8,128)(2,1)S(1)}, bf16[4,64,1024]{2,1,0:T(8,128)(2,1)S(1)}, u32[]{:S(2)}, u32[]{:S(2)}) collective-permute-start(bf16[4,64,1024]{2,1,0:T(8,128)(2,1)S(1)} %slice.527), channel_id=1, source_target_pairs={{0,2},{2,0},{4,6},{6,4},{1,3},{3,1},{5,7},{7,5},{8,10},{10,8},{12,... | collective-permute-start | bytes 1572872 | tf_op jit(solution)/shard_map/ppermute | solution.py:134
  96.2 180.1 %all-gather.19.cloned.1.call-start = ((), (), s32[]{:S(2)}) async-start(), calls=%async_computation.16 | async-start | bytes 5242880 | tf_op jit(solution)/shard_map/all_gather | solution.py:1310
  115.5 38.6 %collective-permute-start.17 = (bf16[4,64,3072]{2,1,0:T(8,128)(2,1)}, bf16[4,64,3072]{2,1,0:T(8,128)(2,1)}, u32[]{:S(2)}, u32[]{:S(2)}) collective-permute-start(bf16[4,64,3072]{2,1,0:T(8,128)(2,1)} %bitcast.292), channel_id=1, source_target_pairs={{0,2},{2,0},{4,6},{6,4},{1,3},{3,1},{5,7},{7,5},{8,10},{10,8},{12,... | collective-permute-start | bytes 4718600 | tf_op jit(solution)/shard_map/ppermute | solution.py:134
  117.7 37.1 %collective-permute-start.18 = (bf16[4,64,3072]{2,1,0:T(8,128)(2,1)}, bf16[4,64,3072]{2,1,0:T(8,128)(2,1)}, u32[]{:S(2)}, u32[]{:S(2)}) collective-permute-start(bf16[4,64,3072]{2,1,0:T(8,128)(2,1)} %bitcast.293), channel_id=1, source_target_pairs={{0,4},{2,6},{4,0},{6,2},{1,5},{3,7},{5,1},{7,3},{8,12},{10,14},{12... | collective-permute-start | bytes 4718600 | tf_op jit(solution)/shard_map/ppermute | solution.py:134
  129.0 25.1 %collective-permute-start.16 = (bf16[784,128]{1,0:T(8,128)(2,1)}, bf16[784,128]{1,0:T(8,128)(2,1)S(1)}, u32[]{:S(2)}, u32[]{:S(2)}) collective-permute-start(bf16[784,128]{1,0:T(8,128)(2,1)} %get-tuple-element.287), channel_id=1, source_target_pairs={{0,2},{4,6},{1,3},{5,7},{8,10},{12,14},{9,11},{13,15},{16,18},{20,... | collective-permute-start | bytes 602120 | tf_op jit(solution)/shard_map/ppermute | solution.py:72
  131.0 164.1 %all-gather.17.cloned.1.call-start = ((), (), s32[]{:S(2)}) async-start(), calls=%async_computation.15 | async-start | bytes 2621440 | tf_op jit(solution)/shard_map/all_gather | solution.py:1310
  156.0 16.4 %collective-permute-start.19 = (bf16[4,64,1536]{2,1,0:T(8,128)(2,1)S(1)}, bf16[4,64,1536]{2,1,0:T(8,128)(2,1)}, u32[]{:S(2)}, u32[]{:S(2)}) collective-permute-start(bf16[4,64,1536]{2,1,0:T(8,128)(2,1)S(1)} %slice.540), channel_id=1, source_target_pairs={{0,4},{2,6},{4,0},{6,2},{1,5},{3,7},{5,1},{7,3},{8,12},{10,14},{12... | collective-permute-start | bytes 2359304 | tf_op jit(solution)/shard_map/ppermute | solution.py:134
  159.1 17.6 %collective-permute-start.20 = (bf16[4,64,1536]{2,1,0:T(8,128)(2,1)}, bf16[4,64,1536]{2,1,0:T(8,128)(2,1)}, u32[]{:S(2)}, u32[]{:S(2)}) collective-permute-start(bf16[4,64,1536]{2,1,0:T(8,128)(2,1)} %slice.541), channel_id=1, source_target_pairs={{0,2},{2,0},{4,6},{6,4},{1,3},{3,1},{5,7},{7,5},{8,10},{10,8},{12,... | collective-permute-start | bytes 2359304 | tf_op jit(solution)/shard_map/ppermute | solution.py:134
  186.7 23.5 %collective-permute-start.22 = (bf16[4,64,1920]{2,1,0:T(8,128)(2,1)S(1)}, bf16[4,64,1920]{2,1,0:T(8,128)(2,1)S(1)}, u32[]{:S(2)}, u32[]{:S(2)}) collective-permute-start(bf16[4,64,1920]{2,1,0:T(8,128)(2,1)S(1)} %slice.671), channel_id=1, source_target_pairs={{0,2},{2,0},{4,6},{6,4},{1,3},{3,1},{5,7},{7,5},{8,10},{10,8},{12,... | collective-permute-start | bytes 2949128 | tf_op jit(solution)/shard_map/ppermute | solution.py:134
  188.2 23.1 %collective-permute-start.23 = (bf16[4,64,1920]{2,1,0:T(8,128)(2,1)S(1)}, bf16[4,64,1920]{2,1,0:T(8,128)(2,1)S(1)}, u32[]{:S(2)}, u32[]{:S(2)}) collective-permute-start(bf16[4,64,1920]{2,1,0:T(8,128)(2,1)S(1)} %slice.671), channel_id=1, source_target_pairs={{0,4},{2,6},{4,0},{6,2},{1,5},{3,7},{5,1},{7,3},{8,12},{10,14},{12... | collective-permute-start | bytes 2949128 | tf_op jit(solution)/shard_map/ppermute | solution.py:134
  216.3 15.6 %collective-permute-start.24 = (bf16[512,1024]{1,0:T(8,128)(2,1)}, bf16[512,1024]{1,0:T(8,128)(2,1)}, u32[]{:S(2)}, u32[]{:S(2)}) collective-permute-start(bf16[512,1024]{1,0:T(8,128)(2,1)} %convolution_convert_fusion.2), channel_id=1, source_target_pairs={{0,1},{1,0},{2,3},{3,2},{4,5},{5,4},{6,7},{7,6},{8,9},{9,8},{10,11... | collective-permute-start | bytes 3145736 | tf_op jit(solution)/shard_map/ppermute | solution.py:101
  218.2 13.6 %collective-permute-start.26 = (bf16[4,64,1024]{2,1,0:T(8,128)(2,1)S(1)}, bf16[4,64,1024]{2,1,0:T(8,128)(2,1)S(1)}, u32[]{:S(2)}, u32[]{:S(2)}) collective-permute-start(bf16[4,64,1024]{2,1,0:T(8,128)(2,1)S(1)} %slice.548), channel_id=1, source_target_pairs={{0,2},{2,0},{4,6},{6,4},{1,3},{3,1},{5,7},{7,5},{8,10},{10,8},{12,... | collective-permute-start | bytes 1572872 | tf_op jit(solution)/shard_map/ppermute | solution.py:134
  220.6 196.5 %reduce-scatter.7.cloned.1.call-start = ((), (), s32[]{:S(2)}) async-start(), calls=%async_computation.6 | async-start | bytes 5242880 | tf_op jit(solution)/shard_map/reduce_scatter | solution.py:412
  249.5 26.8 %collective-permute-start.32 = (bf16[4,64,1024]{2,1,0:T(8,128)(2,1)S(1)}, bf16[4,64,1024]{2,1,0:T(8,128)(2,1)S(1)}, u32[]{:S(2)}, u32[]{:S(2)}) collective-permute-start(bf16[4,64,1024]{2,1,0:T(8,128)(2,1)S(1)} %slice.682), channel_id=1, source_target_pairs={{0,2},{2,0},{4,6},{6,4},{1,3},{3,1},{5,7},{7,5},{8,10},{10,8},{12,... | collective-permute-start | bytes 1572872 | tf_op jit(solution)/shard_map/ppermute | solution.py:134
  251.5 24.7 %collective-permute-start.33 = (bf16[4,64,1024]{2,1,0:T(8,128)(2,1)S(1)}, bf16[4,64,1024]{2,1,0:T(8,128)(2,1)}, u32[]{:S(2)}, u32[]{:S(2)}) collective-permute-start(bf16[4,64,1024]{2,1,0:T(8,128)(2,1)S(1)} %slice.682), channel_id=1, source_target_pairs={{0,4},{2,6},{4,0},{6,2},{1,5},{3,7},{5,1},{7,3},{8,12},{10,14},{12... | collective-permute-start | bytes 1572872 | tf_op jit(solution)/shard_map/ppermute | solution.py:134
  253.5 21.4 %collective-permute-start.29 = (bf16[256,512]{1,0:T(8,128)(2,1)S(1)}, bf16[256,512]{1,0:T(8,128)(2,1)S(1)}, u32[]{:S(2)}, u32[]{:S(2)}) collective-permute-start(bf16[256,512]{1,0:T(8,128)(2,1)S(1)} %get-tuple-element.633), channel_id=1, source_target_pairs={{0,0},{4,2},{2,4},{6,6},{1,1},{5,3},{3,5},{7,7},{8,8},{12,10},{10,... | collective-permute-start | bytes 786440 | tf_op jit(solution)/shard_map/ppermute | solution.py:81
  254.1 20.7 %collective-permute-start.30 = (bf16[256,512]{1,0:T(8,128)(2,1)S(1)}, bf16[256,512]{1,0:T(8,128)(2,1)S(1)}, u32[]{:S(2)}, u32[]{:S(2)}) collective-permute-start(bf16[256,512]{1,0:T(8,128)(2,1)S(1)} %get-tuple-element.632), channel_id=1, source_target_pairs={{2,0},{6,2},{0,4},{4,6},{3,1},{7,3},{1,5},{5,7},{10,8},{14,10},{8,... | collective-permute-start | bytes 786440 | tf_op jit(solution)/shard_map/ppermute | solution.py:82
  276.3 18.8 %collective-permute-start.34 = (bf16[4,64,512]{2,1,0:T(8,128)(2,1)S(1)}, bf16[4,64,512]{2,1,0:T(8,128)(2,1)}, u32[]{:S(2)}, u32[]{:S(2)}) collective-permute-start(bf16[4,64,512]{2,1,0:T(8,128)(2,1)S(1)} %slice.563), channel_id=1, source_target_pairs={{0,4},{2,6},{4,0},{6,2},{1,5},{3,7},{5,1},{7,3},{8,12},{10,14},{12... | collective-permute-start | bytes 786440 | tf_op jit(solution)/shard_map/ppermute | solution.py:134
  279.5 15.6 %collective-permute-start.35 = (bf16[4,64,512]{2,1,0:T(8,128)(2,1)}, bf16[4,64,512]{2,1,0:T(8,128)(2,1)}, u32[]{:S(2)}, u32[]{:S(2)}) collective-permute-start(bf16[4,64,512]{2,1,0:T(8,128)(2,1)} %slice.564), channel_id=1, source_target_pairs={{0,2},{2,0},{4,6},{6,4},{1,3},{3,1},{5,7},{7,5},{8,10},{10,8},{12,... | collective-permute-start | bytes 786440 | tf_op jit(solution)/shard_map/ppermute | solution.py:134
  324.4 181.8 %reduce-scatter.17.cloned.1.call-start = ((), (), s32[]{:S(2)}) async-start(), calls=%async_computation.11 | async-start | bytes 1310720 | tf_op jit(solution)/shard_map/reduce_scatter | solution.py:375
  357.8 32.5 %collective-permute-start.42 = (bf16[512,1024]{1,0:T(8,128)(2,1)}, bf16[512,1024]{1,0:T(8,128)(2,1)S(1)}, u32[]{:S(2)}, u32[]{:S(2)}) collective-permute-start(bf16[512,1024]{1,0:T(8,128)(2,1)} %get-tuple-element.347), channel_id=1, source_target_pairs={{0,4},{2,6},{4,0},{6,2},{1,5},{3,7},{5,1},{7,3},{8,12},{10,14},{12... | collective-permute-start | bytes 3145736 | tf_op jit(solution)/shard_map/ppermute | solution.py:134
  359.0 31.4 %collective-permute-start.43 = (bf16[512,1024]{1,0:T(8,128)(2,1)}, bf16[512,1024]{1,0:T(8,128)(2,1)S(1)}, u32[]{:S(2)}, u32[]{:S(2)}) collective-permute-start(bf16[512,1024]{1,0:T(8,128)(2,1)} %get-tuple-element.348), channel_id=1, source_target_pairs={{0,2},{2,0},{4,6},{6,4},{1,3},{3,1},{5,7},{7,5},{8,10},{10,8},{12,... | collective-permute-start | bytes 3145736 | tf_op jit(solution)/shard_map/ppermute | solution.py:134
  370.4 20.0 %collective-permute-start.44 = (bf16[784,128]{1,0:T(8,128)(2,1)}, bf16[784,128]{1,0:T(8,128)(2,1)S(1)}, u32[]{:S(2)}, u32[]{:S(2)}) collective-permute-start(bf16[784,128]{1,0:T(8,128)(2,1)} %get-tuple-element.351), channel_id=1, source_target_pairs={{2,0},{6,4},{3,1},{7,5},{10,8},{14,12},{11,9},{15,13},{18,16},{22,... | collective-permute-start | bytes 602120 | tf_op jit(solution)/shard_map/ppermute | solution.py:72
  394.8 22.3 %collective-permute-start.46 = (bf16[256,1024]{1,0:T(8,128)(2,1)}, bf16[256,1024]{1,0:T(8,128)(2,1)S(1)}, u32[]{:S(2)}, u32[]{:S(2)}) collective-permute-start(bf16[256,1024]{1,0:T(8,128)(2,1)} %get-tuple-element.358), channel_id=1, source_target_pairs={{0,2},{2,0},{4,6},{6,4},{1,3},{3,1},{5,7},{7,5},{8,10},{10,8},{12,... | collective-permute-start | bytes 1572872 | tf_op jit(solution)/shard_map/ppermute | solution.py:134
  394.8 22.3 %collective-permute-start.47 = (bf16[256,1024]{1,0:T(8,128)(2,1)}, bf16[256,1024]{1,0:T(8,128)(2,1)S(1)}, u32[]{:S(2)}, u32[]{:S(2)}) collective-permute-start(bf16[256,1024]{1,0:T(8,128)(2,1)} %get-tuple-element.359), channel_id=1, source_target_pairs={{0,4},{2,6},{4,0},{6,2},{1,5},{3,7},{5,1},{7,3},{8,12},{10,14},{12... | collective-permute-start | bytes 1572872 | tf_op jit(solution)/shard_map/ppermute | solution.py:134
  437.0 32.2 %collective-permute-start.51 = (bf16[512,1152]{1,0:T(8,128)(2,1)}, bf16[512,1152]{1,0:T(8,128)(2,1)S(1)}, u32[]{:S(2)}, u32[]{:S(2)}) collective-permute-start(bf16[512,1152]{1,0:T(8,128)(2,1)} %get-tuple-element.381), channel_id=1, source_target_pairs={{0,4},{2,6},{4,0},{6,2},{1,5},{3,7},{5,1},{7,3},{8,12},{10,14},{12... | collective-permute-start | bytes 3538952 | tf_op jit(solution)/shard_map/ppermute | solution.py:134
  439.0 30.2 %collective-permute-start.52 = (bf16[512,1152]{1,0:T(8,128)(2,1)}, bf16[512,1152]{1,0:T(8,128)(2,1)S(1)}, u32[]{:S(2)}, u32[]{:S(2)}) collective-permute-start(bf16[512,1152]{1,0:T(8,128)(2,1)} %get-tuple-element.382), channel_id=1, source_target_pairs={{0,2},{2,0},{4,6},{6,4},{1,3},{3,1},{5,7},{7,5},{8,10},{10,8},{12,... | collective-permute-start | bytes 3538952 | tf_op jit(solution)/shard_map/ppermute | solution.py:134
  447.3 156.3 %reduce-scatter.9.cloned.1.call-start = ((), (), s32[]{:S(2)}) async-start(), calls=%async_computation.7 | async-start | bytes 5242880 | tf_op jit(solution)/shard_map/reduce_scatter | solution.py:412
  447.3 19.3 %collective-permute-start.48 = (bf16[128,1024]{1,0:T(8,128)(2,1)S(1)}, bf16[128,1024]{1,0:T(8,128)(2,1)S(1)}, u32[]{:S(2)}, u32[]{:S(2)}) collective-permute-start(bf16[128,1024]{1,0:T(8,128)(2,1)S(1)} %get-tuple-element.618), channel_id=1, source_target_pairs={{0,4},{2,6},{4,0},{6,2},{1,5},{3,7},{5,1},{7,3},{8,12},{10,14},{12... | collective-permute-start | bytes 786440 | tf_op jit(solution)/shard_map/ppermute | solution.py:134
  448.3 20.9 %collective-permute-start.49 = (bf16[128,1024]{1,0:T(8,128)(2,1)S(1)}, bf16[128,1024]{1,0:T(8,128)(2,1)S(1)}, u32[]{:S(2)}, u32[]{:S(2)}) collective-permute-start(bf16[128,1024]{1,0:T(8,128)(2,1)S(1)} %get-tuple-element.617), channel_id=1, source_target_pairs={{0,2},{2,0},{4,6},{6,4},{1,3},{3,1},{5,7},{7,5},{8,10},{10,8},{12,... | collective-permute-start | bytes 786440 | tf_op jit(solution)/shard_map/ppermute | solution.py:134
  487.7 125.2 %reduce-scatter.15.cloned.1.call-start = ((), (), s32[]{:S(2)}) async-start(), calls=%async_computation.10 | async-start | bytes 1474560 | tf_op jit(solution)/shard_map/reduce_scatter | solution.py:375
  493.8 13.5 %collective-permute-start.54 = (bf16[512,1024]{1,0:T(8,128)(2,1)S(1)}, bf16[512,1024]{1,0:T(8,128)(2,1)S(1)}, u32[]{:S(2)}, u32[]{:S(2)}) collective-permute-start(bf16[512,1024]{1,0:T(8,128)(2,1)S(1)} %fusion.35.own_ref), channel_id=1, source_target_pairs={{0,1},{1,0},{2,3},{3,2},{4,5},{5,4},{6,7},{7,6},{8,9},{9,8},{10,11... | collective-permute-start | bytes 3145736 | tf_op jit(solution)/shard_map/ppermute | solution.py:101
  498.6 18.0 %collective-permute-start.73 = (bf16[256,1152]{1,0:T(8,128)(2,1)}, bf16[256,1152]{1,0:T(8,128)(2,1)}, u32[]{:S(2)}, u32[]{:S(2)}) collective-permute-start(bf16[256,1152]{1,0:T(8,128)(2,1)} %get-tuple-element.395), channel_id=1, source_target_pairs={{0,2},{2,0},{4,6},{6,4},{1,3},{3,1},{5,7},{7,5},{8,10},{10,8},{12,... | collective-permute-start | bytes 1769480 | tf_op jit(solution)/shard_map/ppermute | solution.py:134
  498.6 18.0 %collective-permute-start.74 = (bf16[256,1152]{1,0:T(8,128)(2,1)}, bf16[256,1152]{1,0:T(8,128)(2,1)}, u32[]{:S(2)}, u32[]{:S(2)}) collective-permute-start(bf16[256,1152]{1,0:T(8,128)(2,1)} %get-tuple-element.396), channel_id=1, source_target_pairs={{0,4},{2,6},{4,0},{6,2},{1,5},{3,7},{5,1},{7,3},{8,12},{10,14},{12... | collective-permute-start | bytes 1769480 | tf_op jit(solution)/shard_map/ppermute | solution.py:134
  520.6 142.7 %reduce-scatter.11.cloned.1.call-start = ((), (), s32[]{:S(2)}) async-start(), calls=%async_computation.8 | async-start | bytes 1310720 | tf_op jit(solution)/shard_map/reduce_scatter | solution.py:375
  528.2 39.5 %collective-permute-start.55 = (bf16[512,1024]{1,0:T(8,128)(2,1)}, bf16[512,1024]{1,0:T(8,128)(2,1)S(1)}, u32[]{:S(2)}, u32[]{:S(2)}) collective-permute-start(bf16[512,1024]{1,0:T(8,128)(2,1)} %get-tuple-element.405), channel_id=1, source_target_pairs={{0,4},{2,6},{4,0},{6,2},{1,5},{3,7},{5,1},{7,3},{8,12},{10,14},{12... | collective-permute-start | bytes 3145736 | tf_op jit(solution)/shard_map/ppermute | solution.py:134
  528.3 39.4 %collective-permute-start.56 = (bf16[512,1024]{1,0:T(8,128)(2,1)}, bf16[512,1024]{1,0:T(8,128)(2,1)S(1)}, u32[]{:S(2)}, u32[]{:S(2)}) collective-permute-start(bf16[512,1024]{1,0:T(8,128)(2,1)} %get-tuple-element.406), channel_id=1, source_target_pairs={{0,2},{2,0},{4,6},{6,4},{1,3},{3,1},{5,7},{7,5},{8,10},{10,8},{12,... | collective-permute-start | bytes 3145736 | tf_op jit(solution)/shard_map/ppermute | solution.py:134
  540.8 14.5 %collective-permute-start.58 = (bf16[512,128]{1,0:T(8,128)(2,1)}, bf16[512,128]{1,0:T(8,128)(2,1)S(1)}, u32[]{:S(2)}, u32[]{:S(2)}) collective-permute-start(bf16[512,128]{1,0:T(8,128)(2,1)} %get-tuple-element.411), channel_id=1, source_target_pairs={{2,0},{6,4},{3,1},{7,5},{10,8},{14,12},{11,9},{15,13},{18,16},{22,... | collective-permute-start | bytes 393224 | tf_op jit(solution)/shard_map/ppermute | solution.py:72
  566.7 36.8 %collective-permute-start.61 = (bf16[512,512]{1,0:T(8,128)(2,1)}, bf16[512,512]{1,0:T(8,128)(2,1)S(1)}, u32[]{:S(2)}, u32[]{:S(2)}) collective-permute-start(bf16[512,512]{1,0:T(8,128)(2,1)} %get-tuple-element.420), channel_id=1, source_target_pairs={{0,4},{2,6},{4,0},{6,2},{1,5},{3,7},{5,1},{7,3},{8,12},{10,14},{12... | collective-permute-start | bytes 1572872 | tf_op jit(solution)/shard_map/ppermute | solution.py:134
  567.7 35.9 %collective-permute-start.62 = (bf16[512,512]{1,0:T(8,128)(2,1)}, bf16[512,512]{1,0:T(8,128)(2,1)}, u32[]{:S(2)}, u32[]{:S(2)}) collective-permute-start(bf16[512,512]{1,0:T(8,128)(2,1)} %get-tuple-element.421), channel_id=1, source_target_pairs={{0,2},{2,0},{4,6},{6,4},{1,3},{3,1},{5,7},{7,5},{8,10},{10,8},{12,... | collective-permute-start | bytes 1572872 | tf_op jit(solution)/shard_map/ppermute | solution.py:134
  572.0 31.5 %collective-permute-start.59 = (bf16[256,1024]{1,0:T(8,128)(2,1)}, bf16[256,1024]{1,0:T(8,128)(2,1)S(1)}, u32[]{:S(2)}, u32[]{:S(2)}) collective-permute-start(bf16[256,1024]{1,0:T(8,128)(2,1)} %get-tuple-element.416), channel_id=1, source_target_pairs={{0,2},{2,0},{4,6},{6,4},{1,3},{3,1},{5,7},{7,5},{8,10},{10,8},{12,... | collective-permute-start | bytes 1572872 | tf_op jit(solution)/shard_map/ppermute | solution.py:134
  573.5 30.1 %collective-permute-start.60 = (bf16[256,1024]{1,0:T(8,128)(2,1)}, bf16[256,1024]{1,0:T(8,128)(2,1)S(1)}, u32[]{:S(2)}, u32[]{:S(2)}) collective-permute-start(bf16[256,1024]{1,0:T(8,128)(2,1)} %get-tuple-element.417), channel_id=1, source_target_pairs={{0,4},{2,6},{4,0},{6,2},{1,5},{3,7},{5,1},{7,3},{8,12},{10,14},{12... | collective-permute-start | bytes 1572872 | tf_op jit(solution)/shard_map/ppermute | solution.py:134
  633.2 57.7 %reduce-scatter.13.cloned.1.call-start = ((), (), s32[]{:S(2)}) async-start(), calls=%async_computation.9 | async-start | bytes 655360 | tf_op jit(solution)/shard_map/reduce_scatter | solution.py:375
  635.5 16.2 %collective-permute-start.65 = (bf16[256,512]{1,0:T(8,128)(2,1)}, bf16[256,512]{1,0:T(8,128)(2,1)}, u32[]{:S(2)}, u32[]{:S(2)}) collective-permute-start(bf16[256,512]{1,0:T(8,128)(2,1)} %get-tuple-element.440), channel_id=1, source_target_pairs={{0,2},{2,0},{4,6},{6,4},{1,3},{3,1},{5,7},{7,5},{8,10},{10,8},{12,... | collective-permute-start | bytes 786440 | tf_op jit(solution)/shard_map/ppermute | solution.py:134
  635.5 17.4 %collective-permute-start.66 = (bf16[256,512]{1,0:T(8,128)(2,1)}, bf16[256,512]{1,0:T(8,128)(2,1)}, u32[]{:S(2)}, u32[]{:S(2)}) collective-permute-start(bf16[256,512]{1,0:T(8,128)(2,1)} %get-tuple-element.441), channel_id=1, source_target_pairs={{0,4},{2,6},{4,0},{6,2},{1,5},{3,7},{5,1},{7,3},{8,12},{10,14},{12... | collective-permute-start | bytes 786440 | tf_op jit(solution)/shard_map/ppermute | solution.py:134
  636.7 16.3 %collective-permute-start.63 = (bf16[128,1024]{1,0:T(8,128)(2,1)}, bf16[128,1024]{1,0:T(8,128)(2,1)S(1)}, u32[]{:S(2)}, u32[]{:S(2)}) collective-permute-start(bf16[128,1024]{1,0:T(8,128)(2,1)} %get-tuple-element.616), channel_id=1, source_target_pairs={{0,4},{2,6},{4,0},{6,2},{1,5},{3,7},{5,1},{7,3},{8,12},{10,14},{12... | collective-permute-start | bytes 786440 | tf_op jit(solution)/shard_map/ppermute | solution.py:134
  637.8 25.5 %collective-permute-start.68 = (bf16[512,640]{1,0:T(8,128)(2,1)}, bf16[512,640]{1,0:T(8,128)(2,1)S(1)}, u32[]{:S(2)}, u32[]{:S(2)}) collective-permute-start(bf16[512,640]{1,0:T(8,128)(2,1)} %get-tuple-element.448), channel_id=1, source_target_pairs={{0,4},{2,6},{4,0},{6,2},{1,5},{3,7},{5,1},{7,3},{8,12},{10,14},{12... | collective-permute-start | bytes 1966088 | tf_op jit(solution)/shard_map/ppermute | solution.py:134
  639.1 24.2 %collective-permute-start.69 = (bf16[512,640]{1,0:T(8,128)(2,1)}, bf16[512,640]{1,0:T(8,128)(2,1)S(1)}, u32[]{:S(2)}, u32[]{:S(2)}) collective-permute-start(bf16[512,640]{1,0:T(8,128)(2,1)} %get-tuple-element.449), channel_id=1, source_target_pairs={{0,2},{2,0},{4,6},{6,4},{1,3},{3,1},{5,7},{7,5},{8,10},{10,8},{12,... | collective-permute-start | bytes 1966088 | tf_op jit(solution)/shard_map/ppermute | solution.py:134
  652.9 29.5 %collective-permute-start.81 = (f32[192,128]{1,0:T(8,128)}, f32[192,128]{1,0:T(8,128)}, u32[]{:S(2)}, u32[]{:S(2)}) collective-permute-start(f32[192,128]{1,0:T(8,128)} %constant_dynamic-update-slice_fusion.7), channel_id=1, source_target_pairs={{0,8},{8,0},{16,24},{24,16},{1,9},{9,1},{17,25},{25,17},{2,10},{10... | collective-permute-start | bytes 294920 | tf_op jit(solution)/shard_map/ppermute | solution.py:476
  668.7 19.7 %collective-permute-start.79 = (bf16[256,640]{1,0:T(8,128)(2,1)}, bf16[256,640]{1,0:T(8,128)(2,1)}, u32[]{:S(2)}, u32[]{:S(2)}) collective-permute-start(bf16[256,640]{1,0:T(8,128)(2,1)} %get-tuple-element.471), channel_id=1, source_target_pairs={{0,2},{2,0},{4,6},{6,4},{1,3},{3,1},{5,7},{7,5},{8,10},{10,8},{12,... | collective-permute-start | bytes 983048 | tf_op jit(solution)/shard_map/ppermute | solution.py:134
  669.9 18.5 %collective-permute-start.80 = (bf16[256,640]{1,0:T(8,128)(2,1)}, bf16[256,640]{1,0:T(8,128)(2,1)}, u32[]{:S(2)}, u32[]{:S(2)}) collective-permute-start(bf16[256,640]{1,0:T(8,128)(2,1)} %get-tuple-element.472), channel_id=1, source_target_pairs={{0,4},{2,6},{4,0},{6,2},{1,5},{3,7},{5,1},{7,3},{8,12},{10,14},{12... | collective-permute-start | bytes 983048 | tf_op jit(solution)/shard_map/ppermute | solution.py:134
  682.4 16.0 %collective-permute-start.75 = (bf16[256,512]{1,0:T(8,128)(2,1)S(1)}, bf16[256,512]{1,0:T(8,128)(2,1)S(1)}, u32[]{:S(2)}, u32[]{:S(2)}) collective-permute-start(bf16[256,512]{1,0:T(8,128)(2,1)S(1)} %get-tuple-element.628), channel_id=1, source_target_pairs={{0,0},{2,4},{4,2},{6,6},{1,1},{3,5},{5,3},{7,7},{8,8},{10,12},{12,... | collective-permute-start | bytes 786440 | tf_op jit(solution)/shard_map/ppermute | solution.py:95
  683.1 15.3 %collective-permute-start.76 = (bf16[256,512]{1,0:T(8,128)(2,1)S(1)}, bf16[256,512]{1,0:T(8,128)(2,1)S(1)}, u32[]{:S(2)}, u32[]{:S(2)}) collective-permute-start(bf16[256,512]{1,0:T(8,128)(2,1)S(1)} %get-tuple-element.629), channel_id=1, source_target_pairs={{0,2},{2,6},{4,0},{6,4},{1,3},{3,7},{5,1},{7,5},{8,10},{10,14},{12... | collective-permute-start | bytes 786440 | tf_op jit(solution)/shard_map/ppermute | solution.py:96
  694.8 20.1 %collective-permute-start.82 = (bf16[64,1280]{1,0:T(8,128)(2,1)S(1)}, bf16[64,1280]{1,0:T(8,128)(2,1)S(1)}, u32[]{:S(2)}, u32[]{:S(2)}) collective-permute-start(bf16[64,1280]{1,0:T(8,128)(2,1)S(1)} %get-tuple-element.621), channel_id=1, source_target_pairs={{0,8},{8,0},{16,24},{24,16},{1,9},{9,1},{17,25},{25,17},{2,10},{10... | collective-permute-start | bytes 491528 | tf_op jit(solution)/shard_map/ppermute | solution.py:383
  694.9 20.0 %collective-permute-start.83 = (bf16[64,1280]{1,0:T(8,128)(2,1)S(1)}, bf16[64,1280]{1,0:T(8,128)(2,1)S(1)}, u32[]{:S(2)}, u32[]{:S(2)}) collective-permute-start(bf16[64,1280]{1,0:T(8,128)(2,1)S(1)} %get-tuple-element.620), channel_id=1, source_target_pairs={{0,16},{8,24},{16,0},{24,8},{1,17},{9,25},{17,1},{25,9},{2,18},{10... | collective-permute-start | bytes 491528 | tf_op jit(solution)/shard_map/ppermute | solution.py:383
  696.6 18.3 %collective-permute-start.84 = (bf16[64,1280]{1,0:T(8,128)(2,1)S(1)}, bf16[64,1280]{1,0:T(8,128)(2,1)S(1)}, u32[]{:S(2)}, u32[]{:S(2)}) collective-permute-start(bf16[64,1280]{1,0:T(8,128)(2,1)S(1)} %get-tuple-element.619), channel_id=1, source_target_pairs={{0,24},{8,16},{16,8},{24,0},{1,25},{9,17},{17,9},{25,1},{2,26},{10... | collective-permute-start | bytes 491528 | tf_op jit(solution)/shard_map/ppermute | solution.py:383
  (193 other events, 2106.9 us)
Sparse Core Ops, SparseCore 0:
  43.3 41.2 all-gather.10
  86.3 34.2 all-gather.12
  122.1 45.5 all-gather.14
  169.1 79.5 all-gather.18
  250.6 44.4 all-gather.16
  324.6 75.2 reduce-scatter.6
  447.4 25.4 reduce-scatter.16
  487.8 76.6 reduce-scatter.8
  566.9 29.5 reduce-scatter.14
  633.4 24.1 reduce-scatter.10
  673.8 17.0 reduce-scatter.12
